TPU v7x, 128 devices: a whole 4x4x4 slice. The times are simulated.
128 devices in a mesh: row: 16 (over y, z), col: 8 (over x, core).
Axes of the slice: x: 4, y: 4, z: 4, core: 2. Of those that a mesh axis runs over, the one named last changes fastest.
Arguments:
- frontal: float32 [16384, 24576], P('row', 'col'), may hold values from -0.0390625 to 0.0390625
- sketch: float32 [24576, 512], P(('col', 'row')), may hold values from -6 to 6
- leaf_ranks: int32 [128], replicated, may hold values from 48 to 96, as said below
- leaf_pivots: int32 [128, 128], replicated, may hold values from 0 to 127, each once within a row
- mid_ranks: int32 [64], replicated, may hold values from 48 to 96, as said below
- mid_pivots: int32 [64, 192], replicated, may hold values from 0 to 191, as said below
- top_ranks: int32 [32], replicated, may hold values from 48 to 96, as said below
- top_pivots: int32 [32, 192], replicated, may hold values from 0 to 191, as said below
Outputs:
- leaf_interp: float32 [128, 96, 128], P(('row', 'col'))
- mid_interp: float32 [128, 96, 192], P(('row', 'col'))
- top_interp: float32 [128, 96, 192], P(('row', 'col'))
- top_rows: float32 [128, 96, 512], P(('row', 'col'))
Inputs may be any that keep to these rules, and one draw needn't show every extreme that they name: `leaf_ranks`: some leaf has rank exactly 96. `mid_ranks`: some parent has rank exactly 96. `top_ranks`: some grandparent has rank exactly 96. `mid_pivots`: each row is a permutation of the slots; slot s < 96 holds row s of the left child's skeleton and slot 96 + s row s of the right child's; the first mid_ranks[j] entries of row j name only slots below the children's ranks. `top_pivots`: each row is a permutation of the slots, built like mid_pivots over the two parents' skeletons with top_ranks.
All inputs are finite; a program needn't handle non-finite values.
Results may differ from a plain program's by a relative error of at most 0.0003.
Values sent between devices are 32-bit elements; how exact they have to be, the bound alone decides.
No kernel may reach another device: no remote copies, remote signals or barrier semaphores. Data moves between devices by JAX's collectives and lax.ppermute only.
A program may use at most 64 MiB of HBM per device.

v0:
```python
import jax
import jax.numpy as jnp
from jax import lax
from jax.sharding import PartitionSpec as P

SAMPLES = 512
KMAX = 96


def from_partner(value, axis, apart):
    mask = 2**apart
    pairs = [(source, source ^ mask) for source in range(lax.axis_size(axis))]
    return lax.ppermute(value, axis, pairs)


def interpolate(candidates, pivots, skeleton_rank):
    slot_ids = jnp.arange(KMAX)
    keep_mask = (slot_ids < skeleton_rank).astype(candidates.dtype)
    skeleton = jnp.take(candidates, pivots[:KMAX], axis=0) * keep_mask[:, None]
    gram_matrix = jnp.dot(skeleton, skeleton.T, precision=lax.Precision.HIGHEST) / SAMPLES
    gram_matrix = gram_matrix + jnp.diag(1.0 - keep_mask)
    cross_terms = jnp.dot(skeleton, candidates.T, precision=lax.Precision.HIGHEST) / SAMPLES
    factor = jnp.linalg.cholesky(gram_matrix)
    solved = jax.scipy.linalg.cho_solve((factor, True), cross_terms)
    return (solved, skeleton)


def pick_entry(table, position):
    return lax.dynamic_index_in_dim(table, position, 0, keepdims=False)


def on_device(
    frontal, sketch, leaf_ranks, leaf_pivots, mid_ranks, mid_pivots, top_ranks, top_pivots
):
    col_count = lax.axis_size("col")
    col_index = lax.axis_index("col")
    leaf_index = lax.axis_index("row") * col_count + col_index
    partial_value = jnp.dot(
        frontal,
        lax.all_gather(sketch, "row", axis=0, tiled=True),
        precision=lax.Precision.HIGHEST,
        preferred_element_type=jnp.float32,
    )
    own_samples = lax.psum_scatter(partial_value, "col", scatter_dimension=0, tiled=True)
    leaf_own, skeleton = interpolate(
        own_samples, pick_entry(leaf_pivots, leaf_index), pick_entry(leaf_ranks, leaf_index)
    )
    sibling = from_partner(skeleton, "col", 0)
    parity = col_index % 2
    mid_rows = jnp.where(
        parity == 0,
        jnp.concatenate([skeleton, sibling], 0),
        jnp.concatenate([sibling, skeleton], 0),
    )
    mid_node = leaf_index // 2
    mid_own, mid_skeleton = interpolate(
        mid_rows, pick_entry(mid_pivots, mid_node), pick_entry(mid_ranks, mid_node)
    )
    cousin = from_partner(mid_skeleton, "col", 1)
    upper_half = col_index // 2 % 2
    top_rows_in = jnp.where(
        upper_half == 0,
        jnp.concatenate([mid_skeleton, cousin], 0),
        jnp.concatenate([cousin, mid_skeleton], 0),
    )
    top_node = leaf_index // 4
    top_solved, top_skeleton = interpolate(
        top_rows_in, pick_entry(top_pivots, top_node), pick_entry(top_ranks, top_node)
    )
    return (leaf_own[None], mid_own[None], top_solved[None], top_skeleton[None])


def solution(mesh):
    return jax.shard_map(
        on_device,
        mesh=mesh,
        in_specs=(P("row", "col"), P(("col", "row"), None), P(), P(), P(), P(), P(), P()),
        out_specs=(
            P(("row", "col"), None, None),
            P(("row", "col"), None, None),
            P(("row", "col"), None, None),
            P(("row", "col"), None, None),
        ),
        check_vma=False,
    )
```

profile of v0, /device:TPU:1, one launch (start us, length us, event | category | flops | bytes accessed | tf_op | source)
XLA Modules:
  0.0 204.4 jit_solution(8991993633766723255)
XLA Ops:
  7.2 0.0 copy-start
  7.2 0.0 all-gather.2.cloned.1.call-start
  7.2 0.7 all-gather.2.cloned.1.call-update
  7.9 0.0 copy-start.1
  7.9 0.0 copy-start.2
  7.9 0.0 copy-start.3
  7.9 0.0 reduce-scatter.2.cloned.1.call-start
  8.0 66.9 %all-gather.2.cloned.1.call-done = f32[3072,512]{1,0:T(8,128)} async-done(((f32[192,512]{1,0:T(8,128)}), f32[3072,512]{1,0:T(8,128)}) %all-gather.2.cloned.1.call-update) | async-done | bytes 6291472 | tf_op jit(solution)/shard_map/all_gather | solution.py:40
  74.9 24.3 %fusion.33 = f32[1024,512]{1,0:T(8,128)} fusion(f32[1024,3072]{1,0:T(8,128)} %param.13, f32[3072,512]{1,0:T(8,128)} %all-gather.2.cloned.1.call-done), kind=kOutput, calls=%fused_computation.85 | convolution fusion | flops 19327352832 | bytes 20971520 | tf_op jit(solution)/shard_map/dot_general | solution.py:38
  99.2 0.0 reduce-scatter.2.cloned.1.call-update
  99.2 0.0 copy-done.1
  99.3 0.6 dynamic_slice.25
  99.8 0.0 copy-done.2
  99.8 0.6 dynamic_slice.27
  100.4 0.6 dynamic_slice.29
  101.0 0.6 compare_convert_fusion
  101.7 0.7 broadcast_subtract_fusion
  102.3 0.0 copy-done
  102.4 0.7 broadcast_subtract_fusion.2
  103.0 0.7 broadcast_subtract_fusion.1
  103.7 0.7 compare_and_fusion
  104.4 1.3 compare_and_fusion.1
  105.8 0.7 compare_convert_fusion.2
  106.4 23.2 %reduce-scatter.2.cloned.1.call-done = f32[128,512]{1,0:T(8,128)} async-done(((f32[1024,512]{1,0:T(8,128)}), f32[128,512]{1,0:T(8,128)}) %reduce-scatter.2.cloned.1.call-update) | async-done | bytes 262160 | tf_op jit(solution)/shard_map/reduce_scatter | solution.py:44
  129.6 1.7 gather_fusion
  131.3 0.1 select_multiply_fusion.2
  131.4 3.6 %collective-permute-start = (f32[96,512]{1,0:T(8,128)S(1)}, f32[96,512]{1,0:T(8,128)S(1)}, u32[]{:S(2)}, u32[]{:S(2)}) collective-permute-start(f32[96,512]{1,0:T(8,128)S(1)} %select_multiply_fusion.2), channel_id=1, source_target_pairs={{0,1},{1,0},{2,3},{3,2},{4,5},{5,4},{6,7},{7,6},{8,9},{9,8},{10,11... | collective-permute-start | bytes 589832 | tf_op jit(solution)/shard_map/ppermute | solution.py:13
  135.0 0.3 fusion.2
  135.4 0.1 copy.13
  135.5 8.8 %cholesky.59 = f32[96,96]{1,0:T(8,128)S(1)} custom-call(f32[96,96]{1,0:T(8,128)S(1)} %fusion.24), custom_call_target="Cholesky" | custom-call | tf_op jit(solution)/shard_map/jit(cholesky)/cholesky | solution.py:23
  144.2 0.1 copy.14
  144.3 0.1 select_reduce_fusion.2
  144.5 0.6 compare_reduce_fusion.2
  145.1 0.7 fusion.10
  145.8 0.1 copy.16
  145.9 7.4 %custom-call.14 = f32[1,96,96]{1,2,0:T(8,128)S(1)} custom-call(f32[1,96,96]{2,1,0:T(8,128)S(1)} %copy.16), custom_call_target="InvertDiagBlocksLowerTriangular" | custom-call | tf_op jit(solution)/shard_map/jit(_cho_solve)/triangular_solve | solution.py:24
  153.2 1.3 convolution_multiply_fusion.4
  154.6 0.3 fusion.22
  154.8 0.8 convolution_bitcast_fusion.2
  155.6 0.0 collective-permute-done
  155.7 0.7 gather_fusion.1
  156.4 0.1 select_multiply_fusion.1
  156.5 0.5 convolution_multiply_fusion.1
  157.0 0.3 collective-permute-start.1
  157.3 0.3 fusion.1
  157.6 0.1 copy.18
  157.7 8.8 %cholesky.70 = f32[96,96]{1,0:T(8,128)S(1)} custom-call(f32[96,96]{1,0:T(8,128)S(1)} %fusion.20), custom_call_target="Cholesky" | custom-call | tf_op jit(solution)/shard_map/jit(cholesky)/cholesky | solution.py:23
  166.5 0.6 compare_reduce_fusion.1
  167.2 0.7 fusion.11
  167.8 7.4 %custom-call.16 = f32[1,96,96]{1,2,0:T(8,128)S(1)} custom-call(f32[1,96,96]{2,1,0:T(8,128)S(1)} %fusion.11), custom_call_target="InvertDiagBlocksLowerTriangular" | custom-call | tf_op jit(solution)/shard_map/jit(_cho_solve)/triangular_solve | solution.py:24
  175.2 0.3 fusion.18
  175.5 0.9 convolution_bitcast_fusion.1
  176.4 0.0 collective-permute-done.1
  176.4 0.7 gather_fusion.2
  177.1 0.5 convolution_multiply_fusion
  177.7 0.8 fusion.3
  178.4 0.4 fusion
  178.8 0.1 copy.20
  178.9 8.8 %cholesky.81 = f32[96,96]{1,0:T(8,128)S(1)} custom-call(f32[96,96]{1,0:T(8,128)S(1)} %fusion.16), custom_call_target="Cholesky" | custom-call | tf_op jit(solution)/shard_map/jit(cholesky)/cholesky | solution.py:23
  187.8 0.6 compare_reduce_fusion
  188.4 0.7 fusion.12
  189.1 7.4 %custom-call.17 = f32[1,96,96]{1,2,0:T(8,128)S(1)} custom-call(f32[1,96,96]{2,1,0:T(8,128)S(1)} %fusion.12), custom_call_target="InvertDiagBlocksLowerTriangular" | custom-call | tf_op jit(solution)/shard_map/jit(_cho_solve)/triangular_solve | solution.py:24
  196.4 0.3 fusion.14
  196.7 0.9 convolution_bitcast_fusion
  (13 shorter events, 0.2 us)
Async XLA Ops:
  7.2 95.2 %copy-start = (s32[128,128]{1,0:T(8,128)S(1)}, s32[128,128]{1,0:T(8,128)}, u32[]{:S(2)}) copy-start(s32[128,128]{1,0:T(8,128)} %param.16) | copy-start | bytes 196612
  7.2 67.7 %all-gather.2.cloned.1.call-start = ((), (), s32[]{:S(2)}) async-start(), calls=%async_computation.1 | async-start | bytes 6684672 | tf_op jit(solution)/shard_map/all_gather | solution.py:40
  7.9 91.3 %copy-start.1 = (s32[128]{0:T(128)S(1)}, s32[128]{0:T(128)}, u32[]{:S(2)}) copy-start(s32[128]{0:T(128)} %param.15) | copy-start | bytes 1540
  7.9 91.9 %copy-start.2 = (s32[64]{0:T(128)S(1)}, s32[64]{0:T(128)}, u32[]{:S(2)}) copy-start(s32[64]{0:T(128)} %param.17) | copy-start | bytes 772
  7.9 92.5 %copy-start.3 = (s32[32]{0:T(128)S(1)}, s32[32]{0:T(128)}, u32[]{:S(2)}) copy-start(s32[32]{0:T(128)} %param.19) | copy-start | bytes 388
  7.9 121.6 %reduce-scatter.2.cloned.1.call-start = ((), (), s32[]{:S(2)}) async-start(), calls=%async_computation.2 | async-start | bytes 2359296 | tf_op jit(solution)/shard_map/reduce_scatter | solution.py:44
  131.4 24.2 %collective-permute-start = (f32[96,512]{1,0:T(8,128)S(1)}, f32[96,512]{1,0:T(8,128)S(1)}, u32[]{:S(2)}, u32[]{:S(2)}) collective-permute-start(f32[96,512]{1,0:T(8,128)S(1)} %select_multiply_fusion.2), channel_id=1, source_target_pairs={{0,1},{1,0},{2,3},{3,2},{4,5},{5,4},{6,7},{7,6},{8,9},{9,8},{10,11... | collective-permute-start | bytes 589832 | tf_op jit(solution)/shard_map/ppermute | solution.py:13
  157.0 19.4 %collective-permute-start.1 = (f32[96,512]{1,0:T(8,128)S(1)}, f32[96,512]{1,0:T(8,128)S(1)}, u32[]{:S(2)}, u32[]{:S(2)}) collective-permute-start(f32[96,512]{1,0:T(8,128)S(1)} %select_multiply_fusion.1), channel_id=1, source_target_pairs={{0,2},{1,3},{2,0},{3,1},{4,6},{5,7},{6,4},{7,5},{8,10},{9,11},{10,... | collective-permute-start | bytes 589832 | tf_op jit(solution)/shard_map/ppermute | solution.py:13
Sparse Core Ops, SparseCore 0:
  10.2 64.6 all-gather.1
  99.3 30.2 reduce-scatter.1
where the time goes:
time: 205 us; the launch traced here: 204 us
  waiting for transfers between devices  90.7 us (44%)
  other arithmetic  58.9 us (29%)
  matrix products  31.1 us (15%)
  between operations  14.4 us (7%)
  local copies, waits for them, and re-layouts  5.34 us (3%)
  starting transfers between devices  3.93 us (2%)
    all_gather x1, waiting for transfers between devices, on_device(): lax.all_gather(sketch, 'row', axis=0, tiled=True)  66.9 us
    another operation x9, other arithmetic, interpolate(): factor = jnp.linalg.cholesky(gram_matrix)  28.4 us
    dot_general x1, matrix products, on_device(): jnp.dot(frontal, lax.all_gather(sketch, 'row', axis=0, tiled=True), preci...  24.3 us
    another operation x6, other arithmetic, interpolate(): solved = jax.scipy.linalg.cho_solve((factor, True), cross_terms)  24 us
    reduce_scatter x1, waiting for transfers between devices, on_device(): lax.psum_scatter(partial_value, 'col', scatter_dimension=0, tiled=True)  23.2 us
  transfers between devices with their start and end apart: 4, of which 2 were waited for; matrix products, arithmetic and copies ran while one was open for 23% of the time, Pallas kernels for 0%

commit v1 on v0

v1 whole, which is shorter than its diff:
```python
import functools

import jax
import jax.numpy as jnp
from jax import lax
from jax.experimental import pallas as pl
from jax.experimental.pallas import tpu as pltpu
from jax.sharding import PartitionSpec as P

SAMPLES = 512
KMAX = 96
SIDE = 4
LEAF = 128
CHUNKS = 2
K_STEPS = 4


def from_partner(value, axis, apart):
    mask = 2**apart
    pairs = [(source, source ^ mask) for source in range(lax.axis_size(axis))]
    return lax.ppermute(value, axis, pairs)


def pick_entry(table, position):
    return lax.dynamic_index_in_dim(table, position, 0, keepdims=False)


def shift_x(value, dx):
    pairs = []
    for x in range(SIDE):
        for core in range(2):
            pairs.append((x * 2 + core, (x + dx) % SIDE * 2 + core))
    return lax.ppermute(value, "col", pairs)


FIRST, SECOND = 1, 3
ROUTES = (
    (("y", FIRST), ("y", SECOND), ("z", FIRST), ("z", SECOND)),
    (("y", SECOND), ("y", FIRST), ("z", SECOND), ("z", FIRST)),
    (("z", FIRST), ("z", SECOND), ("y", FIRST), ("y", SECOND)),
    (("z", SECOND), ("z", FIRST), ("y", SECOND), ("y", FIRST)),
)


def row_mask(step):
    axis, mask = step
    return mask * SIDE if axis == "y" else mask


def from_row(value, step):
    mask = row_mask(step)
    return lax.ppermute(value, "row", [(source, source ^ mask) for source in range(SIDE * SIDE)])


def origins(route):
    masks = [0]
    for step in route:
        masks += [mask ^ row_mask(step) for mask in masks]
    return masks


def gather_parts(sketch):
    depth = sketch.shape[0] // len(ROUTES)
    stacks = [sketch[None, part * depth : (part + 1) * depth] for part in range(len(ROUTES))]
    for at in range(3):
        received = [from_row(stack, route[at]) for stack, route in zip(stacks, ROUTES)]
        stacks = [jnp.concatenate(pair, 0) for pair in zip(stacks, received)]
    width = SAMPLES // CHUNKS
    halves = []
    for chunk in range(CHUNKS):
        own = [stack[:, :, chunk * width : (chunk + 1) * width] for stack in stacks]
        halves.append(own + [from_row(value, route[3]) for value, route in zip(own, ROUTES)])
    return halves


def split_kernel(value_ref, high_ref, low_ref):
    value = value_ref[...]
    high = value.astype(jnp.bfloat16)
    high_ref[...] = high
    low_ref[...] = (value - high.astype(jnp.float32)).astype(jnp.bfloat16)


def split(value):
    rows, order = value.shape
    block = pl.BlockSpec((LEAF, order), lambda i: (i, 0))
    return pl.pallas_call(
        split_kernel,
        out_shape=[jax.ShapeDtypeStruct(value.shape, jnp.bfloat16)] * 2,
        grid=(rows // LEAF,),
        in_specs=[block],
        out_specs=[block] * 2,
        compiler_params=pltpu.CompilerParams(vmem_limit_bytes=16 * 2**20),
        cost_estimate=pl.CostEstimate(
            flops=4 * rows * order, bytes_accessed=8 * rows * order, transcendentals=0
        ),
        name="split",
    )(value)


def product_kernel(place_ref, a_high, a_low, *refs):
    parts = len(ROUTES)
    pieces = refs[: 2 * parts]
    other_ref, own_ref, high, low, total = refs[2 * parts :]
    step = pl.program_id(0)

    @pl.when(step == 0)
    def _():
        depth = pieces[0].shape[1]
        for part, route in enumerate(ROUTES):
            masks = origins(route)
            for at, mask in enumerate(masks):
                source = pieces[part + parts * (at // 8)]
                block = jnp.bitwise_xor(place_ref[1], mask)
                start = pl.multiple_of((block * parts + part) * depth, depth)
                value = source[at % 8]
                top = value.astype(jnp.bfloat16)
                high[pl.ds(start, depth), :] = top
                low[pl.ds(start, depth), :] = (value - top.astype(jnp.float32)).astype(
                    jnp.bfloat16
                )

    k_rows = a_high.shape[-1]
    rows = pl.ds(pl.multiple_of(step * k_rows, 256), k_rows)
    left, right = a_high[...], high[rows, :]
    result = jnp.dot(
        jnp.concatenate([left, left, a_low[...]], 1),
        jnp.concatenate([right, low[rows, :], right], 0),
        preferred_element_type=jnp.float32,
    )

    @pl.when(step == 0)
    def _():
        total[...] = result.reshape(total.shape)

    @pl.when(step > 0)
    def _():
        total[...] += result.reshape(total.shape)

    @pl.when(step == K_STEPS - 1)
    def _():
        core, x = place_ref[0], place_ref[2]
        for away in range(SIDE):
            chip = lax.rem(x + away, SIDE)
            own_ref[away] = total[chip * 2 + core]
            other_ref[away] = total[chip * 2 + 1 - core]


def chunk_product(high, low, pieces, place):
    rows, order = high.shape
    width = pieces[0].shape[-1]
    k_rows = order // K_STEPS
    leaves = rows // LEAF // 2
    left = pl.BlockSpec((rows, k_rows), lambda k, place: (0, k))
    out = jax.ShapeDtypeStruct((leaves, LEAF, width), jnp.float32)
    return pl.pallas_call(
        product_kernel,
        out_shape=[out] * 2,
        grid_spec=pltpu.PrefetchScalarGridSpec(
            num_scalar_prefetch=1,
            grid=(K_STEPS,),
            in_specs=[left] * 2 + [pl.BlockSpec(memory_space=pltpu.VMEM)] * len(pieces),
            out_specs=[pl.BlockSpec(memory_space=pltpu.VMEM)] * 2,
            scratch_shapes=[
                pltpu.VMEM((order, width), jnp.bfloat16),
                pltpu.VMEM((order, width), jnp.bfloat16),
                pltpu.VMEM((2 * leaves, LEAF, width), jnp.float32),
            ],
        ),
        compiler_params=pltpu.CompilerParams(vmem_limit_bytes=36 * 2**20),
        cost_estimate=pl.CostEstimate(
            flops=6 * rows * order * width,
            bytes_accessed=4 * (rows * order + order * width + rows * width),
            transcendentals=0,
        ),
        name="chunk_product",
    )(place, high, low, *pieces)


def sum_over_col(other, own):
    core_sum = own + from_partner(other, "col", 0)
    return [core_sum[0]] + [shift_x(core_sum[step % SIDE], step) for step in (1, -1, 2)]


BLOCK = 8
NODES = 3


def lane_of(value, lane):
    return jnp.broadcast_to(value[:, lane : lane + 1], value.shape)


def invert_pivot(entry):
    def at(i, j):
        return entry[max(i, j)][min(i, j)]

    def put(i, j, value):
        entry[max(i, j)][min(i, j)] = value

    for p in range(0, BLOCK, 2):
        q = p + 1
        a, b, c = at(p, p), at(q, p), at(q, q)
        scale = 1.0 / (a * c - b * b)
        w_pp, w_pq, w_qq = c * scale, -b * scale, a * scale
        rest = [i for i in range(BLOCK) if i not in (p, q)]
        first = {i: at(i, p) for i in rest}
        second = {i: at(i, q) for i in rest}
        left = {i: w_pp * first[i] + w_pq * second[i] for i in rest}
        right = {i: w_pq * first[i] + w_qq * second[i] for i in rest}
        for i in rest:
            for j in rest:
                if j <= i:
                    put(i, j, at(i, j) - (left[i] * first[j] + right[i] * second[j]))
        for i in rest:
            put(i, p, left[i])
            put(i, q, right[i])
        put(p, p, -w_pp)
        put(q, p, -w_pq)
        put(q, q, -w_qq)
    return at


def sweep(tiles, rows_scratch, new_scratch):
    lanes = lax.broadcasted_iota(jnp.int32, (BLOCK, 128), 1)
    count = KMAX // BLOCK
    for block in range(count):
        at_lane = block * BLOCK
        slot = block % 2
        inside = (lanes >= at_lane) & (lanes < at_lane + BLOCK)
        for node in range(NODES):
            rows_scratch[slot, node * BLOCK : (node + 1) * BLOCK, :] = tiles[node][block]
        rows = [rows_scratch[slot, pl.ds(k, BLOCK, stride=BLOCK), :] for k in range(BLOCK)]
        entry = [[lane_of(rows[k], at_lane + i) for i in range(k + 1)] for k in range(BLOCK)]
        at = invert_pivot(entry)
        wide = [
            jnp.where(lanes == at_lane + k, 1.0, jnp.where(inside, 0.0, -rows[k]))
            for k in range(BLOCK)
        ]
        for k in range(BLOCK):
            total = at(k, 0) * wide[0]
            for i in range(1, BLOCK):
                total = total + at(k, i) * wide[i]
            new_scratch[slot, pl.ds(k, BLOCK, stride=BLOCK), :] = total
        for node in range(NODES):
            new_rows = [
                jnp.broadcast_to(
                    new_scratch[slot, node * BLOCK + k : node * BLOCK + k + 1, :], (BLOCK, 128)
                )
                for k in range(BLOCK)
            ]
            for t in range(count):
                if t == block:
                    continue
                old = tiles[node][t]
                value = jnp.where(inside, 0.0, old)
                for k in range(BLOCK):
                    value = value - lane_of(old, at_lane + k) * new_rows[k]
                tiles[node][t] = value
            tiles[node][block] = new_scratch[slot, node * BLOCK : (node + 1) * BLOCK, :]
    return tiles


def invert_all(matrices, rows_scratch, new_scratch):
    count = KMAX // BLOCK
    lanes = lax.broadcasted_iota(jnp.int32, (BLOCK, 128), 1)
    sublanes = lax.broadcasted_iota(jnp.int32, (BLOCK, 128), 0)
    rows_scratch[...] = jnp.zeros_like(rows_scratch)
    all_tiles, all_down, all_across = [], [], []
    for matrix in matrices:
        wide = jnp.concatenate([matrix, jnp.zeros((KMAX, 128 - KMAX), jnp.float32)], 1)
        tiles = [wide[t * BLOCK : (t + 1) * BLOCK] for t in range(count)]
        on_diagonal = [
            jnp.where(lanes == sublanes + t * BLOCK, tiles[t], 0.0) for t in range(count)
        ]
        down = [lax.rsqrt(jnp.sum(part, axis=1, keepdims=True)) for part in on_diagonal]
        line = functools.reduce(jnp.add, on_diagonal)
        line = jnp.sum(line, axis=0, keepdims=True)
        across = lax.rsqrt(jnp.where(lanes[:1] < KMAX, line, 1.0))
        all_tiles.append([tiles[t] * down[t] * across for t in range(count)])
        all_down.append(down)
        all_across.append(across)
    all_tiles = sweep(all_tiles, rows_scratch, new_scratch)
    inverses = []
    for tiles, down, across in zip(all_tiles, all_down, all_across):
        scaled = [-(tiles[t] * down[t] * across) for t in range(count)]
        inverses.append(jnp.concatenate(scaled, 0)[:, :KMAX])
    return inverses


def select_rows(source, pivots_ref, node, rank, target, target_at):
    for row in range(KMAX):
        picked = source[pl.ds(pivots_ref[node, row], 1), :]
        target[target_at + row : target_at + row + 1, :] = jnp.where(row < rank, picked, 0.0)


def leaf_kernel(info_ref, pivots_ref, *refs):
    parts, (rows_ref, skeleton_ref) = refs[:-2], refs[-2:]
    each = len(parts) // CHUNKS
    wide = SAMPLES // CHUNKS
    for chunk in range(CHUNKS):
        group = parts[chunk * each : (chunk + 1) * each]
        total = functools.reduce(jnp.add, [part[...] for part in group])
        rows_ref[:, chunk * wide : (chunk + 1) * wide] = total
    select_rows(rows_ref, pivots_ref, 0, info_ref[2], skeleton_ref, 0)


def mid_kernel(info_ref, pivots_ref, own_ref, other_ref, rows_ref, skeleton_ref):
    own_at = pl.multiple_of(info_ref[0] * KMAX, KMAX)
    other_at = pl.multiple_of((1 - info_ref[0]) * KMAX, KMAX)
    rows_ref[pl.ds(own_at, KMAX), :] = own_ref[...]
    rows_ref[pl.ds(other_at, KMAX), :] = other_ref[...]
    select_rows(rows_ref, pivots_ref, 1, info_ref[3], skeleton_ref, 0)


def top_kernel(
    info_ref, pivots_ref, leaf_rows, leaf_skeleton, mid_rows, mid_skeleton, cousin_ref,
    leaf_out, mid_out, top_out, rows_out, top_rows, rows_scratch, new_scratch,
):
    own_at = pl.multiple_of(info_ref[1] * KMAX, KMAX)
    other_at = pl.multiple_of((1 - info_ref[1]) * KMAX, KMAX)
    top_rows[pl.ds(own_at, KMAX), :] = mid_skeleton[...]
    top_rows[pl.ds(other_at, KMAX), :] = cousin_ref[...]
    select_rows(top_rows, pivots_ref, 2, info_ref[4], rows_out, 0)
    row_ids = lax.broadcasted_iota(jnp.int32, (KMAX, KMAX), 0)
    column_ids = lax.broadcasted_iota(jnp.int32, (KMAX, KMAX), 1)
    dot = functools.partial(
        lax.dot_general,
        dimension_numbers=(((1,), (1,)), ((), ())),
        precision=lax.Precision.HIGHEST,
        preferred_element_type=jnp.float32,
    )
    grams, crosses = [], []
    for node, (rows, skeleton) in enumerate(
        ((leaf_rows, leaf_skeleton), (mid_rows, mid_skeleton), (top_rows, rows_out))
    ):
        chosen = skeleton[...]
        gram = dot(chosen, chosen) * (1.0 / SAMPLES)
        empty = (row_ids == column_ids) & (row_ids >= info_ref[2 + node])
        grams.append(gram + jnp.where(empty, 1.0, 0.0))
        crosses.append(dot(rows[...], chosen) * (1.0 / SAMPLES))
    inverses = invert_all(grams, rows_scratch, new_scratch)
    for inverse, cross, out in zip(inverses, crosses, (leaf_out, mid_out, top_out)):
        out[...] = dot(inverse, cross)


def vmem_call(kernel, outs, scratch, name):
    in_vmem = pl.BlockSpec(memory_space=pltpu.VMEM)

    def call(info, pivots, *arrays):
        return pl.pallas_call(
            kernel,
            out_shape=[jax.ShapeDtypeStruct(shape, jnp.float32) for shape in outs],
            in_specs=[pl.BlockSpec(memory_space=pltpu.SMEM)] * 2 + [in_vmem] * len(arrays),
            out_specs=[in_vmem] * len(outs),
            scratch_shapes=scratch,
            compiler_params=pltpu.CompilerParams(vmem_limit_bytes=32 * 2**20),
            name=name,
        )(info, pivots, *arrays)

    return call


def on_device(
    frontal, sketch, leaf_ranks, leaf_pivots, mid_ranks, mid_pivots, top_ranks, top_pivots
):
    col_count = lax.axis_size("col")
    col_index = lax.axis_index("col")
    row_index = lax.axis_index("row")
    leaf_index = row_index * col_count + col_index
    place = jnp.stack([col_index % 2, row_index, col_index // 2]).astype(jnp.int32)
    nodes = (leaf_index, leaf_index // 2, leaf_index // 4)
    ranks = [
        pick_entry(table, node)
        for table, node in zip((leaf_ranks, mid_ranks, top_ranks), nodes)
    ]
    info = jnp.stack([col_index % 2, col_index // 2 % 2] + ranks).astype(jnp.int32)
    pivots = jnp.stack(
        [
            pick_entry(table, node)[:KMAX]
            for table, node in zip((leaf_pivots, mid_pivots, top_pivots), nodes)
        ]
    )
    high, low = split(frontal)
    high, low, info, pivots = lax.optimization_barrier((high, low, info, pivots))
    parts = []
    for pieces in gather_parts(sketch):
        parts += sum_over_col(*chunk_product(high, low, pieces, place))
    skeleton_shape, pair_shape = (KMAX, SAMPLES), (2 * KMAX, SAMPLES)
    leaf_rows, leaf_skeleton = vmem_call(
        leaf_kernel, [(LEAF, SAMPLES), skeleton_shape], [], "leaf_rows"
    )(info, pivots, *parts)
    sibling = from_partner(leaf_skeleton, "col", 0)
    mid_rows, mid_skeleton = vmem_call(
        mid_kernel, [pair_shape, skeleton_shape], [], "mid_rows"
    )(info, pivots, leaf_skeleton, sibling)
    cousin = from_partner(mid_skeleton, "col", 1)
    scratch = [pltpu.VMEM(pair_shape, jnp.float32)]
    scratch += [pltpu.VMEM((2, BLOCK * BLOCK, 128), jnp.float32)] * 2
    outs = vmem_call(
        top_kernel,
        [(KMAX, LEAF), (KMAX, 2 * KMAX), (KMAX, 2 * KMAX), skeleton_shape],
        scratch,
        "interpolation",
    )(info, pivots, leaf_rows, leaf_skeleton, mid_rows, mid_skeleton, cousin)
    return tuple(out[None] for out in outs)


def solution(mesh):
    return jax.shard_map(
        on_device,
        mesh=mesh,
        in_specs=(P("row", "col"), P(("col", "row"), None), P(), P(), P(), P(), P(), P()),
        out_specs=(
            P(("row", "col"), None, None),
            P(("row", "col"), None, None),
            P(("row", "col"), None, None),
            P(("row", "col"), None, None),
        ),
        check_vma=False,
    )
```

time: 205 us -> 114 us (0.56)
  other arithmetic: 58.9 us -> 0.62 us
  waiting for transfers between devices: 90.7 us -> 32.5 us
  starting transfers between devices: 3.93 us -> 39 us
  matrix products: 31.1 us -> 0 us
  Pallas kernels: 0 us -> 29.9 us
  between operations: 14.4 us -> 0.96 us
  local copies, waits for them, and re-layouts: 5.34 us -> 10.6 us
    all_gather x1 -> x0, waiting for transfers between devices: 66.9 us -> none  [on_device(): lax.all_gather(sketch, 'row', axis=0, tiled=True)]
    another operation x15 -> x2, other arithmetic: 52.5 us -> 0.09 us  [the longest x1 0.08 us: on_device(): jnp.stack([col_index % 2, row_index, col_index // 2]).astype(jnp.int32)]
    pallas_call x0 -> x6, Pallas kernels: none -> 29.9 us  [the longest x2 16.8 us: chunk_product(): pl.pallas_call(product_kernel, out_shape=[out] * 2, grid_spec=pltpu.Prefe...]
    ppermute x0 -> x26, starting transfers between devices: none -> 29.4 us  [the longest x20 22.1 us: from_row(): lax.ppermute(value, 'row', [(source, source ^ mask) for source in range(S...]
    dot_general x7 -> x0, matrix products: 27.7 us -> none  [the longest x1 24.3 us: on_device(): jnp.dot(frontal, lax.all_gather(sketch, 'row', axis=0, tiled=True), preci...]
    ppermute x0 -> x26, waiting for transfers between devices: none -> 26.1 us  [the longest x20 18.1 us: from_row(): lax.ppermute(value, 'row', [(source, source ^ mask) for source in range(S...]
    reduce_scatter x1 -> x0, waiting for transfers between devices: 23.2 us -> none  [on_device(): lax.psum_scatter(partial_value, 'col', scatter_dimension=0, tiled=True)]
    ppermute x2 -> x4, waiting for transfers between devices: 0.01 us -> 6.38 us  [from_partner(): return lax.ppermute(value, axis, pairs)]
  transfers between devices with their start and end apart: 4 -> 30, of which waited for: 2 -> 8; matrix products, arithmetic and copies ran while one was open for 23% -> 5% of each run, Pallas kernels for 0% -> 16%
where the time goes in v1:
time: 114 us
  starting transfers between devices  39 us (34%)
  waiting for transfers between devices  32.5 us (29%)
  Pallas kernels  29.9 us (26%)
  local copies, waits for them, and re-layouts  10.6 us (9%)
    ppermute x20, starting transfers between devices, from_row(): lax.ppermute(value, 'row', [(source, source ^ mask) for source in range(S...  22.1 us
    ppermute x20, waiting for transfers between devices, from_row(): lax.ppermute(value, 'row', [(source, source ^ mask) for source in range(S...  18.1 us
    pallas_call x2, Pallas kernels, chunk_product(): pl.pallas_call(product_kernel, out_shape=[out] * 2, grid_spec=pltpu.Prefe...  16.8 us
    pallas_call x3, Pallas kernels, call(): pl.pallas_call(kernel, out_shape=[jax.ShapeDtypeStruct(shape, jnp.float32...  11.2 us
    ppermute x4, starting transfers between devices, from_partner(): return lax.ppermute(value, axis, pairs)  9.64 us
    ppermute x6, waiting for transfers between devices, shift_x(): return lax.ppermute(value, 'col', pairs)  8.03 us
    ppermute x6, starting transfers between devices, shift_x(): return lax.ppermute(value, 'col', pairs)  7.28 us
    ppermute x4, waiting for transfers between devices, from_partner(): return lax.ppermute(value, axis, pairs)  6.38 us
  transfers between devices with their start and end apart: 30, of which 8 were waited for; matrix products, arithmetic and copies ran while one was open for 5% of the time, Pallas kernels for 16%

profile of v1, /device:TPU:1, one launch (start us, length us, event | category | flops | bytes accessed | tf_op | source)
XLA Modules:
  0.0 113.6 jit_solution(3897049145293363601)
XLA Ops:
  0.6 0.0 copy-start
  0.6 1.1 slice_bitcast_fusion.8
  1.7 2.2 %collective-permute-start = (f32[1,48,512]{2,1,0:T(8,128)S(1)}, f32[1,48,512]{2,1,0:T(8,128)S(1)}, u32[]{:S(2)}, u32[]{:S(2)}) collective-permute-start(f32[1,48,512]{2,1,0:T(8,128)S(1)} %get-tuple-element.58), channel_id=1, source_target_pairs={{0,32},{8,40},{16,48},{24,56},{32,0},{40,8},{48,16},{56,24},{64,96... | collective-permute-start | bytes 294920 | tf_op jit(solution)/shard_map/ppermute | solution.py:52
  3.9 1.9 %collective-permute-start.3 = (f32[1,48,512]{2,1,0:T(8,128)S(1)}, f32[1,48,512]{2,1,0:T(8,128)S(1)}, u32[]{:S(2)}, u32[]{:S(2)}) collective-permute-start(f32[1,48,512]{2,1,0:T(8,128)S(1)} %get-tuple-element.57), channel_id=1, source_target_pairs={{0,96},{8,104},{16,112},{24,120},{32,64},{40,72},{48,80},{56,88},{... | collective-permute-start | bytes 294920 | tf_op jit(solution)/shard_map/ppermute | solution.py:52
  5.9 1.6 %collective-permute-start.6 = (f32[1,48,512]{2,1,0:T(8,128)S(1)}, f32[1,48,512]{2,1,0:T(8,128)S(1)}, u32[]{:S(2)}, u32[]{:S(2)}) collective-permute-start(f32[1,48,512]{2,1,0:T(8,128)S(1)} %get-tuple-element.59), channel_id=1, source_target_pairs={{0,8},{8,0},{16,24},{24,16},{32,40},{40,32},{48,56},{56,48},{64,72... | collective-permute-start | bytes 294920 | tf_op jit(solution)/shard_map/ppermute | solution.py:52
  7.5 2.2 %collective-permute-start.9 = (f32[1,48,512]{2,1,0:T(8,128)S(1)}, f32[1,48,512]{2,1,0:T(8,128)S(1)}, u32[]{:S(2)}, u32[]{:S(2)}) collective-permute-start(f32[1,48,512]{2,1,0:T(8,128)S(1)} %get-tuple-element.56), channel_id=1, source_target_pairs={{0,24},{8,16},{16,8},{24,0},{32,56},{40,48},{48,40},{56,32},{64,88... | collective-permute-start | bytes 294920 | tf_op jit(solution)/shard_map/ppermute | solution.py:52
  9.8 0.9 collective-permute-start.1
  10.6 0.1 collective-permute-start.4
  10.8 2.7 %collective-permute-start.7 = (f32[2,48,512]{2,1,0:T(8,128)S(1)}, f32[2,48,512]{2,1,0:T(8,128)S(1)}, u32[]{:S(2)}, u32[]{:S(2)}) collective-permute-start(f32[2,48,512]{2,1,0:T(8,128)S(1)} %pad_maximum_fusion.10), channel_id=1, source_target_pairs={{0,24},{8,16},{16,8},{24,0},{32,56},{40,48},{48,40},{56,32},{64,88... | collective-permute-start | bytes 589832 | tf_op jit(solution)/shard_map/ppermute | solution.py:52
  13.5 2.1 %collective-permute-done.1 = f32[2,48,512]{2,1,0:T(8,128)S(1)} collective-permute-done((f32[2,48,512]{2,1,0:T(8,128)S(1)}, f32[2,48,512]{2,1,0:T(8,128)S(1)}, u32[]{:S(2)}, u32[]{:S(2)}) %collective-permute-start.1) | collective-permute-done | bytes 196640 | tf_op jit(solution)/shard_map/ppermute | solution.py:52
  15.6 0.8 collective-permute-start.2
  16.4 0.8 collective-permute-start.10
  17.3 0.8 collective-permute-start.5
  18.1 0.1 collective-permute-start.8
  18.2 9.3 %collective-permute-done.10 = f32[2,48,512]{2,1,0:T(8,128)S(1)} collective-permute-done((f32[2,48,512]{2,1,0:T(8,128)S(1)}, f32[2,48,512]{2,1,0:T(8,128)S(1)}, u32[]{:S(2)}, u32[]{:S(2)}) %collective-permute-start.10) | collective-permute-done | bytes 196640 | tf_op jit(solution)/shard_map/ppermute | solution.py:52
  27.6 0.0 copy-start.3
  27.6 0.0 copy-start.4
  27.6 0.9 collective-permute-start.11
  28.5 0.1 pad_maximum_fusion
  28.5 0.1 fusion.3
  28.6 0.1 pad_maximum_fusion.1
  28.7 0.1 fusion.2
  28.8 0.1 pad_maximum_fusion.2
  28.9 0.1 fusion.1
  29.0 6.6 %collective-permute-done.11 = f32[4,48,512]{2,1,0:T(8,128)S(1)} collective-permute-done((f32[4,48,512]{2,1,0:T(8,128)S(1)}, f32[4,48,512]{2,1,0:T(8,128)S(1)}, u32[]{:S(2)}, u32[]{:S(2)}) %collective-permute-start.11) | collective-permute-done | bytes 393248 | tf_op jit(solution)/shard_map/ppermute | solution.py:52
  35.5 0.1 pad_maximum_fusion.3
  35.6 0.1 fusion
  35.7 1.5 %collective-permute-start.12 = (f32[8,48,256]{2,1,0:T(8,128)S(1)}, f32[8,48,256]{2,1,0:T(8,128)}, u32[]{:S(2)}, u32[]{:S(2)}) collective-permute-start(f32[8,48,256]{2,1,0:T(8,128)S(1)} %get-tuple-element.47.refs_0_), channel_id=1, source_target_pairs={{0,24},{8,16},{16,8},{24,0},{32,56},{40,48},{48,40},{56,32},{64,88... | collective-permute-start | bytes 1179656 | tf_op jit(solution)/shard_map/ppermute | solution.py:52
  37.2 0.8 collective-permute-start.13
  38.0 0.6 collective-permute-start.14
  38.7 0.6 dynamic_slice.24
  39.3 0.7 dynamic_slice.25
  39.9 0.6 dynamic_slice.26
  40.5 1.9 %stack.30.info_ref = s32[5]{0:T(128)S(1)} concatenate(s32[1]{0:T(128)} %bitcast, s32[1]{0:T(128)} %bitcast.1, s32[1]{0:T(128)} %dynamic_slice.24, s32[1]{0:T(128)} %dynamic_slice.25, s32[1]{0:T(128)} %dynamic_slice.26), dimensions={0} | concatenate | bytes 40 | tf_op jit(solution)/shard_map/stack | solution.py:375
  42.5 4.6 %copy-done.1 = f32[1024,3072]{1,0:T(8,128)S(1)} copy-done((f32[1024,3072]{1,0:T(8,128)S(1)}, f32[1024,3072]{1,0:T(8,128)}, u32[]{:S(2)}) %copy-start.1) | copy-done | bytes 12582936
  47.0 1.9 %split.1 = (bf16[1024,3072]{1,0:T(8,128)(2,1)S(1)}, bf16[1024,3072]{1,0:T(8,128)(2,1)S(1)}) custom-call(f32[1024,3072]{1,0:T(8,128)S(1)} %copy-done.1), custom_call_target="tpu_custom_call" | custom-call | flops 12582912 | bytes 25165824 | tf_op jit(solution)/shard_map/split/pallas_call | solution.py:86
  48.9 0.7 constant_dynamic-slice_fusion
  49.7 0.1 pad_add_fusion.1.place_ref
  49.7 0.7 collective-permute-start.20
  50.5 0.8 collective-permute-start.21
  51.3 1.8 %collective-permute-start.22 = (f32[8,48,256]{2,1,0:T(8,128)S(1)}, f32[8,48,256]{2,1,0:T(8,128)S(1)}, u32[]{:S(2)}, u32[]{:S(2)}) collective-permute-start(f32[8,48,256]{2,1,0:T(8,128)S(1)} %get-tuple-element.42.refs_2_), channel_id=1, source_target_pairs={{0,96},{8,104},{16,112},{24,120},{32,64},{40,72},{48,80},{56,88},{... | collective-permute-start | bytes 1179656 | tf_op jit(solution)/shard_map/ppermute | solution.py:52
  53.1 0.8 collective-permute-start.23
  53.9 9.0 %chunk_product.2 = (f32[4,128,256]{2,1,0:T(8,128)S(1)}, f32[4,128,256]{2,1,0:T(8,128)S(1)}) custom-call(s32[3]{0:T(128)S(1)} %pad_add_fusion.1.place_ref, bf16[1024,3072]{1,0:T(8,128)(2,1)S(1)} %get-tuple-element.26.a_high, bf16[1024,3072]{1,0:T(8,128)(2,1)S(1)} %get-tuple-element.27.a_low, f32[8,48,256]{2,1,0:T(8,128)S(1)} %get-tuple-element.47.refs_0_, ...), custom_call_target="tpu_custom_call" | custom-call | flops 4831838208 | bytes 16777216 | tf_op jit(solution)/shard_map/chunk_product/pallas_call | solution.py:155
  63.0 7.3 %collective-permute-start.16 = (f32[4,128,256]{2,1,0:T(8,128)S(1)}, f32[4,128,256]{2,1,0:T(8,128)S(1)}, u32[]{:S(2)}, u32[]{:S(2)}) collective-permute-start(f32[4,128,256]{2,1,0:T(8,128)S(1)} %get-tuple-element.29), channel_id=1, source_target_pairs={{0,1},{1,0},{2,3},{3,2},{4,5},{5,4},{6,7},{7,6},{8,9},{9,8},{10,11... | collective-permute-start | bytes 1572872 | tf_op jit(solution)/shard_map/ppermute | solution.py:21
  70.3 7.8 %chunk_product.3 = (f32[4,128,256]{2,1,0:T(8,128)S(1)}, f32[4,128,256]{2,1,0:T(8,128)S(1)}) custom-call(s32[3]{0:T(128)S(1)} %pad_add_fusion.1.place_ref, bf16[1024,3072]{1,0:T(8,128)(2,1)S(1)} %get-tuple-element.26.a_high, bf16[1024,3072]{1,0:T(8,128)(2,1)S(1)} %get-tuple-element.27.a_low, f32[8,48,256]{2,1,0:T(8,128)S(1)} %get-tuple-element.46.refs_0_, ...), custom_call_target="tpu_custom_call" | custom-call | flops 4831838208 | bytes 16777216 | tf_op jit(solution)/shard_map/chunk_product/pallas_call | solution.py:155
  78.2 0.1 collective-permute-start.24
  78.3 0.1 add.44
  78.4 1.3 %collective-permute-start.17 = (f32[128,256]{1,0:T(8,128)S(1)}, f32[128,256]{1,0:T(8,128)S(1)}, u32[]{:S(2)}, u32[]{:S(2)}) collective-permute-start(f32[128,256]{1,0:T(8,128)S(1)} %get-tuple-element.54), channel_id=1, source_target_pairs={{0,2},{1,3},{2,4},{3,5},{4,6},{5,7},{6,0},{7,1},{8,10},{9,11},{10,... | collective-permute-start | bytes 393224 | tf_op jit(solution)/shard_map/ppermute | solution.py:33
  79.7 1.5 %collective-permute-start.18 = (f32[128,256]{1,0:T(8,128)S(1)}, f32[128,256]{1,0:T(8,128)S(1)}, u32[]{:S(2)}, u32[]{:S(2)}) collective-permute-start(f32[128,256]{1,0:T(8,128)S(1)} %get-tuple-element.53), channel_id=1, source_target_pairs={{0,6},{1,7},{2,0},{3,1},{4,2},{5,3},{6,4},{7,5},{8,14},{9,15},{10,... | collective-permute-start | bytes 393224 | tf_op jit(solution)/shard_map/ppermute | solution.py:33
  81.1 1.5 %collective-permute-start.19 = (f32[128,256]{1,0:T(8,128)S(1)}, f32[128,256]{1,0:T(8,128)S(1)}, u32[]{:S(2)}, u32[]{:S(2)}) collective-permute-start(f32[128,256]{1,0:T(8,128)S(1)} %get-tuple-element.52), channel_id=1, source_target_pairs={{0,4},{1,5},{2,6},{3,7},{4,0},{5,1},{6,2},{7,3},{8,12},{9,13},{10,... | collective-permute-start | bytes 393224 | tf_op jit(solution)/shard_map/ppermute | solution.py:33
  82.7 0.1 add.45
  82.8 0.4 collective-permute-start.25
  83.2 2.4 %collective-permute-start.26 = (f32[128,256]{1,0:T(8,128)S(1)}, f32[128,256]{1,0:T(8,128)S(1)}, u32[]{:S(2)}, u32[]{:S(2)}) collective-permute-start(f32[128,256]{1,0:T(8,128)S(1)} %get-tuple-element.49), channel_id=1, source_target_pairs={{0,6},{1,7},{2,0},{3,1},{4,2},{5,3},{6,4},{7,5},{8,14},{9,15},{10,... | collective-permute-start | bytes 393224 | tf_op jit(solution)/shard_map/ppermute | solution.py:33
  85.5 0.3 collective-permute-start.27
  85.8 2.4 %collective-permute-done.19.refs_3_ = f32[128,256]{1,0:T(8,128)S(1)} collective-permute-done((f32[128,256]{1,0:T(8,128)S(1)}, f32[128,256]{1,0:T(8,128)S(1)}, u32[]{:S(2)}, u32[]{:S(2)}) %collective-permute-start.19) | collective-permute-done | bytes 131104 | tf_op jit(solution)/shard_map/ppermute | solution.py:33
  88.2 3.5 %collective-permute-done.25.refs_5_ = f32[128,256]{1,0:T(8,128)S(1)} collective-permute-done((f32[128,256]{1,0:T(8,128)S(1)}, f32[128,256]{1,0:T(8,128)S(1)}, u32[]{:S(2)}, u32[]{:S(2)}) %collective-permute-start.25) | collective-permute-done | bytes 131104 | tf_op jit(solution)/shard_map/ppermute | solution.py:33
  91.7 2.1 %collective-permute-done.27.refs_7_ = f32[128,256]{1,0:T(8,128)S(1)} collective-permute-done((f32[128,256]{1,0:T(8,128)S(1)}, f32[128,256]{1,0:T(8,128)S(1)}, u32[]{:S(2)}, u32[]{:S(2)}) %collective-permute-start.27) | collective-permute-done | bytes 131104 | tf_op jit(solution)/shard_map/ppermute | solution.py:33
  93.8 0.8 leaf_rows.1
  94.6 1.3 %collective-permute-start.28 = (f32[96,512]{1,0:T(8,128)S(1)}, f32[96,512]{1,0:T(8,128)S(1)}, u32[]{:S(2)}, u32[]{:S(2)}) collective-permute-start(f32[96,512]{1,0:T(8,128)S(1)} %get-tuple-element.33.own_ref.leaf_skeleton), channel_id=1, source_target_pairs={{0,1},{1,0},{2,3},{3,2},{4,5},{5,4},{6,7},{7,6},{8,9},{9,8},{10,11... | collective-permute-start | bytes 589832 | tf_op jit(solution)/shard_map/ppermute | solution.py:21
  95.9 1.1 collective-permute-done.28.other_ref
  97.0 0.8 mid_rows.1
  97.8 0.9 collective-permute-start.29
  98.7 5.3 %collective-permute-done.29.cousin_ref = f32[96,512]{1,0:T(8,128)S(1)} collective-permute-done((f32[96,512]{1,0:T(8,128)S(1)}, f32[96,512]{1,0:T(8,128)S(1)}, u32[]{:S(2)}, u32[]{:S(2)}) %collective-permute-start.29) | collective-permute-done | bytes 196640 | tf_op jit(solution)/shard_map/ppermute | solution.py:21
  104.0 9.6 %interpolation.1 = (f32[96,128]{1,0:T(8,128)}, f32[96,192]{1,0:T(8,128)}, f32[96,192]{1,0:T(8,128)}, f32[96,512]{1,0:T(8,128)}) custom-call(s32[5]{0:T(128)S(1)} %stack.30.info_ref, s32[3,96]{1,0:T(4,128)S(1)} %pad_add_fusion.pivots_ref, f32[128,512]{1,0:T(8,128)S(1)} %get-tuple-element.32.leaf_rows, f32[96,512]{1,0:T(8,128)S(1)} %get-tuple-element.33.own_ref.leaf_skeleton, ...), custom_call_target="tpu_custom_call" | custom-call | tf_op jit(solution)/shard_map/interpolation/pallas_call | solution.py:349
  (41 shorter events, 0.3 us)
Async XLA Ops:
  0.6 38.0 %copy-start = (s32[128,128]{1,0:T(8,128)S(1)}, s32[128,128]{1,0:T(8,128)}, u32[]{:S(2)}) copy-start(s32[128,128]{1,0:T(8,128)} %param.11) | copy-start | bytes 196612
  1.7 8.0 %collective-permute-start = (f32[1,48,512]{2,1,0:T(8,128)S(1)}, f32[1,48,512]{2,1,0:T(8,128)S(1)}, u32[]{:S(2)}, u32[]{:S(2)}) collective-permute-start(f32[1,48,512]{2,1,0:T(8,128)S(1)} %get-tuple-element.58), channel_id=1, source_target_pairs={{0,32},{8,40},{16,48},{24,56},{32,0},{40,8},{48,16},{56,24},{64,96... | collective-permute-start | bytes 294920 | tf_op jit(solution)/shard_map/ppermute | solution.py:52
  3.9 6.7 %collective-permute-start.3 = (f32[1,48,512]{2,1,0:T(8,128)S(1)}, f32[1,48,512]{2,1,0:T(8,128)S(1)}, u32[]{:S(2)}, u32[]{:S(2)}) collective-permute-start(f32[1,48,512]{2,1,0:T(8,128)S(1)} %get-tuple-element.57), channel_id=1, source_target_pairs={{0,96},{8,104},{16,112},{24,120},{32,64},{40,72},{48,80},{56,88},{... | collective-permute-start | bytes 294920 | tf_op jit(solution)/shard_map/ppermute | solution.py:52
  5.9 4.9 %collective-permute-start.6 = (f32[1,48,512]{2,1,0:T(8,128)S(1)}, f32[1,48,512]{2,1,0:T(8,128)S(1)}, u32[]{:S(2)}, u32[]{:S(2)}) collective-permute-start(f32[1,48,512]{2,1,0:T(8,128)S(1)} %get-tuple-element.59), channel_id=1, source_target_pairs={{0,8},{8,0},{16,24},{24,16},{32,40},{40,32},{48,56},{56,48},{64,72... | collective-permute-start | bytes 294920 | tf_op jit(solution)/shard_map/ppermute | solution.py:52
  7.5 8.9 %collective-permute-start.9 = (f32[1,48,512]{2,1,0:T(8,128)S(1)}, f32[1,48,512]{2,1,0:T(8,128)S(1)}, u32[]{:S(2)}, u32[]{:S(2)}) collective-permute-start(f32[1,48,512]{2,1,0:T(8,128)S(1)} %get-tuple-element.56), channel_id=1, source_target_pairs={{0,24},{8,16},{16,8},{24,0},{32,56},{40,48},{48,40},{56,32},{64,88... | collective-permute-start | bytes 294920 | tf_op jit(solution)/shard_map/ppermute | solution.py:52
  9.8 5.8 %collective-permute-start.1 = (f32[2,48,512]{2,1,0:T(8,128)S(1)}, f32[2,48,512]{2,1,0:T(8,128)S(1)}, u32[]{:S(2)}, u32[]{:S(2)}) collective-permute-start(f32[2,48,512]{2,1,0:T(8,128)S(1)} %pad_maximum_fusion.8), channel_id=1, source_target_pairs={{0,96},{8,104},{16,112},{24,120},{32,64},{40,72},{48,80},{56,88},{... | collective-permute-start | bytes 589832 | tf_op jit(solution)/shard_map/ppermute | solution.py:52
  10.6 6.6 %collective-permute-start.4 = (f32[2,48,512]{2,1,0:T(8,128)S(1)}, f32[2,48,512]{2,1,0:T(8,128)S(1)}, u32[]{:S(2)}, u32[]{:S(2)}) collective-permute-start(f32[2,48,512]{2,1,0:T(8,128)S(1)} %pad_maximum_fusion.9), channel_id=1, source_target_pairs={{0,32},{8,40},{16,48},{24,56},{32,0},{40,8},{48,16},{56,24},{64,96... | collective-permute-start | bytes 589832 | tf_op jit(solution)/shard_map/ppermute | solution.py:52
  10.8 7.3 %collective-permute-start.7 = (f32[2,48,512]{2,1,0:T(8,128)S(1)}, f32[2,48,512]{2,1,0:T(8,128)S(1)}, u32[]{:S(2)}, u32[]{:S(2)}) collective-permute-start(f32[2,48,512]{2,1,0:T(8,128)S(1)} %pad_maximum_fusion.10), channel_id=1, source_target_pairs={{0,24},{8,16},{16,8},{24,0},{32,56},{40,48},{48,40},{56,32},{64,88... | collective-permute-start | bytes 589832 | tf_op jit(solution)/shard_map/ppermute | solution.py:52
  15.6 12.9 %collective-permute-start.2 = (f32[4,48,512]{2,1,0:T(8,128)S(1)}, f32[4,48,512]{2,1,0:T(8,128)S(1)}, u32[]{:S(2)}, u32[]{:S(2)}) collective-permute-start(f32[4,48,512]{2,1,0:T(8,128)S(1)} %pad_maximum_fusion.4), channel_id=1, source_target_pairs={{0,8},{8,0},{16,24},{24,16},{32,40},{40,32},{48,56},{56,48},{64,72... | collective-permute-start | bytes 1179656 | tf_op jit(solution)/shard_map/ppermute | solution.py:52
  16.4 11.1 %collective-permute-start.10 = (f32[2,48,512]{2,1,0:T(8,128)S(1)}, f32[2,48,512]{2,1,0:T(8,128)S(1)}, u32[]{:S(2)}, u32[]{:S(2)}) collective-permute-start(f32[2,48,512]{2,1,0:T(8,128)S(1)} %pad_maximum_fusion.11), channel_id=1, source_target_pairs={{0,8},{8,0},{16,24},{24,16},{32,40},{40,32},{48,56},{56,48},{64,72... | collective-permute-start | bytes 589832 | tf_op jit(solution)/shard_map/ppermute | solution.py:52
  17.3 11.4 %collective-permute-start.5 = (f32[4,48,512]{2,1,0:T(8,128)S(1)}, f32[4,48,512]{2,1,0:T(8,128)S(1)}, u32[]{:S(2)}, u32[]{:S(2)}) collective-permute-start(f32[4,48,512]{2,1,0:T(8,128)S(1)} %pad_maximum_fusion.5), channel_id=1, source_target_pairs={{0,24},{8,16},{16,8},{24,0},{32,56},{40,48},{48,40},{56,32},{64,88... | collective-permute-start | bytes 1179656 | tf_op jit(solution)/shard_map/ppermute | solution.py:52
  18.1 10.7 %collective-permute-start.8 = (f32[4,48,512]{2,1,0:T(8,128)S(1)}, f32[4,48,512]{2,1,0:T(8,128)S(1)}, u32[]{:S(2)}, u32[]{:S(2)}) collective-permute-start(f32[4,48,512]{2,1,0:T(8,128)S(1)} %pad_maximum_fusion.6), channel_id=1, source_target_pairs={{0,32},{8,40},{16,48},{24,56},{32,0},{40,8},{48,16},{56,24},{64,96... | collective-permute-start | bytes 1179656 | tf_op jit(solution)/shard_map/ppermute | solution.py:52
  27.6 11.1 %copy-start.2 = (s32[128]{0:T(128)S(1)}, s32[128]{0:T(128)}, u32[]{:S(2)}) copy-start(s32[128]{0:T(128)} %param.10) | copy-start | bytes 1540
  27.6 11.7 %copy-start.3 = (s32[64]{0:T(128)S(1)}, s32[64]{0:T(128)}, u32[]{:S(2)}) copy-start(s32[64]{0:T(128)} %param.12) | copy-start | bytes 772
  27.6 12.3 %copy-start.4 = (s32[32]{0:T(128)S(1)}, s32[32]{0:T(128)}, u32[]{:S(2)}) copy-start(s32[32]{0:T(128)} %param.14) | copy-start | bytes 388
  27.6 7.9 %collective-permute-start.11 = (f32[4,48,512]{2,1,0:T(8,128)S(1)}, f32[4,48,512]{2,1,0:T(8,128)S(1)}, u32[]{:S(2)}, u32[]{:S(2)}) collective-permute-start(f32[4,48,512]{2,1,0:T(8,128)S(1)} %pad_maximum_fusion.7), channel_id=1, source_target_pairs={{0,96},{8,104},{16,112},{24,120},{32,64},{40,72},{48,80},{56,88},{... | collective-permute-start | bytes 1179656 | tf_op jit(solution)/shard_map/ppermute | solution.py:52
  35.7 14.8 %collective-permute-start.12 = (f32[8,48,256]{2,1,0:T(8,128)S(1)}, f32[8,48,256]{2,1,0:T(8,128)}, u32[]{:S(2)}, u32[]{:S(2)}) collective-permute-start(f32[8,48,256]{2,1,0:T(8,128)S(1)} %get-tuple-element.47.refs_0_), channel_id=1, source_target_pairs={{0,24},{8,16},{16,8},{24,0},{32,56},{40,48},{48,40},{56,32},{64,88... | collective-permute-start | bytes 1179656 | tf_op jit(solution)/shard_map/ppermute | solution.py:52
  37.2 14.1 %collective-permute-start.13 = (f32[8,48,256]{2,1,0:T(8,128)S(1)}, f32[8,48,256]{2,1,0:T(8,128)}, u32[]{:S(2)}, u32[]{:S(2)}) collective-permute-start(f32[8,48,256]{2,1,0:T(8,128)S(1)} %get-tuple-element.45.refs_1_), channel_id=1, source_target_pairs={{0,8},{8,0},{16,24},{24,16},{32,40},{40,32},{48,56},{56,48},{64,72... | collective-permute-start | bytes 1179656 | tf_op jit(solution)/shard_map/ppermute | solution.py:52
  38.0 15.1 %collective-permute-start.14 = (f32[8,48,256]{2,1,0:T(8,128)S(1)}, f32[8,48,256]{2,1,0:T(8,128)}, u32[]{:S(2)}, u32[]{:S(2)}) collective-permute-start(f32[8,48,256]{2,1,0:T(8,128)S(1)} %get-tuple-element.43.refs_2_), channel_id=1, source_target_pairs={{0,96},{8,104},{16,112},{24,120},{32,64},{40,72},{48,80},{56,88},{... | collective-permute-start | bytes 1179656 | tf_op jit(solution)/shard_map/ppermute | solution.py:52
  38.6 15.3 %collective-permute-start.15 = (f32[8,48,256]{2,1,0:T(8,128)S(1)}, f32[8,48,256]{2,1,0:T(8,128)}, u32[]{:S(2)}, u32[]{:S(2)}) collective-permute-start(f32[8,48,256]{2,1,0:T(8,128)S(1)} %get-tuple-element.41.refs_3_), channel_id=1, source_target_pairs={{0,32},{8,40},{16,48},{24,56},{32,0},{40,8},{48,16},{56,24},{64,96... | collective-permute-start | bytes 1179656 | tf_op jit(solution)/shard_map/ppermute | solution.py:52
  42.5 4.6 %copy-start.1 = (f32[1024,3072]{1,0:T(8,128)S(1)}, f32[1024,3072]{1,0:T(8,128)}, u32[]{:S(2)}) copy-start(f32[1024,3072]{1,0:T(8,128)} %value_ref.1) | copy-start | bytes 37748740
  49.7 20.6 %collective-permute-start.20 = (f32[8,48,256]{2,1,0:T(8,128)S(1)}, f32[8,48,256]{2,1,0:T(8,128)S(1)}, u32[]{:S(2)}, u32[]{:S(2)}) collective-permute-start(f32[8,48,256]{2,1,0:T(8,128)S(1)} %get-tuple-element.46.refs_0_), channel_id=1, source_target_pairs={{0,24},{8,16},{16,8},{24,0},{32,56},{40,48},{48,40},{56,32},{64,88... | collective-permute-start | bytes 1179656 | tf_op jit(solution)/shard_map/ppermute | solution.py:52
  50.5 19.8 %collective-permute-start.21 = (f32[8,48,256]{2,1,0:T(8,128)S(1)}, f32[8,48,256]{2,1,0:T(8,128)S(1)}, u32[]{:S(2)}, u32[]{:S(2)}) collective-permute-start(f32[8,48,256]{2,1,0:T(8,128)S(1)} %get-tuple-element.44.refs_1_), channel_id=1, source_target_pairs={{0,8},{8,0},{16,24},{24,16},{32,40},{40,32},{48,56},{56,48},{64,72... | collective-permute-start | bytes 1179656 | tf_op jit(solution)/shard_map/ppermute | solution.py:52
  51.3 19.0 %collective-permute-start.22 = (f32[8,48,256]{2,1,0:T(8,128)S(1)}, f32[8,48,256]{2,1,0:T(8,128)S(1)}, u32[]{:S(2)}, u32[]{:S(2)}) collective-permute-start(f32[8,48,256]{2,1,0:T(8,128)S(1)} %get-tuple-element.42.refs_2_), channel_id=1, source_target_pairs={{0,96},{8,104},{16,112},{24,120},{32,64},{40,72},{48,80},{56,88},{... | collective-permute-start | bytes 1179656 | tf_op jit(solution)/shard_map/ppermute | solution.py:52
  53.1 17.2 %collective-permute-start.23 = (f32[8,48,256]{2,1,0:T(8,128)S(1)}, f32[8,48,256]{2,1,0:T(8,128)S(1)}, u32[]{:S(2)}, u32[]{:S(2)}) collective-permute-start(f32[8,48,256]{2,1,0:T(8,128)S(1)} %get-tuple-element.40.refs_3_), channel_id=1, source_target_pairs={{0,32},{8,40},{16,48},{24,56},{32,0},{40,8},{48,16},{56,24},{64,96... | collective-permute-start | bytes 1179656 | tf_op jit(solution)/shard_map/ppermute | solution.py:52
  63.0 15.3 %collective-permute-start.16 = (f32[4,128,256]{2,1,0:T(8,128)S(1)}, f32[4,128,256]{2,1,0:T(8,128)S(1)}, u32[]{:S(2)}, u32[]{:S(2)}) collective-permute-start(f32[4,128,256]{2,1,0:T(8,128)S(1)} %get-tuple-element.29), channel_id=1, source_target_pairs={{0,1},{1,0},{2,3},{3,2},{4,5},{5,4},{6,7},{7,6},{8,9},{9,8},{10,11... | collective-permute-start | bytes 1572872 | tf_op jit(solution)/shard_map/ppermute | solution.py:21
  78.2 4.5 %collective-permute-start.24 = (f32[4,128,256]{2,1,0:T(8,128)S(1)}, f32[4,128,256]{2,1,0:T(8,128)S(1)}, u32[]{:S(2)}, u32[]{:S(2)}) collective-permute-start(f32[4,128,256]{2,1,0:T(8,128)S(1)} %get-tuple-element.31), channel_id=1, source_target_pairs={{0,1},{1,0},{2,3},{3,2},{4,5},{5,4},{6,7},{7,6},{8,9},{9,8},{10,11... | collective-permute-start | bytes 1572872 | tf_op jit(solution)/shard_map/ppermute | solution.py:21
  78.4 7.2 %collective-permute-start.17 = (f32[128,256]{1,0:T(8,128)S(1)}, f32[128,256]{1,0:T(8,128)S(1)}, u32[]{:S(2)}, u32[]{:S(2)}) collective-permute-start(f32[128,256]{1,0:T(8,128)S(1)} %get-tuple-element.54), channel_id=1, source_target_pairs={{0,2},{1,3},{2,4},{3,5},{4,6},{5,7},{6,0},{7,1},{8,10},{9,11},{10,... | collective-permute-start | bytes 393224 | tf_op jit(solution)/shard_map/ppermute | solution.py:33
  79.7 6.1 %collective-permute-start.18 = (f32[128,256]{1,0:T(8,128)S(1)}, f32[128,256]{1,0:T(8,128)S(1)}, u32[]{:S(2)}, u32[]{:S(2)}) collective-permute-start(f32[128,256]{1,0:T(8,128)S(1)} %get-tuple-element.53), channel_id=1, source_target_pairs={{0,6},{1,7},{2,0},{3,1},{4,2},{5,3},{6,4},{7,5},{8,14},{9,15},{10,... | collective-permute-start | bytes 393224 | tf_op jit(solution)/shard_map/ppermute | solution.py:33
  81.1 7.1 %collective-permute-start.19 = (f32[128,256]{1,0:T(8,128)S(1)}, f32[128,256]{1,0:T(8,128)S(1)}, u32[]{:S(2)}, u32[]{:S(2)}) collective-permute-start(f32[128,256]{1,0:T(8,128)S(1)} %get-tuple-element.52), channel_id=1, source_target_pairs={{0,4},{1,5},{2,6},{3,7},{4,0},{5,1},{6,2},{7,3},{8,12},{9,13},{10,... | collective-permute-start | bytes 393224 | tf_op jit(solution)/shard_map/ppermute | solution.py:33
  82.8 8.9 %collective-permute-start.25 = (f32[128,256]{1,0:T(8,128)S(1)}, f32[128,256]{1,0:T(8,128)S(1)}, u32[]{:S(2)}, u32[]{:S(2)}) collective-permute-start(f32[128,256]{1,0:T(8,128)S(1)} %get-tuple-element.50), channel_id=1, source_target_pairs={{0,2},{1,3},{2,4},{3,5},{4,6},{5,7},{6,0},{7,1},{8,10},{9,11},{10,... | collective-permute-start | bytes 393224 | tf_op jit(solution)/shard_map/ppermute | solution.py:33
  83.2 8.5 %collective-permute-start.26 = (f32[128,256]{1,0:T(8,128)S(1)}, f32[128,256]{1,0:T(8,128)S(1)}, u32[]{:S(2)}, u32[]{:S(2)}) collective-permute-start(f32[128,256]{1,0:T(8,128)S(1)} %get-tuple-element.49), channel_id=1, source_target_pairs={{0,6},{1,7},{2,0},{3,1},{4,2},{5,3},{6,4},{7,5},{8,14},{9,15},{10,... | collective-permute-start | bytes 393224 | tf_op jit(solution)/shard_map/ppermute | solution.py:33
  85.5 8.3 %collective-permute-start.27 = (f32[128,256]{1,0:T(8,128)S(1)}, f32[128,256]{1,0:T(8,128)S(1)}, u32[]{:S(2)}, u32[]{:S(2)}) collective-permute-start(f32[128,256]{1,0:T(8,128)S(1)} %get-tuple-element.48), channel_id=1, source_target_pairs={{0,4},{1,5},{2,6},{3,7},{4,0},{5,1},{6,2},{7,3},{8,12},{9,13},{10,... | collective-permute-start | bytes 393224 | tf_op jit(solution)/shard_map/ppermute | solution.py:33
  94.6 2.4 %collective-permute-start.28 = (f32[96,512]{1,0:T(8,128)S(1)}, f32[96,512]{1,0:T(8,128)S(1)}, u32[]{:S(2)}, u32[]{:S(2)}) collective-permute-start(f32[96,512]{1,0:T(8,128)S(1)} %get-tuple-element.33.own_ref.leaf_skeleton), channel_id=1, source_target_pairs={{0,1},{1,0},{2,3},{3,2},{4,5},{5,4},{6,7},{7,6},{8,9},{9,8},{10,11... | collective-permute-start | bytes 589832 | tf_op jit(solution)/shard_map/ppermute | solution.py:21
  97.8 6.2 %collective-permute-start.29 = (f32[96,512]{1,0:T(8,128)S(1)}, f32[96,512]{1,0:T(8,128)S(1)}, u32[]{:S(2)}, u32[]{:S(2)}) collective-permute-start(f32[96,512]{1,0:T(8,128)S(1)} %get-tuple-element.35.mid_skeleton), channel_id=1, source_target_pairs={{0,2},{1,3},{2,0},{3,1},{4,6},{5,7},{6,4},{7,5},{8,10},{9,11},{10,... | collective-permute-start | bytes 589832 | tf_op jit(solution)/shard_map/ppermute | solution.py:21

commit v2 on v1

--- a/solution.py
+++ b/solution.py
@@ -11,7 +11,7 @@
 KMAX = 96
 SIDE = 4
 LEAF = 128
-CHUNKS = 2
+WIDTHS = (256, 256)
 K_STEPS = 4
 
 
@@ -23,14 +23,6 @@
 
 def pick_entry(table, position):
     return lax.dynamic_index_in_dim(table, position, 0, keepdims=False)
-
-
-def shift_x(value, dx):
-    pairs = []
-    for x in range(SIDE):
-        for core in range(2):
-            pairs.append((x * 2 + core, (x + dx) % SIDE * 2 + core))
-    return lax.ppermute(value, "col", pairs)
 
 
 FIRST, SECOND = 1, 3
@@ -59,18 +51,21 @@
     return masks
 
 
-def gather_parts(sketch):
+def gather_parts(sketch, ready):
     depth = sketch.shape[0] // len(ROUTES)
     stacks = [sketch[None, part * depth : (part + 1) * depth] for part in range(len(ROUTES))]
     for at in range(3):
         received = [from_row(stack, route[at]) for stack, route in zip(stacks, ROUTES)]
+        if at == 0:
+            received = lax.optimization_barrier(received)
         stacks = [jnp.concatenate(pair, 0) for pair in zip(stacks, received)]
-    width = SAMPLES // CHUNKS
-    halves = []
-    for chunk in range(CHUNKS):
-        own = [stack[:, :, chunk * width : (chunk + 1) * width] for stack in stacks]
-        halves.append(own + [from_row(value, route[3]) for value, route in zip(own, ROUTES)])
-    return halves
+    stacks, ready = lax.optimization_barrier((stacks, ready))
+    chunks, start = [], 0
+    for width in WIDTHS:
+        own = [stack[:, :, start : start + width] for stack in stacks]
+        chunks.append(own + [from_row(value, route[3]) for value, route in zip(own, ROUTES)])
+        start += width
+    return chunks, ready
 
 
 def split_kernel(value_ref, high_ref, low_ref):
@@ -140,7 +135,7 @@
     def _():
         core, x = place_ref[0], place_ref[2]
         for away in range(SIDE):
-            chip = lax.rem(x + away, SIDE)
+            chip = jnp.bitwise_xor(x, away)
             own_ref[away] = total[chip * 2 + core]
             other_ref[away] = total[chip * 2 + 1 - core]
 
@@ -167,18 +162,23 @@
             ],
         ),
         compiler_params=pltpu.CompilerParams(vmem_limit_bytes=36 * 2**20),
-        cost_estimate=pl.CostEstimate(
-            flops=6 * rows * order * width,
-            bytes_accessed=4 * (rows * order + order * width + rows * width),
-            transcendentals=0,
-        ),
         name="chunk_product",
     )(place, high, low, *pieces)
 
 
-def sum_over_col(other, own):
+X_ROUTES = ((FIRST, SECOND), (SECOND, FIRST))
+
+
+def from_x(value, mask):
+    pairs = [(source, source ^ (2 * mask)) for source in range(2 * SIDE)]
+    return lax.ppermute(value, "col", pairs)
+
+
+def sum_over_col(other, own, route):
+    near, far = route
     core_sum = own + from_partner(other, "col", 0)
-    return [core_sum[0]] + [shift_x(core_sum[step % SIDE], step) for step in (1, -1, 2)]
+    kept = from_x(jnp.stack([core_sum[near], core_sum[near ^ far]]), near)
+    return [core_sum[0], kept[0], from_x(core_sum[far] + kept[1], far)]
 
 
 BLOCK = 8
@@ -294,12 +294,7 @@
 
 def leaf_kernel(info_ref, pivots_ref, *refs):
     parts, (rows_ref, skeleton_ref) = refs[:-2], refs[-2:]
-    each = len(parts) // CHUNKS
-    wide = SAMPLES // CHUNKS
-    for chunk in range(CHUNKS):
-        group = parts[chunk * each : (chunk + 1) * each]
-        total = functools.reduce(jnp.add, [part[...] for part in group])
-        rows_ref[:, chunk * wide : (chunk + 1) * wide] = total
+    rows_ref[...] = functools.reduce(jnp.add, [part[...] for part in parts])
     select_rows(rows_ref, pivots_ref, 0, info_ref[2], skeleton_ref, 0)
 
 
@@ -311,15 +306,24 @@
     select_rows(rows_ref, pivots_ref, 1, info_ref[3], skeleton_ref, 0)
 
 
-def top_kernel(
-    info_ref, pivots_ref, leaf_rows, leaf_skeleton, mid_rows, mid_skeleton, cousin_ref,
-    leaf_out, mid_out, top_out, rows_out, top_rows, rows_scratch, new_scratch,
-):
+def top_kernel(info_ref, pivots_ref, *refs):
+    chunks = len(WIDTHS)
+    groups = [refs[5 * chunk : 5 * chunk + 5] for chunk in range(chunks)]
+    leaf_out, mid_out, top_out, rows_out = refs[5 * chunks : 5 * chunks + 4]
+    scratch = refs[5 * chunks + 4 :]
+    tops, chosen, (rows_scratch, new_scratch) = (
+        scratch[:chunks], scratch[chunks : 2 * chunks], scratch[2 * chunks :]
+    )
     own_at = pl.multiple_of(info_ref[1] * KMAX, KMAX)
     other_at = pl.multiple_of((1 - info_ref[1]) * KMAX, KMAX)
-    top_rows[pl.ds(own_at, KMAX), :] = mid_skeleton[...]
-    top_rows[pl.ds(other_at, KMAX), :] = cousin_ref[...]
-    select_rows(top_rows, pivots_ref, 2, info_ref[4], rows_out, 0)
+    start = 0
+    for group, top, skeleton in zip(groups, tops, chosen):
+        top[pl.ds(own_at, KMAX), :] = group[3][...]
+        top[pl.ds(other_at, KMAX), :] = group[4][...]
+        select_rows(top, pivots_ref, 2, info_ref[4], skeleton, 0)
+        width = skeleton.shape[-1]
+        rows_out[:, start : start + width] = skeleton[...]
+        start += width
     row_ids = lax.broadcasted_iota(jnp.int32, (KMAX, KMAX), 0)
     column_ids = lax.broadcasted_iota(jnp.int32, (KMAX, KMAX), 1)
     dot = functools.partial(
@@ -328,15 +332,20 @@
         precision=lax.Precision.HIGHEST,
         preferred_element_type=jnp.float32,
     )
+    levels = (
+        ([group[0] for group in groups], [group[1] for group in groups]),
+        ([group[2] for group in groups], [group[3] for group in groups]),
+        (tops, chosen),
+    )
     grams, crosses = [], []
-    for node, (rows, skeleton) in enumerate(
-        ((leaf_rows, leaf_skeleton), (mid_rows, mid_skeleton), (top_rows, rows_out))
-    ):
-        chosen = skeleton[...]
-        gram = dot(chosen, chosen) * (1.0 / SAMPLES)
+    for node, (rows, skeletons) in enumerate(levels):
+        gram = functools.reduce(jnp.add, [dot(part[...], part[...]) for part in skeletons])
+        cross = functools.reduce(
+            jnp.add, [dot(row[...], part[...]) for row, part in zip(rows, skeletons)]
+        )
         empty = (row_ids == column_ids) & (row_ids >= info_ref[2 + node])
-        grams.append(gram + jnp.where(empty, 1.0, 0.0))
-        crosses.append(dot(rows[...], chosen) * (1.0 / SAMPLES))
+        grams.append(gram * (1.0 / SAMPLES) + jnp.where(empty, 1.0, 0.0))
+        crosses.append(cross * (1.0 / SAMPLES))
     inverses = invert_all(grams, rows_scratch, new_scratch)
     for inverse, cross, out in zip(inverses, crosses, (leaf_out, mid_out, top_out)):
         out[...] = dot(inverse, cross)
@@ -379,28 +388,30 @@
             for table, node in zip((leaf_pivots, mid_pivots, top_pivots), nodes)
         ]
     )
-    high, low = split(frontal)
-    high, low, info, pivots = lax.optimization_barrier((high, low, info, pivots))
-    parts = []
-    for pieces in gather_parts(sketch):
-        parts += sum_over_col(*chunk_product(high, low, pieces, place))
-    skeleton_shape, pair_shape = (KMAX, SAMPLES), (2 * KMAX, SAMPLES)
-    leaf_rows, leaf_skeleton = vmem_call(
-        leaf_kernel, [(LEAF, SAMPLES), skeleton_shape], [], "leaf_rows"
-    )(info, pivots, *parts)
-    sibling = from_partner(leaf_skeleton, "col", 0)
-    mid_rows, mid_skeleton = vmem_call(
-        mid_kernel, [pair_shape, skeleton_shape], [], "mid_rows"
-    )(info, pivots, leaf_skeleton, sibling)
-    cousin = from_partner(mid_skeleton, "col", 1)
-    scratch = [pltpu.VMEM(pair_shape, jnp.float32)]
+    chunks, (high, low, info, pivots) = gather_parts(sketch, (*split(frontal), info, pivots))
+    groups = [
+        sum_over_col(*chunk_product(high, low, pieces, place), route)
+        for pieces, route in zip(chunks, X_ROUTES)
+    ]
+    arrays = []
+    for group, width in zip(groups, WIDTHS):
+        skeleton_shape, pair_shape = (KMAX, width), (2 * KMAX, width)
+        rows, skeleton = vmem_call(
+            leaf_kernel, [(LEAF, width), skeleton_shape], [], "leaf_rows"
+        )(info, pivots, *group)
+        mid_rows, mid_skeleton = vmem_call(
+            mid_kernel, [pair_shape, skeleton_shape], [], "mid_rows"
+        )(info, pivots, skeleton, from_partner(skeleton, "col", 0))
+        arrays += [rows, skeleton, mid_rows, mid_skeleton, from_partner(mid_skeleton, "col", 1)]
+    scratch = [pltpu.VMEM((2 * KMAX, width), jnp.float32) for width in WIDTHS]
+    scratch += [pltpu.VMEM((KMAX, width), jnp.float32) for width in WIDTHS]
     scratch += [pltpu.VMEM((2, BLOCK * BLOCK, 128), jnp.float32)] * 2
     outs = vmem_call(
         top_kernel,
-        [(KMAX, LEAF), (KMAX, 2 * KMAX), (KMAX, 2 * KMAX), skeleton_shape],
+        [(KMAX, LEAF), (KMAX, 2 * KMAX), (KMAX, 2 * KMAX), (KMAX, SAMPLES)],
         scratch,
         "interpolation",
-    )(info, pivots, leaf_rows, leaf_skeleton, mid_rows, mid_skeleton, cousin)
+    )(info, pivots, *arrays)
     return tuple(out[None] for out in outs)
 
 

time: 114 us -> 116 us (1.018)
  waiting for transfers between devices: 32.5 us -> 22.4 us
  starting transfers between devices: 39 us -> 46.3 us
  other arithmetic: 0.62 us -> 2.7 us
  local copies, waits for them, and re-layouts: 10.6 us -> 12.6 us
    ppermute x4 -> x6, starting transfers between devices: 9.64 us -> 17.5 us  [from_partner(): return lax.ppermute(value, axis, pairs)]
    ppermute x20, waiting for transfers between devices: 18.1 us -> 12.4 us  [from_row(): lax.ppermute(value, 'row', [(source, source ^ mask) for source in range(S...]
    ppermute x6 -> x4, waiting for transfers between devices: 8.03 us -> 5.31 us  [from_x(): return lax.ppermute(value, 'col', pairs)]
    dynamic_slice x4, local copies, waits for them, and re-layouts: 1.84 us -> 3.88 us  [pick_entry(): return lax.dynamic_index_in_dim(table, position, 0, keepdims=False)]
    concatenate x12, other arithmetic: 0.38 us -> 2.39 us  [gather_parts(): stacks = [jnp.concatenate(pair, 0) for pair in zip(stacks, received)]]
    pallas_call x3 -> x5, Pallas kernels: 11.2 us -> 13 us  [call(): pl.pallas_call(kernel, out_shape=[jax.ShapeDtypeStruct(shape, jnp.float32...]
    ppermute x4 -> x6, waiting for transfers between devices: 6.38 us -> 4.68 us  [from_partner(): return lax.ppermute(value, axis, pairs)]
    pallas_call x2, Pallas kernels: 16.8 us -> 15.7 us  [chunk_product(): pl.pallas_call(product_kernel, out_shape=[out] * 2, grid_spec=pltpu.Prefe...]
  transfers between devices with their start and end apart: 30 -> 30, of which waited for: 8 -> 12; matrix products, arithmetic and copies ran while one was open for 5% -> 8% of each run, Pallas kernels for 16% -> 18%
where the time goes in v2:
time: 116 us
  starting transfers between devices  46.3 us (40%)
  Pallas kernels  30.5 us (26%)
  waiting for transfers between devices  22.4 us (19%)
  local copies, waits for them, and re-layouts  12.6 us (11%)
  other arithmetic  2.7 us (2%)
    ppermute x20, starting transfers between devices, from_row(): lax.ppermute(value, 'row', [(source, source ^ mask) for source in range(S...  22.1 us
    ppermute x6, starting transfers between devices, from_partner(): return lax.ppermute(value, axis, pairs)  17.5 us
    pallas_call x2, Pallas kernels, chunk_product(): pl.pallas_call(product_kernel, out_shape=[out] * 2, grid_spec=pltpu.Prefe...  15.7 us
    pallas_call x5, Pallas kernels, call(): pl.pallas_call(kernel, out_shape=[jax.ShapeDtypeStruct(shape, jnp.float32...  13 us
    ppermute x20, waiting for transfers between devices, from_row(): lax.ppermute(value, 'row', [(source, source ^ mask) for source in range(S...  12.4 us
    ppermute x4, starting transfers between devices, from_x(): return lax.ppermute(value, 'col', pairs)  6.8 us
    ppermute x4, waiting for transfers between devices, from_x(): return lax.ppermute(value, 'col', pairs)  5.31 us
    ppermute x6, waiting for transfers between devices, from_partner(): return lax.ppermute(value, axis, pairs)  4.68 us
  transfers between devices with their start and end apart: 30, of which 12 were waited for; matrix products, arithmetic and copies ran while one was open for 8% of the time, Pallas kernels for 18%

profile of v2, /device:TPU:1, one launch (start us, length us, event | category | flops | bytes accessed | tf_op | source)
XLA Modules:
  0.0 115.6 jit_solution(13853660570133965180)
XLA Ops:
  0.6 1.1 slice_bitcast_fusion.4
  1.7 2.2 %collective-permute-start = (f32[1,48,512]{2,1,0:T(8,128)S(1)}, f32[1,48,512]{2,1,0:T(8,128)S(1)}, u32[]{:S(2)}, u32[]{:S(2)}) collective-permute-start(f32[1,48,512]{2,1,0:T(8,128)S(1)} %get-tuple-element.80), channel_id=1, source_target_pairs={{0,32},{8,40},{16,48},{24,56},{32,0},{40,8},{48,16},{56,24},{64,96... | collective-permute-start | bytes 294920 | tf_op jit(solution)/shard_map/ppermute | solution.py:44
  3.9 1.9 %collective-permute-start.1 = (f32[1,48,512]{2,1,0:T(8,128)S(1)}, f32[1,48,512]{2,1,0:T(8,128)S(1)}, u32[]{:S(2)}, u32[]{:S(2)}) collective-permute-start(f32[1,48,512]{2,1,0:T(8,128)S(1)} %get-tuple-element.79), channel_id=1, source_target_pairs={{0,96},{8,104},{16,112},{24,120},{32,64},{40,72},{48,80},{56,88},{... | collective-permute-start | bytes 294920 | tf_op jit(solution)/shard_map/ppermute | solution.py:44
  5.9 1.6 %collective-permute-start.2 = (f32[1,48,512]{2,1,0:T(8,128)S(1)}, f32[1,48,512]{2,1,0:T(8,128)S(1)}, u32[]{:S(2)}, u32[]{:S(2)}) collective-permute-start(f32[1,48,512]{2,1,0:T(8,128)S(1)} %get-tuple-element.81), channel_id=1, source_target_pairs={{0,8},{8,0},{16,24},{24,16},{32,40},{40,32},{48,56},{56,48},{64,72... | collective-permute-start | bytes 294920 | tf_op jit(solution)/shard_map/ppermute | solution.py:44
  7.5 2.2 %collective-permute-start.3 = (f32[1,48,512]{2,1,0:T(8,128)S(1)}, f32[1,48,512]{2,1,0:T(8,128)S(1)}, u32[]{:S(2)}, u32[]{:S(2)}) collective-permute-start(f32[1,48,512]{2,1,0:T(8,128)S(1)} %get-tuple-element.78), channel_id=1, source_target_pairs={{0,24},{8,16},{16,8},{24,0},{32,56},{40,48},{48,40},{56,32},{64,88... | collective-permute-start | bytes 294920 | tf_op jit(solution)/shard_map/ppermute | solution.py:44
  9.7 0.7 constant_dynamic-slice_fusion
  10.5 1.7 %collective-permute-done.3 = f32[1,48,512]{2,1,0:T(8,128)S(1)} collective-permute-done((f32[1,48,512]{2,1,0:T(8,128)S(1)}, f32[1,48,512]{2,1,0:T(8,128)S(1)}, u32[]{:S(2)}, u32[]{:S(2)}) %collective-permute-start.3) | collective-permute-done | bytes 98336 | tf_op jit(solution)/shard_map/ppermute | solution.py:44
  12.2 0.9 collective-permute-start.4
  13.1 0.1 collective-permute-start.6
  13.2 2.6 %collective-permute-start.8 = (f32[2,48,512]{2,1,0:T(8,128)S(1)}, f32[2,48,512]{2,1,0:T(8,128)S(1)}, u32[]{:S(2)}, u32[]{:S(2)}) collective-permute-start(f32[2,48,512]{2,1,0:T(8,128)S(1)} %pad_maximum_fusion.11), channel_id=1, source_target_pairs={{0,24},{8,16},{16,8},{24,0},{32,56},{40,48},{48,40},{56,32},{64,88... | collective-permute-start | bytes 589832 | tf_op jit(solution)/shard_map/ppermute | solution.py:44
  15.8 0.1 collective-permute-start.10
  15.9 2.1 %collective-permute-done.4 = f32[2,48,512]{2,1,0:T(8,128)S(1)} collective-permute-done((f32[2,48,512]{2,1,0:T(8,128)S(1)}, f32[2,48,512]{2,1,0:T(8,128)S(1)}, u32[]{:S(2)}, u32[]{:S(2)}) %collective-permute-start.4) | collective-permute-done | bytes 196640 | tf_op jit(solution)/shard_map/ppermute | solution.py:44
  18.0 0.7 collective-permute-start.5
  18.7 2.1 %collective-permute-start.7 = (f32[4,48,512]{2,1,0:T(8,128)S(1)}, f32[4,48,512]{2,1,0:T(8,128)}, u32[]{:S(2)}, u32[]{:S(2)}) collective-permute-start(f32[4,48,512]{2,1,0:T(8,128)S(1)} %pad_maximum_fusion.5), channel_id=1, source_target_pairs={{0,24},{8,16},{16,8},{24,0},{32,56},{40,48},{48,40},{56,32},{64,88... | collective-permute-start | bytes 1179656 | tf_op jit(solution)/shard_map/ppermute | solution.py:44
  20.9 0.1 collective-permute-start.9
  21.1 1.3 %dynamic_slice.24 = s32[1]{0:T(128)} dynamic-slice(s32[128]{0:T(128)} %param.10, s32[]{:T(128)S(6)} %select_n.45), dynamic_slice_sizes={1} | dynamic-slice | bytes 12 | tf_op jit(solution)/shard_map/jit(dynamic_index_in_dim)/dynamic_slice | solution.py:25
  22.4 1.3 %dynamic_slice.25 = s32[1]{0:T(128)} dynamic-slice(s32[64]{0:T(128)} %param.12, s32[]{:T(128)S(6)} %select_n.47), dynamic_slice_sizes={1} | dynamic-slice | bytes 12 | tf_op jit(solution)/shard_map/jit(dynamic_index_in_dim)/dynamic_slice | solution.py:25
  23.6 1.3 %dynamic_slice.26 = s32[1]{0:T(128)} dynamic-slice(s32[32]{0:T(128)} %param.14, s32[]{:T(128)S(6)} %select_n.49), dynamic_slice_sizes={1} | dynamic-slice | bytes 12 | tf_op jit(solution)/shard_map/jit(dynamic_index_in_dim)/dynamic_slice | solution.py:25
  24.9 2.0 %stack.36.info_ref = s32[5]{0:T(128)S(1)} concatenate(s32[1]{0:T(128)} %bitcast.4, s32[1]{0:T(128)} %bitcast.5, s32[1]{0:T(128)} %dynamic_slice.24, s32[1]{0:T(128)} %dynamic_slice.25, s32[1]{0:T(128)} %dynamic_slice.26), dimensions={0} | concatenate | bytes 40 | tf_op jit(solution)/shard_map/stack | solution.py:384
  26.9 4.6 %copy-done.1 = f32[1024,3072]{1,0:T(8,128)S(1)} copy-done((f32[1024,3072]{1,0:T(8,128)S(1)}, f32[1024,3072]{1,0:T(8,128)}, u32[]{:S(2)}) %copy-start.1) | copy-done | bytes 12582936
  31.5 1.9 %split.1 = (bf16[1024,3072]{1,0:T(8,128)(2,1)S(1)}, bf16[1024,3072]{1,0:T(8,128)(2,1)S(1)}) custom-call(f32[1024,3072]{1,0:T(8,128)S(1)} %copy-done.1), custom_call_target="tpu_custom_call" | custom-call | flops 12582912 | bytes 25165824 | tf_op jit(solution)/shard_map/split/pallas_call | solution.py:81
  33.4 1.5 %collective-permute-start.11 = (f32[4,48,512]{2,1,0:T(8,128)S(1)}, f32[4,48,512]{2,1,0:T(8,128)S(1)}, u32[]{:S(2)}, u32[]{:S(2)}) collective-permute-start(f32[4,48,512]{2,1,0:T(8,128)S(1)} %pad_maximum_fusion.7), channel_id=1, source_target_pairs={{0,96},{8,104},{16,112},{24,120},{32,64},{40,72},{48,80},{56,88},{... | collective-permute-start | bytes 1179656 | tf_op jit(solution)/shard_map/ppermute | solution.py:44
  34.9 0.1 pad_maximum_fusion
  35.0 1.0 pad_maximum_fusion.1
  36.1 1.0 pad_maximum_fusion.2
  37.1 4.2 %collective-permute-done.11 = f32[4,48,512]{2,1,0:T(8,128)S(1)} collective-permute-done((f32[4,48,512]{2,1,0:T(8,128)S(1)}, f32[4,48,512]{2,1,0:T(8,128)S(1)}, u32[]{:S(2)}, u32[]{:S(2)}) %collective-permute-start.11) | collective-permute-done | bytes 393248 | tf_op jit(solution)/shard_map/ppermute | solution.py:44
  41.4 0.1 fusion.5
  41.5 0.1 fusion.4
  41.6 2.1 %collective-permute-start.12 = (f32[8,48,256]{2,1,0:T(8,128)S(1)}, f32[8,48,256]{2,1,0:T(8,128)S(1)}, u32[]{:S(2)}, u32[]{:S(2)}) collective-permute-start(f32[8,48,256]{2,1,0:T(8,128)S(1)} %get-tuple-element.71.refs_0_), channel_id=1, source_target_pairs={{0,24},{8,16},{16,8},{24,0},{32,56},{40,48},{48,40},{56,32},{64,88... | collective-permute-start | bytes 1179656 | tf_op jit(solution)/shard_map/ppermute | solution.py:44
  43.7 0.1 fusion.3
  43.8 1.7 %collective-permute-start.14 = (f32[8,48,256]{2,1,0:T(8,128)S(1)}, f32[8,48,256]{2,1,0:T(8,128)S(1)}, u32[]{:S(2)}, u32[]{:S(2)}) collective-permute-start(f32[8,48,256]{2,1,0:T(8,128)S(1)} %get-tuple-element.67.refs_2_), channel_id=1, source_target_pairs={{0,96},{8,104},{16,112},{24,120},{32,64},{40,72},{48,80},{56,88},{... | collective-permute-start | bytes 1179656 | tf_op jit(solution)/shard_map/ppermute | solution.py:44
  45.5 0.1 fusion.2
  45.6 0.1 collective-permute-start.15
  45.6 0.5 collective-permute-start.21
  46.2 3.3 %collective-permute-done.12.refs_4_ = f32[8,48,256]{2,1,0:T(8,128)S(1)} collective-permute-done((f32[8,48,256]{2,1,0:T(8,128)S(1)}, f32[8,48,256]{2,1,0:T(8,128)S(1)}, u32[]{:S(2)}, u32[]{:S(2)}) %collective-permute-start.12) | collective-permute-done | bytes 393248 | tf_op jit(solution)/shard_map/ppermute | solution.py:44
  49.5 0.8 collective-permute-done.13.refs_5_
  50.3 1.6 %collective-permute-start.23 = (f32[8,48,256]{2,1,0:T(8,128)S(1)}, f32[8,48,256]{2,1,0:T(8,128)S(1)}, u32[]{:S(2)}, u32[]{:S(2)}) collective-permute-start(f32[8,48,256]{2,1,0:T(8,128)S(1)} %get-tuple-element.66.refs_2_), channel_id=1, source_target_pairs={{0,96},{8,104},{16,112},{24,120},{32,64},{40,72},{48,80},{56,88},{... | collective-permute-start | bytes 1179656 | tf_op jit(solution)/shard_map/ppermute | solution.py:44
  51.9 0.1 pad_add_fusion.1.place_ref
  52.0 0.3 collective-permute-done.15.refs_7_
  52.3 7.8 %chunk_product.2 = (f32[4,128,256]{2,1,0:T(8,128)S(1)}, f32[4,128,256]{2,1,0:T(8,128)S(1)}) custom-call(s32[3]{0:T(128)S(1)} %pad_add_fusion.1.place_ref, bf16[1024,3072]{1,0:T(8,128)(2,1)S(1)} %get-tuple-element.42.a_high, bf16[1024,3072]{1,0:T(8,128)(2,1)S(1)} %get-tuple-element.43.a_low, f32[8,48,256]{2,1,0:T(8,128)S(1)} %get-tuple-element.71.refs_0_, ...), custom_call_target="tpu_custom_call" | custom-call | tf_op jit(solution)/shard_map/chunk_product/pallas_call | solution.py:150
  60.1 12.3 %collective-permute-start.16 = (f32[4,128,256]{2,1,0:T(8,128)S(1)}, f32[4,128,256]{2,1,0:T(8,128)S(1)}, u32[]{:S(2)}, u32[]{:S(2)}) collective-permute-start(f32[4,128,256]{2,1,0:T(8,128)S(1)} %get-tuple-element.49), channel_id=1, source_target_pairs={{0,1},{1,0},{2,3},{3,2},{4,5},{5,4},{6,7},{7,6},{8,9},{9,8},{10,11... | collective-permute-start | bytes 1572872 | tf_op jit(solution)/shard_map/ppermute | solution.py:21
  72.4 7.8 %chunk_product.3 = (f32[4,128,256]{2,1,0:T(8,128)S(1)}, f32[4,128,256]{2,1,0:T(8,128)S(1)}) custom-call(s32[3]{0:T(128)S(1)} %pad_add_fusion.1.place_ref, bf16[1024,3072]{1,0:T(8,128)(2,1)S(1)} %get-tuple-element.42.a_high, bf16[1024,3072]{1,0:T(8,128)(2,1)S(1)} %get-tuple-element.43.a_low, f32[8,48,256]{2,1,0:T(8,128)S(1)} %get-tuple-element.70.refs_0_, ...), custom_call_target="tpu_custom_call" | custom-call | tf_op jit(solution)/shard_map/chunk_product/pallas_call | solution.py:150
  80.3 0.1 collective-permute-start.25
  80.4 0.1 add.56
  80.5 1.3 %collective-permute-start.17 = (f32[2,128,256]{2,1,0:T(8,128)S(1)}, f32[2,128,256]{2,1,0:T(8,128)S(1)}, u32[]{:S(2)}, u32[]{:S(2)}) collective-permute-start(f32[2,128,256]{2,1,0:T(8,128)S(1)} %stack.43), channel_id=1, source_target_pairs={{0,2},{1,3},{2,0},{3,1},{4,6},{5,7},{6,4},{7,5},{8,10},{9,11},{10,... | collective-permute-start | bytes 786440 | tf_op jit(solution)/shard_map/ppermute | solution.py:174
  81.8 0.5 collective-permute-done.25
  82.3 0.1 add.59
  82.4 2.6 %collective-permute-start.26 = (f32[2,128,256]{2,1,0:T(8,128)S(1)}, f32[2,128,256]{2,1,0:T(8,128)S(1)}, u32[]{:S(2)}, u32[]{:S(2)}) collective-permute-start(f32[2,128,256]{2,1,0:T(8,128)S(1)} %pad_maximum_fusion.8), channel_id=1, source_target_pairs={{0,6},{1,7},{2,4},{3,5},{4,2},{5,3},{6,0},{7,1},{8,14},{9,15},{10,... | collective-permute-start | bytes 786440 | tf_op jit(solution)/shard_map/ppermute | solution.py:174
  84.9 3.0 %collective-permute-done.17 = f32[2,128,256]{2,1,0:T(8,128)S(1)} collective-permute-done((f32[2,128,256]{2,1,0:T(8,128)S(1)}, f32[2,128,256]{2,1,0:T(8,128)S(1)}, u32[]{:S(2)}, u32[]{:S(2)}) %collective-permute-start.17) | collective-permute-done | bytes 262176 | tf_op jit(solution)/shard_map/ppermute | solution.py:174
  88.0 2.7 %collective-permute-start.18 = (f32[128,256]{1,0:T(8,128)S(1)}, f32[128,256]{1,0:T(8,128)S(1)}, u32[]{:S(2)}, u32[]{:S(2)}) collective-permute-start(f32[128,256]{1,0:T(8,128)S(1)} %get-tuple-element.76), channel_id=1, source_target_pairs={{0,6},{1,7},{2,4},{3,5},{4,2},{5,3},{6,0},{7,1},{8,14},{9,15},{10,... | collective-permute-start | bytes 393224 | tf_op jit(solution)/shard_map/ppermute | solution.py:174
  90.7 0.6 collective-permute-done.26
  91.3 0.2 collective-permute-start.27
  91.6 1.7 %collective-permute-done.18.refs_2_ = f32[128,256]{1,0:T(8,128)S(1)} collective-permute-done((f32[128,256]{1,0:T(8,128)S(1)}, f32[128,256]{1,0:T(8,128)S(1)}, u32[]{:S(2)}, u32[]{:S(2)}) %collective-permute-start.18) | collective-permute-done | bytes 131104 | tf_op jit(solution)/shard_map/ppermute | solution.py:174
  93.3 0.8 leaf_rows.2
  94.1 2.6 %collective-permute-start.19 = (f32[96,256]{1,0:T(8,128)S(1)}, f32[96,256]{1,0:T(8,128)S(1)}, u32[]{:S(2)}, u32[]{:S(2)}) collective-permute-start(f32[96,256]{1,0:T(8,128)S(1)} %get-tuple-element.51.own_ref.refs_1_), channel_id=1, source_target_pairs={{0,1},{1,0},{2,3},{3,2},{4,5},{5,4},{6,7},{7,6},{8,9},{9,8},{10,11... | collective-permute-start | bytes 294920 | tf_op jit(solution)/shard_map/ppermute | solution.py:21
  96.7 0.8 leaf_rows.3
  97.5 0.9 collective-permute-start.28
  98.4 0.8 mid_rows.2
  99.2 0.1 collective-permute-start.20
  99.3 0.8 mid_rows.3
  100.1 1.5 %collective-permute-start.29 = (f32[96,256]{1,0:T(8,128)S(1)}, f32[96,256]{1,0:T(8,128)S(1)}, u32[]{:S(2)}, u32[]{:S(2)}) collective-permute-start(f32[96,256]{1,0:T(8,128)S(1)} %get-tuple-element.59.refs_8_), channel_id=1, source_target_pairs={{0,2},{1,3},{2,0},{3,1},{4,6},{5,7},{6,4},{7,5},{8,10},{9,11},{10,... | collective-permute-start | bytes 294920 | tf_op jit(solution)/shard_map/ppermute | solution.py:21
  101.6 2.0 %collective-permute-done.20.refs_4_ = f32[96,256]{1,0:T(8,128)S(1)} collective-permute-done((f32[96,256]{1,0:T(8,128)S(1)}, f32[96,256]{1,0:T(8,128)S(1)}, u32[]{:S(2)}, u32[]{:S(2)}) %collective-permute-start.20) | collective-permute-done | bytes 98336 | tf_op jit(solution)/shard_map/ppermute | solution.py:21
  103.7 2.1 %collective-permute-done.29.refs_9_ = f32[96,256]{1,0:T(8,128)S(1)} collective-permute-done((f32[96,256]{1,0:T(8,128)S(1)}, f32[96,256]{1,0:T(8,128)S(1)}, u32[]{:S(2)}, u32[]{:S(2)}) %collective-permute-start.29) | collective-permute-done | bytes 98336 | tf_op jit(solution)/shard_map/ppermute | solution.py:21
  105.8 9.8 %interpolation.1 = (f32[96,128]{1,0:T(8,128)}, f32[96,192]{1,0:T(8,128)}, f32[96,192]{1,0:T(8,128)}, f32[96,512]{1,0:T(8,128)}) custom-call(s32[5]{0:T(128)S(1)} %stack.36.info_ref, s32[3,96]{1,0:T(4,128)S(1)} %pad_add_fusion.pivots_ref, f32[128,256]{1,0:T(8,128)S(1)} %get-tuple-element.50.refs_0_, f32[96,256]{1,0:T(8,128)S(1)} %get-tuple-element.51.own_ref.refs_1_, ...), custom_call_target="tpu_custom_call" | custom-call | tf_op jit(solution)/shard_map/interpolation/pallas_call | solution.py:358
  (40 shorter events, 0.5 us)
Async XLA Ops:
  0.6 9.8 %copy-start = (s32[128,128]{1,0:T(8,128)S(1)}, s32[128,128]{1,0:T(8,128)}, u32[]{:S(2)}) copy-start(s32[128,128]{1,0:T(8,128)} %param.11) | copy-start | bytes 196612
  1.7 8.7 %collective-permute-start = (f32[1,48,512]{2,1,0:T(8,128)S(1)}, f32[1,48,512]{2,1,0:T(8,128)S(1)}, u32[]{:S(2)}, u32[]{:S(2)}) collective-permute-start(f32[1,48,512]{2,1,0:T(8,128)S(1)} %get-tuple-element.80), channel_id=1, source_target_pairs={{0,32},{8,40},{16,48},{24,56},{32,0},{40,8},{48,16},{56,24},{64,96... | collective-permute-start | bytes 294920 | tf_op jit(solution)/shard_map/ppermute | solution.py:44
  3.9 6.5 %collective-permute-start.1 = (f32[1,48,512]{2,1,0:T(8,128)S(1)}, f32[1,48,512]{2,1,0:T(8,128)S(1)}, u32[]{:S(2)}, u32[]{:S(2)}) collective-permute-start(f32[1,48,512]{2,1,0:T(8,128)S(1)} %get-tuple-element.79), channel_id=1, source_target_pairs={{0,96},{8,104},{16,112},{24,120},{32,64},{40,72},{48,80},{56,88},{... | collective-permute-start | bytes 294920 | tf_op jit(solution)/shard_map/ppermute | solution.py:44
  5.9 4.6 %collective-permute-start.2 = (f32[1,48,512]{2,1,0:T(8,128)S(1)}, f32[1,48,512]{2,1,0:T(8,128)S(1)}, u32[]{:S(2)}, u32[]{:S(2)}) collective-permute-start(f32[1,48,512]{2,1,0:T(8,128)S(1)} %get-tuple-element.81), channel_id=1, source_target_pairs={{0,8},{8,0},{16,24},{24,16},{32,40},{40,32},{48,56},{56,48},{64,72... | collective-permute-start | bytes 294920 | tf_op jit(solution)/shard_map/ppermute | solution.py:44
  7.5 4.7 %collective-permute-start.3 = (f32[1,48,512]{2,1,0:T(8,128)S(1)}, f32[1,48,512]{2,1,0:T(8,128)S(1)}, u32[]{:S(2)}, u32[]{:S(2)}) collective-permute-start(f32[1,48,512]{2,1,0:T(8,128)S(1)} %get-tuple-element.78), channel_id=1, source_target_pairs={{0,24},{8,16},{16,8},{24,0},{32,56},{40,48},{48,40},{56,32},{64,88... | collective-permute-start | bytes 294920 | tf_op jit(solution)/shard_map/ppermute | solution.py:44
  12.2 5.8 %collective-permute-start.4 = (f32[2,48,512]{2,1,0:T(8,128)S(1)}, f32[2,48,512]{2,1,0:T(8,128)S(1)}, u32[]{:S(2)}, u32[]{:S(2)}) collective-permute-start(f32[2,48,512]{2,1,0:T(8,128)S(1)} %pad_maximum_fusion.9), channel_id=1, source_target_pairs={{0,96},{8,104},{16,112},{24,120},{32,64},{40,72},{48,80},{56,88},{... | collective-permute-start | bytes 589832 | tf_op jit(solution)/shard_map/ppermute | solution.py:44
  13.1 5.7 %collective-permute-start.6 = (f32[2,48,512]{2,1,0:T(8,128)S(1)}, f32[2,48,512]{2,1,0:T(8,128)S(1)}, u32[]{:S(2)}, u32[]{:S(2)}) collective-permute-start(f32[2,48,512]{2,1,0:T(8,128)S(1)} %pad_maximum_fusion.10), channel_id=1, source_target_pairs={{0,32},{8,40},{16,48},{24,56},{32,0},{40,8},{48,16},{56,24},{64,96... | collective-permute-start | bytes 589832 | tf_op jit(solution)/shard_map/ppermute | solution.py:44
  13.2 7.7 %collective-permute-start.8 = (f32[2,48,512]{2,1,0:T(8,128)S(1)}, f32[2,48,512]{2,1,0:T(8,128)S(1)}, u32[]{:S(2)}, u32[]{:S(2)}) collective-permute-start(f32[2,48,512]{2,1,0:T(8,128)S(1)} %pad_maximum_fusion.11), channel_id=1, source_target_pairs={{0,24},{8,16},{16,8},{24,0},{32,56},{40,48},{48,40},{56,32},{64,88... | collective-permute-start | bytes 589832 | tf_op jit(solution)/shard_map/ppermute | solution.py:44
  15.8 17.6 %collective-permute-start.10 = (f32[2,48,512]{2,1,0:T(8,128)S(1)}, f32[2,48,512]{2,1,0:T(8,128)S(1)}, u32[]{:S(2)}, u32[]{:S(2)}) collective-permute-start(f32[2,48,512]{2,1,0:T(8,128)S(1)} %pad_maximum_fusion.12), channel_id=1, source_target_pairs={{0,8},{8,0},{16,24},{24,16},{32,40},{40,32},{48,56},{56,48},{64,72... | collective-permute-start | bytes 589832 | tf_op jit(solution)/shard_map/ppermute | solution.py:44
  18.0 16.9 %collective-permute-start.5 = (f32[4,48,512]{2,1,0:T(8,128)S(1)}, f32[4,48,512]{2,1,0:T(8,128)S(1)}, u32[]{:S(2)}, u32[]{:S(2)}) collective-permute-start(f32[4,48,512]{2,1,0:T(8,128)S(1)} %pad_maximum_fusion.4), channel_id=1, source_target_pairs={{0,8},{8,0},{16,24},{24,16},{32,40},{40,32},{48,56},{56,48},{64,72... | collective-permute-start | bytes 1179656 | tf_op jit(solution)/shard_map/ppermute | solution.py:44
  18.7 16.3 %collective-permute-start.7 = (f32[4,48,512]{2,1,0:T(8,128)S(1)}, f32[4,48,512]{2,1,0:T(8,128)}, u32[]{:S(2)}, u32[]{:S(2)}) collective-permute-start(f32[4,48,512]{2,1,0:T(8,128)S(1)} %pad_maximum_fusion.5), channel_id=1, source_target_pairs={{0,24},{8,16},{16,8},{24,0},{32,56},{40,48},{48,40},{56,32},{64,88... | collective-permute-start | bytes 1179656 | tf_op jit(solution)/shard_map/ppermute | solution.py:44
  20.9 15.1 %collective-permute-start.9 = (f32[4,48,512]{2,1,0:T(8,128)S(1)}, f32[4,48,512]{2,1,0:T(8,128)}, u32[]{:S(2)}, u32[]{:S(2)}) collective-permute-start(f32[4,48,512]{2,1,0:T(8,128)S(1)} %pad_maximum_fusion.6), channel_id=1, source_target_pairs={{0,32},{8,40},{16,48},{24,56},{32,0},{40,8},{48,16},{56,24},{64,96... | collective-permute-start | bytes 1179656 | tf_op jit(solution)/shard_map/ppermute | solution.py:44
  26.9 4.6 %copy-start.1 = (f32[1024,3072]{1,0:T(8,128)S(1)}, f32[1024,3072]{1,0:T(8,128)}, u32[]{:S(2)}) copy-start(f32[1024,3072]{1,0:T(8,128)} %value_ref.1) | copy-start | bytes 37748740
  33.4 7.9 %collective-permute-start.11 = (f32[4,48,512]{2,1,0:T(8,128)S(1)}, f32[4,48,512]{2,1,0:T(8,128)S(1)}, u32[]{:S(2)}, u32[]{:S(2)}) collective-permute-start(f32[4,48,512]{2,1,0:T(8,128)S(1)} %pad_maximum_fusion.7), channel_id=1, source_target_pairs={{0,96},{8,104},{16,112},{24,120},{32,64},{40,72},{48,80},{56,88},{... | collective-permute-start | bytes 1179656 | tf_op jit(solution)/shard_map/ppermute | solution.py:44
  41.6 7.9 %collective-permute-start.12 = (f32[8,48,256]{2,1,0:T(8,128)S(1)}, f32[8,48,256]{2,1,0:T(8,128)S(1)}, u32[]{:S(2)}, u32[]{:S(2)}) collective-permute-start(f32[8,48,256]{2,1,0:T(8,128)S(1)} %get-tuple-element.71.refs_0_), channel_id=1, source_target_pairs={{0,24},{8,16},{16,8},{24,0},{32,56},{40,48},{48,40},{56,32},{64,88... | collective-permute-start | bytes 1179656 | tf_op jit(solution)/shard_map/ppermute | solution.py:44
  43.7 6.6 %collective-permute-start.13 = (f32[8,48,256]{2,1,0:T(8,128)S(1)}, f32[8,48,256]{2,1,0:T(8,128)S(1)}, u32[]{:S(2)}, u32[]{:S(2)}) collective-permute-start(f32[8,48,256]{2,1,0:T(8,128)S(1)} %get-tuple-element.69.refs_1_), channel_id=1, source_target_pairs={{0,8},{8,0},{16,24},{24,16},{32,40},{40,32},{48,56},{56,48},{64,72... | collective-permute-start | bytes 1179656 | tf_op jit(solution)/shard_map/ppermute | solution.py:44
  43.8 8.1 %collective-permute-start.14 = (f32[8,48,256]{2,1,0:T(8,128)S(1)}, f32[8,48,256]{2,1,0:T(8,128)S(1)}, u32[]{:S(2)}, u32[]{:S(2)}) collective-permute-start(f32[8,48,256]{2,1,0:T(8,128)S(1)} %get-tuple-element.67.refs_2_), channel_id=1, source_target_pairs={{0,96},{8,104},{16,112},{24,120},{32,64},{40,72},{48,80},{56,88},{... | collective-permute-start | bytes 1179656 | tf_op jit(solution)/shard_map/ppermute | solution.py:44
  45.6 6.7 %collective-permute-start.15 = (f32[8,48,256]{2,1,0:T(8,128)S(1)}, f32[8,48,256]{2,1,0:T(8,128)S(1)}, u32[]{:S(2)}, u32[]{:S(2)}) collective-permute-start(f32[8,48,256]{2,1,0:T(8,128)S(1)} %get-tuple-element.65.refs_3_), channel_id=1, source_target_pairs={{0,32},{8,40},{16,48},{24,56},{32,0},{40,8},{48,16},{56,24},{64,96... | collective-permute-start | bytes 1179656 | tf_op jit(solution)/shard_map/ppermute | solution.py:44
  45.6 26.8 %collective-permute-start.21 = (f32[8,48,256]{2,1,0:T(8,128)S(1)}, f32[8,48,256]{2,1,0:T(8,128)S(1)}, u32[]{:S(2)}, u32[]{:S(2)}) collective-permute-start(f32[8,48,256]{2,1,0:T(8,128)S(1)} %get-tuple-element.70.refs_0_), channel_id=1, source_target_pairs={{0,24},{8,16},{16,8},{24,0},{32,56},{40,48},{48,40},{56,32},{64,88... | collective-permute-start | bytes 1179656 | tf_op jit(solution)/shard_map/ppermute | solution.py:44
  49.5 22.9 %collective-permute-start.22 = (f32[8,48,256]{2,1,0:T(8,128)S(1)}, f32[8,48,256]{2,1,0:T(8,128)S(1)}, u32[]{:S(2)}, u32[]{:S(2)}) collective-permute-start(f32[8,48,256]{2,1,0:T(8,128)S(1)} %get-tuple-element.68.refs_1_), channel_id=1, source_target_pairs={{0,8},{8,0},{16,24},{24,16},{32,40},{40,32},{48,56},{56,48},{64,72... | collective-permute-start | bytes 1179656 | tf_op jit(solution)/shard_map/ppermute | solution.py:44
  50.3 22.1 %collective-permute-start.23 = (f32[8,48,256]{2,1,0:T(8,128)S(1)}, f32[8,48,256]{2,1,0:T(8,128)S(1)}, u32[]{:S(2)}, u32[]{:S(2)}) collective-permute-start(f32[8,48,256]{2,1,0:T(8,128)S(1)} %get-tuple-element.66.refs_2_), channel_id=1, source_target_pairs={{0,96},{8,104},{16,112},{24,120},{32,64},{40,72},{48,80},{56,88},{... | collective-permute-start | bytes 1179656 | tf_op jit(solution)/shard_map/ppermute | solution.py:44
  51.9 20.5 %collective-permute-start.24 = (f32[8,48,256]{2,1,0:T(8,128)S(1)}, f32[8,48,256]{2,1,0:T(8,128)S(1)}, u32[]{:S(2)}, u32[]{:S(2)}) collective-permute-start(f32[8,48,256]{2,1,0:T(8,128)S(1)} %get-tuple-element.64.refs_3_), channel_id=1, source_target_pairs={{0,32},{8,40},{16,48},{24,56},{32,0},{40,8},{48,16},{56,24},{64,96... | collective-permute-start | bytes 1179656 | tf_op jit(solution)/shard_map/ppermute | solution.py:44
  60.1 20.3 %collective-permute-start.16 = (f32[4,128,256]{2,1,0:T(8,128)S(1)}, f32[4,128,256]{2,1,0:T(8,128)S(1)}, u32[]{:S(2)}, u32[]{:S(2)}) collective-permute-start(f32[4,128,256]{2,1,0:T(8,128)S(1)} %get-tuple-element.49), channel_id=1, source_target_pairs={{0,1},{1,0},{2,3},{3,2},{4,5},{5,4},{6,7},{7,6},{8,9},{9,8},{10,11... | collective-permute-start | bytes 1572872 | tf_op jit(solution)/shard_map/ppermute | solution.py:21
  80.3 2.0 %collective-permute-start.25 = (f32[4,128,256]{2,1,0:T(8,128)S(1)}, f32[4,128,256]{2,1,0:T(8,128)S(1)}, u32[]{:S(2)}, u32[]{:S(2)}) collective-permute-start(f32[4,128,256]{2,1,0:T(8,128)S(1)} %get-tuple-element.55), channel_id=1, source_target_pairs={{0,1},{1,0},{2,3},{3,2},{4,5},{5,4},{6,7},{7,6},{8,9},{9,8},{10,11... | collective-permute-start | bytes 1572872 | tf_op jit(solution)/shard_map/ppermute | solution.py:21
  80.5 7.5 %collective-permute-start.17 = (f32[2,128,256]{2,1,0:T(8,128)S(1)}, f32[2,128,256]{2,1,0:T(8,128)S(1)}, u32[]{:S(2)}, u32[]{:S(2)}) collective-permute-start(f32[2,128,256]{2,1,0:T(8,128)S(1)} %stack.43), channel_id=1, source_target_pairs={{0,2},{1,3},{2,0},{3,1},{4,6},{5,7},{6,4},{7,5},{8,10},{9,11},{10,... | collective-permute-start | bytes 786440 | tf_op jit(solution)/shard_map/ppermute | solution.py:174
  82.4 8.9 %collective-permute-start.26 = (f32[2,128,256]{2,1,0:T(8,128)S(1)}, f32[2,128,256]{2,1,0:T(8,128)S(1)}, u32[]{:S(2)}, u32[]{:S(2)}) collective-permute-start(f32[2,128,256]{2,1,0:T(8,128)S(1)} %pad_maximum_fusion.8), channel_id=1, source_target_pairs={{0,6},{1,7},{2,4},{3,5},{4,2},{5,3},{6,0},{7,1},{8,14},{9,15},{10,... | collective-permute-start | bytes 786440 | tf_op jit(solution)/shard_map/ppermute | solution.py:174
  88.0 5.3 %collective-permute-start.18 = (f32[128,256]{1,0:T(8,128)S(1)}, f32[128,256]{1,0:T(8,128)S(1)}, u32[]{:S(2)}, u32[]{:S(2)}) collective-permute-start(f32[128,256]{1,0:T(8,128)S(1)} %get-tuple-element.76), channel_id=1, source_target_pairs={{0,6},{1,7},{2,4},{3,5},{4,2},{5,3},{6,0},{7,1},{8,14},{9,15},{10,... | collective-permute-start | bytes 393224 | tf_op jit(solution)/shard_map/ppermute | solution.py:174
  91.3 5.3 %collective-permute-start.27 = (f32[128,256]{1,0:T(8,128)S(1)}, f32[128,256]{1,0:T(8,128)S(1)}, u32[]{:S(2)}, u32[]{:S(2)}) collective-permute-start(f32[128,256]{1,0:T(8,128)S(1)} %get-tuple-element.72), channel_id=1, source_target_pairs={{0,2},{1,3},{2,0},{3,1},{4,6},{5,7},{6,4},{7,5},{8,10},{9,11},{10,... | collective-permute-start | bytes 393224 | tf_op jit(solution)/shard_map/ppermute | solution.py:174
  94.1 4.3 %collective-permute-start.19 = (f32[96,256]{1,0:T(8,128)S(1)}, f32[96,256]{1,0:T(8,128)S(1)}, u32[]{:S(2)}, u32[]{:S(2)}) collective-permute-start(f32[96,256]{1,0:T(8,128)S(1)} %get-tuple-element.51.own_ref.refs_1_), channel_id=1, source_target_pairs={{0,1},{1,0},{2,3},{3,2},{4,5},{5,4},{6,7},{7,6},{8,9},{9,8},{10,11... | collective-permute-start | bytes 294920 | tf_op jit(solution)/shard_map/ppermute | solution.py:21
  97.5 1.9 %collective-permute-start.28 = (f32[96,256]{1,0:T(8,128)S(1)}, f32[96,256]{1,0:T(8,128)S(1)}, u32[]{:S(2)}, u32[]{:S(2)}) collective-permute-start(f32[96,256]{1,0:T(8,128)S(1)} %get-tuple-element.57.own_ref.refs_6_), channel_id=1, source_target_pairs={{0,1},{1,0},{2,3},{3,2},{4,5},{5,4},{6,7},{7,6},{8,9},{9,8},{10,11... | collective-permute-start | bytes 294920 | tf_op jit(solution)/shard_map/ppermute | solution.py:21
  99.2 4.5 %collective-permute-start.20 = (f32[96,256]{1,0:T(8,128)S(1)}, f32[96,256]{1,0:T(8,128)S(1)}, u32[]{:S(2)}, u32[]{:S(2)}) collective-permute-start(f32[96,256]{1,0:T(8,128)S(1)} %get-tuple-element.53.refs_3_), channel_id=1, source_target_pairs={{0,2},{1,3},{2,0},{3,1},{4,6},{5,7},{6,4},{7,5},{8,10},{9,11},{10,... | collective-permute-start | bytes 294920 | tf_op jit(solution)/shard_map/ppermute | solution.py:21
  100.1 5.7 %collective-permute-start.29 = (f32[96,256]{1,0:T(8,128)S(1)}, f32[96,256]{1,0:T(8,128)S(1)}, u32[]{:S(2)}, u32[]{:S(2)}) collective-permute-start(f32[96,256]{1,0:T(8,128)S(1)} %get-tuple-element.59.refs_8_), channel_id=1, source_target_pairs={{0,2},{1,3},{2,0},{3,1},{4,6},{5,7},{6,4},{7,5},{8,10},{9,11},{10,... | collective-permute-start | bytes 294920 | tf_op jit(solution)/shard_map/ppermute | solution.py:21

commit v3 on v2

--- a/solution.py
+++ b/solution.py
@@ -11,6 +11,7 @@
 KMAX = 96
 SIDE = 4
 LEAF = 128
+LEAVES = 128
 WIDTHS = (256, 256)
 K_STEPS = 4
 
@@ -26,44 +27,44 @@
 
 
 FIRST, SECOND = 1, 3
-ROUTES = (
-    (("y", FIRST), ("y", SECOND), ("z", FIRST), ("z", SECOND)),
-    (("y", SECOND), ("y", FIRST), ("z", SECOND), ("z", FIRST)),
-    (("z", FIRST), ("z", SECOND), ("y", FIRST), ("y", SECOND)),
-    (("z", SECOND), ("z", FIRST), ("y", SECOND), ("y", FIRST)),
-)
-
-
-def row_mask(step):
-    axis, mask = step
-    return mask * SIDE if axis == "y" else mask
-
-
-def from_row(value, step):
-    mask = row_mask(step)
-    return lax.ppermute(value, "row", [(source, source ^ mask) for source in range(SIDE * SIDE)])
-
-
-def origins(route):
-    masks = [0]
-    for step in route:
-        masks += [mask ^ row_mask(step) for mask in masks]
-    return masks
-
-
-def gather_parts(sketch, ready):
-    depth = sketch.shape[0] // len(ROUTES)
-    stacks = [sketch[None, part * depth : (part + 1) * depth] for part in range(len(ROUTES))]
-    for at in range(3):
-        received = [from_row(stack, route[at]) for stack, route in zip(stacks, ROUTES)]
-        if at == 0:
-            received = lax.optimization_barrier(received)
+ORDERS = ((FIRST, SECOND), (SECOND, FIRST))
+
+
+def row_mask(core, step, masks):
+    along_y = (step < 2) == (core == 0)
+    return masks[step % 2] * SIDE if along_y else masks[step % 2]
+
+
+def from_row(value, step, masks):
+    columns = 2 * SIDE
+    pairs = []
+    for row in range(SIDE * SIDE):
+        for column in range(columns):
+            partner = row ^ row_mask(column % 2, step, masks)
+            pairs.append((row * columns + column, partner * columns + column))
+    return lax.ppermute(value, ("row", "col"), pairs)
+
+
+def origins(core, masks):
+    found = [0]
+    for step in range(4):
+        found += [mask ^ row_mask(core, step, masks) for mask in found]
+    return found
+
+
+def gather_parts(sketch, before, after):
+    depth = sketch.shape[0] // len(ORDERS)
+    stacks = [sketch[None, part * depth : (part + 1) * depth] for part in range(len(ORDERS))]
+    for step in range(3):
+        received = [from_row(stack, step, masks) for stack, masks in zip(stacks, ORDERS)]
+        if step == 1:
+            received, before = lax.optimization_barrier((received, before))
         stacks = [jnp.concatenate(pair, 0) for pair in zip(stacks, received)]
-    stacks, ready = lax.optimization_barrier((stacks, ready))
+    stacks, ready = lax.optimization_barrier((stacks, after(*before)))
     chunks, start = [], 0
     for width in WIDTHS:
         own = [stack[:, :, start : start + width] for stack in stacks]
-        chunks.append(own + [from_row(value, route[3]) for value, route in zip(own, ROUTES)])
+        chunks.append(own + [from_row(value, 3, masks) for value, masks in zip(own, ORDERS)])
         start += width
     return chunks, ready
 
@@ -84,7 +85,7 @@
         grid=(rows // LEAF,),
         in_specs=[block],
         out_specs=[block] * 2,
-        compiler_params=pltpu.CompilerParams(vmem_limit_bytes=16 * 2**20),
+        compiler_params=pltpu.CompilerParams(vmem_limit_bytes=8 * 2**20),
         cost_estimate=pl.CostEstimate(
             flops=4 * rows * order, bytes_accessed=8 * rows * order, transcendentals=0
         ),
@@ -93,19 +94,19 @@
 
 
 def product_kernel(place_ref, a_high, a_low, *refs):
-    parts = len(ROUTES)
+    parts = len(ORDERS)
     pieces = refs[: 2 * parts]
-    other_ref, own_ref, high, low, total = refs[2 * parts :]
+    own_ref, other_ref, high, low, total = refs[2 * parts :]
     step = pl.program_id(0)
 
     @pl.when(step == 0)
     def _():
         depth = pieces[0].shape[1]
-        for part, route in enumerate(ROUTES):
-            masks = origins(route)
-            for at, mask in enumerate(masks):
+        for part, masks in enumerate(ORDERS):
+            for at, (mask_0, mask_1) in enumerate(zip(origins(0, masks), origins(1, masks))):
                 source = pieces[part + parts * (at // 8)]
-                block = jnp.bitwise_xor(place_ref[1], mask)
+                mask = jnp.where(place_ref[2] == 0, mask_0, mask_1)
+                block = jnp.bitwise_xor(place_ref[0], mask)
                 start = pl.multiple_of((block * parts + part) * depth, depth)
                 value = source[at % 8]
                 top = value.astype(jnp.bfloat16)
@@ -114,11 +115,11 @@
                     jnp.bfloat16
                 )
 
-    k_rows = a_high.shape[-1]
+    k_rows = a_high.shape[-1] // K_STEPS
     rows = pl.ds(pl.multiple_of(step * k_rows, 256), k_rows)
-    left, right = a_high[...], high[rows, :]
+    left, right = a_high[:, rows], high[rows, :]
     result = jnp.dot(
-        jnp.concatenate([left, left, a_low[...]], 1),
+        jnp.concatenate([left, left, a_low[:, rows]], 1),
         jnp.concatenate([right, low[rows, :], right], 0),
         preferred_element_type=jnp.float32,
     )
@@ -133,19 +134,17 @@
 
     @pl.when(step == K_STEPS - 1)
     def _():
-        core, x = place_ref[0], place_ref[2]
-        for away in range(SIDE):
-            chip = jnp.bitwise_xor(x, away)
-            own_ref[away] = total[chip * 2 + core]
-            other_ref[away] = total[chip * 2 + 1 - core]
+        for at, masks in enumerate(zip((0, SECOND, FIRST, FIRST ^ SECOND), (0, FIRST, SECOND, FIRST ^ SECOND))):
+            for out_ref, core in ((own_ref, place_ref[2]), (other_ref, 1 - place_ref[2])):
+                chip = jnp.bitwise_xor(place_ref[1], jnp.where(core == 0, *masks))
+                out_ref[at] = total[chip * 2 + core]
 
 
 def chunk_product(high, low, pieces, place):
     rows, order = high.shape
     width = pieces[0].shape[-1]
-    k_rows = order // K_STEPS
     leaves = rows // LEAF // 2
-    left = pl.BlockSpec((rows, k_rows), lambda k, place: (0, k))
+    in_vmem = pl.BlockSpec(memory_space=pltpu.VMEM)
     out = jax.ShapeDtypeStruct((leaves, LEAF, width), jnp.float32)
     return pl.pallas_call(
         product_kernel,
@@ -153,32 +152,31 @@
         grid_spec=pltpu.PrefetchScalarGridSpec(
             num_scalar_prefetch=1,
             grid=(K_STEPS,),
-            in_specs=[left] * 2 + [pl.BlockSpec(memory_space=pltpu.VMEM)] * len(pieces),
-            out_specs=[pl.BlockSpec(memory_space=pltpu.VMEM)] * 2,
+            in_specs=[in_vmem] * (2 + len(pieces)),
+            out_specs=[in_vmem] * 2,
             scratch_shapes=[
                 pltpu.VMEM((order, width), jnp.bfloat16),
                 pltpu.VMEM((order, width), jnp.bfloat16),
                 pltpu.VMEM((2 * leaves, LEAF, width), jnp.float32),
             ],
         ),
-        compiler_params=pltpu.CompilerParams(vmem_limit_bytes=36 * 2**20),
+        compiler_params=pltpu.CompilerParams(vmem_limit_bytes=24 * 2**20),
         name="chunk_product",
     )(place, high, low, *pieces)
 
 
-X_ROUTES = ((FIRST, SECOND), (SECOND, FIRST))
-
-
-def from_x(value, mask):
-    pairs = [(source, source ^ (2 * mask)) for source in range(2 * SIDE)]
+def from_x(value, step):
+    pairs = []
+    for column in range(2 * SIDE):
+        mask = ORDERS[column % 2][step]
+        pairs.append((column, column ^ (2 * mask)))
     return lax.ppermute(value, "col", pairs)
 
 
-def sum_over_col(other, own, route):
-    near, far = route
+def sum_over_col(own, other):
     core_sum = own + from_partner(other, "col", 0)
-    kept = from_x(jnp.stack([core_sum[near], core_sum[near ^ far]]), near)
-    return [core_sum[0], kept[0], from_x(core_sum[far] + kept[1], far)]
+    kept = from_x(core_sum[2:], 0)
+    return [core_sum[0], kept[0], from_x(core_sum[1] + kept[1], 1)]
 
 
 BLOCK = 8
@@ -292,21 +290,27 @@
         target[target_at + row : target_at + row + 1, :] = jnp.where(row < rank, picked, 0.0)
 
 
-def leaf_kernel(info_ref, pivots_ref, *refs):
+def rank_of(info_ref, ranks_ref, level):
+    place = info_ref[0] // 2**level
+    starts = [0, LEAVES, LEAVES + LEAVES // 2]
+    return ranks_ref[starts[level] + place]
+
+
+def leaf_kernel(info_ref, ranks_ref, pivots_ref, *refs):
     parts, (rows_ref, skeleton_ref) = refs[:-2], refs[-2:]
     rows_ref[...] = functools.reduce(jnp.add, [part[...] for part in parts])
-    select_rows(rows_ref, pivots_ref, 0, info_ref[2], skeleton_ref, 0)
-
-
-def mid_kernel(info_ref, pivots_ref, own_ref, other_ref, rows_ref, skeleton_ref):
-    own_at = pl.multiple_of(info_ref[0] * KMAX, KMAX)
-    other_at = pl.multiple_of((1 - info_ref[0]) * KMAX, KMAX)
+    select_rows(rows_ref, pivots_ref, 0, rank_of(info_ref, ranks_ref, 0), skeleton_ref, 0)
+
+
+def mid_kernel(info_ref, ranks_ref, pivots_ref, own_ref, other_ref, rows_ref, skeleton_ref):
+    own_at = pl.multiple_of((info_ref[0] % 2) * KMAX, KMAX)
+    other_at = pl.multiple_of((1 - info_ref[0] % 2) * KMAX, KMAX)
     rows_ref[pl.ds(own_at, KMAX), :] = own_ref[...]
     rows_ref[pl.ds(other_at, KMAX), :] = other_ref[...]
-    select_rows(rows_ref, pivots_ref, 1, info_ref[3], skeleton_ref, 0)
-
-
-def top_kernel(info_ref, pivots_ref, *refs):
+    select_rows(rows_ref, pivots_ref, 1, rank_of(info_ref, ranks_ref, 1), skeleton_ref, 0)
+
+
+def top_kernel(info_ref, ranks_ref, pivots_ref, *refs):
     chunks = len(WIDTHS)
     groups = [refs[5 * chunk : 5 * chunk + 5] for chunk in range(chunks)]
     leaf_out, mid_out, top_out, rows_out = refs[5 * chunks : 5 * chunks + 4]
@@ -314,13 +318,13 @@
     tops, chosen, (rows_scratch, new_scratch) = (
         scratch[:chunks], scratch[chunks : 2 * chunks], scratch[2 * chunks :]
     )
-    own_at = pl.multiple_of(info_ref[1] * KMAX, KMAX)
-    other_at = pl.multiple_of((1 - info_ref[1]) * KMAX, KMAX)
+    own_at = pl.multiple_of((info_ref[0] // 2 % 2) * KMAX, KMAX)
+    other_at = pl.multiple_of((1 - info_ref[0] // 2 % 2) * KMAX, KMAX)
     start = 0
     for group, top, skeleton in zip(groups, tops, chosen):
         top[pl.ds(own_at, KMAX), :] = group[3][...]
         top[pl.ds(other_at, KMAX), :] = group[4][...]
-        select_rows(top, pivots_ref, 2, info_ref[4], skeleton, 0)
+        select_rows(top, pivots_ref, 2, rank_of(info_ref, ranks_ref, 2), skeleton, 0)
         width = skeleton.shape[-1]
         rows_out[:, start : start + width] = skeleton[...]
         start += width
@@ -343,7 +347,7 @@
         cross = functools.reduce(
             jnp.add, [dot(row[...], part[...]) for row, part in zip(rows, skeletons)]
         )
-        empty = (row_ids == column_ids) & (row_ids >= info_ref[2 + node])
+        empty = (row_ids == column_ids) & (row_ids >= rank_of(info_ref, ranks_ref, node))
         grams.append(gram * (1.0 / SAMPLES) + jnp.where(empty, 1.0, 0.0))
         crosses.append(cross * (1.0 / SAMPLES))
     inverses = invert_all(grams, rows_scratch, new_scratch)
@@ -354,16 +358,16 @@
 def vmem_call(kernel, outs, scratch, name):
     in_vmem = pl.BlockSpec(memory_space=pltpu.VMEM)
 
-    def call(info, pivots, *arrays):
+    def call(info, ranks, pivots, *arrays):
         return pl.pallas_call(
             kernel,
             out_shape=[jax.ShapeDtypeStruct(shape, jnp.float32) for shape in outs],
-            in_specs=[pl.BlockSpec(memory_space=pltpu.SMEM)] * 2 + [in_vmem] * len(arrays),
+            in_specs=[pl.BlockSpec(memory_space=pltpu.SMEM)] * 3 + [in_vmem] * len(arrays),
             out_specs=[in_vmem] * len(outs),
             scratch_shapes=scratch,
-            compiler_params=pltpu.CompilerParams(vmem_limit_bytes=32 * 2**20),
+            compiler_params=pltpu.CompilerParams(vmem_limit_bytes=8 * 2**20),
             name=name,
-        )(info, pivots, *arrays)
+        )(info, ranks, pivots, *arrays)
 
     return call
 
@@ -375,33 +379,27 @@
     col_index = lax.axis_index("col")
     row_index = lax.axis_index("row")
     leaf_index = row_index * col_count + col_index
-    place = jnp.stack([col_index % 2, row_index, col_index // 2]).astype(jnp.int32)
+    place = jnp.stack([row_index, col_index // 2, col_index % 2]).astype(jnp.int32)
     nodes = (leaf_index, leaf_index // 2, leaf_index // 4)
-    ranks = [
-        pick_entry(table, node)
-        for table, node in zip((leaf_ranks, mid_ranks, top_ranks), nodes)
-    ]
-    info = jnp.stack([col_index % 2, col_index // 2 % 2] + ranks).astype(jnp.int32)
-    pivots = jnp.stack(
-        [
-            pick_entry(table, node)[:KMAX]
-            for table, node in zip((leaf_pivots, mid_pivots, top_pivots), nodes)
-        ]
-    )
-    chunks, (high, low, info, pivots) = gather_parts(sketch, (*split(frontal), info, pivots))
-    groups = [
-        sum_over_col(*chunk_product(high, low, pieces, place), route)
-        for pieces, route in zip(chunks, X_ROUTES)
-    ]
+
+    def prepare(frontal, *tables):
+        ranks = jnp.concatenate(tables[:3])
+        pivots = [pick_entry(table, node)[:KMAX] for table, node in zip(tables[3:], nodes)]
+        return (*split(frontal), ranks, jnp.stack(pivots))
+
+    tables = (leaf_ranks, mid_ranks, top_ranks, leaf_pivots, mid_pivots, top_pivots)
+    chunks, (high, low, ranks, pivots) = gather_parts(sketch, (frontal, *tables), prepare)
+    info = jnp.stack([leaf_index]).astype(jnp.int32)
+    groups = [sum_over_col(*chunk_product(high, low, pieces, place)) for pieces in chunks]
     arrays = []
     for group, width in zip(groups, WIDTHS):
         skeleton_shape, pair_shape = (KMAX, width), (2 * KMAX, width)
         rows, skeleton = vmem_call(
             leaf_kernel, [(LEAF, width), skeleton_shape], [], "leaf_rows"
-        )(info, pivots, *group)
+        )(info, ranks, pivots, *group)
         mid_rows, mid_skeleton = vmem_call(
             mid_kernel, [pair_shape, skeleton_shape], [], "mid_rows"
-        )(info, pivots, skeleton, from_partner(skeleton, "col", 0))
+        )(info, ranks, pivots, skeleton, from_partner(skeleton, "col", 0))
         arrays += [rows, skeleton, mid_rows, mid_skeleton, from_partner(mid_skeleton, "col", 1)]
     scratch = [pltpu.VMEM((2 * KMAX, width), jnp.float32) for width in WIDTHS]
     scratch += [pltpu.VMEM((KMAX, width), jnp.float32) for width in WIDTHS]
@@ -411,7 +409,7 @@
         [(KMAX, LEAF), (KMAX, 2 * KMAX), (KMAX, 2 * KMAX), (KMAX, SAMPLES)],
         scratch,
         "interpolation",
-    )(info, pivots, *arrays)
+    )(info, ranks, pivots, *arrays)
     return tuple(out[None] for out in outs)
 
 

time: 116 us -> 112 us (0.966)
  starting transfers between devices: 46.3 us -> 32.3 us
  local copies, waits for them, and re-layouts: 12.6 us -> 17.6 us
  waiting for transfers between devices: 22.4 us -> 25.9 us
    unnamed x4 -> x18, local copies, waits for them, and re-layouts: 4.59 us -> 15.5 us
    ppermute x20 -> x10, starting transfers between devices: 22.1 us -> 15.2 us  [from_row(): return lax.ppermute(value, ('row', 'col'), pairs)]
    ppermute x6, starting transfers between devices: 17.5 us -> 12 us  [from_partner(): return lax.ppermute(value, axis, pairs)]
    ppermute x20 -> x10, waiting for transfers between devices: 12.4 us -> 16.9 us  [from_row(): return lax.ppermute(value, ('row', 'col'), pairs)]
    dynamic_slice x4 -> x1, local copies, waits for them, and re-layouts: 3.88 us -> 0.01 us  [pick_entry(): return lax.dynamic_index_in_dim(table, position, 0, keepdims=False)]
    another operation x2 -> x0, local copies, waits for them, and re-layouts: 2 us -> none  [the longest x1 1.98 us: on_device(): jnp.stack([col_index % 2, col_index // 2 % 2] + ranks).astype(jnp.int32)]
    ppermute x4, starting transfers between devices: 6.8 us -> 5.11 us  [from_x(): return lax.ppermute(value, 'col', pairs)]
    concatenate x12 -> x6, other arithmetic: 2.39 us -> 2.74 us  [gather_parts(): stacks = [jnp.concatenate(pair, 0) for pair in zip(stacks, received)]]
  transfers between devices with their start and end apart: 30 -> 20, of which waited for: 12 -> 9; matrix products, arithmetic and copies ran while one was open for 8% -> 2% of each run, Pallas kernels for 18% -> 20%
where the time goes in v3:
time: 112 us; the launch traced here: 111 us
  starting transfers between devices  32.3 us (29%)
  Pallas kernels  31.6 us (28%)
  waiting for transfers between devices  25.9 us (23%)
  local copies, waits for them, and re-layouts  17.6 us (16%)
  other arithmetic  3.11 us (3%)
    ppermute x10, waiting for transfers between devices, from_row(): return lax.ppermute(value, ('row', 'col'), pairs)  16.9 us
    pallas_call x2, Pallas kernels, chunk_product(): pl.pallas_call(product_kernel, out_shape=[out] * 2, grid_spec=pltpu.Prefe...  16.7 us
    unnamed x18, local copies, waits for them, and re-layouts  15.5 us
    ppermute x10, starting transfers between devices, from_row(): return lax.ppermute(value, ('row', 'col'), pairs)  15.2 us
    pallas_call x5, Pallas kernels, call(): pl.pallas_call(kernel, out_shape=[jax.ShapeDtypeStruct(shape, jnp.float32...  13 us
    ppermute x6, starting transfers between devices, from_partner(): return lax.ppermute(value, axis, pairs)  12 us
    ppermute x4, waiting for transfers between devices, from_x(): return lax.ppermute(value, 'col', pairs)  5.17 us
    ppermute x4, starting transfers between devices, from_x(): return lax.ppermute(value, 'col', pairs)  5.11 us
  transfers between devices with their start and end apart: 20, of which 9 were waited for; matrix products, arithmetic and copies ran while one was open for 2% of the time, Pallas kernels for 20%

profile of v3, /device:TPU:1, one launch (start us, length us, event | category | flops | bytes accessed | tf_op | source)
XLA Modules:
  0.0 111.4 jit_solution(7331779769665214753)
XLA Ops:
  0.6 0.0 copy-start
  0.6 1.1 slice_bitcast_fusion
  1.7 2.5 %collective-permute-start = (f32[1,96,512]{2,1,0:T(8,128)S(1)}, f32[1,96,512]{2,1,0:T(8,128)S(1)}, u32[]{:S(2)}, u32[]{:S(2)}) collective-permute-start(f32[1,96,512]{2,1,0:T(8,128)S(1)} %get-tuple-element.79), channel_id=1, source_target_pairs={{0,32},{1,9},{2,34},{3,11},{4,36},{5,13},{6,38},{7,15},{8,40},{9,1... | collective-permute-start | bytes 589832 | tf_op jit(solution)/shard_map/ppermute | solution.py:45
  4.3 2.2 %collective-permute-start.2 = (f32[1,96,512]{2,1,0:T(8,128)S(1)}, f32[1,96,512]{2,1,0:T(8,128)S(1)}, u32[]{:S(2)}, u32[]{:S(2)}) collective-permute-start(f32[1,96,512]{2,1,0:T(8,128)S(1)} %get-tuple-element.78), channel_id=1, source_target_pairs={{0,96},{1,25},{2,98},{3,27},{4,100},{5,29},{6,102},{7,31},{8,104},... | collective-permute-start | bytes 589832 | tf_op jit(solution)/shard_map/ppermute | solution.py:45
  6.5 1.1 collective-permute-done
  7.7 3.7 %collective-permute-start.1 = (f32[2,96,512]{2,1,0:T(8,128)S(1)}, f32[2,96,512]{2,1,0:T(8,128)S(1)}, u32[]{:S(2)}, u32[]{:S(2)}) collective-permute-start(f32[2,96,512]{2,1,0:T(8,128)S(1)} %pad_maximum_fusion.4), channel_id=1, source_target_pairs={{0,96},{1,25},{2,98},{3,27},{4,100},{5,29},{6,102},{7,31},{8,104},... | collective-permute-start | bytes 1179656 | tf_op jit(solution)/shard_map/ppermute | solution.py:45
  11.3 0.0 collective-permute-done.2
  11.4 0.1 collective-permute-start.3
  11.4 5.3 %collective-permute-done.1 = f32[2,96,512]{2,1,0:T(8,128)S(1)} collective-permute-done((f32[2,96,512]{2,1,0:T(8,128)S(1)}, f32[2,96,512]{2,1,0:T(8,128)S(1)}, u32[]{:S(2)}, u32[]{:S(2)}) %collective-permute-start.1) | collective-permute-done | bytes 393248 | tf_op jit(solution)/shard_map/ppermute | solution.py:45
  16.8 1.6 %collective-permute-done.3 = f32[2,96,512]{2,1,0:T(8,128)S(1)} collective-permute-done((f32[2,96,512]{2,1,0:T(8,128)S(1)}, f32[2,96,512]{2,1,0:T(8,128)S(1)}, u32[]{:S(2)}, u32[]{:S(2)}) %collective-permute-start.3) | collective-permute-done | bytes 393248 | tf_op jit(solution)/shard_map/ppermute | solution.py:45
  18.4 0.1 pad_maximum_fusion.2
  18.4 1.2 %collective-permute-start.4 = (f32[4,96,512]{2,1,0:T(8,128)S(1)}, f32[4,96,512]{2,1,0:T(8,128)}, u32[]{:S(2)}, u32[]{:S(2)}) collective-permute-start(f32[4,96,512]{2,1,0:T(8,128)S(1)} %pad_maximum_fusion.2), channel_id=1, source_target_pairs={{0,8},{1,33},{2,10},{3,35},{4,12},{5,37},{6,14},{7,39},{8,0},{9,41... | collective-permute-start | bytes 2359304 | tf_op jit(solution)/shard_map/ppermute | solution.py:45
  19.6 0.1 pad_maximum_fusion.3
  19.7 1.9 %collective-permute-start.5 = (f32[4,96,512]{2,1,0:T(8,128)S(1)}, f32[4,96,512]{2,1,0:T(8,128)}, u32[]{:S(2)}, u32[]{:S(2)}) collective-permute-start(f32[4,96,512]{2,1,0:T(8,128)S(1)} %pad_maximum_fusion.3), channel_id=1, source_target_pairs={{0,24},{1,97},{2,26},{3,99},{4,28},{5,101},{6,30},{7,103},{8,16},{... | collective-permute-start | bytes 2359304 | tf_op jit(solution)/shard_map/ppermute | solution.py:45
  21.5 4.6 %copy-done.5 = f32[1024,3072]{1,0:T(8,128)S(1)} copy-done((f32[1024,3072]{1,0:T(8,128)S(1)}, f32[1024,3072]{1,0:T(8,128)}, u32[]{:S(2)}) %copy-start.5) | copy-done | bytes 12582936
  26.1 1.9 %split.1 = (bf16[1024,3072]{1,0:T(8,128)(2,1)S(1)}, bf16[1024,3072]{1,0:T(8,128)(2,1)S(1)}) custom-call(f32[1024,3072]{1,0:T(8,128)S(1)} %copy-done.5), custom_call_target="tpu_custom_call" | custom-call | flops 12582912 | bytes 25165824 | tf_op jit(solution)/shard_map/split/pallas_call | solution.py:82
  28.0 2.6 %copy-done.1 = bf16[1024,3072]{1,0:T(8,128)(2,1)} copy-done((bf16[1024,3072]{1,0:T(8,128)(2,1)}, bf16[1024,3072]{1,0:T(8,128)(2,1)S(1)}, u32[]{:S(2)}) %copy-start.1) | copy-done | bytes 6291480
  30.6 2.7 %copy-done.3 = bf16[1024,3072]{1,0:T(8,128)(2,1)} copy-done((bf16[1024,3072]{1,0:T(8,128)(2,1)}, bf16[1024,3072]{1,0:T(8,128)(2,1)S(1)}, u32[]{:S(2)}) %copy-start.3) | copy-done | bytes 6291480
  33.3 0.1 pad_add_fusion.1.ranks_ref
  33.4 0.7 constant_dynamic-slice_fusion
  34.1 0.0 collective-permute-done.4
  34.1 1.3 %pad_maximum_fusion = f32[8,96,512]{2,1,0:T(8,128)S(1)} fusion(f32[4,96,512]{2,1,0:T(8,128)} %collective-permute-done.4, f32[2,96,512]{2,1,0:T(8,128)S(1)} %collective-permute-done.1, f32[1,96,512]{2,1,0:T(8,128)S(1)} %collective-permute-done, f32[1,96,512]{2,1,0:T(8,128)S(1)} %get-tuple-element.79), kind=kLoop, calls=%fused_computation | loop fusion | flops 1179648 | bytes 3145728 | tf_op jit(solution)/shard_map/concatenate | solution.py:62
  35.4 0.0 collective-permute-done.5
  35.4 1.3 %pad_maximum_fusion.1 = f32[8,96,512]{2,1,0:T(8,128)S(1)} fusion(f32[4,96,512]{2,1,0:T(8,128)} %collective-permute-done.5, f32[2,96,512]{2,1,0:T(8,128)S(1)} %collective-permute-done.3, f32[1,96,512]{2,1,0:T(8,128)S(1)} %collective-permute-done.2, f32[1,96,512]{2,1,0:T(8,128)S(1)} %get-tuple-element.78), kind=kLoop, calls=%fused_computation.1 | loop fusion | flops 1179648 | bytes 3145728 | tf_op jit(solution)/shard_map/concatenate | solution.py:62
  36.7 0.1 fusion.3
  36.9 0.1 fusion.2
  37.0 1.0 collective-permute-start.6
  38.0 0.0 collective-permute-start.7
  38.0 1.9 %collective-permute-start.13 = (f32[8,96,256]{2,1,0:T(8,128)S(1)}, f32[8,96,256]{2,1,0:T(8,128)}, u32[]{:S(2)}, u32[]{:S(2)}) collective-permute-start(f32[8,96,256]{2,1,0:T(8,128)S(1)} %get-tuple-element.72.refs_0_), channel_id=1, source_target_pairs={{0,24},{1,97},{2,26},{3,99},{4,28},{5,101},{6,30},{7,103},{8,16},{... | collective-permute-start | bytes 2359304 | tf_op jit(solution)/shard_map/ppermute | solution.py:45
  39.9 0.8 collective-permute-start.14
  40.7 0.1 pad_add_fusion.2.place_ref
  40.7 8.8 %collective-permute-done.6.refs_2_ = f32[8,96,256]{2,1,0:T(8,128)} collective-permute-done((f32[8,96,256]{2,1,0:T(8,128)S(1)}, f32[8,96,256]{2,1,0:T(8,128)}, u32[]{:S(2)}, u32[]{:S(2)}) %collective-permute-start.6) | collective-permute-done | bytes 786464 | tf_op jit(solution)/shard_map/ppermute | solution.py:45
  49.6 0.0 collective-permute-done.7.refs_3_
  49.6 2.8 %copy-done.2 = bf16[1024,3072]{1,0:T(8,128)(2,1)S(1)} copy-done((bf16[1024,3072]{1,0:T(8,128)(2,1)S(1)}, bf16[1024,3072]{1,0:T(8,128)(2,1)}, u32[]{:S(2)}) %copy-start.2) | copy-done | bytes 6291480
  52.4 2.8 %copy-done.4 = bf16[1024,3072]{1,0:T(8,128)(2,1)S(1)} copy-done((bf16[1024,3072]{1,0:T(8,128)(2,1)S(1)}, bf16[1024,3072]{1,0:T(8,128)(2,1)}, u32[]{:S(2)}) %copy-start.4) | copy-done | bytes 6291480
  55.1 8.3 %chunk_product.2 = (f32[4,128,256]{2,1,0:T(8,128)S(1)}, f32[4,128,256]{2,1,0:T(8,128)S(1)}) custom-call(s32[3]{0:T(128)S(1)} %pad_add_fusion.2.place_ref, bf16[1024,3072]{1,0:T(8,128)(2,1)S(1)} %copy-done.2, bf16[1024,3072]{1,0:T(8,128)(2,1)S(1)} %copy-done.4, f32[8,96,256]{2,1,0:T(8,128)S(1)} %get-tuple-element.73.refs_0_, ...), custom_call_target="tpu_custom_call" | custom-call | tf_op jit(solution)/shard_map/chunk_product/pallas_call | solution.py:149
  63.5 5.1 %collective-permute-start.8 = (f32[4,128,256]{2,1,0:T(8,128)S(1)}, f32[4,128,256]{2,1,0:T(8,128)S(1)}, u32[]{:S(2)}, u32[]{:S(2)}) collective-permute-start(f32[4,128,256]{2,1,0:T(8,128)S(1)} %get-tuple-element.55), channel_id=1, source_target_pairs={{0,1},{1,0},{2,3},{3,2},{4,5},{5,4},{6,7},{7,6},{8,9},{9,8},{10,11... | collective-permute-start | bytes 1572872 | tf_op jit(solution)/shard_map/ppermute | solution.py:22
  68.6 8.3 %chunk_product.3 = (f32[4,128,256]{2,1,0:T(8,128)S(1)}, f32[4,128,256]{2,1,0:T(8,128)S(1)}) custom-call(s32[3]{0:T(128)S(1)} %pad_add_fusion.2.place_ref, bf16[1024,3072]{1,0:T(8,128)(2,1)S(1)} %copy-done.2, bf16[1024,3072]{1,0:T(8,128)(2,1)S(1)} %copy-done.4, f32[8,96,256]{2,1,0:T(8,128)S(1)} %get-tuple-element.72.refs_0_, ...), custom_call_target="tpu_custom_call" | custom-call | tf_op jit(solution)/shard_map/chunk_product/pallas_call | solution.py:149
  77.0 0.1 collective-permute-start.15
  77.1 0.0 collective-permute-done.8
  77.1 0.1 add.45
  77.2 2.6 %collective-permute-start.9 = (f32[2,128,256]{2,1,0:T(8,128)S(1)}, f32[2,128,256]{2,1,0:T(8,128)S(1)}, u32[]{:S(2)}, u32[]{:S(2)}) collective-permute-start(f32[2,128,256]{2,1,0:T(8,128)S(1)} %slice.80), channel_id=1, source_target_pairs={{0,2},{1,7},{2,0},{3,5},{4,6},{5,3},{6,4},{7,1},{8,10},{9,15},{10,... | collective-permute-start | bytes 786440 | tf_op jit(solution)/shard_map/ppermute | solution.py:173
  79.8 0.0 collective-permute-done.15
  79.8 0.1 add.48
  79.9 1.8 %collective-permute-start.16 = (f32[2,128,256]{2,1,0:T(8,128)S(1)}, f32[2,128,256]{2,1,0:T(8,128)S(1)}, u32[]{:S(2)}, u32[]{:S(2)}) collective-permute-start(f32[2,128,256]{2,1,0:T(8,128)S(1)} %slice.85), channel_id=1, source_target_pairs={{0,2},{1,7},{2,0},{3,5},{4,6},{5,3},{6,4},{7,1},{8,10},{9,15},{10,... | collective-permute-start | bytes 786440 | tf_op jit(solution)/shard_map/ppermute | solution.py:173
  81.6 2.1 %collective-permute-done.9 = f32[2,128,256]{2,1,0:T(8,128)S(1)} collective-permute-done((f32[2,128,256]{2,1,0:T(8,128)S(1)}, f32[2,128,256]{2,1,0:T(8,128)S(1)}, u32[]{:S(2)}, u32[]{:S(2)}) %collective-permute-start.9) | collective-permute-done | bytes 262176 | tf_op jit(solution)/shard_map/ppermute | solution.py:173
  83.8 0.4 collective-permute-start.10
  84.1 2.4 %collective-permute-done.16 = f32[2,128,256]{2,1,0:T(8,128)S(1)} collective-permute-done((f32[2,128,256]{2,1,0:T(8,128)S(1)}, f32[2,128,256]{2,1,0:T(8,128)S(1)}, u32[]{:S(2)}, u32[]{:S(2)}) %collective-permute-start.16) | collective-permute-done | bytes 262176 | tf_op jit(solution)/shard_map/ppermute | solution.py:173
  86.6 0.4 collective-permute-start.17
  86.9 0.7 collective-permute-done.10.refs_2_
  87.7 0.8 leaf_rows.2
  88.5 2.9 %collective-permute-start.11 = (f32[96,256]{1,0:T(8,128)S(1)}, f32[96,256]{1,0:T(8,128)S(1)}, u32[]{:S(2)}, u32[]{:S(2)}) collective-permute-start(f32[96,256]{1,0:T(8,128)S(1)} %get-tuple-element.57.own_ref.refs_1_), channel_id=1, source_target_pairs={{0,1},{1,0},{2,3},{3,2},{4,5},{5,4},{6,7},{7,6},{8,9},{9,8},{10,11... | collective-permute-start | bytes 294920 | tf_op jit(solution)/shard_map/ppermute | solution.py:22
  91.3 0.0 collective-permute-done.17.refs_2_
  91.3 0.8 leaf_rows.3
  92.2 2.1 %collective-permute-start.18 = (f32[96,256]{1,0:T(8,128)S(1)}, f32[96,256]{1,0:T(8,128)S(1)}, u32[]{:S(2)}, u32[]{:S(2)}) collective-permute-start(f32[96,256]{1,0:T(8,128)S(1)} %get-tuple-element.63.own_ref.refs_6_), channel_id=1, source_target_pairs={{0,1},{1,0},{2,3},{3,2},{4,5},{5,4},{6,7},{7,6},{8,9},{9,8},{10,11... | collective-permute-start | bytes 294920 | tf_op jit(solution)/shard_map/ppermute | solution.py:22
  94.2 0.0 collective-permute-done.11.other_ref
  94.2 0.8 mid_rows.2
  95.0 0.8 collective-permute-start.12
  95.9 0.0 collective-permute-done.18.other_ref
  95.9 0.8 mid_rows.3
  96.7 1.0 collective-permute-start.19
  97.7 1.9 %collective-permute-done.12.refs_4_ = f32[96,256]{1,0:T(8,128)S(1)} collective-permute-done((f32[96,256]{1,0:T(8,128)S(1)}, f32[96,256]{1,0:T(8,128)S(1)}, u32[]{:S(2)}, u32[]{:S(2)}) %collective-permute-start.12) | collective-permute-done | bytes 98336 | tf_op jit(solution)/shard_map/ppermute | solution.py:22
  99.5 2.0 %collective-permute-done.19.refs_9_ = f32[96,256]{1,0:T(8,128)S(1)} collective-permute-done((f32[96,256]{1,0:T(8,128)S(1)}, f32[96,256]{1,0:T(8,128)S(1)}, u32[]{:S(2)}, u32[]{:S(2)}) %collective-permute-start.19) | collective-permute-done | bytes 98336 | tf_op jit(solution)/shard_map/ppermute | solution.py:22
  101.6 9.8 %interpolation.1 = (f32[96,128]{1,0:T(8,128)}, f32[96,192]{1,0:T(8,128)}, f32[96,192]{1,0:T(8,128)}, f32[96,512]{1,0:T(8,128)}) custom-call(s32[1]{0:T(128)} %bitcast.info_ref, s32[224]{0:T(256)S(1)} %pad_add_fusion.1.ranks_ref, s32[3,96]{1,0:T(4,128)S(1)} %pad_add_fusion.pivots_ref, f32[128,256]{1,0:T(8,128)S(1)} %get-tuple-element.56.refs_0_, ...), custom_call_target="tpu_custom_call" | custom-call | tf_op jit(solution)/shard_map/interpolation/pallas_call | solution.py:362
  (22 shorter events, 0.2 us)
Async XLA Ops:
  0.6 32.7 %copy-start = (s32[128,128]{1,0:T(8,128)S(1)}, s32[128,128]{1,0:T(8,128)}, u32[]{:S(2)}) copy-start(s32[128,128]{1,0:T(8,128)} %param.11) | copy-start | bytes 196612
  1.7 5.9 %collective-permute-start = (f32[1,96,512]{2,1,0:T(8,128)S(1)}, f32[1,96,512]{2,1,0:T(8,128)S(1)}, u32[]{:S(2)}, u32[]{:S(2)}) collective-permute-start(f32[1,96,512]{2,1,0:T(8,128)S(1)} %get-tuple-element.79), channel_id=1, source_target_pairs={{0,32},{1,9},{2,34},{3,11},{4,36},{5,13},{6,38},{7,15},{8,40},{9,1... | collective-permute-start | bytes 589832 | tf_op jit(solution)/shard_map/ppermute | solution.py:45
  4.3 7.0 %collective-permute-start.2 = (f32[1,96,512]{2,1,0:T(8,128)S(1)}, f32[1,96,512]{2,1,0:T(8,128)S(1)}, u32[]{:S(2)}, u32[]{:S(2)}) collective-permute-start(f32[1,96,512]{2,1,0:T(8,128)S(1)} %get-tuple-element.78), channel_id=1, source_target_pairs={{0,96},{1,25},{2,98},{3,27},{4,100},{5,29},{6,102},{7,31},{8,104},... | collective-permute-start | bytes 589832 | tf_op jit(solution)/shard_map/ppermute | solution.py:45
  7.7 9.1 %collective-permute-start.1 = (f32[2,96,512]{2,1,0:T(8,128)S(1)}, f32[2,96,512]{2,1,0:T(8,128)S(1)}, u32[]{:S(2)}, u32[]{:S(2)}) collective-permute-start(f32[2,96,512]{2,1,0:T(8,128)S(1)} %pad_maximum_fusion.4), channel_id=1, source_target_pairs={{0,96},{1,25},{2,98},{3,27},{4,100},{5,29},{6,102},{7,31},{8,104},... | collective-permute-start | bytes 1179656 | tf_op jit(solution)/shard_map/ppermute | solution.py:45
  11.4 7.0 %collective-permute-start.3 = (f32[2,96,512]{2,1,0:T(8,128)S(1)}, f32[2,96,512]{2,1,0:T(8,128)S(1)}, u32[]{:S(2)}, u32[]{:S(2)}) collective-permute-start(f32[2,96,512]{2,1,0:T(8,128)S(1)} %pad_maximum_fusion.5), channel_id=1, source_target_pairs={{0,32},{1,9},{2,34},{3,11},{4,36},{5,13},{6,38},{7,15},{8,40},{9,1... | collective-permute-start | bytes 1179656 | tf_op jit(solution)/shard_map/ppermute | solution.py:45
  18.4 15.7 %collective-permute-start.4 = (f32[4,96,512]{2,1,0:T(8,128)S(1)}, f32[4,96,512]{2,1,0:T(8,128)}, u32[]{:S(2)}, u32[]{:S(2)}) collective-permute-start(f32[4,96,512]{2,1,0:T(8,128)S(1)} %pad_maximum_fusion.2), channel_id=1, source_target_pairs={{0,8},{1,33},{2,10},{3,35},{4,12},{5,37},{6,14},{7,39},{8,0},{9,41... | collective-permute-start | bytes 2359304 | tf_op jit(solution)/shard_map/ppermute | solution.py:45
  19.7 15.8 %collective-permute-start.5 = (f32[4,96,512]{2,1,0:T(8,128)S(1)}, f32[4,96,512]{2,1,0:T(8,128)}, u32[]{:S(2)}, u32[]{:S(2)}) collective-permute-start(f32[4,96,512]{2,1,0:T(8,128)S(1)} %pad_maximum_fusion.3), channel_id=1, source_target_pairs={{0,24},{1,97},{2,26},{3,99},{4,28},{5,101},{6,30},{7,103},{8,16},{... | collective-permute-start | bytes 2359304 | tf_op jit(solution)/shard_map/ppermute | solution.py:45
  21.5 4.6 %copy-start.5 = (f32[1024,3072]{1,0:T(8,128)S(1)}, f32[1024,3072]{1,0:T(8,128)}, u32[]{:S(2)}) copy-start(f32[1024,3072]{1,0:T(8,128)} %value_ref) | copy-start | bytes 37748740
  26.1 7.2 %copy-start.6 = (s32[32]{0:T(128)S(1)}, s32[32]{0:T(128)}, u32[]{:S(2)}) copy-start(s32[32]{0:T(128)} %param.14) | copy-start | bytes 388
  26.1 7.2 %copy-start.7 = (s32[64]{0:T(128)S(1)}, s32[64]{0:T(128)}, u32[]{:S(2)}) copy-start(s32[64]{0:T(128)} %param.12) | copy-start | bytes 772
  26.1 7.2 %copy-start.8 = (s32[128]{0:T(128)S(1)}, s32[128]{0:T(128)}, u32[]{:S(2)}) copy-start(s32[128]{0:T(128)} %param.10) | copy-start | bytes 1540
  28.0 2.7 %copy-start.1 = (bf16[1024,3072]{1,0:T(8,128)(2,1)}, bf16[1024,3072]{1,0:T(8,128)(2,1)S(1)}, u32[]{:S(2)}) copy-start(bf16[1024,3072]{1,0:T(8,128)(2,1)S(1)} %get-tuple-element.50.a_high) | copy-start | bytes 18874372
  30.6 2.7 %copy-start.3 = (bf16[1024,3072]{1,0:T(8,128)(2,1)}, bf16[1024,3072]{1,0:T(8,128)(2,1)S(1)}, u32[]{:S(2)}) copy-start(bf16[1024,3072]{1,0:T(8,128)(2,1)S(1)} %get-tuple-element.51.a_low) | copy-start | bytes 18874372
  37.0 12.5 %collective-permute-start.6 = (f32[8,96,256]{2,1,0:T(8,128)S(1)}, f32[8,96,256]{2,1,0:T(8,128)}, u32[]{:S(2)}, u32[]{:S(2)}) collective-permute-start(f32[8,96,256]{2,1,0:T(8,128)S(1)} %get-tuple-element.73.refs_0_), channel_id=1, source_target_pairs={{0,24},{1,97},{2,26},{3,99},{4,28},{5,101},{6,30},{7,103},{8,16},{... | collective-permute-start | bytes 2359304 | tf_op jit(solution)/shard_map/ppermute | solution.py:45
  38.0 11.6 %collective-permute-start.7 = (f32[8,96,256]{2,1,0:T(8,128)S(1)}, f32[8,96,256]{2,1,0:T(8,128)}, u32[]{:S(2)}, u32[]{:S(2)}) collective-permute-start(f32[8,96,256]{2,1,0:T(8,128)S(1)} %get-tuple-element.71.refs_1_), channel_id=1, source_target_pairs={{0,8},{1,33},{2,10},{3,35},{4,12},{5,37},{6,14},{7,39},{8,0},{9,41... | collective-permute-start | bytes 2359304 | tf_op jit(solution)/shard_map/ppermute | solution.py:45
  38.0 30.6 %collective-permute-start.13 = (f32[8,96,256]{2,1,0:T(8,128)S(1)}, f32[8,96,256]{2,1,0:T(8,128)}, u32[]{:S(2)}, u32[]{:S(2)}) collective-permute-start(f32[8,96,256]{2,1,0:T(8,128)S(1)} %get-tuple-element.72.refs_0_), channel_id=1, source_target_pairs={{0,24},{1,97},{2,26},{3,99},{4,28},{5,101},{6,30},{7,103},{8,16},{... | collective-permute-start | bytes 2359304 | tf_op jit(solution)/shard_map/ppermute | solution.py:45
  39.9 28.8 %collective-permute-start.14 = (f32[8,96,256]{2,1,0:T(8,128)S(1)}, f32[8,96,256]{2,1,0:T(8,128)}, u32[]{:S(2)}, u32[]{:S(2)}) collective-permute-start(f32[8,96,256]{2,1,0:T(8,128)S(1)} %get-tuple-element.70.refs_1_), channel_id=1, source_target_pairs={{0,8},{1,33},{2,10},{3,35},{4,12},{5,37},{6,14},{7,39},{8,0},{9,41... | collective-permute-start | bytes 2359304 | tf_op jit(solution)/shard_map/ppermute | solution.py:45
  49.6 2.8 %copy-start.2 = (bf16[1024,3072]{1,0:T(8,128)(2,1)S(1)}, bf16[1024,3072]{1,0:T(8,128)(2,1)}, u32[]{:S(2)}) copy-start(bf16[1024,3072]{1,0:T(8,128)(2,1)} %copy-done.1) | copy-start | bytes 18874372
  52.4 2.8 %copy-start.4 = (bf16[1024,3072]{1,0:T(8,128)(2,1)S(1)}, bf16[1024,3072]{1,0:T(8,128)(2,1)}, u32[]{:S(2)}) copy-start(bf16[1024,3072]{1,0:T(8,128)(2,1)} %copy-done.3) | copy-start | bytes 18874372
  63.5 13.6 %collective-permute-start.8 = (f32[4,128,256]{2,1,0:T(8,128)S(1)}, f32[4,128,256]{2,1,0:T(8,128)S(1)}, u32[]{:S(2)}, u32[]{:S(2)}) collective-permute-start(f32[4,128,256]{2,1,0:T(8,128)S(1)} %get-tuple-element.55), channel_id=1, source_target_pairs={{0,1},{1,0},{2,3},{3,2},{4,5},{5,4},{6,7},{7,6},{8,9},{9,8},{10,11... | collective-permute-start | bytes 1572872 | tf_op jit(solution)/shard_map/ppermute | solution.py:22
  77.0 2.8 %collective-permute-start.15 = (f32[4,128,256]{2,1,0:T(8,128)S(1)}, f32[4,128,256]{2,1,0:T(8,128)S(1)}, u32[]{:S(2)}, u32[]{:S(2)}) collective-permute-start(f32[4,128,256]{2,1,0:T(8,128)S(1)} %get-tuple-element.61), channel_id=1, source_target_pairs={{0,1},{1,0},{2,3},{3,2},{4,5},{5,4},{6,7},{7,6},{8,9},{9,8},{10,11... | collective-permute-start | bytes 1572872 | tf_op jit(solution)/shard_map/ppermute | solution.py:22
  77.2 6.5 %collective-permute-start.9 = (f32[2,128,256]{2,1,0:T(8,128)S(1)}, f32[2,128,256]{2,1,0:T(8,128)S(1)}, u32[]{:S(2)}, u32[]{:S(2)}) collective-permute-start(f32[2,128,256]{2,1,0:T(8,128)S(1)} %slice.80), channel_id=1, source_target_pairs={{0,2},{1,7},{2,0},{3,5},{4,6},{5,3},{6,4},{7,1},{8,10},{9,15},{10,... | collective-permute-start | bytes 786440 | tf_op jit(solution)/shard_map/ppermute | solution.py:173
  79.9 6.7 %collective-permute-start.16 = (f32[2,128,256]{2,1,0:T(8,128)S(1)}, f32[2,128,256]{2,1,0:T(8,128)S(1)}, u32[]{:S(2)}, u32[]{:S(2)}) collective-permute-start(f32[2,128,256]{2,1,0:T(8,128)S(1)} %slice.85), channel_id=1, source_target_pairs={{0,2},{1,7},{2,0},{3,5},{4,6},{5,3},{6,4},{7,1},{8,10},{9,15},{10,... | collective-permute-start | bytes 786440 | tf_op jit(solution)/shard_map/ppermute | solution.py:173
  83.8 3.9 %collective-permute-start.10 = (f32[128,256]{1,0:T(8,128)S(1)}, f32[128,256]{1,0:T(8,128)S(1)}, u32[]{:S(2)}, u32[]{:S(2)}) collective-permute-start(f32[128,256]{1,0:T(8,128)S(1)} %get-tuple-element.76), channel_id=1, source_target_pairs={{0,6},{1,3},{2,4},{3,1},{4,2},{5,7},{6,0},{7,5},{8,14},{9,11},{10,... | collective-permute-start | bytes 393224 | tf_op jit(solution)/shard_map/ppermute | solution.py:173
  86.6 4.8 %collective-permute-start.17 = (f32[128,256]{1,0:T(8,128)S(1)}, f32[128,256]{1,0:T(8,128)S(1)}, u32[]{:S(2)}, u32[]{:S(2)}) collective-permute-start(f32[128,256]{1,0:T(8,128)S(1)} %get-tuple-element.74), channel_id=1, source_target_pairs={{0,6},{1,3},{2,4},{3,1},{4,2},{5,7},{6,0},{7,5},{8,14},{9,11},{10,... | collective-permute-start | bytes 393224 | tf_op jit(solution)/shard_map/ppermute | solution.py:173
  88.5 5.7 %collective-permute-start.11 = (f32[96,256]{1,0:T(8,128)S(1)}, f32[96,256]{1,0:T(8,128)S(1)}, u32[]{:S(2)}, u32[]{:S(2)}) collective-permute-start(f32[96,256]{1,0:T(8,128)S(1)} %get-tuple-element.57.own_ref.refs_1_), channel_id=1, source_target_pairs={{0,1},{1,0},{2,3},{3,2},{4,5},{5,4},{6,7},{7,6},{8,9},{9,8},{10,11... | collective-permute-start | bytes 294920 | tf_op jit(solution)/shard_map/ppermute | solution.py:22
  92.2 3.7 %collective-permute-start.18 = (f32[96,256]{1,0:T(8,128)S(1)}, f32[96,256]{1,0:T(8,128)S(1)}, u32[]{:S(2)}, u32[]{:S(2)}) collective-permute-start(f32[96,256]{1,0:T(8,128)S(1)} %get-tuple-element.63.own_ref.refs_6_), channel_id=1, source_target_pairs={{0,1},{1,0},{2,3},{3,2},{4,5},{5,4},{6,7},{7,6},{8,9},{9,8},{10,11... | collective-permute-start | bytes 294920 | tf_op jit(solution)/shard_map/ppermute | solution.py:22
  95.0 4.5 %collective-permute-start.12 = (f32[96,256]{1,0:T(8,128)S(1)}, f32[96,256]{1,0:T(8,128)S(1)}, u32[]{:S(2)}, u32[]{:S(2)}) collective-permute-start(f32[96,256]{1,0:T(8,128)S(1)} %get-tuple-element.59.refs_3_), channel_id=1, source_target_pairs={{0,2},{1,3},{2,0},{3,1},{4,6},{5,7},{6,4},{7,5},{8,10},{9,11},{10,... | collective-permute-start | bytes 294920 | tf_op jit(solution)/shard_map/ppermute | solution.py:22
  96.7 4.9 %collective-permute-start.19 = (f32[96,256]{1,0:T(8,128)S(1)}, f32[96,256]{1,0:T(8,128)S(1)}, u32[]{:S(2)}, u32[]{:S(2)}) collective-permute-start(f32[96,256]{1,0:T(8,128)S(1)} %get-tuple-element.65.refs_8_), channel_id=1, source_target_pairs={{0,2},{1,3},{2,0},{3,1},{4,6},{5,7},{6,4},{7,5},{8,10},{9,11},{10,... | collective-permute-start | bytes 294920 | tf_op jit(solution)/shard_map/ppermute | solution.py:22

commit v4 on v3

--- a/solution.py
+++ b/solution.py
@@ -13,7 +13,6 @@
 LEAF = 128
 LEAVES = 128
 WIDTHS = (256, 256)
-K_STEPS = 4
 
 
 def from_partner(value, axis, apart):
@@ -59,11 +58,16 @@
         received = [from_row(stack, step, masks) for stack, masks in zip(stacks, ORDERS)]
         if step == 1:
             received, before = lax.optimization_barrier((received, before))
-        stacks = [jnp.concatenate(pair, 0) for pair in zip(stacks, received)]
-    stacks, ready = lax.optimization_barrier((stacks, after(*before)))
+        if step < 2:
+            stacks = [jnp.concatenate(pair, 0) for pair in zip(stacks, received)]
+    stacks, received, ready = lax.optimization_barrier((stacks, received, after(*before)))
     chunks, start = [], 0
     for width in WIDTHS:
-        own = [stack[:, :, start : start + width] for stack in stacks]
+        columns = slice(start, start + width)
+        own = [
+            jnp.concatenate([stack[:, :, columns], other[:, :, columns]], 0)
+            for stack, other in zip(stacks, received)
+        ]
         chunks.append(own + [from_row(value, 3, masks) for value, masks in zip(own, ORDERS)])
         start += width
     return chunks, ready
@@ -71,98 +75,98 @@
 
 def split_kernel(value_ref, high_ref, low_ref):
     value = value_ref[...]
+    rows = pl.ds(pl.multiple_of(pl.program_id(0) * LEAF, LEAF), LEAF)
     high = value.astype(jnp.bfloat16)
-    high_ref[...] = high
-    low_ref[...] = (value - high.astype(jnp.float32)).astype(jnp.bfloat16)
+    high_ref[rows, :] = high
+    low_ref[rows, :] = (value - high.astype(jnp.float32)).astype(jnp.bfloat16)
 
 
 def split(value):
     rows, order = value.shape
-    block = pl.BlockSpec((LEAF, order), lambda i: (i, 0))
     return pl.pallas_call(
         split_kernel,
-        out_shape=[jax.ShapeDtypeStruct(value.shape, jnp.bfloat16)] * 2,
+        out_shape=[pltpu.VMEM(value.shape, jnp.bfloat16)] * 2,
         grid=(rows // LEAF,),
-        in_specs=[block],
-        out_specs=[block] * 2,
+        in_specs=[pl.BlockSpec((LEAF, order), lambda i: (i, 0))],
+        out_specs=[pl.BlockSpec(memory_space=pltpu.VMEM)] * 2,
         compiler_params=pltpu.CompilerParams(vmem_limit_bytes=8 * 2**20),
         cost_estimate=pl.CostEstimate(
             flops=4 * rows * order, bytes_accessed=8 * rows * order, transcendentals=0
         ),
         name="split",
-    )(value)
-
-
-def product_kernel(place_ref, a_high, a_low, *refs):
+    )(pltpu.with_memory_space_constraint(value, pltpu.HBM))
+
+
+def convert(place_ref, pieces, high, low):
     parts = len(ORDERS)
-    pieces = refs[: 2 * parts]
-    own_ref, other_ref, high, low, total = refs[2 * parts :]
-    step = pl.program_id(0)
-
-    @pl.when(step == 0)
-    def _():
-        depth = pieces[0].shape[1]
-        for part, masks in enumerate(ORDERS):
-            for at, (mask_0, mask_1) in enumerate(zip(origins(0, masks), origins(1, masks))):
-                source = pieces[part + parts * (at // 8)]
-                mask = jnp.where(place_ref[2] == 0, mask_0, mask_1)
-                block = jnp.bitwise_xor(place_ref[0], mask)
-                start = pl.multiple_of((block * parts + part) * depth, depth)
-                value = source[at % 8]
-                top = value.astype(jnp.bfloat16)
-                high[pl.ds(start, depth), :] = top
-                low[pl.ds(start, depth), :] = (value - top.astype(jnp.float32)).astype(
-                    jnp.bfloat16
-                )
-
-    k_rows = a_high.shape[-1] // K_STEPS
-    rows = pl.ds(pl.multiple_of(step * k_rows, 256), k_rows)
-    left, right = a_high[:, rows], high[rows, :]
-    result = jnp.dot(
-        jnp.concatenate([left, left, a_low[:, rows]], 1),
-        jnp.concatenate([right, low[rows, :], right], 0),
+    depth = pieces[0].shape[1]
+    for part, masks in enumerate(ORDERS):
+        for at, (mask_0, mask_1) in enumerate(zip(origins(0, masks), origins(1, masks))):
+            source = pieces[part + parts * (at // 8)]
+            mask = jnp.where(place_ref[2] == 0, mask_0, mask_1)
+            block = jnp.bitwise_xor(place_ref[0], mask)
+            start = pl.multiple_of((block * parts + part) * depth, depth)
+            value = source[at % 8]
+            top = value.astype(jnp.bfloat16)
+            high[pl.ds(start, depth), :] = top
+            low[pl.ds(start, depth), :] = (value - top.astype(jnp.float32)).astype(jnp.bfloat16)
+
+
+def multiply(place_ref, core, a_high, a_low, high, low, total, out_ref):
+    left = a_high[:, core].reshape(-1, high.shape[0])
+    low_left = a_low[:, core].reshape(-1, high.shape[0])
+    right = high[...]
+    total[...] = jnp.dot(
+        jnp.concatenate([left, left, low_left], 1),
+        jnp.concatenate([right, low[...], right], 0),
         preferred_element_type=jnp.float32,
-    )
-
-    @pl.when(step == 0)
-    def _():
-        total[...] = result.reshape(total.shape)
-
-    @pl.when(step > 0)
-    def _():
-        total[...] += result.reshape(total.shape)
-
-    @pl.when(step == K_STEPS - 1)
-    def _():
-        for at, masks in enumerate(zip((0, SECOND, FIRST, FIRST ^ SECOND), (0, FIRST, SECOND, FIRST ^ SECOND))):
-            for out_ref, core in ((own_ref, place_ref[2]), (other_ref, 1 - place_ref[2])):
-                chip = jnp.bitwise_xor(place_ref[1], jnp.where(core == 0, *masks))
-                out_ref[at] = total[chip * 2 + core]
-
-
-def chunk_product(high, low, pieces, place):
-    rows, order = high.shape
+    ).reshape(total.shape)
+    orders = zip((0, SECOND, FIRST, FIRST ^ SECOND), (0, FIRST, SECOND, FIRST ^ SECOND))
+    for at, masks in enumerate(orders):
+        chip = jnp.bitwise_xor(place_ref[1], jnp.where(core == 0, *masks))
+        out_ref[at] = total[chip]
+
+
+def other_kernel(place_ref, a_high, a_low, *refs):
+    pieces = refs[: 2 * len(ORDERS)]
+    out_ref, high, low, total = refs[2 * len(ORDERS) :]
+    convert(place_ref, pieces, high, low)
+    multiply(place_ref, 1 - place_ref[2], a_high, a_low, high, low, total, out_ref)
+
+
+def own_kernel(place_ref, a_high, a_low, high, low, out_ref, total):
+    multiply(place_ref, place_ref[2], a_high, a_low, high, low, total, out_ref)
+
+
+def product(kernel, place, halves, arrays, outs, cost, name):
+    in_vmem = pl.BlockSpec(memory_space=pltpu.VMEM)
+    halves = [pltpu.with_memory_space_constraint(half, pltpu.VMEM) for half in halves]
+    return pl.pallas_call(
+        kernel,
+        out_shape=outs,
+        in_specs=[pl.BlockSpec(memory_space=pltpu.SMEM)] + [in_vmem] * (2 + len(arrays)),
+        out_specs=[in_vmem] * len(outs),
+        scratch_shapes=[pltpu.VMEM(outs[0].shape, jnp.float32)],
+        compiler_params=pltpu.CompilerParams(vmem_limit_bytes=24 * 2**20),
+        cost_estimate=pl.CostEstimate(flops=cost, bytes_accessed=cost // 400, transcendentals=0),
+        name=name,
+    )(place, *halves, *arrays)
+
+
+def product_other(halves, pieces, place):
+    leaves, _, leaf, order = halves[0].shape
     width = pieces[0].shape[-1]
-    leaves = rows // LEAF // 2
-    in_vmem = pl.BlockSpec(memory_space=pltpu.VMEM)
-    out = jax.ShapeDtypeStruct((leaves, LEAF, width), jnp.float32)
-    return pl.pallas_call(
-        product_kernel,
-        out_shape=[out] * 2,
-        grid_spec=pltpu.PrefetchScalarGridSpec(
-            num_scalar_prefetch=1,
-            grid=(K_STEPS,),
-            in_specs=[in_vmem] * (2 + len(pieces)),
-            out_specs=[in_vmem] * 2,
-            scratch_shapes=[
-                pltpu.VMEM((order, width), jnp.bfloat16),
-                pltpu.VMEM((order, width), jnp.bfloat16),
-                pltpu.VMEM((2 * leaves, LEAF, width), jnp.float32),
-            ],
-        ),
-        compiler_params=pltpu.CompilerParams(vmem_limit_bytes=24 * 2**20),
-        name="chunk_product",
-    )(place, high, low, *pieces)
+    outs = [jax.ShapeDtypeStruct((leaves, leaf, width), jnp.float32)]
+    outs += [jax.ShapeDtypeStruct((order, width), jnp.bfloat16)] * 2
+    return product(other_kernel, place, halves, pieces, outs, 1, "product_other")
+
+
+def product_own(halves, sketch, place, last):
+    leaves, _, leaf, order = halves[0].shape
+    width = sketch[0].shape[-1]
+    outs = [jax.ShapeDtypeStruct((leaves, leaf, width), jnp.float32)]
+    cost = 6 * leaves * leaf * order * width if last else 1
+    return product(own_kernel, place, halves, sketch, outs, cost, "product_own")[0]
 
 
 def from_x(value, step):
@@ -173,8 +177,7 @@
     return lax.ppermute(value, "col", pairs)
 
 
-def sum_over_col(own, other):
-    core_sum = own + from_partner(other, "col", 0)
+def sum_over_x(core_sum):
     kept = from_x(core_sum[2:], 0)
     return [core_sum[0], kept[0], from_x(core_sum[1] + kept[1], 1)]
 
@@ -390,7 +393,20 @@
     tables = (leaf_ranks, mid_ranks, top_ranks, leaf_pivots, mid_pivots, top_pivots)
     chunks, (high, low, ranks, pivots) = gather_parts(sketch, (frontal, *tables), prepare)
     info = jnp.stack([leaf_index]).astype(jnp.int32)
-    groups = [sum_over_col(*chunk_product(high, low, pieces, place)) for pieces in chunks]
+    halves = [part.reshape(SIDE, 2, LEAF, -1) for part in (high, low)]
+    core_sums, own = [], ()
+    for chunk, pieces in enumerate(chunks):
+        place, own = lax.optimization_barrier((place, own))
+        other, *parts = product_other(halves, pieces, place)
+        received = from_partner(other, "col", 0)
+        last = chunk == len(chunks) - 1
+        if chunk > 0:
+            core_sums[-1] = own + core_sums[-1]
+            place, core_sums = lax.optimization_barrier((place, core_sums))
+        own = product_own(halves, parts, place, last)
+        core_sums.append(received)
+    core_sums[-1] = own + core_sums[-1]
+    groups = [sum_over_x(core_sum) for core_sum in core_sums]
     arrays = []
     for group, width in zip(groups, WIDTHS):
         skeleton_shape, pair_shape = (KMAX, width), (2 * KMAX, width)

time: 112 us -> 110 us (0.982)
  Pallas kernels: 31.6 us -> 35.7 us
  waiting for transfers between devices: 25.9 us -> 29.7 us
  local copies, waits for them, and re-layouts: 17.6 us -> 14.1 us
  starting transfers between devices: 32.3 us -> 28.8 us
  other arithmetic: 3.11 us -> 0.78 us
    unnamed x18 -> x16, local copies, waits for them, and re-layouts: 15.5 us -> 10.9 us
    pallas_call x3 -> x5, Pallas kernels: 18.5 us -> 22.7 us  [the longest x4 15.3 us: product(): pl.pallas_call(kernel, out_shape=outs, in_specs=[pl.BlockSpec(memory_spac...]
    ppermute x4, waiting for transfers between devices: 5.17 us -> 9.08 us  [from_x(): return lax.ppermute(value, 'col', pairs)]
    concatenate x6 -> x4, other arithmetic: 2.74 us -> 0.16 us  [gather_parts(): stacks = [jnp.concatenate(pair, 0) for pair in zip(stacks, received)]]
    ppermute x6, starting transfers between devices: 12 us -> 9.83 us  [from_partner(): return lax.ppermute(value, axis, pairs)]
    ppermute x4, starting transfers between devices: 5.11 us -> 3.48 us  [from_x(): return lax.ppermute(value, 'col', pairs)]
  transfers between devices with their start and end apart: 20 -> 20, of which waited for: 9 -> 9; matrix products, arithmetic and copies ran while one was open for 2% -> 1% of each run, Pallas kernels for 20% -> 24%
where the time goes in v4:
time: 110 us
  Pallas kernels  35.7 us (32%)
  waiting for transfers between devices  29.7 us (27%)
  starting transfers between devices  28.8 us (26%)
  local copies, waits for them, and re-layouts  14.1 us (13%)
    ppermute x10, waiting for transfers between devices, from_row(): return lax.ppermute(value, ('row', 'col'), pairs)  16.4 us
    ppermute x10, starting transfers between devices, from_row(): return lax.ppermute(value, ('row', 'col'), pairs)  15.4 us
    pallas_call x4, Pallas kernels, product(): pl.pallas_call(kernel, out_shape=outs, in_specs=[pl.BlockSpec(memory_spac...  15.3 us
    pallas_call x5, Pallas kernels, call(): pl.pallas_call(kernel, out_shape=[jax.ShapeDtypeStruct(shape, jnp.float32...  13 us
    unnamed x16, local copies, waits for them, and re-layouts  10.9 us
    ppermute x6, starting transfers between devices, from_partner(): return lax.ppermute(value, axis, pairs)  9.83 us
    ppermute x4, waiting for transfers between devices, from_x(): return lax.ppermute(value, 'col', pairs)  9.08 us
    pallas_call x1, Pallas kernels, split(): pl.pallas_call(split_kernel, out_shape=[pltpu.VMEM(value.shape, jnp.bfloa...  7.39 us
  transfers between devices with their start and end apart: 20, of which 9 were waited for; matrix products, arithmetic and copies ran while one was open for 1% of the time, Pallas kernels for 24%

profile of v4, /device:TPU:1, one launch (start us, length us, event | category | flops | bytes accessed | tf_op | source)
XLA Modules:
  0.0 110.0 jit_solution(3269745822452326403)
XLA Ops:
  0.6 0.0 copy-start
  0.6 1.1 slice_bitcast_fusion
  1.7 2.5 %collective-permute-start = (f32[1,96,512]{2,1,0:T(8,128)S(1)}, f32[1,96,512]{2,1,0:T(8,128)S(1)}, u32[]{:S(2)}, u32[]{:S(2)}) collective-permute-start(f32[1,96,512]{2,1,0:T(8,128)S(1)} %get-tuple-element.99), channel_id=1, source_target_pairs={{0,32},{1,9},{2,34},{3,11},{4,36},{5,13},{6,38},{7,15},{8,40},{9,1... | collective-permute-start | bytes 589832 | tf_op jit(solution)/shard_map/ppermute | solution.py:44
  4.3 2.2 %collective-permute-start.2 = (f32[1,96,512]{2,1,0:T(8,128)S(1)}, f32[1,96,512]{2,1,0:T(8,128)S(1)}, u32[]{:S(2)}, u32[]{:S(2)}) collective-permute-start(f32[1,96,512]{2,1,0:T(8,128)S(1)} %get-tuple-element.98), channel_id=1, source_target_pairs={{0,96},{1,25},{2,98},{3,27},{4,100},{5,29},{6,102},{7,31},{8,104},... | collective-permute-start | bytes 589832 | tf_op jit(solution)/shard_map/ppermute | solution.py:44
  6.5 1.1 %collective-permute-done = f32[1,96,512]{2,1,0:T(8,128)S(1)} collective-permute-done((f32[1,96,512]{2,1,0:T(8,128)S(1)}, f32[1,96,512]{2,1,0:T(8,128)S(1)}, u32[]{:S(2)}, u32[]{:S(2)}) %collective-permute-start) | collective-permute-done | bytes 196640 | tf_op jit(solution)/shard_map/ppermute | solution.py:44
  7.7 3.7 %collective-permute-start.1 = (f32[2,96,512]{2,1,0:T(8,128)S(1)}, f32[2,96,512]{2,1,0:T(8,128)S(1)}, u32[]{:S(2)}, u32[]{:S(2)}) collective-permute-start(f32[2,96,512]{2,1,0:T(8,128)S(1)} %pad_maximum_fusion.6), channel_id=1, source_target_pairs={{0,96},{1,25},{2,98},{3,27},{4,100},{5,29},{6,102},{7,31},{8,104},... | collective-permute-start | bytes 1179656 | tf_op jit(solution)/shard_map/ppermute | solution.py:44
  11.3 0.0 collective-permute-done.2
  11.4 0.1 collective-permute-start.3
  11.4 5.3 %collective-permute-done.1 = f32[2,96,512]{2,1,0:T(8,128)S(1)} collective-permute-done((f32[2,96,512]{2,1,0:T(8,128)S(1)}, f32[2,96,512]{2,1,0:T(8,128)S(1)}, u32[]{:S(2)}, u32[]{:S(2)}) %collective-permute-start.1) | collective-permute-done | bytes 393248 | tf_op jit(solution)/shard_map/ppermute | solution.py:44
  16.8 1.6 %collective-permute-done.3 = f32[2,96,512]{2,1,0:T(8,128)S(1)} collective-permute-done((f32[2,96,512]{2,1,0:T(8,128)S(1)}, f32[2,96,512]{2,1,0:T(8,128)S(1)}, u32[]{:S(2)}, u32[]{:S(2)}) %collective-permute-start.3) | collective-permute-done | bytes 393248 | tf_op jit(solution)/shard_map/ppermute | solution.py:44
  18.4 0.1 pad_maximum_fusion
  18.4 1.2 %collective-permute-start.4 = (f32[4,96,512]{2,1,0:T(8,128)S(1)}, f32[4,96,512]{2,1,0:T(8,128)S(1)}, u32[]{:S(2)}, u32[]{:S(2)}) collective-permute-start(f32[4,96,512]{2,1,0:T(8,128)S(1)} %pad_maximum_fusion), channel_id=1, source_target_pairs={{0,8},{1,33},{2,10},{3,35},{4,12},{5,37},{6,14},{7,39},{8,0},{9,41... | collective-permute-start | bytes 2359304 | tf_op jit(solution)/shard_map/ppermute | solution.py:44
  19.6 0.1 pad_maximum_fusion.1
  19.7 1.9 %collective-permute-start.5 = (f32[4,96,512]{2,1,0:T(8,128)S(1)}, f32[4,96,512]{2,1,0:T(8,128)}, u32[]{:S(2)}, u32[]{:S(2)}) collective-permute-start(f32[4,96,512]{2,1,0:T(8,128)S(1)} %pad_maximum_fusion.1), channel_id=1, source_target_pairs={{0,24},{1,97},{2,26},{3,99},{4,28},{5,101},{6,30},{7,103},{8,16},{... | collective-permute-start | bytes 2359304 | tf_op jit(solution)/shard_map/ppermute | solution.py:44
  21.5 7.4 %split.1 = (bf16[1024,3072]{1,0:T(8,128)(2,1)S(1)}, bf16[1024,3072]{1,0:T(8,128)(2,1)S(1)}) custom-call(f32[1024,3072]{1,0:T(8,128)} %value_ref), custom_call_target="tpu_custom_call" | custom-call | flops 12582912 | bytes 25165824 | tf_op jit(solution)/shard_map/split/pallas_call | solution.py:86
  28.9 2.7 %copy-done.1 = bf16[1024,3072]{1,0:T(8,128)(2,1)} copy-done((bf16[1024,3072]{1,0:T(8,128)(2,1)}, bf16[1024,3072]{1,0:T(8,128)(2,1)S(1)}, u32[]{:S(2)}) %copy-start.1) | copy-done | bytes 6291480
  31.6 2.6 %copy-done.3 = bf16[1024,3072]{1,0:T(8,128)(2,1)} copy-done((bf16[1024,3072]{1,0:T(8,128)(2,1)}, bf16[1024,3072]{1,0:T(8,128)(2,1)S(1)}, u32[]{:S(2)}) %copy-start.3) | copy-done | bytes 6291480
  34.3 0.1 pad_add_fusion.1.ranks_ref
  34.4 0.7 constant_dynamic-slice_fusion
  35.1 0.0 collective-permute-done.5
  35.1 0.1 fusion.5
  35.2 0.1 fusion.4
  35.2 1.2 %fusion.3 = (f32[4,96,256]{2,1,0:T(8,128)S(1)}, f32[4,96,256]{2,1,0:T(8,128)S(1)}) fusion(f32[4,96,512]{2,1,0:T(8,128)} %collective-permute-done.5), kind=kLoop, calls=%fused_computation.25 | loop fusion | bytes 1572864 | tf_op jit(solution)/shard_map/slice | solution.py:68
  36.4 0.1 fusion.2
  36.5 0.1 pad_maximum_fusion.2.refs_0_
  36.6 1.0 collective-permute-start.6
  37.5 0.1 pad_maximum_fusion.3.refs_1_
  37.6 0.1 collective-permute-start.7
  37.7 0.1 pad_maximum_fusion.4.refs_0_
  37.7 1.9 %collective-permute-start.13 = (f32[8,96,256]{2,1,0:T(8,128)S(1)}, f32[8,96,256]{2,1,0:T(8,128)}, u32[]{:S(2)}, u32[]{:S(2)}) collective-permute-start(f32[8,96,256]{2,1,0:T(8,128)S(1)} %pad_maximum_fusion.4.refs_0_), channel_id=1, source_target_pairs={{0,24},{1,97},{2,26},{3,99},{4,28},{5,101},{6,30},{7,103},{8,16},{... | collective-permute-start | bytes 2359304 | tf_op jit(solution)/shard_map/ppermute | solution.py:44
  39.7 0.1 pad_maximum_fusion.5.refs_1_
  39.8 0.9 collective-permute-start.14
  40.6 0.1 pad_add_fusion.2.place_ref
  40.7 8.4 %collective-permute-done.6.refs_2_ = f32[8,96,256]{2,1,0:T(8,128)} collective-permute-done((f32[8,96,256]{2,1,0:T(8,128)S(1)}, f32[8,96,256]{2,1,0:T(8,128)}, u32[]{:S(2)}, u32[]{:S(2)}) %collective-permute-start.6) | collective-permute-done | bytes 786464 | tf_op jit(solution)/shard_map/ppermute | solution.py:44
  49.1 2.8 %copy-done.2 = bf16[1024,3072]{1,0:T(8,128)(2,1)S(1)} copy-done((bf16[1024,3072]{1,0:T(8,128)(2,1)S(1)}, bf16[1024,3072]{1,0:T(8,128)(2,1)}, u32[]{:S(2)}) %copy-start.2) | copy-done | bytes 6291480
  51.9 2.8 %copy-done.4 = bf16[1024,3072]{1,0:T(8,128)(2,1)S(1)} copy-done((bf16[1024,3072]{1,0:T(8,128)(2,1)S(1)}, bf16[1024,3072]{1,0:T(8,128)(2,1)}, u32[]{:S(2)}) %copy-start.4) | copy-done | bytes 6291480
  54.7 4.5 %product_other.2 = (f32[4,128,256]{2,1,0:T(8,128)S(1)}, bf16[3072,256]{1,0:T(8,128)(2,1)S(1)}, bf16[3072,256]{1,0:T(8,128)(2,1)S(1)}) custom-call(s32[3]{0:T(128)S(1)} %pad_add_fusion.2.place_ref, bf16[4,2,128,3072]{3,2,1,0:T(8,128)(2,1)S(1)} %bitcast.27, bf16[4,2,128,3072]{3,2,1,0:T(8,128)(2,1)S(1)} %bitcast.31, ...), custom_call_target="tpu_custom_call" | custom-call | flops 1 | tf_op jit(solution)/shard_map/product_other/pallas_call | solution.py:144
  59.1 5.1 %collective-permute-start.8 = (f32[4,128,256]{2,1,0:T(8,128)S(1)}, f32[4,128,256]{2,1,0:T(8,128)S(1)}, u32[]{:S(2)}, u32[]{:S(2)}) collective-permute-start(f32[4,128,256]{2,1,0:T(8,128)S(1)} %get-tuple-element.68), channel_id=1, source_target_pairs={{0,1},{1,0},{2,3},{3,2},{4,5},{5,4},{6,7},{7,6},{8,9},{9,8},{10,11... | collective-permute-start | bytes 1572872 | tf_op jit(solution)/shard_map/ppermute | solution.py:21
  64.3 3.2 %product_own.2 = f32[4,128,256]{2,1,0:T(8,128)S(1)} custom-call(s32[3]{0:T(128)S(1)} %pad_add_fusion.2.place_ref, bf16[4,2,128,3072]{3,2,1,0:T(8,128)(2,1)S(1)} %bitcast.28, bf16[4,2,128,3072]{3,2,1,0:T(8,128)(2,1)S(1)} %bitcast.32, bf16[3072,256]{1,0:T(8,128)(2,1)S(1)} %get-tuple-element.64.high, bf16[3072,256]{1,0:T(8,128)(2,1)S(1)} %get-tuple-element.65.low), custom_call_target="tpu_custom_call" | custom-call | flops 1 | tf_op jit(solution)/shard_map/product_own/pallas_call | solution.py:144
  67.5 0.0 collective-permute-done.14.refs_3_
  67.5 4.5 %product_other.3 = (f32[4,128,256]{2,1,0:T(8,128)S(1)}, bf16[3072,256]{1,0:T(8,128)(2,1)S(1)}, bf16[3072,256]{1,0:T(8,128)(2,1)S(1)}) custom-call(s32[3]{0:T(128)S(1)} %pad_add_fusion.2.place_ref, bf16[4,2,128,3072]{3,2,1,0:T(8,128)(2,1)S(1)} %bitcast.29, bf16[4,2,128,3072]{3,2,1,0:T(8,128)(2,1)S(1)} %bitcast.33, ...), custom_call_target="tpu_custom_call" | custom-call | flops 1 | tf_op jit(solution)/shard_map/product_other/pallas_call | solution.py:144
  72.0 0.1 collective-permute-start.15
  72.1 0.1 add.45
  72.2 2.7 %collective-permute-start.9 = (f32[2,128,256]{2,1,0:T(8,128)S(1)}, f32[2,128,256]{2,1,0:T(8,128)S(1)}, u32[]{:S(2)}, u32[]{:S(2)}) collective-permute-start(f32[2,128,256]{2,1,0:T(8,128)S(1)} %slice.82), channel_id=1, source_target_pairs={{0,2},{1,7},{2,0},{3,5},{4,6},{5,3},{6,4},{7,1},{8,10},{9,15},{10,... | collective-permute-start | bytes 786440 | tf_op jit(solution)/shard_map/ppermute | solution.py:177
  74.9 3.2 %product_own.3 = f32[4,128,256]{2,1,0:T(8,128)S(1)} custom-call(s32[3]{0:T(128)S(1)} %pad_add_fusion.2.place_ref, bf16[4,2,128,3072]{3,2,1,0:T(8,128)(2,1)S(1)} %bitcast.30, bf16[4,2,128,3072]{3,2,1,0:T(8,128)(2,1)S(1)} %bitcast.34, bf16[3072,256]{1,0:T(8,128)(2,1)S(1)} %get-tuple-element.75.high, bf16[3072,256]{1,0:T(8,128)(2,1)S(1)} %get-tuple-element.76.low), custom_call_target="tpu_custom_call" | custom-call | flops 2415919104 | bytes 6039797 | tf_op jit(solution)/shard_map/product_own/pallas_call | solution.py:144
  78.1 0.1 add.48
  78.2 0.3 collective-permute-start.16
  78.5 0.4 collective-permute-done.9
  78.9 0.4 collective-permute-start.10
  79.3 6.9 %collective-permute-done.16 = f32[2,128,256]{2,1,0:T(8,128)S(1)} collective-permute-done((f32[2,128,256]{2,1,0:T(8,128)S(1)}, f32[2,128,256]{2,1,0:T(8,128)S(1)}, u32[]{:S(2)}, u32[]{:S(2)}) %collective-permute-start.16) | collective-permute-done | bytes 262176 | tf_op jit(solution)/shard_map/ppermute | solution.py:177
  86.3 0.1 collective-permute-start.17
  86.4 0.8 leaf_rows.2
  87.2 1.5 %collective-permute-start.11 = (f32[96,256]{1,0:T(8,128)S(1)}, f32[96,256]{1,0:T(8,128)S(1)}, u32[]{:S(2)}, u32[]{:S(2)}) collective-permute-start(f32[96,256]{1,0:T(8,128)S(1)} %get-tuple-element.71.own_ref.refs_1_), channel_id=1, source_target_pairs={{0,1},{1,0},{2,3},{3,2},{4,5},{5,4},{6,7},{7,6},{8,9},{9,8},{10,11... | collective-permute-start | bytes 294920 | tf_op jit(solution)/shard_map/ppermute | solution.py:21
  88.7 1.8 %collective-permute-done.17.refs_2_ = f32[128,256]{1,0:T(8,128)S(1)} collective-permute-done((f32[128,256]{1,0:T(8,128)S(1)}, f32[128,256]{1,0:T(8,128)S(1)}, u32[]{:S(2)}, u32[]{:S(2)}) %collective-permute-start.17) | collective-permute-done | bytes 131104 | tf_op jit(solution)/shard_map/ppermute | solution.py:177
  90.5 0.8 leaf_rows.3
  91.3 1.5 %collective-permute-start.18 = (f32[96,256]{1,0:T(8,128)S(1)}, f32[96,256]{1,0:T(8,128)S(1)}, u32[]{:S(2)}, u32[]{:S(2)}) collective-permute-start(f32[96,256]{1,0:T(8,128)S(1)} %get-tuple-element.79.own_ref.refs_6_), channel_id=1, source_target_pairs={{0,1},{1,0},{2,3},{3,2},{4,5},{5,4},{6,7},{7,6},{8,9},{9,8},{10,11... | collective-permute-start | bytes 294920 | tf_op jit(solution)/shard_map/ppermute | solution.py:21
  92.8 0.8 mid_rows.2
  93.6 0.1 collective-permute-start.12
  93.7 0.0 collective-permute-done.18.other_ref
  93.7 0.8 mid_rows.3
  94.5 1.5 %collective-permute-start.19 = (f32[96,256]{1,0:T(8,128)S(1)}, f32[96,256]{1,0:T(8,128)S(1)}, u32[]{:S(2)}, u32[]{:S(2)}) collective-permute-start(f32[96,256]{1,0:T(8,128)S(1)} %get-tuple-element.81.refs_8_), channel_id=1, source_target_pairs={{0,2},{1,3},{2,0},{3,1},{4,6},{5,7},{6,4},{7,5},{8,10},{9,11},{10,... | collective-permute-start | bytes 294920 | tf_op jit(solution)/shard_map/ppermute | solution.py:21
  96.1 2.0 %collective-permute-done.12.refs_4_ = f32[96,256]{1,0:T(8,128)S(1)} collective-permute-done((f32[96,256]{1,0:T(8,128)S(1)}, f32[96,256]{1,0:T(8,128)S(1)}, u32[]{:S(2)}, u32[]{:S(2)}) %collective-permute-start.12) | collective-permute-done | bytes 98336 | tf_op jit(solution)/shard_map/ppermute | solution.py:21
  98.1 2.1 %collective-permute-done.19.refs_9_ = f32[96,256]{1,0:T(8,128)S(1)} collective-permute-done((f32[96,256]{1,0:T(8,128)S(1)}, f32[96,256]{1,0:T(8,128)S(1)}, u32[]{:S(2)}, u32[]{:S(2)}) %collective-permute-start.19) | collective-permute-done | bytes 98336 | tf_op jit(solution)/shard_map/ppermute | solution.py:21
  100.2 9.8 %interpolation.1 = (f32[96,128]{1,0:T(8,128)}, f32[96,192]{1,0:T(8,128)}, f32[96,192]{1,0:T(8,128)}, f32[96,512]{1,0:T(8,128)}) custom-call(s32[1]{0:T(128)} %bitcast.info_ref, s32[224]{0:T(256)S(1)} %pad_add_fusion.1.ranks_ref, s32[3,96]{1,0:T(4,128)S(1)} %pad_add_fusion.pivots_ref, f32[128,256]{1,0:T(8,128)S(1)} %get-tuple-element.70.refs_0_, ...), custom_call_target="tpu_custom_call" | custom-call | tf_op jit(solution)/shard_map/interpolation/pallas_call | solution.py:365
  (26 shorter events, 0.2 us)
Async XLA Ops:
  0.6 33.6 %copy-start = (s32[128,128]{1,0:T(8,128)S(1)}, s32[128,128]{1,0:T(8,128)}, u32[]{:S(2)}) copy-start(s32[128,128]{1,0:T(8,128)} %param.11) | copy-start | bytes 196612
  1.7 5.9 %collective-permute-start = (f32[1,96,512]{2,1,0:T(8,128)S(1)}, f32[1,96,512]{2,1,0:T(8,128)S(1)}, u32[]{:S(2)}, u32[]{:S(2)}) collective-permute-start(f32[1,96,512]{2,1,0:T(8,128)S(1)} %get-tuple-element.99), channel_id=1, source_target_pairs={{0,32},{1,9},{2,34},{3,11},{4,36},{5,13},{6,38},{7,15},{8,40},{9,1... | collective-permute-start | bytes 589832 | tf_op jit(solution)/shard_map/ppermute | solution.py:44
  4.3 7.0 %collective-permute-start.2 = (f32[1,96,512]{2,1,0:T(8,128)S(1)}, f32[1,96,512]{2,1,0:T(8,128)S(1)}, u32[]{:S(2)}, u32[]{:S(2)}) collective-permute-start(f32[1,96,512]{2,1,0:T(8,128)S(1)} %get-tuple-element.98), channel_id=1, source_target_pairs={{0,96},{1,25},{2,98},{3,27},{4,100},{5,29},{6,102},{7,31},{8,104},... | collective-permute-start | bytes 589832 | tf_op jit(solution)/shard_map/ppermute | solution.py:44
  7.7 9.1 %collective-permute-start.1 = (f32[2,96,512]{2,1,0:T(8,128)S(1)}, f32[2,96,512]{2,1,0:T(8,128)S(1)}, u32[]{:S(2)}, u32[]{:S(2)}) collective-permute-start(f32[2,96,512]{2,1,0:T(8,128)S(1)} %pad_maximum_fusion.6), channel_id=1, source_target_pairs={{0,96},{1,25},{2,98},{3,27},{4,100},{5,29},{6,102},{7,31},{8,104},... | collective-permute-start | bytes 1179656 | tf_op jit(solution)/shard_map/ppermute | solution.py:44
  11.4 7.0 %collective-permute-start.3 = (f32[2,96,512]{2,1,0:T(8,128)S(1)}, f32[2,96,512]{2,1,0:T(8,128)S(1)}, u32[]{:S(2)}, u32[]{:S(2)}) collective-permute-start(f32[2,96,512]{2,1,0:T(8,128)S(1)} %pad_maximum_fusion.7), channel_id=1, source_target_pairs={{0,32},{1,9},{2,34},{3,11},{4,36},{5,13},{6,38},{7,15},{8,40},{9,1... | collective-permute-start | bytes 1179656 | tf_op jit(solution)/shard_map/ppermute | solution.py:44
  18.4 16.7 %collective-permute-start.4 = (f32[4,96,512]{2,1,0:T(8,128)S(1)}, f32[4,96,512]{2,1,0:T(8,128)S(1)}, u32[]{:S(2)}, u32[]{:S(2)}) collective-permute-start(f32[4,96,512]{2,1,0:T(8,128)S(1)} %pad_maximum_fusion), channel_id=1, source_target_pairs={{0,8},{1,33},{2,10},{3,35},{4,12},{5,37},{6,14},{7,39},{8,0},{9,41... | collective-permute-start | bytes 2359304 | tf_op jit(solution)/shard_map/ppermute | solution.py:44
  19.7 15.4 %collective-permute-start.5 = (f32[4,96,512]{2,1,0:T(8,128)S(1)}, f32[4,96,512]{2,1,0:T(8,128)}, u32[]{:S(2)}, u32[]{:S(2)}) collective-permute-start(f32[4,96,512]{2,1,0:T(8,128)S(1)} %pad_maximum_fusion.1), channel_id=1, source_target_pairs={{0,24},{1,97},{2,26},{3,99},{4,28},{5,101},{6,30},{7,103},{8,16},{... | collective-permute-start | bytes 2359304 | tf_op jit(solution)/shard_map/ppermute | solution.py:44
  21.5 12.7 %copy-start.5 = (s32[32]{0:T(128)S(1)}, s32[32]{0:T(128)}, u32[]{:S(2)}) copy-start(s32[32]{0:T(128)} %param.14) | copy-start | bytes 388
  21.5 12.7 %copy-start.6 = (s32[64]{0:T(128)S(1)}, s32[64]{0:T(128)}, u32[]{:S(2)}) copy-start(s32[64]{0:T(128)} %param.12) | copy-start | bytes 772
  21.5 12.7 %copy-start.7 = (s32[128]{0:T(128)S(1)}, s32[128]{0:T(128)}, u32[]{:S(2)}) copy-start(s32[128]{0:T(128)} %param.10) | copy-start | bytes 1540
  28.9 2.7 %copy-start.1 = (bf16[1024,3072]{1,0:T(8,128)(2,1)}, bf16[1024,3072]{1,0:T(8,128)(2,1)S(1)}, u32[]{:S(2)}) copy-start(bf16[1024,3072]{1,0:T(8,128)(2,1)S(1)} %get-tuple-element.58) | copy-start | bytes 18874372
  31.6 2.6 %copy-start.3 = (bf16[1024,3072]{1,0:T(8,128)(2,1)}, bf16[1024,3072]{1,0:T(8,128)(2,1)S(1)}, u32[]{:S(2)}) copy-start(bf16[1024,3072]{1,0:T(8,128)(2,1)S(1)} %get-tuple-element.59) | copy-start | bytes 18874372
  36.6 12.5 %collective-permute-start.6 = (f32[8,96,256]{2,1,0:T(8,128)S(1)}, f32[8,96,256]{2,1,0:T(8,128)}, u32[]{:S(2)}, u32[]{:S(2)}) collective-permute-start(f32[8,96,256]{2,1,0:T(8,128)S(1)} %pad_maximum_fusion.2.refs_0_), channel_id=1, source_target_pairs={{0,24},{1,97},{2,26},{3,99},{4,28},{5,101},{6,30},{7,103},{8,16},{... | collective-permute-start | bytes 2359304 | tf_op jit(solution)/shard_map/ppermute | solution.py:44
  37.6 11.5 %collective-permute-start.7 = (f32[8,96,256]{2,1,0:T(8,128)S(1)}, f32[8,96,256]{2,1,0:T(8,128)}, u32[]{:S(2)}, u32[]{:S(2)}) collective-permute-start(f32[8,96,256]{2,1,0:T(8,128)S(1)} %pad_maximum_fusion.3.refs_1_), channel_id=1, source_target_pairs={{0,8},{1,33},{2,10},{3,35},{4,12},{5,37},{6,14},{7,39},{8,0},{9,41... | collective-permute-start | bytes 2359304 | tf_op jit(solution)/shard_map/ppermute | solution.py:44
  37.7 29.7 %collective-permute-start.13 = (f32[8,96,256]{2,1,0:T(8,128)S(1)}, f32[8,96,256]{2,1,0:T(8,128)}, u32[]{:S(2)}, u32[]{:S(2)}) collective-permute-start(f32[8,96,256]{2,1,0:T(8,128)S(1)} %pad_maximum_fusion.4.refs_0_), channel_id=1, source_target_pairs={{0,24},{1,97},{2,26},{3,99},{4,28},{5,101},{6,30},{7,103},{8,16},{... | collective-permute-start | bytes 2359304 | tf_op jit(solution)/shard_map/ppermute | solution.py:44
  39.8 27.7 %collective-permute-start.14 = (f32[8,96,256]{2,1,0:T(8,128)S(1)}, f32[8,96,256]{2,1,0:T(8,128)}, u32[]{:S(2)}, u32[]{:S(2)}) collective-permute-start(f32[8,96,256]{2,1,0:T(8,128)S(1)} %pad_maximum_fusion.5.refs_1_), channel_id=1, source_target_pairs={{0,8},{1,33},{2,10},{3,35},{4,12},{5,37},{6,14},{7,39},{8,0},{9,41... | collective-permute-start | bytes 2359304 | tf_op jit(solution)/shard_map/ppermute | solution.py:44
  49.1 2.8 %copy-start.2 = (bf16[1024,3072]{1,0:T(8,128)(2,1)S(1)}, bf16[1024,3072]{1,0:T(8,128)(2,1)}, u32[]{:S(2)}) copy-start(bf16[1024,3072]{1,0:T(8,128)(2,1)} %copy-done.1) | copy-start | bytes 18874372
  51.9 2.8 %copy-start.4 = (bf16[1024,3072]{1,0:T(8,128)(2,1)S(1)}, bf16[1024,3072]{1,0:T(8,128)(2,1)}, u32[]{:S(2)}) copy-start(bf16[1024,3072]{1,0:T(8,128)(2,1)} %copy-done.3) | copy-start | bytes 18874372
  59.1 12.9 %collective-permute-start.8 = (f32[4,128,256]{2,1,0:T(8,128)S(1)}, f32[4,128,256]{2,1,0:T(8,128)S(1)}, u32[]{:S(2)}, u32[]{:S(2)}) collective-permute-start(f32[4,128,256]{2,1,0:T(8,128)S(1)} %get-tuple-element.68), channel_id=1, source_target_pairs={{0,1},{1,0},{2,3},{3,2},{4,5},{5,4},{6,7},{7,6},{8,9},{9,8},{10,11... | collective-permute-start | bytes 1572872 | tf_op jit(solution)/shard_map/ppermute | solution.py:21
  72.0 6.1 %collective-permute-start.15 = (f32[4,128,256]{2,1,0:T(8,128)S(1)}, f32[4,128,256]{2,1,0:T(8,128)S(1)}, u32[]{:S(2)}, u32[]{:S(2)}) collective-permute-start(f32[4,128,256]{2,1,0:T(8,128)S(1)} %get-tuple-element.77), channel_id=1, source_target_pairs={{0,1},{1,0},{2,3},{3,2},{4,5},{5,4},{6,7},{7,6},{8,9},{9,8},{10,11... | collective-permute-start | bytes 1572872 | tf_op jit(solution)/shard_map/ppermute | solution.py:21
  72.2 6.7 %collective-permute-start.9 = (f32[2,128,256]{2,1,0:T(8,128)S(1)}, f32[2,128,256]{2,1,0:T(8,128)S(1)}, u32[]{:S(2)}, u32[]{:S(2)}) collective-permute-start(f32[2,128,256]{2,1,0:T(8,128)S(1)} %slice.82), channel_id=1, source_target_pairs={{0,2},{1,7},{2,0},{3,5},{4,6},{5,3},{6,4},{7,1},{8,10},{9,15},{10,... | collective-permute-start | bytes 786440 | tf_op jit(solution)/shard_map/ppermute | solution.py:177
  78.2 8.0 %collective-permute-start.16 = (f32[2,128,256]{2,1,0:T(8,128)S(1)}, f32[2,128,256]{2,1,0:T(8,128)S(1)}, u32[]{:S(2)}, u32[]{:S(2)}) collective-permute-start(f32[2,128,256]{2,1,0:T(8,128)S(1)} %slice.98), channel_id=1, source_target_pairs={{0,2},{1,7},{2,0},{3,5},{4,6},{5,3},{6,4},{7,1},{8,10},{9,15},{10,... | collective-permute-start | bytes 786440 | tf_op jit(solution)/shard_map/ppermute | solution.py:177
  78.9 7.4 %collective-permute-start.10 = (f32[128,256]{1,0:T(8,128)S(1)}, f32[128,256]{1,0:T(8,128)S(1)}, u32[]{:S(2)}, u32[]{:S(2)}) collective-permute-start(f32[128,256]{1,0:T(8,128)S(1)} %get-tuple-element.96), channel_id=1, source_target_pairs={{0,6},{1,3},{2,4},{3,1},{4,2},{5,7},{6,0},{7,5},{8,14},{9,11},{10,... | collective-permute-start | bytes 393224 | tf_op jit(solution)/shard_map/ppermute | solution.py:177
  86.3 4.2 %collective-permute-start.17 = (f32[128,256]{1,0:T(8,128)S(1)}, f32[128,256]{1,0:T(8,128)S(1)}, u32[]{:S(2)}, u32[]{:S(2)}) collective-permute-start(f32[128,256]{1,0:T(8,128)S(1)} %get-tuple-element.94), channel_id=1, source_target_pairs={{0,6},{1,3},{2,4},{3,1},{4,2},{5,7},{6,0},{7,5},{8,14},{9,11},{10,... | collective-permute-start | bytes 393224 | tf_op jit(solution)/shard_map/ppermute | solution.py:177
  87.2 5.6 %collective-permute-start.11 = (f32[96,256]{1,0:T(8,128)S(1)}, f32[96,256]{1,0:T(8,128)S(1)}, u32[]{:S(2)}, u32[]{:S(2)}) collective-permute-start(f32[96,256]{1,0:T(8,128)S(1)} %get-tuple-element.71.own_ref.refs_1_), channel_id=1, source_target_pairs={{0,1},{1,0},{2,3},{3,2},{4,5},{5,4},{6,7},{7,6},{8,9},{9,8},{10,11... | collective-permute-start | bytes 294920 | tf_op jit(solution)/shard_map/ppermute | solution.py:21
  91.3 2.5 %collective-permute-start.18 = (f32[96,256]{1,0:T(8,128)S(1)}, f32[96,256]{1,0:T(8,128)S(1)}, u32[]{:S(2)}, u32[]{:S(2)}) collective-permute-start(f32[96,256]{1,0:T(8,128)S(1)} %get-tuple-element.79.own_ref.refs_6_), channel_id=1, source_target_pairs={{0,1},{1,0},{2,3},{3,2},{4,5},{5,4},{6,7},{7,6},{8,9},{9,8},{10,11... | collective-permute-start | bytes 294920 | tf_op jit(solution)/shard_map/ppermute | solution.py:21
  93.6 4.5 %collective-permute-start.12 = (f32[96,256]{1,0:T(8,128)S(1)}, f32[96,256]{1,0:T(8,128)S(1)}, u32[]{:S(2)}, u32[]{:S(2)}) collective-permute-start(f32[96,256]{1,0:T(8,128)S(1)} %get-tuple-element.73.refs_3_), channel_id=1, source_target_pairs={{0,2},{1,3},{2,0},{3,1},{4,6},{5,7},{6,4},{7,5},{8,10},{9,11},{10,... | collective-permute-start | bytes 294920 | tf_op jit(solution)/shard_map/ppermute | solution.py:21
  94.5 5.7 %collective-permute-start.19 = (f32[96,256]{1,0:T(8,128)S(1)}, f32[96,256]{1,0:T(8,128)S(1)}, u32[]{:S(2)}, u32[]{:S(2)}) collective-permute-start(f32[96,256]{1,0:T(8,128)S(1)} %get-tuple-element.81.refs_8_), channel_id=1, source_target_pairs={{0,2},{1,3},{2,0},{3,1},{4,6},{5,7},{6,4},{7,5},{8,10},{9,11},{10,... | collective-permute-start | bytes 294920 | tf_op jit(solution)/shard_map/ppermute | solution.py:21

commit v5 on v4

--- a/solution.py
+++ b/solution.py
@@ -89,7 +89,7 @@
         grid=(rows // LEAF,),
         in_specs=[pl.BlockSpec((LEAF, order), lambda i: (i, 0))],
         out_specs=[pl.BlockSpec(memory_space=pltpu.VMEM)] * 2,
-        compiler_params=pltpu.CompilerParams(vmem_limit_bytes=8 * 2**20),
+        compiler_params=pltpu.CompilerParams(vmem_limit_bytes=6 * 2**20),
         cost_estimate=pl.CostEstimate(
             flops=4 * rows * order, bytes_accessed=8 * rows * order, transcendentals=0
         ),
@@ -147,7 +147,7 @@
         in_specs=[pl.BlockSpec(memory_space=pltpu.SMEM)] + [in_vmem] * (2 + len(arrays)),
         out_specs=[in_vmem] * len(outs),
         scratch_shapes=[pltpu.VMEM(outs[0].shape, jnp.float32)],
-        compiler_params=pltpu.CompilerParams(vmem_limit_bytes=24 * 2**20),
+        compiler_params=pltpu.CompilerParams(vmem_limit_bytes=8 * 2**20),
         cost_estimate=pl.CostEstimate(flops=cost, bytes_accessed=cost // 400, transcendentals=0),
         name=name,
     )(place, *halves, *arrays)
@@ -368,7 +368,7 @@
             in_specs=[pl.BlockSpec(memory_space=pltpu.SMEM)] * 3 + [in_vmem] * len(arrays),
             out_specs=[in_vmem] * len(outs),
             scratch_shapes=scratch,
-            compiler_params=pltpu.CompilerParams(vmem_limit_bytes=8 * 2**20),
+            compiler_params=pltpu.CompilerParams(vmem_limit_bytes=6 * 2**20),
             name=name,
         )(info, ranks, pivots, *arrays)
 

time: 110 us -> 111 us (level)
    unnamed x16 -> x20, local copies, waits for them, and re-layouts: 10.9 us -> 10.9 us
where the time goes in v5:
time: 111 us; the launch traced here: 110 us
  Pallas kernels  36 us (32%)
  waiting for transfers between devices  29.7 us (27%)
  starting transfers between devices  28.8 us (26%)
  local copies, waits for them, and re-layouts  14.1 us (13%)
    ppermute x10, waiting for transfers between devices, from_row(): return lax.ppermute(value, ('row', 'col'), pairs)  16.4 us
    pallas_call x4, Pallas kernels, product(): pl.pallas_call(kernel, out_shape=outs, in_specs=[pl.BlockSpec(memory_spac...  15.6 us
    ppermute x10, starting transfers between devices, from_row(): return lax.ppermute(value, ('row', 'col'), pairs)  15.4 us
    pallas_call x5, Pallas kernels, call(): pl.pallas_call(kernel, out_shape=[jax.ShapeDtypeStruct(shape, jnp.float32...  13 us
    unnamed x20, local copies, waits for them, and re-layouts  10.9 us
    ppermute x6, starting transfers between devices, from_partner(): return lax.ppermute(value, axis, pairs)  9.84 us
    ppermute x4, waiting for transfers between devices, from_x(): return lax.ppermute(value, 'col', pairs)  9.07 us
    pallas_call x1, Pallas kernels, split(): pl.pallas_call(split_kernel, out_shape=[pltpu.VMEM(value.shape, jnp.bfloa...  7.39 us
  transfers between devices with their start and end apart: 20, of which 9 were waited for; matrix products, arithmetic and copies ran while one was open for 1% of the time, Pallas kernels for 24%

profile of v5, /device:TPU:1, one launch (start us, length us, event | category | flops | bytes accessed | tf_op | source)
XLA Modules:
  0.0 110.3 jit_solution(5658228665145590226)
XLA Ops:
  0.6 0.0 copy-start
  0.6 1.1 slice_bitcast_fusion
  1.7 2.5 %collective-permute-start = (f32[1,96,512]{2,1,0:T(8,128)S(1)}, f32[1,96,512]{2,1,0:T(8,128)S(1)}, u32[]{:S(2)}, u32[]{:S(2)}) collective-permute-start(f32[1,96,512]{2,1,0:T(8,128)S(1)} %get-tuple-element.99), channel_id=1, source_target_pairs={{0,32},{1,9},{2,34},{3,11},{4,36},{5,13},{6,38},{7,15},{8,40},{9,1... | collective-permute-start | bytes 589832 | tf_op jit(solution)/shard_map/ppermute | solution.py:44
  4.3 2.2 %collective-permute-start.2 = (f32[1,96,512]{2,1,0:T(8,128)S(1)}, f32[1,96,512]{2,1,0:T(8,128)S(1)}, u32[]{:S(2)}, u32[]{:S(2)}) collective-permute-start(f32[1,96,512]{2,1,0:T(8,128)S(1)} %get-tuple-element.98), channel_id=1, source_target_pairs={{0,96},{1,25},{2,98},{3,27},{4,100},{5,29},{6,102},{7,31},{8,104},... | collective-permute-start | bytes 589832 | tf_op jit(solution)/shard_map/ppermute | solution.py:44
  6.5 1.1 %collective-permute-done = f32[1,96,512]{2,1,0:T(8,128)S(1)} collective-permute-done((f32[1,96,512]{2,1,0:T(8,128)S(1)}, f32[1,96,512]{2,1,0:T(8,128)S(1)}, u32[]{:S(2)}, u32[]{:S(2)}) %collective-permute-start) | collective-permute-done | bytes 196640 | tf_op jit(solution)/shard_map/ppermute | solution.py:44
  7.7 3.7 %collective-permute-start.1 = (f32[2,96,512]{2,1,0:T(8,128)S(1)}, f32[2,96,512]{2,1,0:T(8,128)S(1)}, u32[]{:S(2)}, u32[]{:S(2)}) collective-permute-start(f32[2,96,512]{2,1,0:T(8,128)S(1)} %pad_maximum_fusion.6), channel_id=1, source_target_pairs={{0,96},{1,25},{2,98},{3,27},{4,100},{5,29},{6,102},{7,31},{8,104},... | collective-permute-start | bytes 1179656 | tf_op jit(solution)/shard_map/ppermute | solution.py:44
  11.3 0.0 collective-permute-done.2
  11.4 0.1 collective-permute-start.3
  11.4 5.3 %collective-permute-done.1 = f32[2,96,512]{2,1,0:T(8,128)S(1)} collective-permute-done((f32[2,96,512]{2,1,0:T(8,128)S(1)}, f32[2,96,512]{2,1,0:T(8,128)S(1)}, u32[]{:S(2)}, u32[]{:S(2)}) %collective-permute-start.1) | collective-permute-done | bytes 393248 | tf_op jit(solution)/shard_map/ppermute | solution.py:44
  16.8 1.6 %collective-permute-done.3 = f32[2,96,512]{2,1,0:T(8,128)S(1)} collective-permute-done((f32[2,96,512]{2,1,0:T(8,128)S(1)}, f32[2,96,512]{2,1,0:T(8,128)S(1)}, u32[]{:S(2)}, u32[]{:S(2)}) %collective-permute-start.3) | collective-permute-done | bytes 393248 | tf_op jit(solution)/shard_map/ppermute | solution.py:44
  18.4 0.1 pad_maximum_fusion
  18.4 1.2 %collective-permute-start.4 = (f32[4,96,512]{2,1,0:T(8,128)S(1)}, f32[4,96,512]{2,1,0:T(8,128)S(1)}, u32[]{:S(2)}, u32[]{:S(2)}) collective-permute-start(f32[4,96,512]{2,1,0:T(8,128)S(1)} %pad_maximum_fusion), channel_id=1, source_target_pairs={{0,8},{1,33},{2,10},{3,35},{4,12},{5,37},{6,14},{7,39},{8,0},{9,41... | collective-permute-start | bytes 2359304 | tf_op jit(solution)/shard_map/ppermute | solution.py:44
  19.6 0.1 pad_maximum_fusion.1
  19.7 1.9 %collective-permute-start.5 = (f32[4,96,512]{2,1,0:T(8,128)S(1)}, f32[4,96,512]{2,1,0:T(8,128)}, u32[]{:S(2)}, u32[]{:S(2)}) collective-permute-start(f32[4,96,512]{2,1,0:T(8,128)S(1)} %pad_maximum_fusion.1), channel_id=1, source_target_pairs={{0,24},{1,97},{2,26},{3,99},{4,28},{5,101},{6,30},{7,103},{8,16},{... | collective-permute-start | bytes 2359304 | tf_op jit(solution)/shard_map/ppermute | solution.py:44
  21.5 7.4 %split.1 = (bf16[1024,3072]{1,0:T(8,128)(2,1)S(1)}, bf16[1024,3072]{1,0:T(8,128)(2,1)S(1)}) custom-call(f32[1024,3072]{1,0:T(8,128)} %value_ref), custom_call_target="tpu_custom_call" | custom-call | flops 12582912 | bytes 25165824 | tf_op jit(solution)/shard_map/split/pallas_call | solution.py:86
  28.9 2.7 %copy-done.1 = bf16[1024,3072]{1,0:T(8,128)(2,1)} copy-done((bf16[1024,3072]{1,0:T(8,128)(2,1)}, bf16[1024,3072]{1,0:T(8,128)(2,1)S(1)}, u32[]{:S(2)}) %copy-start.1) | copy-done | bytes 6291480
  31.6 2.7 %copy-done.3 = bf16[1024,3072]{1,0:T(8,128)(2,1)} copy-done((bf16[1024,3072]{1,0:T(8,128)(2,1)}, bf16[1024,3072]{1,0:T(8,128)(2,1)S(1)}, u32[]{:S(2)}) %copy-start.3) | copy-done | bytes 6291480
  34.3 0.1 pad_add_fusion.1.ranks_ref
  34.4 0.7 constant_dynamic-slice_fusion
  35.1 0.0 collective-permute-done.4
  35.1 0.1 fusion.5
  35.2 0.1 fusion.4
  35.3 1.2 %fusion.3 = (f32[4,96,256]{2,1,0:T(8,128)S(1)}, f32[4,96,256]{2,1,0:T(8,128)S(1)}) fusion(f32[4,96,512]{2,1,0:T(8,128)} %collective-permute-done.5), kind=kLoop, calls=%fused_computation.25 | loop fusion | bytes 1572864 | tf_op jit(solution)/shard_map/slice | solution.py:68
  36.5 0.1 fusion.2
  36.5 0.1 pad_maximum_fusion.2.refs_0_
  36.6 1.0 collective-permute-start.6
  37.6 0.1 pad_maximum_fusion.3.refs_1_
  37.6 0.1 collective-permute-start.7
  37.7 0.1 pad_maximum_fusion.4.refs_0_
  37.8 1.9 %collective-permute-start.13 = (f32[8,96,256]{2,1,0:T(8,128)S(1)}, f32[8,96,256]{2,1,0:T(8,128)}, u32[]{:S(2)}, u32[]{:S(2)}) collective-permute-start(f32[8,96,256]{2,1,0:T(8,128)S(1)} %pad_maximum_fusion.4.refs_0_), channel_id=1, source_target_pairs={{0,24},{1,97},{2,26},{3,99},{4,28},{5,101},{6,30},{7,103},{8,16},{... | collective-permute-start | bytes 2359304 | tf_op jit(solution)/shard_map/ppermute | solution.py:44
  39.7 0.1 pad_maximum_fusion.5.refs_1_
  39.8 0.9 collective-permute-start.14
  40.6 0.1 pad_add_fusion.2.place_ref
  40.7 8.4 %collective-permute-done.6.refs_2_ = f32[8,96,256]{2,1,0:T(8,128)} collective-permute-done((f32[8,96,256]{2,1,0:T(8,128)S(1)}, f32[8,96,256]{2,1,0:T(8,128)}, u32[]{:S(2)}, u32[]{:S(2)}) %collective-permute-start.6) | collective-permute-done | bytes 786464 | tf_op jit(solution)/shard_map/ppermute | solution.py:44
  49.1 0.0 collective-permute-done.7.refs_3_
  49.1 2.8 %copy-done.2 = bf16[1024,3072]{1,0:T(8,128)(2,1)S(1)} copy-done((bf16[1024,3072]{1,0:T(8,128)(2,1)S(1)}, bf16[1024,3072]{1,0:T(8,128)(2,1)}, u32[]{:S(2)}) %copy-start.2) | copy-done | bytes 6291480
  51.9 2.8 %copy-done.4 = bf16[1024,3072]{1,0:T(8,128)(2,1)S(1)} copy-done((bf16[1024,3072]{1,0:T(8,128)(2,1)S(1)}, bf16[1024,3072]{1,0:T(8,128)(2,1)}, u32[]{:S(2)}) %copy-start.4) | copy-done | bytes 6291480
  54.7 4.5 %product_other.2 = (f32[4,128,256]{2,1,0:T(8,128)S(1)}, bf16[3072,256]{1,0:T(8,128)(2,1)S(1)}, bf16[3072,256]{1,0:T(8,128)(2,1)S(1)}) custom-call(s32[3]{0:T(128)S(1)} %pad_add_fusion.2.place_ref, bf16[4,2,128,3072]{3,2,1,0:T(8,128)(2,1)S(1)} %bitcast.27, bf16[4,2,128,3072]{3,2,1,0:T(8,128)(2,1)S(1)} %bitcast.33, ...), custom_call_target="tpu_custom_call" | custom-call | flops 1 | tf_op jit(solution)/shard_map/product_other/pallas_call | solution.py:144
  59.2 5.1 %collective-permute-start.8 = (f32[4,128,256]{2,1,0:T(8,128)S(1)}, f32[4,128,256]{2,1,0:T(8,128)S(1)}, u32[]{:S(2)}, u32[]{:S(2)}) collective-permute-start(f32[4,128,256]{2,1,0:T(8,128)S(1)} %get-tuple-element.68), channel_id=1, source_target_pairs={{0,1},{1,0},{2,3},{3,2},{4,5},{5,4},{6,7},{7,6},{8,9},{9,8},{10,11... | collective-permute-start | bytes 1572872 | tf_op jit(solution)/shard_map/ppermute | solution.py:21
  64.4 3.2 %product_own.2 = f32[4,128,256]{2,1,0:T(8,128)S(1)} custom-call(s32[3]{0:T(128)S(1)} %pad_add_fusion.2.place_ref, bf16[4,2,128,3072]{3,2,1,0:T(8,128)(2,1)S(1)} %bitcast.28, bf16[4,2,128,3072]{3,2,1,0:T(8,128)(2,1)S(1)} %bitcast.34, bf16[3072,256]{1,0:T(8,128)(2,1)S(1)} %get-tuple-element.64.high, bf16[3072,256]{1,0:T(8,128)(2,1)S(1)} %get-tuple-element.65.low), custom_call_target="tpu_custom_call" | custom-call | flops 1 | tf_op jit(solution)/shard_map/product_own/pallas_call | solution.py:144
  67.6 4.6 %product_other.3 = (f32[4,128,256]{2,1,0:T(8,128)S(1)}, bf16[3072,256]{1,0:T(8,128)(2,1)S(1)}, bf16[3072,256]{1,0:T(8,128)(2,1)S(1)}) custom-call(s32[3]{0:T(128)S(1)} %pad_add_fusion.2.place_ref, bf16[4,2,128,3072]{3,2,1,0:T(8,128)(2,1)S(1)} %bitcast.29, bf16[4,2,128,3072]{3,2,1,0:T(8,128)(2,1)S(1)} %bitcast.35, ...), custom_call_target="tpu_custom_call" | custom-call | flops 1 | tf_op jit(solution)/shard_map/product_other/pallas_call | solution.py:144
  72.2 0.1 collective-permute-start.15
  72.4 0.1 add.45
  72.5 2.7 %collective-permute-start.9 = (f32[2,128,256]{2,1,0:T(8,128)S(1)}, f32[2,128,256]{2,1,0:T(8,128)S(1)}, u32[]{:S(2)}, u32[]{:S(2)}) collective-permute-start(f32[2,128,256]{2,1,0:T(8,128)S(1)} %slice.82), channel_id=1, source_target_pairs={{0,2},{1,7},{2,0},{3,5},{4,6},{5,3},{6,4},{7,1},{8,10},{9,15},{10,... | collective-permute-start | bytes 786440 | tf_op jit(solution)/shard_map/ppermute | solution.py:177
  75.2 3.2 %product_own.3 = f32[4,128,256]{2,1,0:T(8,128)S(1)} custom-call(s32[3]{0:T(128)S(1)} %pad_add_fusion.2.place_ref, bf16[4,2,128,3072]{3,2,1,0:T(8,128)(2,1)S(1)} %bitcast.32, bf16[4,2,128,3072]{3,2,1,0:T(8,128)(2,1)S(1)} %bitcast.36, bf16[3072,256]{1,0:T(8,128)(2,1)S(1)} %get-tuple-element.75.high, bf16[3072,256]{1,0:T(8,128)(2,1)S(1)} %get-tuple-element.76.low), custom_call_target="tpu_custom_call" | custom-call | flops 2415919104 | bytes 6039797 | tf_op jit(solution)/shard_map/product_own/pallas_call | solution.py:144
  78.4 0.1 add.48
  78.5 0.3 collective-permute-start.16
  78.8 0.3 collective-permute-done.9
  79.2 0.4 collective-permute-start.10
  79.6 7.0 %collective-permute-done.16 = f32[2,128,256]{2,1,0:T(8,128)S(1)} collective-permute-done((f32[2,128,256]{2,1,0:T(8,128)S(1)}, f32[2,128,256]{2,1,0:T(8,128)S(1)}, u32[]{:S(2)}, u32[]{:S(2)}) %collective-permute-start.16) | collective-permute-done | bytes 262176 | tf_op jit(solution)/shard_map/ppermute | solution.py:177
  86.6 0.1 collective-permute-start.17
  86.7 0.8 leaf_rows.2
  87.5 1.5 %collective-permute-start.11 = (f32[96,256]{1,0:T(8,128)S(1)}, f32[96,256]{1,0:T(8,128)S(1)}, u32[]{:S(2)}, u32[]{:S(2)}) collective-permute-start(f32[96,256]{1,0:T(8,128)S(1)} %get-tuple-element.71.own_ref.refs_1_), channel_id=1, source_target_pairs={{0,1},{1,0},{2,3},{3,2},{4,5},{5,4},{6,7},{7,6},{8,9},{9,8},{10,11... | collective-permute-start | bytes 294920 | tf_op jit(solution)/shard_map/ppermute | solution.py:21
  89.0 1.8 %collective-permute-done.17.refs_2_ = f32[128,256]{1,0:T(8,128)S(1)} collective-permute-done((f32[128,256]{1,0:T(8,128)S(1)}, f32[128,256]{1,0:T(8,128)S(1)}, u32[]{:S(2)}, u32[]{:S(2)}) %collective-permute-start.17) | collective-permute-done | bytes 131104 | tf_op jit(solution)/shard_map/ppermute | solution.py:177
  90.8 0.8 leaf_rows.3
  91.6 1.5 %collective-permute-start.18 = (f32[96,256]{1,0:T(8,128)S(1)}, f32[96,256]{1,0:T(8,128)S(1)}, u32[]{:S(2)}, u32[]{:S(2)}) collective-permute-start(f32[96,256]{1,0:T(8,128)S(1)} %get-tuple-element.79.own_ref.refs_6_), channel_id=1, source_target_pairs={{0,1},{1,0},{2,3},{3,2},{4,5},{5,4},{6,7},{7,6},{8,9},{9,8},{10,11... | collective-permute-start | bytes 294920 | tf_op jit(solution)/shard_map/ppermute | solution.py:21
  93.1 0.8 mid_rows.2
  93.9 0.1 collective-permute-start.12
  94.0 0.0 collective-permute-done.18.other_ref
  94.0 0.8 mid_rows.3
  94.9 1.5 %collective-permute-start.19 = (f32[96,256]{1,0:T(8,128)S(1)}, f32[96,256]{1,0:T(8,128)S(1)}, u32[]{:S(2)}, u32[]{:S(2)}) collective-permute-start(f32[96,256]{1,0:T(8,128)S(1)} %get-tuple-element.81.refs_8_), channel_id=1, source_target_pairs={{0,2},{1,3},{2,0},{3,1},{4,6},{5,7},{6,4},{7,5},{8,10},{9,11},{10,... | collective-permute-start | bytes 294920 | tf_op jit(solution)/shard_map/ppermute | solution.py:21
  96.4 2.0 %collective-permute-done.12.refs_4_ = f32[96,256]{1,0:T(8,128)S(1)} collective-permute-done((f32[96,256]{1,0:T(8,128)S(1)}, f32[96,256]{1,0:T(8,128)S(1)}, u32[]{:S(2)}, u32[]{:S(2)}) %collective-permute-start.12) | collective-permute-done | bytes 98336 | tf_op jit(solution)/shard_map/ppermute | solution.py:21
  98.4 2.1 %collective-permute-done.19.refs_9_ = f32[96,256]{1,0:T(8,128)S(1)} collective-permute-done((f32[96,256]{1,0:T(8,128)S(1)}, f32[96,256]{1,0:T(8,128)S(1)}, u32[]{:S(2)}, u32[]{:S(2)}) %collective-permute-start.19) | collective-permute-done | bytes 98336 | tf_op jit(solution)/shard_map/ppermute | solution.py:21
  100.5 9.8 %interpolation.1 = (f32[96,128]{1,0:T(8,128)}, f32[96,192]{1,0:T(8,128)}, f32[96,192]{1,0:T(8,128)}, f32[96,512]{1,0:T(8,128)}) custom-call(s32[1]{0:T(128)} %bitcast.info_ref, s32[224]{0:T(256)S(1)} %pad_add_fusion.1.ranks_ref, s32[3,96]{1,0:T(4,128)S(1)} %pad_add_fusion.pivots_ref, f32[128,256]{1,0:T(8,128)S(1)} %get-tuple-element.70.refs_0_, ...), custom_call_target="tpu_custom_call" | custom-call | tf_op jit(solution)/shard_map/interpolation/pallas_call | solution.py:365
  (31 shorter events, 0.2 us)
Async XLA Ops:
  0.6 33.7 %copy-start = (s32[128,128]{1,0:T(8,128)S(1)}, s32[128,128]{1,0:T(8,128)}, u32[]{:S(2)}) copy-start(s32[128,128]{1,0:T(8,128)} %param.11) | copy-start | bytes 196612
  1.7 5.9 %collective-permute-start = (f32[1,96,512]{2,1,0:T(8,128)S(1)}, f32[1,96,512]{2,1,0:T(8,128)S(1)}, u32[]{:S(2)}, u32[]{:S(2)}) collective-permute-start(f32[1,96,512]{2,1,0:T(8,128)S(1)} %get-tuple-element.99), channel_id=1, source_target_pairs={{0,32},{1,9},{2,34},{3,11},{4,36},{5,13},{6,38},{7,15},{8,40},{9,1... | collective-permute-start | bytes 589832 | tf_op jit(solution)/shard_map/ppermute | solution.py:44
  4.3 7.0 %collective-permute-start.2 = (f32[1,96,512]{2,1,0:T(8,128)S(1)}, f32[1,96,512]{2,1,0:T(8,128)S(1)}, u32[]{:S(2)}, u32[]{:S(2)}) collective-permute-start(f32[1,96,512]{2,1,0:T(8,128)S(1)} %get-tuple-element.98), channel_id=1, source_target_pairs={{0,96},{1,25},{2,98},{3,27},{4,100},{5,29},{6,102},{7,31},{8,104},... | collective-permute-start | bytes 589832 | tf_op jit(solution)/shard_map/ppermute | solution.py:44
  7.7 9.1 %collective-permute-start.1 = (f32[2,96,512]{2,1,0:T(8,128)S(1)}, f32[2,96,512]{2,1,0:T(8,128)S(1)}, u32[]{:S(2)}, u32[]{:S(2)}) collective-permute-start(f32[2,96,512]{2,1,0:T(8,128)S(1)} %pad_maximum_fusion.6), channel_id=1, source_target_pairs={{0,96},{1,25},{2,98},{3,27},{4,100},{5,29},{6,102},{7,31},{8,104},... | collective-permute-start | bytes 1179656 | tf_op jit(solution)/shard_map/ppermute | solution.py:44
  11.4 7.0 %collective-permute-start.3 = (f32[2,96,512]{2,1,0:T(8,128)S(1)}, f32[2,96,512]{2,1,0:T(8,128)S(1)}, u32[]{:S(2)}, u32[]{:S(2)}) collective-permute-start(f32[2,96,512]{2,1,0:T(8,128)S(1)} %pad_maximum_fusion.7), channel_id=1, source_target_pairs={{0,32},{1,9},{2,34},{3,11},{4,36},{5,13},{6,38},{7,15},{8,40},{9,1... | collective-permute-start | bytes 1179656 | tf_op jit(solution)/shard_map/ppermute | solution.py:44
  18.4 16.7 %collective-permute-start.4 = (f32[4,96,512]{2,1,0:T(8,128)S(1)}, f32[4,96,512]{2,1,0:T(8,128)S(1)}, u32[]{:S(2)}, u32[]{:S(2)}) collective-permute-start(f32[4,96,512]{2,1,0:T(8,128)S(1)} %pad_maximum_fusion), channel_id=1, source_target_pairs={{0,8},{1,33},{2,10},{3,35},{4,12},{5,37},{6,14},{7,39},{8,0},{9,41... | collective-permute-start | bytes 2359304 | tf_op jit(solution)/shard_map/ppermute | solution.py:44
  19.7 15.5 %collective-permute-start.5 = (f32[4,96,512]{2,1,0:T(8,128)S(1)}, f32[4,96,512]{2,1,0:T(8,128)}, u32[]{:S(2)}, u32[]{:S(2)}) collective-permute-start(f32[4,96,512]{2,1,0:T(8,128)S(1)} %pad_maximum_fusion.1), channel_id=1, source_target_pairs={{0,24},{1,97},{2,26},{3,99},{4,28},{5,101},{6,30},{7,103},{8,16},{... | collective-permute-start | bytes 2359304 | tf_op jit(solution)/shard_map/ppermute | solution.py:44
  21.5 12.8 %copy-start.5 = (s32[32]{0:T(128)S(1)}, s32[32]{0:T(128)}, u32[]{:S(2)}) copy-start(s32[32]{0:T(128)} %param.14) | copy-start | bytes 388
  21.5 12.8 %copy-start.6 = (s32[64]{0:T(128)S(1)}, s32[64]{0:T(128)}, u32[]{:S(2)}) copy-start(s32[64]{0:T(128)} %param.12) | copy-start | bytes 772
  21.5 12.8 %copy-start.7 = (s32[128]{0:T(128)S(1)}, s32[128]{0:T(128)}, u32[]{:S(2)}) copy-start(s32[128]{0:T(128)} %param.10) | copy-start | bytes 1540
  28.9 2.7 %copy-start.1 = (bf16[1024,3072]{1,0:T(8,128)(2,1)}, bf16[1024,3072]{1,0:T(8,128)(2,1)S(1)}, u32[]{:S(2)}) copy-start(bf16[1024,3072]{1,0:T(8,128)(2,1)S(1)} %get-tuple-element.58) | copy-start | bytes 18874372
  31.6 2.7 %copy-start.3 = (bf16[1024,3072]{1,0:T(8,128)(2,1)}, bf16[1024,3072]{1,0:T(8,128)(2,1)S(1)}, u32[]{:S(2)}) copy-start(bf16[1024,3072]{1,0:T(8,128)(2,1)S(1)} %get-tuple-element.59) | copy-start | bytes 18874372
  36.6 12.5 %collective-permute-start.6 = (f32[8,96,256]{2,1,0:T(8,128)S(1)}, f32[8,96,256]{2,1,0:T(8,128)}, u32[]{:S(2)}, u32[]{:S(2)}) collective-permute-start(f32[8,96,256]{2,1,0:T(8,128)S(1)} %pad_maximum_fusion.2.refs_0_), channel_id=1, source_target_pairs={{0,24},{1,97},{2,26},{3,99},{4,28},{5,101},{6,30},{7,103},{8,16},{... | collective-permute-start | bytes 2359304 | tf_op jit(solution)/shard_map/ppermute | solution.py:44
  37.6 11.5 %collective-permute-start.7 = (f32[8,96,256]{2,1,0:T(8,128)S(1)}, f32[8,96,256]{2,1,0:T(8,128)}, u32[]{:S(2)}, u32[]{:S(2)}) collective-permute-start(f32[8,96,256]{2,1,0:T(8,128)S(1)} %pad_maximum_fusion.3.refs_1_), channel_id=1, source_target_pairs={{0,8},{1,33},{2,10},{3,35},{4,12},{5,37},{6,14},{7,39},{8,0},{9,41... | collective-permute-start | bytes 2359304 | tf_op jit(solution)/shard_map/ppermute | solution.py:44
  37.8 29.8 %collective-permute-start.13 = (f32[8,96,256]{2,1,0:T(8,128)S(1)}, f32[8,96,256]{2,1,0:T(8,128)}, u32[]{:S(2)}, u32[]{:S(2)}) collective-permute-start(f32[8,96,256]{2,1,0:T(8,128)S(1)} %pad_maximum_fusion.4.refs_0_), channel_id=1, source_target_pairs={{0,24},{1,97},{2,26},{3,99},{4,28},{5,101},{6,30},{7,103},{8,16},{... | collective-permute-start | bytes 2359304 | tf_op jit(solution)/shard_map/ppermute | solution.py:44
  39.8 27.8 %collective-permute-start.14 = (f32[8,96,256]{2,1,0:T(8,128)S(1)}, f32[8,96,256]{2,1,0:T(8,128)}, u32[]{:S(2)}, u32[]{:S(2)}) collective-permute-start(f32[8,96,256]{2,1,0:T(8,128)S(1)} %pad_maximum_fusion.5.refs_1_), channel_id=1, source_target_pairs={{0,8},{1,33},{2,10},{3,35},{4,12},{5,37},{6,14},{7,39},{8,0},{9,41... | collective-permute-start | bytes 2359304 | tf_op jit(solution)/shard_map/ppermute | solution.py:44
  49.1 2.8 %copy-start.2 = (bf16[1024,3072]{1,0:T(8,128)(2,1)S(1)}, bf16[1024,3072]{1,0:T(8,128)(2,1)}, u32[]{:S(2)}) copy-start(bf16[1024,3072]{1,0:T(8,128)(2,1)} %copy-done.1) | copy-start | bytes 18874372
  51.9 2.8 %copy-start.4 = (bf16[1024,3072]{1,0:T(8,128)(2,1)S(1)}, bf16[1024,3072]{1,0:T(8,128)(2,1)}, u32[]{:S(2)}) copy-start(bf16[1024,3072]{1,0:T(8,128)(2,1)} %copy-done.3) | copy-start | bytes 18874372
  59.2 13.1 %collective-permute-start.8 = (f32[4,128,256]{2,1,0:T(8,128)S(1)}, f32[4,128,256]{2,1,0:T(8,128)S(1)}, u32[]{:S(2)}, u32[]{:S(2)}) collective-permute-start(f32[4,128,256]{2,1,0:T(8,128)S(1)} %get-tuple-element.68), channel_id=1, source_target_pairs={{0,1},{1,0},{2,3},{3,2},{4,5},{5,4},{6,7},{7,6},{8,9},{9,8},{10,11... | collective-permute-start | bytes 1572872 | tf_op jit(solution)/shard_map/ppermute | solution.py:21
  64.4 10.8 %slice-start = ((s8[6291456]{0:T(1024)(128)(4,1)}), s8[4194304]{0:T(1024)(128)(4,1)S(1)}, s32[]{:S(2)}) async-start(s8[6291456]{0:T(1024)(128)(4,1)} %bitcast.30), calls=%async_computation | async-start | bytes 8388608
  67.6 7.6 %slice-start.1 = ((s8[6291456]{0:T(1024)(128)(4,1)}), s8[2097152]{0:T(1024)(128)(4,1)S(1)}, s32[]{:S(2)}) async-start(s8[6291456]{0:T(1024)(128)(4,1)} %bitcast.30), calls=%async_computation.1 | async-start | bytes 4194304
  72.2 6.2 %collective-permute-start.15 = (f32[4,128,256]{2,1,0:T(8,128)S(1)}, f32[4,128,256]{2,1,0:T(8,128)S(1)}, u32[]{:S(2)}, u32[]{:S(2)}) collective-permute-start(f32[4,128,256]{2,1,0:T(8,128)S(1)} %get-tuple-element.77), channel_id=1, source_target_pairs={{0,1},{1,0},{2,3},{3,2},{4,5},{5,4},{6,7},{7,6},{8,9},{9,8},{10,11... | collective-permute-start | bytes 1572872 | tf_op jit(solution)/shard_map/ppermute | solution.py:21
  72.5 6.7 %collective-permute-start.9 = (f32[2,128,256]{2,1,0:T(8,128)S(1)}, f32[2,128,256]{2,1,0:T(8,128)S(1)}, u32[]{:S(2)}, u32[]{:S(2)}) collective-permute-start(f32[2,128,256]{2,1,0:T(8,128)S(1)} %slice.82), channel_id=1, source_target_pairs={{0,2},{1,7},{2,0},{3,5},{4,6},{5,3},{6,4},{7,1},{8,10},{9,15},{10,... | collective-permute-start | bytes 786440 | tf_op jit(solution)/shard_map/ppermute | solution.py:177
  78.5 8.0 %collective-permute-start.16 = (f32[2,128,256]{2,1,0:T(8,128)S(1)}, f32[2,128,256]{2,1,0:T(8,128)S(1)}, u32[]{:S(2)}, u32[]{:S(2)}) collective-permute-start(f32[2,128,256]{2,1,0:T(8,128)S(1)} %slice.98), channel_id=1, source_target_pairs={{0,2},{1,7},{2,0},{3,5},{4,6},{5,3},{6,4},{7,1},{8,10},{9,15},{10,... | collective-permute-start | bytes 786440 | tf_op jit(solution)/shard_map/ppermute | solution.py:177
  79.2 7.5 %collective-permute-start.10 = (f32[128,256]{1,0:T(8,128)S(1)}, f32[128,256]{1,0:T(8,128)S(1)}, u32[]{:S(2)}, u32[]{:S(2)}) collective-permute-start(f32[128,256]{1,0:T(8,128)S(1)} %get-tuple-element.96), channel_id=1, source_target_pairs={{0,6},{1,3},{2,4},{3,1},{4,2},{5,7},{6,0},{7,5},{8,14},{9,11},{10,... | collective-permute-start | bytes 393224 | tf_op jit(solution)/shard_map/ppermute | solution.py:177
  86.6 4.2 %collective-permute-start.17 = (f32[128,256]{1,0:T(8,128)S(1)}, f32[128,256]{1,0:T(8,128)S(1)}, u32[]{:S(2)}, u32[]{:S(2)}) collective-permute-start(f32[128,256]{1,0:T(8,128)S(1)} %get-tuple-element.94), channel_id=1, source_target_pairs={{0,6},{1,3},{2,4},{3,1},{4,2},{5,7},{6,0},{7,5},{8,14},{9,11},{10,... | collective-permute-start | bytes 393224 | tf_op jit(solution)/shard_map/ppermute | solution.py:177
  87.5 5.6 %collective-permute-start.11 = (f32[96,256]{1,0:T(8,128)S(1)}, f32[96,256]{1,0:T(8,128)S(1)}, u32[]{:S(2)}, u32[]{:S(2)}) collective-permute-start(f32[96,256]{1,0:T(8,128)S(1)} %get-tuple-element.71.own_ref.refs_1_), channel_id=1, source_target_pairs={{0,1},{1,0},{2,3},{3,2},{4,5},{5,4},{6,7},{7,6},{8,9},{9,8},{10,11... | collective-permute-start | bytes 294920 | tf_op jit(solution)/shard_map/ppermute | solution.py:21
  91.6 2.4 %collective-permute-start.18 = (f32[96,256]{1,0:T(8,128)S(1)}, f32[96,256]{1,0:T(8,128)S(1)}, u32[]{:S(2)}, u32[]{:S(2)}) collective-permute-start(f32[96,256]{1,0:T(8,128)S(1)} %get-tuple-element.79.own_ref.refs_6_), channel_id=1, source_target_pairs={{0,1},{1,0},{2,3},{3,2},{4,5},{5,4},{6,7},{7,6},{8,9},{9,8},{10,11... | collective-permute-start | bytes 294920 | tf_op jit(solution)/shard_map/ppermute | solution.py:21
  93.9 4.5 %collective-permute-start.12 = (f32[96,256]{1,0:T(8,128)S(1)}, f32[96,256]{1,0:T(8,128)S(1)}, u32[]{:S(2)}, u32[]{:S(2)}) collective-permute-start(f32[96,256]{1,0:T(8,128)S(1)} %get-tuple-element.73.refs_3_), channel_id=1, source_target_pairs={{0,2},{1,3},{2,0},{3,1},{4,6},{5,7},{6,4},{7,5},{8,10},{9,11},{10,... | collective-permute-start | bytes 294920 | tf_op jit(solution)/shard_map/ppermute | solution.py:21
  94.9 5.7 %collective-permute-start.19 = (f32[96,256]{1,0:T(8,128)S(1)}, f32[96,256]{1,0:T(8,128)S(1)}, u32[]{:S(2)}, u32[]{:S(2)}) collective-permute-start(f32[96,256]{1,0:T(8,128)S(1)} %get-tuple-element.81.refs_8_), channel_id=1, source_target_pairs={{0,2},{1,3},{2,0},{3,1},{4,6},{5,7},{6,4},{7,5},{8,10},{9,11},{10,... | collective-permute-start | bytes 294920 | tf_op jit(solution)/shard_map/ppermute | solution.py:21

commit v6 on v5

--- a/solution.py
+++ b/solution.py
@@ -51,7 +51,7 @@
     return found
 
 
-def gather_parts(sketch, before, after):
+def gather_parts(sketch, frontal, before, after):
     depth = sketch.shape[0] // len(ORDERS)
     stacks = [sketch[None, part * depth : (part + 1) * depth] for part in range(len(ORDERS))]
     for step in range(3):
@@ -60,7 +60,9 @@
             received, before = lax.optimization_barrier((received, before))
         if step < 2:
             stacks = [jnp.concatenate(pair, 0) for pair in zip(stacks, received)]
-    stacks, received, ready = lax.optimization_barrier((stacks, received, after(*before)))
+    stacks, received, ready, frontal = lax.optimization_barrier(
+        (stacks, received, after(*before), frontal)
+    )
     chunks, start = [], 0
     for width in WIDTHS:
         columns = slice(start, start + width)
@@ -70,7 +72,7 @@
         ]
         chunks.append(own + [from_row(value, 3, masks) for value, masks in zip(own, ORDERS)])
         start += width
-    return chunks, ready
+    return chunks, ready, frontal
 
 
 def split_kernel(value_ref, high_ref, low_ref):
@@ -385,15 +387,15 @@
     place = jnp.stack([row_index, col_index // 2, col_index % 2]).astype(jnp.int32)
     nodes = (leaf_index, leaf_index // 2, leaf_index // 4)
 
-    def prepare(frontal, *tables):
+    def prepare(*tables):
         ranks = jnp.concatenate(tables[:3])
         pivots = [pick_entry(table, node)[:KMAX] for table, node in zip(tables[3:], nodes)]
-        return (*split(frontal), ranks, jnp.stack(pivots))
+        return ranks, jnp.stack(pivots)
 
     tables = (leaf_ranks, mid_ranks, top_ranks, leaf_pivots, mid_pivots, top_pivots)
-    chunks, (high, low, ranks, pivots) = gather_parts(sketch, (frontal, *tables), prepare)
+    chunks, (ranks, pivots), frontal = gather_parts(sketch, frontal, tables, prepare)
     info = jnp.stack([leaf_index]).astype(jnp.int32)
-    halves = [part.reshape(SIDE, 2, LEAF, -1) for part in (high, low)]
+    halves = [part.reshape(SIDE, 2, LEAF, -1) for part in split(frontal)]
     core_sums, own = [], ()
     for chunk, pieces in enumerate(chunks):
         place, own = lax.optimization_barrier((place, own))

time: 111 us -> 104 us (0.937)
  local copies, waits for them, and re-layouts: 14.1 us -> 3.26 us
  waiting for transfers between devices: 29.7 us -> 33.7 us
    unnamed x20 -> x8, local copies, waits for them, and re-layouts: 10.9 us -> 0.03 us
    ppermute x10, waiting for transfers between devices: 16.4 us -> 19.6 us  [from_row(): return lax.ppermute(value, ('row', 'col'), pairs)]
  transfers between devices with their start and end apart: 20 -> 20, of which waited for: 9 -> 12; matrix products, arithmetic and copies ran while one was open for 1% -> 1% of each run, Pallas kernels for 24% -> 25%
where the time goes in v6:
time: 104 us; the launch traced here: 103 us
  Pallas kernels  35.6 us (34%)
  waiting for transfers between devices  33.7 us (32%)
  starting transfers between devices  28.9 us (28%)
  local copies, waits for them, and re-layouts  3.26 us (3%)
    ppermute x10, waiting for transfers between devices, from_row(): return lax.ppermute(value, ('row', 'col'), pairs)  19.6 us
    ppermute x10, starting transfers between devices, from_row(): return lax.ppermute(value, ('row', 'col'), pairs)  15.4 us
    pallas_call x4, Pallas kernels, product(): pl.pallas_call(kernel, out_shape=outs, in_specs=[pl.BlockSpec(memory_spac...  15.2 us
    pallas_call x5, Pallas kernels, call(): pl.pallas_call(kernel, out_shape=[jax.ShapeDtypeStruct(shape, jnp.float32...  13 us
    ppermute x6, starting transfers between devices, from_partner(): return lax.ppermute(value, axis, pairs)  10 us
    ppermute x4, waiting for transfers between devices, from_x(): return lax.ppermute(value, 'col', pairs)  9.96 us
    pallas_call x1, Pallas kernels, split(): pl.pallas_call(split_kernel, out_shape=[pltpu.VMEM(value.shape, jnp.bfloa...  7.35 us
    ppermute x6, waiting for transfers between devices, from_partner(): return lax.ppermute(value, axis, pairs)  4.17 us
  transfers between devices with their start and end apart: 20, of which 12 were waited for; matrix products, arithmetic and copies ran while one was open for 1% of the time, Pallas kernels for 25%

profile of v6, /device:TPU:1, one launch (start us, length us, event | category | flops | bytes accessed | tf_op | source)
XLA Modules:
  0.0 103.3 jit_solution(7558504377443151392)
XLA Ops:
  0.6 0.0 copy-start
  0.6 1.1 %slice_bitcast_fusion = (f32[1,96,512]{2,1,0:T(8,128)S(1)}, f32[1,96,512]{2,1,0:T(8,128)S(1)}) fusion(f32[192,512]{1,0:T(8,128)} %param.9), kind=kLoop, calls=%fused_computation.8 | loop fusion | bytes 786432 | tf_op jit(solution)/shard_map/broadcast_in_dim | solution.py:56
  1.7 2.5 %collective-permute-start = (f32[1,96,512]{2,1,0:T(8,128)S(1)}, f32[1,96,512]{2,1,0:T(8,128)S(1)}, u32[]{:S(2)}, u32[]{:S(2)}) collective-permute-start(f32[1,96,512]{2,1,0:T(8,128)S(1)} %get-tuple-element.95), channel_id=1, source_target_pairs={{0,32},{1,9},{2,34},{3,11},{4,36},{5,13},{6,38},{7,15},{8,40},{9,1... | collective-permute-start | bytes 589832 | tf_op jit(solution)/shard_map/ppermute | solution.py:44
  4.3 2.2 %collective-permute-start.2 = (f32[1,96,512]{2,1,0:T(8,128)S(1)}, f32[1,96,512]{2,1,0:T(8,128)S(1)}, u32[]{:S(2)}, u32[]{:S(2)}) collective-permute-start(f32[1,96,512]{2,1,0:T(8,128)S(1)} %get-tuple-element.94), channel_id=1, source_target_pairs={{0,96},{1,25},{2,98},{3,27},{4,100},{5,29},{6,102},{7,31},{8,104},... | collective-permute-start | bytes 589832 | tf_op jit(solution)/shard_map/ppermute | solution.py:44
  6.5 1.1 %collective-permute-done = f32[1,96,512]{2,1,0:T(8,128)S(1)} collective-permute-done((f32[1,96,512]{2,1,0:T(8,128)S(1)}, f32[1,96,512]{2,1,0:T(8,128)S(1)}, u32[]{:S(2)}, u32[]{:S(2)}) %collective-permute-start) | collective-permute-done | bytes 196640 | tf_op jit(solution)/shard_map/ppermute | solution.py:44
  7.7 3.7 %collective-permute-start.1 = (f32[2,96,512]{2,1,0:T(8,128)S(1)}, f32[2,96,512]{2,1,0:T(8,128)S(1)}, u32[]{:S(2)}, u32[]{:S(2)}) collective-permute-start(f32[2,96,512]{2,1,0:T(8,128)S(1)} %pad_maximum_fusion.6), channel_id=1, source_target_pairs={{0,96},{1,25},{2,98},{3,27},{4,100},{5,29},{6,102},{7,31},{8,104},... | collective-permute-start | bytes 1179656 | tf_op jit(solution)/shard_map/ppermute | solution.py:44
  11.3 0.0 collective-permute-done.2
  11.4 0.0 copy-start.1
  11.4 0.0 copy-start.2
  11.4 0.0 copy-start.3
  11.4 0.1 collective-permute-start.3
  11.5 5.3 %collective-permute-done.1 = f32[2,96,512]{2,1,0:T(8,128)S(1)} collective-permute-done((f32[2,96,512]{2,1,0:T(8,128)S(1)}, f32[2,96,512]{2,1,0:T(8,128)S(1)}, u32[]{:S(2)}, u32[]{:S(2)}) %collective-permute-start.1) | collective-permute-done | bytes 393248 | tf_op jit(solution)/shard_map/ppermute | solution.py:44
  16.8 1.6 %collective-permute-done.3 = f32[2,96,512]{2,1,0:T(8,128)S(1)} collective-permute-done((f32[2,96,512]{2,1,0:T(8,128)S(1)}, f32[2,96,512]{2,1,0:T(8,128)S(1)}, u32[]{:S(2)}, u32[]{:S(2)}) %collective-permute-start.3) | collective-permute-done | bytes 393248 | tf_op jit(solution)/shard_map/ppermute | solution.py:44
  18.4 0.1 pad_maximum_fusion
  18.5 1.2 %collective-permute-start.4 = (f32[4,96,512]{2,1,0:T(8,128)S(1)}, f32[4,96,512]{2,1,0:T(8,128)S(1)}, u32[]{:S(2)}, u32[]{:S(2)}) collective-permute-start(f32[4,96,512]{2,1,0:T(8,128)S(1)} %pad_maximum_fusion), channel_id=1, source_target_pairs={{0,8},{1,33},{2,10},{3,35},{4,12},{5,37},{6,14},{7,39},{8,0},{9,41... | collective-permute-start | bytes 2359304 | tf_op jit(solution)/shard_map/ppermute | solution.py:44
  19.6 0.1 pad_maximum_fusion.1
  19.7 1.9 %collective-permute-start.5 = (f32[4,96,512]{2,1,0:T(8,128)S(1)}, f32[4,96,512]{2,1,0:T(8,128)}, u32[]{:S(2)}, u32[]{:S(2)}) collective-permute-start(f32[4,96,512]{2,1,0:T(8,128)S(1)} %pad_maximum_fusion.1), channel_id=1, source_target_pairs={{0,24},{1,97},{2,26},{3,99},{4,28},{5,101},{6,30},{7,103},{8,16},{... | collective-permute-start | bytes 2359304 | tf_op jit(solution)/shard_map/ppermute | solution.py:44
  21.6 0.1 pad_add_fusion.1.ranks_ref
  21.7 0.7 constant_dynamic-slice_fusion
  22.4 7.3 %collective-permute-done.4 = f32[4,96,512]{2,1,0:T(8,128)S(1)} collective-permute-done((f32[4,96,512]{2,1,0:T(8,128)S(1)}, f32[4,96,512]{2,1,0:T(8,128)S(1)}, u32[]{:S(2)}, u32[]{:S(2)}) %collective-permute-start.4) | collective-permute-done | bytes 786464 | tf_op jit(solution)/shard_map/ppermute | solution.py:44
  29.8 2.5 %collective-permute-done.5 = f32[4,96,512]{2,1,0:T(8,128)} collective-permute-done((f32[4,96,512]{2,1,0:T(8,128)S(1)}, f32[4,96,512]{2,1,0:T(8,128)}, u32[]{:S(2)}, u32[]{:S(2)}) %collective-permute-start.5) | collective-permute-done | bytes 786464 | tf_op jit(solution)/shard_map/ppermute | solution.py:44
  32.2 0.1 fusion.5
  32.3 0.1 fusion.4
  32.4 1.2 %fusion.3 = (f32[4,96,256]{2,1,0:T(8,128)S(1)}, f32[4,96,256]{2,1,0:T(8,128)S(1)}) fusion(f32[4,96,512]{2,1,0:T(8,128)} %collective-permute-done.5), kind=kLoop, calls=%fused_computation.25 | loop fusion | bytes 1572864 | tf_op jit(solution)/shard_map/slice | solution.py:70
  33.6 0.1 fusion.2
  33.6 0.1 pad_maximum_fusion.2.refs_0_
  33.7 1.9 %collective-permute-start.6 = (f32[8,96,256]{2,1,0:T(8,128)S(1)}, f32[8,96,256]{2,1,0:T(8,128)}, u32[]{:S(2)}, u32[]{:S(2)}) collective-permute-start(f32[8,96,256]{2,1,0:T(8,128)S(1)} %pad_maximum_fusion.2.refs_0_), channel_id=1, source_target_pairs={{0,24},{1,97},{2,26},{3,99},{4,28},{5,101},{6,30},{7,103},{8,16},{... | collective-permute-start | bytes 2359304 | tf_op jit(solution)/shard_map/ppermute | solution.py:44
  35.6 0.1 pad_maximum_fusion.3.refs_1_
  35.7 0.1 collective-permute-start.7
  35.8 0.1 pad_maximum_fusion.4.refs_0_
  35.8 1.0 collective-permute-start.13
  36.8 0.1 pad_maximum_fusion.5.refs_1_
  36.9 0.9 collective-permute-start.14
  37.8 0.1 pad_add_fusion.2.place_ref
  37.9 7.3 %split.1 = (bf16[1024,3072]{1,0:T(8,128)(2,1)S(1)}, bf16[1024,3072]{1,0:T(8,128)(2,1)S(1)}) custom-call(f32[1024,3072]{1,0:T(8,128)} %value_ref), custom_call_target="tpu_custom_call" | custom-call | flops 12582912 | bytes 25165824 | tf_op jit(solution)/shard_map/split/pallas_call | solution.py:88
  45.2 1.0 collective-permute-done.6.refs_2_
  46.3 0.7 collective-permute-done.7.refs_3_
  47.0 4.4 %product_other.2 = (f32[4,128,256]{2,1,0:T(8,128)S(1)}, bf16[3072,256]{1,0:T(8,128)(2,1)S(1)}, bf16[3072,256]{1,0:T(8,128)(2,1)S(1)}) custom-call(s32[3]{0:T(128)S(1)} %pad_add_fusion.2.place_ref, bf16[4,2,128,3072]{3,2,1,0:T(8,128)(2,1)S(1)} %bitcast.27, bf16[4,2,128,3072]{3,2,1,0:T(8,128)(2,1)S(1)} %bitcast.31, ...), custom_call_target="tpu_custom_call" | custom-call | flops 1 | tf_op jit(solution)/shard_map/product_other/pallas_call | solution.py:146
  51.5 6.0 %collective-permute-start.8 = (f32[4,128,256]{2,1,0:T(8,128)S(1)}, f32[4,128,256]{2,1,0:T(8,128)S(1)}, u32[]{:S(2)}, u32[]{:S(2)}) collective-permute-start(f32[4,128,256]{2,1,0:T(8,128)S(1)} %get-tuple-element.64), channel_id=1, source_target_pairs={{0,1},{1,0},{2,3},{3,2},{4,5},{5,4},{6,7},{7,6},{8,9},{9,8},{10,11... | collective-permute-start | bytes 1572872 | tf_op jit(solution)/shard_map/ppermute | solution.py:21
  57.4 3.2 %product_own.2 = f32[4,128,256]{2,1,0:T(8,128)S(1)} custom-call(s32[3]{0:T(128)S(1)} %pad_add_fusion.2.place_ref, bf16[4,2,128,3072]{3,2,1,0:T(8,128)(2,1)S(1)} %bitcast.28, bf16[4,2,128,3072]{3,2,1,0:T(8,128)(2,1)S(1)} %bitcast.32, bf16[3072,256]{1,0:T(8,128)(2,1)S(1)} %get-tuple-element.60.high, bf16[3072,256]{1,0:T(8,128)(2,1)S(1)} %get-tuple-element.61.low), custom_call_target="tpu_custom_call" | custom-call | flops 1 | tf_op jit(solution)/shard_map/product_own/pallas_call | solution.py:146
  60.6 4.4 %product_other.3 = (f32[4,128,256]{2,1,0:T(8,128)S(1)}, bf16[3072,256]{1,0:T(8,128)(2,1)S(1)}, bf16[3072,256]{1,0:T(8,128)(2,1)S(1)}) custom-call(s32[3]{0:T(128)S(1)} %pad_add_fusion.2.place_ref, bf16[4,2,128,3072]{3,2,1,0:T(8,128)(2,1)S(1)} %bitcast.29, bf16[4,2,128,3072]{3,2,1,0:T(8,128)(2,1)S(1)} %bitcast.33, ...), custom_call_target="tpu_custom_call" | custom-call | flops 1 | tf_op jit(solution)/shard_map/product_other/pallas_call | solution.py:146
  65.1 0.8 collective-permute-start.15
  65.9 0.1 add.45
  66.0 2.7 %collective-permute-start.9 = (f32[2,128,256]{2,1,0:T(8,128)S(1)}, f32[2,128,256]{2,1,0:T(8,128)S(1)}, u32[]{:S(2)}, u32[]{:S(2)}) collective-permute-start(f32[2,128,256]{2,1,0:T(8,128)S(1)} %slice.82), channel_id=1, source_target_pairs={{0,2},{1,7},{2,0},{3,5},{4,6},{5,3},{6,4},{7,1},{8,10},{9,15},{10,... | collective-permute-start | bytes 786440 | tf_op jit(solution)/shard_map/ppermute | solution.py:179
  68.7 3.2 %product_own.3 = f32[4,128,256]{2,1,0:T(8,128)S(1)} custom-call(s32[3]{0:T(128)S(1)} %pad_add_fusion.2.place_ref, bf16[4,2,128,3072]{3,2,1,0:T(8,128)(2,1)S(1)} %bitcast.30, bf16[4,2,128,3072]{3,2,1,0:T(8,128)(2,1)S(1)} %bitcast.34, bf16[3072,256]{1,0:T(8,128)(2,1)S(1)} %get-tuple-element.71.high, bf16[3072,256]{1,0:T(8,128)(2,1)S(1)} %get-tuple-element.72.low), custom_call_target="tpu_custom_call" | custom-call | flops 2415919104 | bytes 6039797 | tf_op jit(solution)/shard_map/product_own/pallas_call | solution.py:146
  71.9 0.1 add.48
  72.0 0.3 collective-permute-start.16
  72.3 0.4 collective-permute-done.9
  72.7 0.4 collective-permute-start.10
  73.1 6.9 %collective-permute-done.16 = f32[2,128,256]{2,1,0:T(8,128)S(1)} collective-permute-done((f32[2,128,256]{2,1,0:T(8,128)S(1)}, f32[2,128,256]{2,1,0:T(8,128)S(1)}, u32[]{:S(2)}, u32[]{:S(2)}) %collective-permute-start.16) | collective-permute-done | bytes 262176 | tf_op jit(solution)/shard_map/ppermute | solution.py:179
  80.0 0.1 collective-permute-start.17
  80.1 0.8 leaf_rows.2
  80.9 0.6 collective-permute-start.11
  81.5 2.7 %collective-permute-done.17.refs_2_ = f32[128,256]{1,0:T(8,128)S(1)} collective-permute-done((f32[128,256]{1,0:T(8,128)S(1)}, f32[128,256]{1,0:T(8,128)S(1)}, u32[]{:S(2)}, u32[]{:S(2)}) %collective-permute-start.17) | collective-permute-done | bytes 131104 | tf_op jit(solution)/shard_map/ppermute | solution.py:179
  84.2 0.8 leaf_rows.3
  85.0 1.1 %collective-permute-start.18 = (f32[96,256]{1,0:T(8,128)S(1)}, f32[96,256]{1,0:T(8,128)S(1)}, u32[]{:S(2)}, u32[]{:S(2)}) collective-permute-start(f32[96,256]{1,0:T(8,128)S(1)} %get-tuple-element.75.own_ref.refs_6_), channel_id=1, source_target_pairs={{0,1},{1,0},{2,3},{3,2},{4,5},{5,4},{6,7},{7,6},{8,9},{9,8},{10,11... | collective-permute-start | bytes 294920 | tf_op jit(solution)/shard_map/ppermute | solution.py:21
  86.1 0.8 mid_rows.2
  86.9 0.1 collective-permute-start.12
  87.0 0.0 collective-permute-done.18.other_ref
  87.0 0.8 mid_rows.3
  87.9 1.5 %collective-permute-start.19 = (f32[96,256]{1,0:T(8,128)S(1)}, f32[96,256]{1,0:T(8,128)S(1)}, u32[]{:S(2)}, u32[]{:S(2)}) collective-permute-start(f32[96,256]{1,0:T(8,128)S(1)} %get-tuple-element.77.refs_8_), channel_id=1, source_target_pairs={{0,2},{1,3},{2,0},{3,1},{4,6},{5,7},{6,4},{7,5},{8,10},{9,11},{10,... | collective-permute-start | bytes 294920 | tf_op jit(solution)/shard_map/ppermute | solution.py:21
  89.4 2.0 %collective-permute-done.12.refs_4_ = f32[96,256]{1,0:T(8,128)S(1)} collective-permute-done((f32[96,256]{1,0:T(8,128)S(1)}, f32[96,256]{1,0:T(8,128)S(1)}, u32[]{:S(2)}, u32[]{:S(2)}) %collective-permute-start.12) | collective-permute-done | bytes 98336 | tf_op jit(solution)/shard_map/ppermute | solution.py:21
  91.4 2.1 %collective-permute-done.19.refs_9_ = f32[96,256]{1,0:T(8,128)S(1)} collective-permute-done((f32[96,256]{1,0:T(8,128)S(1)}, f32[96,256]{1,0:T(8,128)S(1)}, u32[]{:S(2)}, u32[]{:S(2)}) %collective-permute-start.19) | collective-permute-done | bytes 98336 | tf_op jit(solution)/shard_map/ppermute | solution.py:21
  93.5 9.8 %interpolation.1 = (f32[96,128]{1,0:T(8,128)}, f32[96,192]{1,0:T(8,128)}, f32[96,192]{1,0:T(8,128)}, f32[96,512]{1,0:T(8,128)}) custom-call(s32[1]{0:T(128)} %bitcast.info_ref, s32[224]{0:T(256)S(1)} %pad_add_fusion.1.ranks_ref, s32[3,96]{1,0:T(4,128)S(1)} %pad_add_fusion.pivots_ref, f32[128,256]{1,0:T(8,128)S(1)} %get-tuple-element.66.refs_0_, ...), custom_call_target="tpu_custom_call" | custom-call | tf_op jit(solution)/shard_map/interpolation/pallas_call | solution.py:367
  (18 shorter events, 0.2 us)
Async XLA Ops:
  0.6 21.0 %copy-start = (s32[128,128]{1,0:T(8,128)S(1)}, s32[128,128]{1,0:T(8,128)}, u32[]{:S(2)}) copy-start(s32[128,128]{1,0:T(8,128)} %param.11) | copy-start | bytes 196612
  1.7 5.9 %collective-permute-start = (f32[1,96,512]{2,1,0:T(8,128)S(1)}, f32[1,96,512]{2,1,0:T(8,128)S(1)}, u32[]{:S(2)}, u32[]{:S(2)}) collective-permute-start(f32[1,96,512]{2,1,0:T(8,128)S(1)} %get-tuple-element.95), channel_id=1, source_target_pairs={{0,32},{1,9},{2,34},{3,11},{4,36},{5,13},{6,38},{7,15},{8,40},{9,1... | collective-permute-start | bytes 589832 | tf_op jit(solution)/shard_map/ppermute | solution.py:44
  4.3 7.0 %collective-permute-start.2 = (f32[1,96,512]{2,1,0:T(8,128)S(1)}, f32[1,96,512]{2,1,0:T(8,128)S(1)}, u32[]{:S(2)}, u32[]{:S(2)}) collective-permute-start(f32[1,96,512]{2,1,0:T(8,128)S(1)} %get-tuple-element.94), channel_id=1, source_target_pairs={{0,96},{1,25},{2,98},{3,27},{4,100},{5,29},{6,102},{7,31},{8,104},... | collective-permute-start | bytes 589832 | tf_op jit(solution)/shard_map/ppermute | solution.py:44
  7.7 9.1 %collective-permute-start.1 = (f32[2,96,512]{2,1,0:T(8,128)S(1)}, f32[2,96,512]{2,1,0:T(8,128)S(1)}, u32[]{:S(2)}, u32[]{:S(2)}) collective-permute-start(f32[2,96,512]{2,1,0:T(8,128)S(1)} %pad_maximum_fusion.6), channel_id=1, source_target_pairs={{0,96},{1,25},{2,98},{3,27},{4,100},{5,29},{6,102},{7,31},{8,104},... | collective-permute-start | bytes 1179656 | tf_op jit(solution)/shard_map/ppermute | solution.py:44
  11.4 10.2 %copy-start.1 = (s32[32]{0:T(128)S(1)}, s32[32]{0:T(128)}, u32[]{:S(2)}) copy-start(s32[32]{0:T(128)} %param.14) | copy-start | bytes 388
  11.4 10.2 %copy-start.2 = (s32[64]{0:T(128)S(1)}, s32[64]{0:T(128)}, u32[]{:S(2)}) copy-start(s32[64]{0:T(128)} %param.12) | copy-start | bytes 772
  11.4 10.2 %copy-start.3 = (s32[128]{0:T(128)S(1)}, s32[128]{0:T(128)}, u32[]{:S(2)}) copy-start(s32[128]{0:T(128)} %param.10) | copy-start | bytes 1540
  11.4 7.0 %collective-permute-start.3 = (f32[2,96,512]{2,1,0:T(8,128)S(1)}, f32[2,96,512]{2,1,0:T(8,128)S(1)}, u32[]{:S(2)}, u32[]{:S(2)}) collective-permute-start(f32[2,96,512]{2,1,0:T(8,128)S(1)} %pad_maximum_fusion.7), channel_id=1, source_target_pairs={{0,32},{1,9},{2,34},{3,11},{4,36},{5,13},{6,38},{7,15},{8,40},{9,1... | collective-permute-start | bytes 1179656 | tf_op jit(solution)/shard_map/ppermute | solution.py:44
  18.5 11.3 %collective-permute-start.4 = (f32[4,96,512]{2,1,0:T(8,128)S(1)}, f32[4,96,512]{2,1,0:T(8,128)S(1)}, u32[]{:S(2)}, u32[]{:S(2)}) collective-permute-start(f32[4,96,512]{2,1,0:T(8,128)S(1)} %pad_maximum_fusion), channel_id=1, source_target_pairs={{0,8},{1,33},{2,10},{3,35},{4,12},{5,37},{6,14},{7,39},{8,0},{9,41... | collective-permute-start | bytes 2359304 | tf_op jit(solution)/shard_map/ppermute | solution.py:44
  19.7 12.5 %collective-permute-start.5 = (f32[4,96,512]{2,1,0:T(8,128)S(1)}, f32[4,96,512]{2,1,0:T(8,128)}, u32[]{:S(2)}, u32[]{:S(2)}) collective-permute-start(f32[4,96,512]{2,1,0:T(8,128)S(1)} %pad_maximum_fusion.1), channel_id=1, source_target_pairs={{0,24},{1,97},{2,26},{3,99},{4,28},{5,101},{6,30},{7,103},{8,16},{... | collective-permute-start | bytes 2359304 | tf_op jit(solution)/shard_map/ppermute | solution.py:44
  33.7 12.5 %collective-permute-start.6 = (f32[8,96,256]{2,1,0:T(8,128)S(1)}, f32[8,96,256]{2,1,0:T(8,128)}, u32[]{:S(2)}, u32[]{:S(2)}) collective-permute-start(f32[8,96,256]{2,1,0:T(8,128)S(1)} %pad_maximum_fusion.2.refs_0_), channel_id=1, source_target_pairs={{0,24},{1,97},{2,26},{3,99},{4,28},{5,101},{6,30},{7,103},{8,16},{... | collective-permute-start | bytes 2359304 | tf_op jit(solution)/shard_map/ppermute | solution.py:44
  35.7 11.3 %collective-permute-start.7 = (f32[8,96,256]{2,1,0:T(8,128)S(1)}, f32[8,96,256]{2,1,0:T(8,128)}, u32[]{:S(2)}, u32[]{:S(2)}) collective-permute-start(f32[8,96,256]{2,1,0:T(8,128)S(1)} %pad_maximum_fusion.3.refs_1_), channel_id=1, source_target_pairs={{0,8},{1,33},{2,10},{3,35},{4,12},{5,37},{6,14},{7,39},{8,0},{9,41... | collective-permute-start | bytes 2359304 | tf_op jit(solution)/shard_map/ppermute | solution.py:44
  35.8 24.8 %collective-permute-start.13 = (f32[8,96,256]{2,1,0:T(8,128)S(1)}, f32[8,96,256]{2,1,0:T(8,128)}, u32[]{:S(2)}, u32[]{:S(2)}) collective-permute-start(f32[8,96,256]{2,1,0:T(8,128)S(1)} %pad_maximum_fusion.4.refs_0_), channel_id=1, source_target_pairs={{0,24},{1,97},{2,26},{3,99},{4,28},{5,101},{6,30},{7,103},{8,16},{... | collective-permute-start | bytes 2359304 | tf_op jit(solution)/shard_map/ppermute | solution.py:44
  36.9 23.7 %collective-permute-start.14 = (f32[8,96,256]{2,1,0:T(8,128)S(1)}, f32[8,96,256]{2,1,0:T(8,128)}, u32[]{:S(2)}, u32[]{:S(2)}) collective-permute-start(f32[8,96,256]{2,1,0:T(8,128)S(1)} %pad_maximum_fusion.5.refs_1_), channel_id=1, source_target_pairs={{0,8},{1,33},{2,10},{3,35},{4,12},{5,37},{6,14},{7,39},{8,0},{9,41... | collective-permute-start | bytes 2359304 | tf_op jit(solution)/shard_map/ppermute | solution.py:44
  51.5 14.4 %collective-permute-start.8 = (f32[4,128,256]{2,1,0:T(8,128)S(1)}, f32[4,128,256]{2,1,0:T(8,128)S(1)}, u32[]{:S(2)}, u32[]{:S(2)}) collective-permute-start(f32[4,128,256]{2,1,0:T(8,128)S(1)} %get-tuple-element.64), channel_id=1, source_target_pairs={{0,1},{1,0},{2,3},{3,2},{4,5},{5,4},{6,7},{7,6},{8,9},{9,8},{10,11... | collective-permute-start | bytes 1572872 | tf_op jit(solution)/shard_map/ppermute | solution.py:21
  65.1 6.8 %collective-permute-start.15 = (f32[4,128,256]{2,1,0:T(8,128)S(1)}, f32[4,128,256]{2,1,0:T(8,128)S(1)}, u32[]{:S(2)}, u32[]{:S(2)}) collective-permute-start(f32[4,128,256]{2,1,0:T(8,128)S(1)} %get-tuple-element.73), channel_id=1, source_target_pairs={{0,1},{1,0},{2,3},{3,2},{4,5},{5,4},{6,7},{7,6},{8,9},{9,8},{10,11... | collective-permute-start | bytes 1572872 | tf_op jit(solution)/shard_map/ppermute | solution.py:21
  66.0 6.7 %collective-permute-start.9 = (f32[2,128,256]{2,1,0:T(8,128)S(1)}, f32[2,128,256]{2,1,0:T(8,128)S(1)}, u32[]{:S(2)}, u32[]{:S(2)}) collective-permute-start(f32[2,128,256]{2,1,0:T(8,128)S(1)} %slice.82), channel_id=1, source_target_pairs={{0,2},{1,7},{2,0},{3,5},{4,6},{5,3},{6,4},{7,1},{8,10},{9,15},{10,... | collective-permute-start | bytes 786440 | tf_op jit(solution)/shard_map/ppermute | solution.py:179
  72.0 7.9 %collective-permute-start.16 = (f32[2,128,256]{2,1,0:T(8,128)S(1)}, f32[2,128,256]{2,1,0:T(8,128)S(1)}, u32[]{:S(2)}, u32[]{:S(2)}) collective-permute-start(f32[2,128,256]{2,1,0:T(8,128)S(1)} %slice.98), channel_id=1, source_target_pairs={{0,2},{1,7},{2,0},{3,5},{4,6},{5,3},{6,4},{7,1},{8,10},{9,15},{10,... | collective-permute-start | bytes 786440 | tf_op jit(solution)/shard_map/ppermute | solution.py:179
  72.7 7.4 %collective-permute-start.10 = (f32[128,256]{1,0:T(8,128)S(1)}, f32[128,256]{1,0:T(8,128)S(1)}, u32[]{:S(2)}, u32[]{:S(2)}) collective-permute-start(f32[128,256]{1,0:T(8,128)S(1)} %get-tuple-element.92), channel_id=1, source_target_pairs={{0,6},{1,3},{2,4},{3,1},{4,2},{5,7},{6,0},{7,5},{8,14},{9,11},{10,... | collective-permute-start | bytes 393224 | tf_op jit(solution)/shard_map/ppermute | solution.py:179
  80.0 4.2 %collective-permute-start.17 = (f32[128,256]{1,0:T(8,128)S(1)}, f32[128,256]{1,0:T(8,128)S(1)}, u32[]{:S(2)}, u32[]{:S(2)}) collective-permute-start(f32[128,256]{1,0:T(8,128)S(1)} %get-tuple-element.90), channel_id=1, source_target_pairs={{0,6},{1,3},{2,4},{3,1},{4,2},{5,7},{6,0},{7,5},{8,14},{9,11},{10,... | collective-permute-start | bytes 393224 | tf_op jit(solution)/shard_map/ppermute | solution.py:179
  80.9 5.2 %collective-permute-start.11 = (f32[96,256]{1,0:T(8,128)S(1)}, f32[96,256]{1,0:T(8,128)S(1)}, u32[]{:S(2)}, u32[]{:S(2)}) collective-permute-start(f32[96,256]{1,0:T(8,128)S(1)} %get-tuple-element.67.own_ref.refs_1_), channel_id=1, source_target_pairs={{0,1},{1,0},{2,3},{3,2},{4,5},{5,4},{6,7},{7,6},{8,9},{9,8},{10,11... | collective-permute-start | bytes 294920 | tf_op jit(solution)/shard_map/ppermute | solution.py:21
  85.0 2.0 %collective-permute-start.18 = (f32[96,256]{1,0:T(8,128)S(1)}, f32[96,256]{1,0:T(8,128)S(1)}, u32[]{:S(2)}, u32[]{:S(2)}) collective-permute-start(f32[96,256]{1,0:T(8,128)S(1)} %get-tuple-element.75.own_ref.refs_6_), channel_id=1, source_target_pairs={{0,1},{1,0},{2,3},{3,2},{4,5},{5,4},{6,7},{7,6},{8,9},{9,8},{10,11... | collective-permute-start | bytes 294920 | tf_op jit(solution)/shard_map/ppermute | solution.py:21
  86.9 4.5 %collective-permute-start.12 = (f32[96,256]{1,0:T(8,128)S(1)}, f32[96,256]{1,0:T(8,128)S(1)}, u32[]{:S(2)}, u32[]{:S(2)}) collective-permute-start(f32[96,256]{1,0:T(8,128)S(1)} %get-tuple-element.69.refs_3_), channel_id=1, source_target_pairs={{0,2},{1,3},{2,0},{3,1},{4,6},{5,7},{6,4},{7,5},{8,10},{9,11},{10,... | collective-permute-start | bytes 294920 | tf_op jit(solution)/shard_map/ppermute | solution.py:21
  87.9 5.7 %collective-permute-start.19 = (f32[96,256]{1,0:T(8,128)S(1)}, f32[96,256]{1,0:T(8,128)S(1)}, u32[]{:S(2)}, u32[]{:S(2)}) collective-permute-start(f32[96,256]{1,0:T(8,128)S(1)} %get-tuple-element.77.refs_8_), channel_id=1, source_target_pairs={{0,2},{1,3},{2,0},{3,1},{4,6},{5,7},{6,4},{7,5},{8,10},{9,11},{10,... | collective-permute-start | bytes 294920 | tf_op jit(solution)/shard_map/ppermute | solution.py:21

commit v7 on v6

--- a/solution.py
+++ b/solution.py
@@ -75,28 +75,37 @@
     return chunks, ready, frontal
 
 
-def split_kernel(value_ref, high_ref, low_ref):
-    value = value_ref[...]
-    rows = pl.ds(pl.multiple_of(pl.program_id(0) * LEAF, LEAF), LEAF)
-    high = value.astype(jnp.bfloat16)
-    high_ref[rows, :] = high
-    low_ref[rows, :] = (value - high.astype(jnp.float32)).astype(jnp.bfloat16)
+def split_kernel(*refs):
+    values, (high_ref, low_ref) = refs[:-2], refs[-2:]
+    for at, value_ref in enumerate(values):
+        value = value_ref[...]
+        depth = value.shape[0]
+        start = (pl.program_id(0) * len(values) + at) * depth
+        rows = pl.ds(pl.multiple_of(start, depth), depth)
+        high = value.astype(jnp.bfloat16)
+        high_ref[rows, :] = high
+        low_ref[rows, :] = (value - high.astype(jnp.float32)).astype(jnp.bfloat16)
 
 
 def split(value):
     rows, order = value.shape
+    depth, streams = LEAF // 2, 4
+    blocks = [
+        pl.BlockSpec((depth, order), lambda i, at=at: (i * streams + at, 0)) for at in range(streams)
+    ]
+    value = pltpu.with_memory_space_constraint(value, pltpu.HBM)
     return pl.pallas_call(
         split_kernel,
-        out_shape=[pltpu.VMEM(value.shape, jnp.bfloat16)] * 2,
-        grid=(rows // LEAF,),
-        in_specs=[pl.BlockSpec((LEAF, order), lambda i: (i, 0))],
+        out_shape=[pltpu.VMEM((rows, order), jnp.bfloat16)] * 2,
+        grid=(rows // depth // streams,),
+        in_specs=blocks,
         out_specs=[pl.BlockSpec(memory_space=pltpu.VMEM)] * 2,
-        compiler_params=pltpu.CompilerParams(vmem_limit_bytes=6 * 2**20),
+        compiler_params=pltpu.CompilerParams(vmem_limit_bytes=10 * 2**20),
         cost_estimate=pl.CostEstimate(
             flops=4 * rows * order, bytes_accessed=8 * rows * order, transcendentals=0
         ),
         name="split",
-    )(pltpu.with_memory_space_constraint(value, pltpu.HBM))
+    )(*[value] * streams)
 
 
 def convert(place_ref, pieces, high, low):
@@ -155,12 +164,13 @@
     )(place, *halves, *arrays)
 
 
-def product_other(halves, pieces, place):
+def product_other(halves, pieces, place, last):
     leaves, _, leaf, order = halves[0].shape
     width = pieces[0].shape[-1]
     outs = [jax.ShapeDtypeStruct((leaves, leaf, width), jnp.float32)]
     outs += [jax.ShapeDtypeStruct((order, width), jnp.bfloat16)] * 2
-    return product(other_kernel, place, halves, pieces, outs, 1, "product_other")
+    cost = 6 * leaves * leaf * order * width if last else 1
+    return product(other_kernel, place, halves, pieces, outs, cost, "product_other")
 
 
 def product_own(halves, sketch, place, last):
@@ -181,7 +191,8 @@
 
 def sum_over_x(core_sum):
     kept = from_x(core_sum[2:], 0)
-    return [core_sum[0], kept[0], from_x(core_sum[1] + kept[1], 1)]
+    second = core_sum[1] + kept[1]
+    return [core_sum[0], kept[0], from_x(second, 1)], second
 
 
 BLOCK = 8
@@ -396,19 +407,18 @@
     chunks, (ranks, pivots), frontal = gather_parts(sketch, frontal, tables, prepare)
     info = jnp.stack([leaf_index]).astype(jnp.int32)
     halves = [part.reshape(SIDE, 2, LEAF, -1) for part in split(frontal)]
-    core_sums, own = [], ()
+    groups, core_sum, ready = [], None, ()
     for chunk, pieces in enumerate(chunks):
-        place, own = lax.optimization_barrier((place, own))
-        other, *parts = product_other(halves, pieces, place)
+        last = chunk == len(chunks) - 1
+        if core_sum is not None:
+            place, core_sum = lax.optimization_barrier((place, core_sum))
+            group, ready = sum_over_x(core_sum)
+            groups.append(group)
+        other, *parts = product_other(halves, pieces, place, last)
         received = from_partner(other, "col", 0)
-        last = chunk == len(chunks) - 1
-        if chunk > 0:
-            core_sums[-1] = own + core_sums[-1]
-            place, core_sums = lax.optimization_barrier((place, core_sums))
-        own = product_own(halves, parts, place, last)
-        core_sums.append(received)
-    core_sums[-1] = own + core_sums[-1]
-    groups = [sum_over_x(core_sum) for core_sum in core_sums]
+        place, ready = lax.optimization_barrier((place, ready))
+        core_sum = product_own(halves, parts, place, last) + received
+    groups.append(sum_over_x(core_sum)[0])
     arrays = []
     for group, width in zip(groups, WIDTHS):
         skeleton_shape, pair_shape = (KMAX, width), (2 * KMAX, width)

time: 104 us -> 104 us (level)
  starting transfers between devices: 28.9 us -> 32.5 us
  Pallas kernels: 35.6 us -> 34.1 us
  waiting for transfers between devices: 33.7 us -> 32.5 us
    ppermute x6, starting transfers between devices: 10 us -> 12.7 us  [from_partner(): return lax.ppermute(value, axis, pairs)]
    ppermute x4, waiting for transfers between devices: 9.96 us -> 7.39 us  [from_x(): return lax.ppermute(value, 'col', pairs)]
    pallas_call x1, Pallas kernels: 7.35 us -> 5.76 us  [split(): pl.pallas_call(split_kernel, out_shape=[pltpu.VMEM((rows, order), jnp.bfl...]
    ppermute x10, waiting for transfers between devices: 19.6 us -> 21.2 us  [from_row(): return lax.ppermute(value, ('row', 'col'), pairs)]
  transfers between devices with their start and end apart: 20 -> 20, of which waited for: 12 -> 11; matrix products, arithmetic and copies ran while one was open for 1% -> 1% of each run, Pallas kernels for 25% -> 23%
where the time goes in v7:
time: 104 us
  Pallas kernels  34.1 us (33%)
  starting transfers between devices  32.5 us (31%)
  waiting for transfers between devices  32.5 us (31%)
  local copies, waits for them, and re-layouts  3.27 us (3%)
    ppermute x10, waiting for transfers between devices, from_row(): return lax.ppermute(value, ('row', 'col'), pairs)  21.2 us
    ppermute x10, starting transfers between devices, from_row(): return lax.ppermute(value, ('row', 'col'), pairs)  15.4 us
    pallas_call x4, Pallas kernels, product(): pl.pallas_call(kernel, out_shape=outs, in_specs=[pl.BlockSpec(memory_spac...  15.3 us
    pallas_call x5, Pallas kernels, call(): pl.pallas_call(kernel, out_shape=[jax.ShapeDtypeStruct(shape, jnp.float32...  13 us
    ppermute x6, starting transfers between devices, from_partner(): return lax.ppermute(value, axis, pairs)  12.7 us
    ppermute x4, waiting for transfers between devices, from_x(): return lax.ppermute(value, 'col', pairs)  7.39 us
    pallas_call x1, Pallas kernels, split(): pl.pallas_call(split_kernel, out_shape=[pltpu.VMEM((rows, order), jnp.bfl...  5.76 us
    ppermute x4, starting transfers between devices, from_x(): return lax.ppermute(value, 'col', pairs)  4.4 us
  transfers between devices with their start and end apart: 20, of which 11 were waited for; matrix products, arithmetic and copies ran while one was open for 1% of the time, Pallas kernels for 23%

profile of v7, /device:TPU:1, one launch (start us, length us, event | category | flops | bytes accessed | tf_op | source)
XLA Modules:
  0.0 104.2 jit_solution(1736075834599177506)
XLA Ops:
  0.6 0.0 copy-start
  0.6 1.1 %slice_bitcast_fusion = (f32[1,96,512]{2,1,0:T(8,128)S(1)}, f32[1,96,512]{2,1,0:T(8,128)S(1)}) fusion(f32[192,512]{1,0:T(8,128)} %param.9), kind=kLoop, calls=%fused_computation.8 | loop fusion | bytes 786432 | tf_op jit(solution)/shard_map/broadcast_in_dim | solution.py:56
  1.7 2.5 %collective-permute-start = (f32[1,96,512]{2,1,0:T(8,128)S(1)}, f32[1,96,512]{2,1,0:T(8,128)S(1)}, u32[]{:S(2)}, u32[]{:S(2)}) collective-permute-start(f32[1,96,512]{2,1,0:T(8,128)S(1)} %get-tuple-element.93), channel_id=1, source_target_pairs={{0,32},{1,9},{2,34},{3,11},{4,36},{5,13},{6,38},{7,15},{8,40},{9,1... | collective-permute-start | bytes 589832 | tf_op jit(solution)/shard_map/ppermute | solution.py:44
  4.3 2.2 %collective-permute-start.2 = (f32[1,96,512]{2,1,0:T(8,128)S(1)}, f32[1,96,512]{2,1,0:T(8,128)S(1)}, u32[]{:S(2)}, u32[]{:S(2)}) collective-permute-start(f32[1,96,512]{2,1,0:T(8,128)S(1)} %get-tuple-element.92), channel_id=1, source_target_pairs={{0,96},{1,25},{2,98},{3,27},{4,100},{5,29},{6,102},{7,31},{8,104},... | collective-permute-start | bytes 589832 | tf_op jit(solution)/shard_map/ppermute | solution.py:44
  6.5 1.1 %collective-permute-done = f32[1,96,512]{2,1,0:T(8,128)S(1)} collective-permute-done((f32[1,96,512]{2,1,0:T(8,128)S(1)}, f32[1,96,512]{2,1,0:T(8,128)S(1)}, u32[]{:S(2)}, u32[]{:S(2)}) %collective-permute-start) | collective-permute-done | bytes 196640 | tf_op jit(solution)/shard_map/ppermute | solution.py:44
  7.7 3.7 %collective-permute-start.1 = (f32[2,96,512]{2,1,0:T(8,128)S(1)}, f32[2,96,512]{2,1,0:T(8,128)S(1)}, u32[]{:S(2)}, u32[]{:S(2)}) collective-permute-start(f32[2,96,512]{2,1,0:T(8,128)S(1)} %pad_maximum_fusion.6), channel_id=1, source_target_pairs={{0,96},{1,25},{2,98},{3,27},{4,100},{5,29},{6,102},{7,31},{8,104},... | collective-permute-start | bytes 1179656 | tf_op jit(solution)/shard_map/ppermute | solution.py:44
  11.4 0.0 copy-start.1
  11.4 0.0 copy-start.2
  11.4 0.0 copy-start.3
  11.4 0.1 collective-permute-start.3
  11.5 5.3 %collective-permute-done.1 = f32[2,96,512]{2,1,0:T(8,128)S(1)} collective-permute-done((f32[2,96,512]{2,1,0:T(8,128)S(1)}, f32[2,96,512]{2,1,0:T(8,128)S(1)}, u32[]{:S(2)}, u32[]{:S(2)}) %collective-permute-start.1) | collective-permute-done | bytes 393248 | tf_op jit(solution)/shard_map/ppermute | solution.py:44
  16.8 1.6 %collective-permute-done.3 = f32[2,96,512]{2,1,0:T(8,128)S(1)} collective-permute-done((f32[2,96,512]{2,1,0:T(8,128)S(1)}, f32[2,96,512]{2,1,0:T(8,128)S(1)}, u32[]{:S(2)}, u32[]{:S(2)}) %collective-permute-start.3) | collective-permute-done | bytes 393248 | tf_op jit(solution)/shard_map/ppermute | solution.py:44
  18.4 0.1 pad_maximum_fusion
  18.4 1.2 %collective-permute-start.4 = (f32[4,96,512]{2,1,0:T(8,128)S(1)}, f32[4,96,512]{2,1,0:T(8,128)S(1)}, u32[]{:S(2)}, u32[]{:S(2)}) collective-permute-start(f32[4,96,512]{2,1,0:T(8,128)S(1)} %pad_maximum_fusion), channel_id=1, source_target_pairs={{0,8},{1,33},{2,10},{3,35},{4,12},{5,37},{6,14},{7,39},{8,0},{9,41... | collective-permute-start | bytes 2359304 | tf_op jit(solution)/shard_map/ppermute | solution.py:44
  19.6 0.1 pad_maximum_fusion.1
  19.7 1.9 %collective-permute-start.5 = (f32[4,96,512]{2,1,0:T(8,128)S(1)}, f32[4,96,512]{2,1,0:T(8,128)}, u32[]{:S(2)}, u32[]{:S(2)}) collective-permute-start(f32[4,96,512]{2,1,0:T(8,128)S(1)} %pad_maximum_fusion.1), channel_id=1, source_target_pairs={{0,24},{1,97},{2,26},{3,99},{4,28},{5,101},{6,30},{7,103},{8,16},{... | collective-permute-start | bytes 2359304 | tf_op jit(solution)/shard_map/ppermute | solution.py:44
  21.6 0.1 pad_add_fusion.1.ranks_ref
  21.7 0.7 constant_dynamic-slice_fusion
  22.4 7.4 %collective-permute-done.4 = f32[4,96,512]{2,1,0:T(8,128)S(1)} collective-permute-done((f32[4,96,512]{2,1,0:T(8,128)S(1)}, f32[4,96,512]{2,1,0:T(8,128)S(1)}, u32[]{:S(2)}, u32[]{:S(2)}) %collective-permute-start.4) | collective-permute-done | bytes 786464 | tf_op jit(solution)/shard_map/ppermute | solution.py:44
  29.8 2.5 %collective-permute-done.5 = f32[4,96,512]{2,1,0:T(8,128)} collective-permute-done((f32[4,96,512]{2,1,0:T(8,128)S(1)}, f32[4,96,512]{2,1,0:T(8,128)}, u32[]{:S(2)}, u32[]{:S(2)}) %collective-permute-start.5) | collective-permute-done | bytes 786464 | tf_op jit(solution)/shard_map/ppermute | solution.py:44
  32.2 0.1 fusion.5
  32.3 0.1 fusion.4
  32.4 1.2 %fusion.3 = (f32[4,96,256]{2,1,0:T(8,128)S(1)}, f32[4,96,256]{2,1,0:T(8,128)S(1)}) fusion(f32[4,96,512]{2,1,0:T(8,128)} %collective-permute-done.5), kind=kLoop, calls=%fused_computation.25 | loop fusion | bytes 1572864 | tf_op jit(solution)/shard_map/slice | solution.py:70
  33.6 0.1 fusion.2
  33.6 0.1 pad_maximum_fusion.2.refs_0_
  33.7 1.9 %collective-permute-start.6 = (f32[8,96,256]{2,1,0:T(8,128)S(1)}, f32[8,96,256]{2,1,0:T(8,128)}, u32[]{:S(2)}, u32[]{:S(2)}) collective-permute-start(f32[8,96,256]{2,1,0:T(8,128)S(1)} %pad_maximum_fusion.2.refs_0_), channel_id=1, source_target_pairs={{0,24},{1,97},{2,26},{3,99},{4,28},{5,101},{6,30},{7,103},{8,16},{... | collective-permute-start | bytes 2359304 | tf_op jit(solution)/shard_map/ppermute | solution.py:44
  35.6 0.1 pad_maximum_fusion.3.refs_1_
  35.6 0.1 collective-permute-start.7
  35.7 0.1 pad_maximum_fusion.4.refs_0_
  35.8 1.0 collective-permute-start.13
  36.8 0.1 pad_maximum_fusion.5.refs_1_
  36.9 0.9 collective-permute-start.14
  37.8 0.1 pad_add_fusion.2.place_ref
  37.9 5.8 %split.1 = (bf16[1024,3072]{1,0:T(8,128)(2,1)S(1)}, bf16[1024,3072]{1,0:T(8,128)(2,1)S(1)}) custom-call(f32[1024,3072]{1,0:T(8,128)} %refs_3_, f32[1024,3072]{1,0:T(8,128)} %refs_3_, f32[1024,3072]{1,0:T(8,128)} %refs_3_, f32[1024,3072]{1,0:T(8,128)} %refs_3_), custom_call_target="tpu_custom_call" | custom-call | flops 12582912 | bytes 25165824 | tf_op jit(solution)/shard_map/split/pallas_call | solution.py:97
  43.6 2.6 %collective-permute-done.6.refs_2_ = f32[8,96,256]{2,1,0:T(8,128)} collective-permute-done((f32[8,96,256]{2,1,0:T(8,128)S(1)}, f32[8,96,256]{2,1,0:T(8,128)}, u32[]{:S(2)}, u32[]{:S(2)}) %collective-permute-start.6) | collective-permute-done | bytes 786464 | tf_op jit(solution)/shard_map/ppermute | solution.py:44
  46.2 0.7 collective-permute-done.7.refs_3_
  47.0 4.5 %product_other.2 = (f32[4,128,256]{2,1,0:T(8,128)S(1)}, bf16[3072,256]{1,0:T(8,128)(2,1)S(1)}, bf16[3072,256]{1,0:T(8,128)(2,1)S(1)}) custom-call(s32[3]{0:T(128)S(1)} %pad_add_fusion.2.place_ref, bf16[4,2,128,3072]{3,2,1,0:T(8,128)(2,1)S(1)} %bitcast.27, bf16[4,2,128,3072]{3,2,1,0:T(8,128)(2,1)S(1)} %bitcast.31, ...), custom_call_target="tpu_custom_call" | custom-call | flops 1 | tf_op jit(solution)/shard_map/product_other/pallas_call | solution.py:155
  51.4 6.0 %collective-permute-start.8 = (f32[4,128,256]{2,1,0:T(8,128)S(1)}, f32[4,128,256]{2,1,0:T(8,128)S(1)}, u32[]{:S(2)}, u32[]{:S(2)}) collective-permute-start(f32[4,128,256]{2,1,0:T(8,128)S(1)} %get-tuple-element.61), channel_id=1, source_target_pairs={{0,1},{1,0},{2,3},{3,2},{4,5},{5,4},{6,7},{7,6},{8,9},{9,8},{10,11... | collective-permute-start | bytes 1572872 | tf_op jit(solution)/shard_map/ppermute | solution.py:21
  57.4 3.2 %product_own.2 = f32[4,128,256]{2,1,0:T(8,128)S(1)} custom-call(s32[3]{0:T(128)S(1)} %pad_add_fusion.2.place_ref, bf16[4,2,128,3072]{3,2,1,0:T(8,128)(2,1)S(1)} %bitcast.28, bf16[4,2,128,3072]{3,2,1,0:T(8,128)(2,1)S(1)} %bitcast.32, bf16[3072,256]{1,0:T(8,128)(2,1)S(1)} %get-tuple-element.59.high, bf16[3072,256]{1,0:T(8,128)(2,1)S(1)} %get-tuple-element.60.low), custom_call_target="tpu_custom_call" | custom-call | flops 1 | tf_op jit(solution)/shard_map/product_own/pallas_call | solution.py:155
  60.6 0.0 collective-permute-done.8
  60.6 0.1 add.45
  60.7 2.6 %collective-permute-start.9 = (f32[2,128,256]{2,1,0:T(8,128)S(1)}, f32[2,128,256]{2,1,0:T(8,128)S(1)}, u32[]{:S(2)}, u32[]{:S(2)}) collective-permute-start(f32[2,128,256]{2,1,0:T(8,128)S(1)} %slice.82), channel_id=1, source_target_pairs={{0,2},{1,7},{2,0},{3,5},{4,6},{5,3},{6,4},{7,1},{8,10},{9,15},{10,... | collective-permute-start | bytes 786440 | tf_op jit(solution)/shard_map/ppermute | solution.py:189
  63.3 0.0 collective-permute-done.13.refs_2_
  63.3 0.0 collective-permute-done.14.refs_3_
  63.3 4.5 %product_other.3 = (f32[4,128,256]{2,1,0:T(8,128)S(1)}, bf16[3072,256]{1,0:T(8,128)(2,1)S(1)}, bf16[3072,256]{1,0:T(8,128)(2,1)S(1)}) custom-call(s32[3]{0:T(128)S(1)} %pad_add_fusion.2.place_ref, bf16[4,2,128,3072]{3,2,1,0:T(8,128)(2,1)S(1)} %bitcast.29, bf16[4,2,128,3072]{3,2,1,0:T(8,128)(2,1)S(1)} %bitcast.33, ...), custom_call_target="tpu_custom_call" | custom-call | flops 2415919104 | bytes 6039797 | tf_op jit(solution)/shard_map/product_other/pallas_call | solution.py:155
  67.8 0.3 collective-permute-start.15
  68.1 3.2 %product_own.3 = f32[4,128,256]{2,1,0:T(8,128)S(1)} custom-call(s32[3]{0:T(128)S(1)} %pad_add_fusion.2.place_ref, bf16[4,2,128,3072]{3,2,1,0:T(8,128)(2,1)S(1)} %bitcast.30, bf16[4,2,128,3072]{3,2,1,0:T(8,128)(2,1)S(1)} %bitcast.34, bf16[3072,256]{1,0:T(8,128)(2,1)S(1)} %get-tuple-element.69.high, bf16[3072,256]{1,0:T(8,128)(2,1)S(1)} %get-tuple-element.70.low), custom_call_target="tpu_custom_call" | custom-call | flops 2415919104 | bytes 6039797 | tf_op jit(solution)/shard_map/product_own/pallas_call | solution.py:155
  71.3 0.1 add.48
  71.4 1.8 %collective-permute-start.16 = (f32[2,128,256]{2,1,0:T(8,128)S(1)}, f32[2,128,256]{2,1,0:T(8,128)S(1)}, u32[]{:S(2)}, u32[]{:S(2)}) collective-permute-start(f32[2,128,256]{2,1,0:T(8,128)S(1)} %slice.98), channel_id=1, source_target_pairs={{0,2},{1,7},{2,0},{3,5},{4,6},{5,3},{6,4},{7,1},{8,10},{9,15},{10,... | collective-permute-start | bytes 786440 | tf_op jit(solution)/shard_map/ppermute | solution.py:189
  73.2 6.2 %collective-permute-done.16 = f32[2,128,256]{2,1,0:T(8,128)S(1)} collective-permute-done((f32[2,128,256]{2,1,0:T(8,128)S(1)}, f32[2,128,256]{2,1,0:T(8,128)S(1)}, u32[]{:S(2)}, u32[]{:S(2)}) %collective-permute-start.16) | collective-permute-done | bytes 262176 | tf_op jit(solution)/shard_map/ppermute | solution.py:189
  79.4 0.1 collective-permute-start.17
  79.5 0.8 leaf_rows.2
  80.4 1.8 %collective-permute-start.11 = (f32[96,256]{1,0:T(8,128)S(1)}, f32[96,256]{1,0:T(8,128)S(1)}, u32[]{:S(2)}, u32[]{:S(2)}) collective-permute-start(f32[96,256]{1,0:T(8,128)S(1)} %get-tuple-element.64.own_ref.refs_1_), channel_id=1, source_target_pairs={{0,1},{1,0},{2,3},{3,2},{4,5},{5,4},{6,7},{7,6},{8,9},{9,8},{10,11... | collective-permute-start | bytes 294920 | tf_op jit(solution)/shard_map/ppermute | solution.py:21
  82.2 1.1 %collective-permute-done.17.refs_2_ = f32[128,256]{1,0:T(8,128)S(1)} collective-permute-done((f32[128,256]{1,0:T(8,128)S(1)}, f32[128,256]{1,0:T(8,128)S(1)}, u32[]{:S(2)}, u32[]{:S(2)}) %collective-permute-start.17) | collective-permute-done | bytes 131104 | tf_op jit(solution)/shard_map/ppermute | solution.py:189
  83.3 0.8 leaf_rows.3
  84.1 2.8 %collective-permute-start.18 = (f32[96,256]{1,0:T(8,128)S(1)}, f32[96,256]{1,0:T(8,128)S(1)}, u32[]{:S(2)}, u32[]{:S(2)}) collective-permute-start(f32[96,256]{1,0:T(8,128)S(1)} %get-tuple-element.73.own_ref.refs_6_), channel_id=1, source_target_pairs={{0,1},{1,0},{2,3},{3,2},{4,5},{5,4},{6,7},{7,6},{8,9},{9,8},{10,11... | collective-permute-start | bytes 294920 | tf_op jit(solution)/shard_map/ppermute | solution.py:21
  86.9 0.8 mid_rows.2
  87.8 0.1 collective-permute-start.12
  87.9 0.0 collective-permute-done.18.other_ref
  87.9 0.8 mid_rows.3
  88.7 1.7 %collective-permute-start.19 = (f32[96,256]{1,0:T(8,128)S(1)}, f32[96,256]{1,0:T(8,128)S(1)}, u32[]{:S(2)}, u32[]{:S(2)}) collective-permute-start(f32[96,256]{1,0:T(8,128)S(1)} %get-tuple-element.75.refs_8_), channel_id=1, source_target_pairs={{0,2},{1,3},{2,0},{3,1},{4,6},{5,7},{6,4},{7,5},{8,10},{9,11},{10,... | collective-permute-start | bytes 294920 | tf_op jit(solution)/shard_map/ppermute | solution.py:21
  90.4 1.8 %collective-permute-done.12.refs_4_ = f32[96,256]{1,0:T(8,128)S(1)} collective-permute-done((f32[96,256]{1,0:T(8,128)S(1)}, f32[96,256]{1,0:T(8,128)S(1)}, u32[]{:S(2)}, u32[]{:S(2)}) %collective-permute-start.12) | collective-permute-done | bytes 98336 | tf_op jit(solution)/shard_map/ppermute | solution.py:21
  92.3 2.1 %collective-permute-done.19.refs_9_ = f32[96,256]{1,0:T(8,128)S(1)} collective-permute-done((f32[96,256]{1,0:T(8,128)S(1)}, f32[96,256]{1,0:T(8,128)S(1)}, u32[]{:S(2)}, u32[]{:S(2)}) %collective-permute-start.19) | collective-permute-done | bytes 98336 | tf_op jit(solution)/shard_map/ppermute | solution.py:21
  94.4 9.8 %interpolation.1 = (f32[96,128]{1,0:T(8,128)}, f32[96,192]{1,0:T(8,128)}, f32[96,192]{1,0:T(8,128)}, f32[96,512]{1,0:T(8,128)}) custom-call(s32[1]{0:T(128)} %bitcast.info_ref, s32[224]{0:T(256)S(1)} %pad_add_fusion.1.ranks_ref, s32[3,96]{1,0:T(4,128)S(1)} %pad_add_fusion.pivots_ref, f32[128,256]{1,0:T(8,128)S(1)} %get-tuple-element.63.refs_0_, ...), custom_call_target="tpu_custom_call" | custom-call | tf_op jit(solution)/shard_map/interpolation/pallas_call | solution.py:378
  (18 shorter events, 0.2 us)
Async XLA Ops:
  0.6 20.9 %copy-start = (s32[128,128]{1,0:T(8,128)S(1)}, s32[128,128]{1,0:T(8,128)}, u32[]{:S(2)}) copy-start(s32[128,128]{1,0:T(8,128)} %param.11) | copy-start | bytes 196612
  1.7 5.9 %collective-permute-start = (f32[1,96,512]{2,1,0:T(8,128)S(1)}, f32[1,96,512]{2,1,0:T(8,128)S(1)}, u32[]{:S(2)}, u32[]{:S(2)}) collective-permute-start(f32[1,96,512]{2,1,0:T(8,128)S(1)} %get-tuple-element.93), channel_id=1, source_target_pairs={{0,32},{1,9},{2,34},{3,11},{4,36},{5,13},{6,38},{7,15},{8,40},{9,1... | collective-permute-start | bytes 589832 | tf_op jit(solution)/shard_map/ppermute | solution.py:44
  4.3 7.0 %collective-permute-start.2 = (f32[1,96,512]{2,1,0:T(8,128)S(1)}, f32[1,96,512]{2,1,0:T(8,128)S(1)}, u32[]{:S(2)}, u32[]{:S(2)}) collective-permute-start(f32[1,96,512]{2,1,0:T(8,128)S(1)} %get-tuple-element.92), channel_id=1, source_target_pairs={{0,96},{1,25},{2,98},{3,27},{4,100},{5,29},{6,102},{7,31},{8,104},... | collective-permute-start | bytes 589832 | tf_op jit(solution)/shard_map/ppermute | solution.py:44
  7.7 9.1 %collective-permute-start.1 = (f32[2,96,512]{2,1,0:T(8,128)S(1)}, f32[2,96,512]{2,1,0:T(8,128)S(1)}, u32[]{:S(2)}, u32[]{:S(2)}) collective-permute-start(f32[2,96,512]{2,1,0:T(8,128)S(1)} %pad_maximum_fusion.6), channel_id=1, source_target_pairs={{0,96},{1,25},{2,98},{3,27},{4,100},{5,29},{6,102},{7,31},{8,104},... | collective-permute-start | bytes 1179656 | tf_op jit(solution)/shard_map/ppermute | solution.py:44
  11.4 10.2 %copy-start.1 = (s32[32]{0:T(128)S(1)}, s32[32]{0:T(128)}, u32[]{:S(2)}) copy-start(s32[32]{0:T(128)} %param.14) | copy-start | bytes 388
  11.4 10.2 %copy-start.2 = (s32[64]{0:T(128)S(1)}, s32[64]{0:T(128)}, u32[]{:S(2)}) copy-start(s32[64]{0:T(128)} %param.12) | copy-start | bytes 772
  11.4 10.2 %copy-start.3 = (s32[128]{0:T(128)S(1)}, s32[128]{0:T(128)}, u32[]{:S(2)}) copy-start(s32[128]{0:T(128)} %param.10) | copy-start | bytes 1540
  11.4 7.0 %collective-permute-start.3 = (f32[2,96,512]{2,1,0:T(8,128)S(1)}, f32[2,96,512]{2,1,0:T(8,128)S(1)}, u32[]{:S(2)}, u32[]{:S(2)}) collective-permute-start(f32[2,96,512]{2,1,0:T(8,128)S(1)} %pad_maximum_fusion.7), channel_id=1, source_target_pairs={{0,32},{1,9},{2,34},{3,11},{4,36},{5,13},{6,38},{7,15},{8,40},{9,1... | collective-permute-start | bytes 1179656 | tf_op jit(solution)/shard_map/ppermute | solution.py:44
  18.4 11.3 %collective-permute-start.4 = (f32[4,96,512]{2,1,0:T(8,128)S(1)}, f32[4,96,512]{2,1,0:T(8,128)S(1)}, u32[]{:S(2)}, u32[]{:S(2)}) collective-permute-start(f32[4,96,512]{2,1,0:T(8,128)S(1)} %pad_maximum_fusion), channel_id=1, source_target_pairs={{0,8},{1,33},{2,10},{3,35},{4,12},{5,37},{6,14},{7,39},{8,0},{9,41... | collective-permute-start | bytes 2359304 | tf_op jit(solution)/shard_map/ppermute | solution.py:44
  19.7 12.5 %collective-permute-start.5 = (f32[4,96,512]{2,1,0:T(8,128)S(1)}, f32[4,96,512]{2,1,0:T(8,128)}, u32[]{:S(2)}, u32[]{:S(2)}) collective-permute-start(f32[4,96,512]{2,1,0:T(8,128)S(1)} %pad_maximum_fusion.1), channel_id=1, source_target_pairs={{0,24},{1,97},{2,26},{3,99},{4,28},{5,101},{6,30},{7,103},{8,16},{... | collective-permute-start | bytes 2359304 | tf_op jit(solution)/shard_map/ppermute | solution.py:44
  33.7 12.5 %collective-permute-start.6 = (f32[8,96,256]{2,1,0:T(8,128)S(1)}, f32[8,96,256]{2,1,0:T(8,128)}, u32[]{:S(2)}, u32[]{:S(2)}) collective-permute-start(f32[8,96,256]{2,1,0:T(8,128)S(1)} %pad_maximum_fusion.2.refs_0_), channel_id=1, source_target_pairs={{0,24},{1,97},{2,26},{3,99},{4,28},{5,101},{6,30},{7,103},{8,16},{... | collective-permute-start | bytes 2359304 | tf_op jit(solution)/shard_map/ppermute | solution.py:44
  35.6 11.3 %collective-permute-start.7 = (f32[8,96,256]{2,1,0:T(8,128)S(1)}, f32[8,96,256]{2,1,0:T(8,128)}, u32[]{:S(2)}, u32[]{:S(2)}) collective-permute-start(f32[8,96,256]{2,1,0:T(8,128)S(1)} %pad_maximum_fusion.3.refs_1_), channel_id=1, source_target_pairs={{0,8},{1,33},{2,10},{3,35},{4,12},{5,37},{6,14},{7,39},{8,0},{9,41... | collective-permute-start | bytes 2359304 | tf_op jit(solution)/shard_map/ppermute | solution.py:44
  35.8 27.5 %collective-permute-start.13 = (f32[8,96,256]{2,1,0:T(8,128)S(1)}, f32[8,96,256]{2,1,0:T(8,128)}, u32[]{:S(2)}, u32[]{:S(2)}) collective-permute-start(f32[8,96,256]{2,1,0:T(8,128)S(1)} %pad_maximum_fusion.4.refs_0_), channel_id=1, source_target_pairs={{0,24},{1,97},{2,26},{3,99},{4,28},{5,101},{6,30},{7,103},{8,16},{... | collective-permute-start | bytes 2359304 | tf_op jit(solution)/shard_map/ppermute | solution.py:44
  36.9 26.4 %collective-permute-start.14 = (f32[8,96,256]{2,1,0:T(8,128)S(1)}, f32[8,96,256]{2,1,0:T(8,128)}, u32[]{:S(2)}, u32[]{:S(2)}) collective-permute-start(f32[8,96,256]{2,1,0:T(8,128)S(1)} %pad_maximum_fusion.5.refs_1_), channel_id=1, source_target_pairs={{0,8},{1,33},{2,10},{3,35},{4,12},{5,37},{6,14},{7,39},{8,0},{9,41... | collective-permute-start | bytes 2359304 | tf_op jit(solution)/shard_map/ppermute | solution.py:44
  51.4 9.2 %collective-permute-start.8 = (f32[4,128,256]{2,1,0:T(8,128)S(1)}, f32[4,128,256]{2,1,0:T(8,128)S(1)}, u32[]{:S(2)}, u32[]{:S(2)}) collective-permute-start(f32[4,128,256]{2,1,0:T(8,128)S(1)} %get-tuple-element.61), channel_id=1, source_target_pairs={{0,1},{1,0},{2,3},{3,2},{4,5},{5,4},{6,7},{7,6},{8,9},{9,8},{10,11... | collective-permute-start | bytes 1572872 | tf_op jit(solution)/shard_map/ppermute | solution.py:21
  60.7 7.3 %collective-permute-start.9 = (f32[2,128,256]{2,1,0:T(8,128)S(1)}, f32[2,128,256]{2,1,0:T(8,128)S(1)}, u32[]{:S(2)}, u32[]{:S(2)}) collective-permute-start(f32[2,128,256]{2,1,0:T(8,128)S(1)} %slice.82), channel_id=1, source_target_pairs={{0,2},{1,7},{2,0},{3,5},{4,6},{5,3},{6,4},{7,1},{8,10},{9,15},{10,... | collective-permute-start | bytes 786440 | tf_op jit(solution)/shard_map/ppermute | solution.py:189
  67.8 3.5 %collective-permute-start.15 = (f32[4,128,256]{2,1,0:T(8,128)S(1)}, f32[4,128,256]{2,1,0:T(8,128)S(1)}, u32[]{:S(2)}, u32[]{:S(2)}) collective-permute-start(f32[4,128,256]{2,1,0:T(8,128)S(1)} %get-tuple-element.71), channel_id=1, source_target_pairs={{0,1},{1,0},{2,3},{3,2},{4,5},{5,4},{6,7},{7,6},{8,9},{9,8},{10,11... | collective-permute-start | bytes 1572872 | tf_op jit(solution)/shard_map/ppermute | solution.py:21
  71.4 8.0 %collective-permute-start.16 = (f32[2,128,256]{2,1,0:T(8,128)S(1)}, f32[2,128,256]{2,1,0:T(8,128)S(1)}, u32[]{:S(2)}, u32[]{:S(2)}) collective-permute-start(f32[2,128,256]{2,1,0:T(8,128)S(1)} %slice.98), channel_id=1, source_target_pairs={{0,2},{1,7},{2,0},{3,5},{4,6},{5,3},{6,4},{7,1},{8,10},{9,15},{10,... | collective-permute-start | bytes 786440 | tf_op jit(solution)/shard_map/ppermute | solution.py:189
  73.2 6.4 %collective-permute-start.10 = (f32[128,256]{1,0:T(8,128)S(1)}, f32[128,256]{1,0:T(8,128)S(1)}, u32[]{:S(2)}, u32[]{:S(2)}) collective-permute-start(f32[128,256]{1,0:T(8,128)S(1)} %get-tuple-element.90), channel_id=1, source_target_pairs={{0,6},{1,3},{2,4},{3,1},{4,2},{5,7},{6,0},{7,5},{8,14},{9,11},{10,... | collective-permute-start | bytes 393224 | tf_op jit(solution)/shard_map/ppermute | solution.py:189
  79.4 3.9 %collective-permute-start.17 = (f32[128,256]{1,0:T(8,128)S(1)}, f32[128,256]{1,0:T(8,128)S(1)}, u32[]{:S(2)}, u32[]{:S(2)}) collective-permute-start(f32[128,256]{1,0:T(8,128)S(1)} %get-tuple-element.88), channel_id=1, source_target_pairs={{0,6},{1,3},{2,4},{3,1},{4,2},{5,7},{6,0},{7,5},{8,14},{9,11},{10,... | collective-permute-start | bytes 393224 | tf_op jit(solution)/shard_map/ppermute | solution.py:189
  80.4 6.6 %collective-permute-start.11 = (f32[96,256]{1,0:T(8,128)S(1)}, f32[96,256]{1,0:T(8,128)S(1)}, u32[]{:S(2)}, u32[]{:S(2)}) collective-permute-start(f32[96,256]{1,0:T(8,128)S(1)} %get-tuple-element.64.own_ref.refs_1_), channel_id=1, source_target_pairs={{0,1},{1,0},{2,3},{3,2},{4,5},{5,4},{6,7},{7,6},{8,9},{9,8},{10,11... | collective-permute-start | bytes 294920 | tf_op jit(solution)/shard_map/ppermute | solution.py:21
  84.1 3.7 %collective-permute-start.18 = (f32[96,256]{1,0:T(8,128)S(1)}, f32[96,256]{1,0:T(8,128)S(1)}, u32[]{:S(2)}, u32[]{:S(2)}) collective-permute-start(f32[96,256]{1,0:T(8,128)S(1)} %get-tuple-element.73.own_ref.refs_6_), channel_id=1, source_target_pairs={{0,1},{1,0},{2,3},{3,2},{4,5},{5,4},{6,7},{7,6},{8,9},{9,8},{10,11... | collective-permute-start | bytes 294920 | tf_op jit(solution)/shard_map/ppermute | solution.py:21
  87.8 4.5 %collective-permute-start.12 = (f32[96,256]{1,0:T(8,128)S(1)}, f32[96,256]{1,0:T(8,128)S(1)}, u32[]{:S(2)}, u32[]{:S(2)}) collective-permute-start(f32[96,256]{1,0:T(8,128)S(1)} %get-tuple-element.66.refs_3_), channel_id=1, source_target_pairs={{0,2},{1,3},{2,0},{3,1},{4,6},{5,7},{6,4},{7,5},{8,10},{9,11},{10,... | collective-permute-start | bytes 294920 | tf_op jit(solution)/shard_map/ppermute | solution.py:21
  88.7 5.7 %collective-permute-start.19 = (f32[96,256]{1,0:T(8,128)S(1)}, f32[96,256]{1,0:T(8,128)S(1)}, u32[]{:S(2)}, u32[]{:S(2)}) collective-permute-start(f32[96,256]{1,0:T(8,128)S(1)} %get-tuple-element.75.refs_8_), channel_id=1, source_target_pairs={{0,2},{1,3},{2,0},{3,1},{4,6},{5,7},{6,4},{7,5},{8,10},{9,11},{10,... | collective-permute-start | bytes 294920 | tf_op jit(solution)/shard_map/ppermute | solution.py:21

commit v8 on v7

--- a/solution.py
+++ b/solution.py
@@ -326,64 +326,80 @@
     select_rows(rows_ref, pivots_ref, 1, rank_of(info_ref, ranks_ref, 1), skeleton_ref, 0)
 
 
-def top_kernel(info_ref, ranks_ref, pivots_ref, *refs):
-    chunks = len(WIDTHS)
-    groups = [refs[5 * chunk : 5 * chunk + 5] for chunk in range(chunks)]
-    leaf_out, mid_out, top_out, rows_out = refs[5 * chunks : 5 * chunks + 4]
-    scratch = refs[5 * chunks + 4 :]
-    tops, chosen, (rows_scratch, new_scratch) = (
-        scratch[:chunks], scratch[chunks : 2 * chunks], scratch[2 * chunks :]
-    )
-    own_at = pl.multiple_of((info_ref[0] // 2 % 2) * KMAX, KMAX)
-    other_at = pl.multiple_of((1 - info_ref[0] // 2 % 2) * KMAX, KMAX)
-    start = 0
-    for group, top, skeleton in zip(groups, tops, chosen):
-        top[pl.ds(own_at, KMAX), :] = group[3][...]
-        top[pl.ds(other_at, KMAX), :] = group[4][...]
-        select_rows(top, pivots_ref, 2, rank_of(info_ref, ranks_ref, 2), skeleton, 0)
-        width = skeleton.shape[-1]
-        rows_out[:, start : start + width] = skeleton[...]
-        start += width
-    row_ids = lax.broadcasted_iota(jnp.int32, (KMAX, KMAX), 0)
-    column_ids = lax.broadcasted_iota(jnp.int32, (KMAX, KMAX), 1)
-    dot = functools.partial(
-        lax.dot_general,
-        dimension_numbers=(((1,), (1,)), ((), ())),
+def dot_rows(left, right):
+    return lax.dot_general(
+        left,
+        right,
+        (((1,), (1,)), ((), ())),
         precision=lax.Precision.HIGHEST,
         preferred_element_type=jnp.float32,
     )
-    levels = (
-        ([group[0] for group in groups], [group[1] for group in groups]),
-        ([group[2] for group in groups], [group[3] for group in groups]),
-        (tops, chosen),
+
+
+def lower_kernel(*refs):
+    arrays, outs = refs[: 4 * len(WIDTHS)], refs[4 * len(WIDTHS) :]
+    for node in range(2):
+        pairs = [arrays[4 * chunk + 2 * node :][:2] for chunk in range(len(WIDTHS))]
+        grams = [dot_rows(skeleton[...], skeleton[...]) for _, skeleton in pairs]
+        crosses = [dot_rows(rows[...], skeleton[...]) for rows, skeleton in pairs]
+        outs[2 * node][...] = functools.reduce(jnp.add, grams)
+        outs[2 * node + 1][...] = functools.reduce(jnp.add, crosses)
+
+
+def select_top(info_ref, ranks_ref, pivots_ref, own_ref, cousin_ref, rows, skeleton):
+    own_at = pl.multiple_of((info_ref[0] // 2 % 2) * KMAX, KMAX)
+    other_at = pl.multiple_of((1 - info_ref[0] // 2 % 2) * KMAX, KMAX)
+    rows[pl.ds(own_at, KMAX), :] = own_ref[...]
+    rows[pl.ds(other_at, KMAX), :] = cousin_ref[...]
+    select_rows(rows, pivots_ref, 2, rank_of(info_ref, ranks_ref, 2), skeleton, 0)
+    chosen = skeleton[...]
+    return dot_rows(chosen, chosen), dot_rows(rows[...], chosen)
+
+
+def upper_kernel(
+    info_ref, ranks_ref, pivots_ref, own_ref, cousin_ref, skeleton_ref, gram_ref, cross_ref, rows
+):
+    gram_ref[...], cross_ref[...] = select_top(
+        info_ref, ranks_ref, pivots_ref, own_ref, cousin_ref, rows, skeleton_ref
     )
-    grams, crosses = [], []
-    for node, (rows, skeletons) in enumerate(levels):
-        gram = functools.reduce(jnp.add, [dot(part[...], part[...]) for part in skeletons])
-        cross = functools.reduce(
-            jnp.add, [dot(row[...], part[...]) for row, part in zip(rows, skeletons)]
-        )
+
+
+def top_kernel(
+    info_ref, ranks_ref, pivots_ref, leaf_gram, leaf_cross, mid_gram, mid_cross, first_skeleton,
+    top_gram, top_cross, own_ref, cousin_ref, leaf_out, mid_out, top_out, rows_out, rows, skeleton,
+    rows_scratch, new_scratch,
+):
+    gram, cross = select_top(
+        info_ref, ranks_ref, pivots_ref, own_ref, cousin_ref, rows, skeleton
+    )
+    rows_out[:, : WIDTHS[0]] = first_skeleton[...]
+    rows_out[:, WIDTHS[0] :] = skeleton[...]
+    row_ids = lax.broadcasted_iota(jnp.int32, (KMAX, KMAX), 0)
+    column_ids = lax.broadcasted_iota(jnp.int32, (KMAX, KMAX), 1)
+    grams = []
+    sums = (leaf_gram[...], mid_gram[...], top_gram[...] + gram)
+    for node, total in enumerate(sums):
         empty = (row_ids == column_ids) & (row_ids >= rank_of(info_ref, ranks_ref, node))
-        grams.append(gram * (1.0 / SAMPLES) + jnp.where(empty, 1.0, 0.0))
-        crosses.append(cross * (1.0 / SAMPLES))
+        grams.append(total * (1.0 / SAMPLES) + jnp.where(empty, 1.0, 0.0))
     inverses = invert_all(grams, rows_scratch, new_scratch)
-    for inverse, cross, out in zip(inverses, crosses, (leaf_out, mid_out, top_out)):
-        out[...] = dot(inverse, cross)
+    crosses = (leaf_cross[...], mid_cross[...], top_cross[...] + cross)
+    for inverse, total, out in zip(inverses, crosses, (leaf_out, mid_out, top_out)):
+        out[...] = dot_rows(inverse, total * (1.0 / SAMPLES))
 
 
 def vmem_call(kernel, outs, scratch, name):
     in_vmem = pl.BlockSpec(memory_space=pltpu.VMEM)
 
-    def call(info, ranks, pivots, *arrays):
+    def call(tables, *arrays):
         return pl.pallas_call(
             kernel,
             out_shape=[jax.ShapeDtypeStruct(shape, jnp.float32) for shape in outs],
-            in_specs=[pl.BlockSpec(memory_space=pltpu.SMEM)] * 3 + [in_vmem] * len(arrays),
+            in_specs=[pl.BlockSpec(memory_space=pltpu.SMEM)] * len(tables) + [in_vmem] * len(arrays),
             out_specs=[in_vmem] * len(outs),
             scratch_shapes=scratch,
             compiler_params=pltpu.CompilerParams(vmem_limit_bytes=6 * 2**20),
             name=name,
-        )(info, ranks, pivots, *arrays)
+        )(*tables, *arrays)
 
     return call
 
@@ -418,26 +434,38 @@
         received = from_partner(other, "col", 0)
         place, ready = lax.optimization_barrier((place, ready))
         core_sum = product_own(halves, parts, place, last) + received
+    core_sum, groups = lax.optimization_barrier((core_sum, groups))
     groups.append(sum_over_x(core_sum)[0])
-    arrays = []
+    tables = (info, ranks, pivots)
+    arrays, tops = [], []
     for group, width in zip(groups, WIDTHS):
         skeleton_shape, pair_shape = (KMAX, width), (2 * KMAX, width)
         rows, skeleton = vmem_call(
             leaf_kernel, [(LEAF, width), skeleton_shape], [], "leaf_rows"
-        )(info, ranks, pivots, *group)
+        )(tables, *group)
         mid_rows, mid_skeleton = vmem_call(
             mid_kernel, [pair_shape, skeleton_shape], [], "mid_rows"
-        )(info, ranks, pivots, skeleton, from_partner(skeleton, "col", 0))
-        arrays += [rows, skeleton, mid_rows, mid_skeleton, from_partner(mid_skeleton, "col", 1)]
-    scratch = [pltpu.VMEM((2 * KMAX, width), jnp.float32) for width in WIDTHS]
-    scratch += [pltpu.VMEM((KMAX, width), jnp.float32) for width in WIDTHS]
+        )(tables, skeleton, from_partner(skeleton, "col", 0))
+        arrays += [rows, skeleton, mid_rows, mid_skeleton]
+        tops.append((mid_skeleton, from_partner(mid_skeleton, "col", 1)))
+    square, leaf_cross, pair_cross = (KMAX, KMAX), (LEAF, KMAX), (2 * KMAX, KMAX)
+    lower = vmem_call(
+        lower_kernel, [square, leaf_cross, square, pair_cross], [], "lower_sums"
+    )((), *arrays)
+    first = vmem_call(
+        upper_kernel,
+        [(KMAX, WIDTHS[0]), square, pair_cross],
+        [pltpu.VMEM((2 * KMAX, WIDTHS[0]), jnp.float32)],
+        "upper_sums",
+    )(tables, *tops[0])
+    scratch = [pltpu.VMEM((rows, WIDTHS[1]), jnp.float32) for rows in (2 * KMAX, KMAX)]
     scratch += [pltpu.VMEM((2, BLOCK * BLOCK, 128), jnp.float32)] * 2
     outs = vmem_call(
         top_kernel,
         [(KMAX, LEAF), (KMAX, 2 * KMAX), (KMAX, 2 * KMAX), (KMAX, SAMPLES)],
         scratch,
         "interpolation",
-    )(info, ranks, pivots, *arrays)
+    )(tables, *lower, *first, *tops[1])
     return tuple(out[None] for out in outs)
 
 

time: 104 us -> 105 us (level)
  waiting for transfers between devices: 32.5 us -> 28.3 us
  starting transfers between devices: 32.5 us -> 36.2 us
  Pallas kernels: 34.1 us -> 35.4 us
    ppermute x6, starting transfers between devices: 12.7 us -> 16.3 us  [from_partner(): return lax.ppermute(value, axis, pairs)]
    ppermute x4, waiting for transfers between devices: 7.39 us -> 5.28 us  [from_x(): return lax.ppermute(value, 'col', pairs)]
    ppermute x6, waiting for transfers between devices: 3.95 us -> 1.85 us  [from_partner(): return lax.ppermute(value, axis, pairs)]
    pallas_call x5 -> x7, Pallas kernels: 13 us -> 14.3 us  [call(): pl.pallas_call(kernel, out_shape=[jax.ShapeDtypeStruct(shape, jnp.float32...]
  transfers between devices with their start and end apart: 20 -> 20, of which waited for: 11 -> 10; matrix products, arithmetic and copies ran while one was open for 1% -> 1% of each run, Pallas kernels for 23% -> 25%
where the time goes in v8:
time: 105 us
  starting transfers between devices  36.2 us (34%)
  Pallas kernels  35.4 us (34%)
  waiting for transfers between devices  28.3 us (27%)
  local copies, waits for them, and re-layouts  3.27 us (3%)
    ppermute x10, waiting for transfers between devices, from_row(): return lax.ppermute(value, ('row', 'col'), pairs)  21.2 us
    ppermute x6, starting transfers between devices, from_partner(): return lax.ppermute(value, axis, pairs)  16.3 us
    ppermute x10, starting transfers between devices, from_row(): return lax.ppermute(value, ('row', 'col'), pairs)  15.4 us
    pallas_call x4, Pallas kernels, product(): pl.pallas_call(kernel, out_shape=outs, in_specs=[pl.BlockSpec(memory_spac...  15.3 us
    pallas_call x7, Pallas kernels, call(): pl.pallas_call(kernel, out_shape=[jax.ShapeDtypeStruct(shape, jnp.float32...  14.3 us
    pallas_call x1, Pallas kernels, split(): pl.pallas_call(split_kernel, out_shape=[pltpu.VMEM((rows, order), jnp.bfl...  5.76 us
    ppermute x4, waiting for transfers between devices, from_x(): return lax.ppermute(value, 'col', pairs)  5.28 us
    ppermute x4, starting transfers between devices, from_x(): return lax.ppermute(value, 'col', pairs)  4.51 us
  transfers between devices with their start and end apart: 20, of which 10 were waited for; matrix products, arithmetic and copies ran while one was open for 1% of the time, Pallas kernels for 25%

profile of v8, /device:TPU:1, one launch (start us, length us, event | category | flops | bytes accessed | tf_op | source)
XLA Modules:
  0.0 104.9 jit_solution(14392672945550720053)
XLA Ops:
  0.6 0.0 copy-start
  0.6 1.1 %slice_bitcast_fusion = (f32[1,96,512]{2,1,0:T(8,128)S(1)}, f32[1,96,512]{2,1,0:T(8,128)S(1)}) fusion(f32[192,512]{1,0:T(8,128)} %param.9), kind=kLoop, calls=%fused_computation.8 | loop fusion | bytes 786432 | tf_op jit(solution)/shard_map/broadcast_in_dim | solution.py:56
  1.7 2.5 %collective-permute-start = (f32[1,96,512]{2,1,0:T(8,128)S(1)}, f32[1,96,512]{2,1,0:T(8,128)S(1)}, u32[]{:S(2)}, u32[]{:S(2)}) collective-permute-start(f32[1,96,512]{2,1,0:T(8,128)S(1)} %get-tuple-element.115), channel_id=1, source_target_pairs={{0,32},{1,9},{2,34},{3,11},{4,36},{5,13},{6,38},{7,15},{8,40},{9,1... | collective-permute-start | bytes 589832 | tf_op jit(solution)/shard_map/ppermute | solution.py:44
  4.3 2.2 %collective-permute-start.2 = (f32[1,96,512]{2,1,0:T(8,128)S(1)}, f32[1,96,512]{2,1,0:T(8,128)S(1)}, u32[]{:S(2)}, u32[]{:S(2)}) collective-permute-start(f32[1,96,512]{2,1,0:T(8,128)S(1)} %get-tuple-element.114), channel_id=1, source_target_pairs={{0,96},{1,25},{2,98},{3,27},{4,100},{5,29},{6,102},{7,31},{8,104},... | collective-permute-start | bytes 589832 | tf_op jit(solution)/shard_map/ppermute | solution.py:44
  6.5 1.1 %collective-permute-done = f32[1,96,512]{2,1,0:T(8,128)S(1)} collective-permute-done((f32[1,96,512]{2,1,0:T(8,128)S(1)}, f32[1,96,512]{2,1,0:T(8,128)S(1)}, u32[]{:S(2)}, u32[]{:S(2)}) %collective-permute-start) | collective-permute-done | bytes 196640 | tf_op jit(solution)/shard_map/ppermute | solution.py:44
  7.7 3.7 %collective-permute-start.1 = (f32[2,96,512]{2,1,0:T(8,128)S(1)}, f32[2,96,512]{2,1,0:T(8,128)S(1)}, u32[]{:S(2)}, u32[]{:S(2)}) collective-permute-start(f32[2,96,512]{2,1,0:T(8,128)S(1)} %pad_maximum_fusion.6), channel_id=1, source_target_pairs={{0,96},{1,25},{2,98},{3,27},{4,100},{5,29},{6,102},{7,31},{8,104},... | collective-permute-start | bytes 1179656 | tf_op jit(solution)/shard_map/ppermute | solution.py:44
  11.3 0.0 collective-permute-done.2
  11.4 0.0 copy-start.1
  11.4 0.0 copy-start.2
  11.4 0.0 copy-start.3
  11.4 0.1 collective-permute-start.3
  11.5 5.3 %collective-permute-done.1 = f32[2,96,512]{2,1,0:T(8,128)S(1)} collective-permute-done((f32[2,96,512]{2,1,0:T(8,128)S(1)}, f32[2,96,512]{2,1,0:T(8,128)S(1)}, u32[]{:S(2)}, u32[]{:S(2)}) %collective-permute-start.1) | collective-permute-done | bytes 393248 | tf_op jit(solution)/shard_map/ppermute | solution.py:44
  16.8 1.6 %collective-permute-done.3 = f32[2,96,512]{2,1,0:T(8,128)S(1)} collective-permute-done((f32[2,96,512]{2,1,0:T(8,128)S(1)}, f32[2,96,512]{2,1,0:T(8,128)S(1)}, u32[]{:S(2)}, u32[]{:S(2)}) %collective-permute-start.3) | collective-permute-done | bytes 393248 | tf_op jit(solution)/shard_map/ppermute | solution.py:44
  18.4 0.1 pad_maximum_fusion
  18.4 1.2 %collective-permute-start.4 = (f32[4,96,512]{2,1,0:T(8,128)S(1)}, f32[4,96,512]{2,1,0:T(8,128)S(1)}, u32[]{:S(2)}, u32[]{:S(2)}) collective-permute-start(f32[4,96,512]{2,1,0:T(8,128)S(1)} %pad_maximum_fusion), channel_id=1, source_target_pairs={{0,8},{1,33},{2,10},{3,35},{4,12},{5,37},{6,14},{7,39},{8,0},{9,41... | collective-permute-start | bytes 2359304 | tf_op jit(solution)/shard_map/ppermute | solution.py:44
  19.6 0.1 pad_maximum_fusion.1
  19.7 1.9 %collective-permute-start.5 = (f32[4,96,512]{2,1,0:T(8,128)S(1)}, f32[4,96,512]{2,1,0:T(8,128)}, u32[]{:S(2)}, u32[]{:S(2)}) collective-permute-start(f32[4,96,512]{2,1,0:T(8,128)S(1)} %pad_maximum_fusion.1), channel_id=1, source_target_pairs={{0,24},{1,97},{2,26},{3,99},{4,28},{5,101},{6,30},{7,103},{8,16},{... | collective-permute-start | bytes 2359304 | tf_op jit(solution)/shard_map/ppermute | solution.py:44
  21.6 0.1 pad_add_fusion.1.ranks_ref
  21.7 0.7 constant_dynamic-slice_fusion
  22.4 7.4 %collective-permute-done.4 = f32[4,96,512]{2,1,0:T(8,128)S(1)} collective-permute-done((f32[4,96,512]{2,1,0:T(8,128)S(1)}, f32[4,96,512]{2,1,0:T(8,128)S(1)}, u32[]{:S(2)}, u32[]{:S(2)}) %collective-permute-start.4) | collective-permute-done | bytes 786464 | tf_op jit(solution)/shard_map/ppermute | solution.py:44
  29.8 2.5 %collective-permute-done.5 = f32[4,96,512]{2,1,0:T(8,128)} collective-permute-done((f32[4,96,512]{2,1,0:T(8,128)S(1)}, f32[4,96,512]{2,1,0:T(8,128)}, u32[]{:S(2)}, u32[]{:S(2)}) %collective-permute-start.5) | collective-permute-done | bytes 786464 | tf_op jit(solution)/shard_map/ppermute | solution.py:44
  32.2 0.1 fusion.5
  32.3 0.1 fusion.4
  32.4 1.2 %fusion.3 = (f32[4,96,256]{2,1,0:T(8,128)S(1)}, f32[4,96,256]{2,1,0:T(8,128)S(1)}) fusion(f32[4,96,512]{2,1,0:T(8,128)} %collective-permute-done.5), kind=kLoop, calls=%fused_computation.25 | loop fusion | bytes 1572864 | tf_op jit(solution)/shard_map/slice | solution.py:70
  33.6 0.1 fusion.2
  33.6 0.1 pad_maximum_fusion.2.refs_0_
  33.7 1.9 %collective-permute-start.6 = (f32[8,96,256]{2,1,0:T(8,128)S(1)}, f32[8,96,256]{2,1,0:T(8,128)}, u32[]{:S(2)}, u32[]{:S(2)}) collective-permute-start(f32[8,96,256]{2,1,0:T(8,128)S(1)} %pad_maximum_fusion.2.refs_0_), channel_id=1, source_target_pairs={{0,24},{1,97},{2,26},{3,99},{4,28},{5,101},{6,30},{7,103},{8,16},{... | collective-permute-start | bytes 2359304 | tf_op jit(solution)/shard_map/ppermute | solution.py:44
  35.6 0.1 pad_maximum_fusion.3.refs_1_
  35.6 0.1 collective-permute-start.7
  35.7 0.1 pad_maximum_fusion.4.refs_0_
  35.8 1.0 collective-permute-start.10
  36.8 0.1 pad_maximum_fusion.5.refs_1_
  36.9 0.9 collective-permute-start.11
  37.8 0.1 pad_add_fusion.2.place_ref
  37.9 5.8 %split.1 = (bf16[1024,3072]{1,0:T(8,128)(2,1)S(1)}, bf16[1024,3072]{1,0:T(8,128)(2,1)S(1)}) custom-call(f32[1024,3072]{1,0:T(8,128)} %refs_3_, f32[1024,3072]{1,0:T(8,128)} %refs_3_, f32[1024,3072]{1,0:T(8,128)} %refs_3_, f32[1024,3072]{1,0:T(8,128)} %refs_3_), custom_call_target="tpu_custom_call" | custom-call | flops 12582912 | bytes 25165824 | tf_op jit(solution)/shard_map/split/pallas_call | solution.py:97
  43.6 2.6 %collective-permute-done.6.refs_2_ = f32[8,96,256]{2,1,0:T(8,128)} collective-permute-done((f32[8,96,256]{2,1,0:T(8,128)S(1)}, f32[8,96,256]{2,1,0:T(8,128)}, u32[]{:S(2)}, u32[]{:S(2)}) %collective-permute-start.6) | collective-permute-done | bytes 786464 | tf_op jit(solution)/shard_map/ppermute | solution.py:44
  46.2 0.7 collective-permute-done.7.refs_3_
  47.0 4.5 %product_other.2 = (f32[4,128,256]{2,1,0:T(8,128)S(1)}, bf16[3072,256]{1,0:T(8,128)(2,1)S(1)}, bf16[3072,256]{1,0:T(8,128)(2,1)S(1)}) custom-call(s32[3]{0:T(128)S(1)} %pad_add_fusion.2.place_ref, bf16[4,2,128,3072]{3,2,1,0:T(8,128)(2,1)S(1)} %bitcast.27, bf16[4,2,128,3072]{3,2,1,0:T(8,128)(2,1)S(1)} %bitcast.31, ...), custom_call_target="tpu_custom_call" | custom-call | flops 1 | tf_op jit(solution)/shard_map/product_other/pallas_call | solution.py:155
  51.4 6.0 %collective-permute-start.8 = (f32[4,128,256]{2,1,0:T(8,128)S(1)}, f32[4,128,256]{2,1,0:T(8,128)S(1)}, u32[]{:S(2)}, u32[]{:S(2)}) collective-permute-start(f32[4,128,256]{2,1,0:T(8,128)S(1)} %get-tuple-element.72), channel_id=1, source_target_pairs={{0,1},{1,0},{2,3},{3,2},{4,5},{5,4},{6,7},{7,6},{8,9},{9,8},{10,11... | collective-permute-start | bytes 1572872 | tf_op jit(solution)/shard_map/ppermute | solution.py:21
  57.4 3.2 %product_own.2 = f32[4,128,256]{2,1,0:T(8,128)S(1)} custom-call(s32[3]{0:T(128)S(1)} %pad_add_fusion.2.place_ref, bf16[4,2,128,3072]{3,2,1,0:T(8,128)(2,1)S(1)} %bitcast.28, bf16[4,2,128,3072]{3,2,1,0:T(8,128)(2,1)S(1)} %bitcast.32, bf16[3072,256]{1,0:T(8,128)(2,1)S(1)} %get-tuple-element.70.high, bf16[3072,256]{1,0:T(8,128)(2,1)S(1)} %get-tuple-element.71.low), custom_call_target="tpu_custom_call" | custom-call | flops 1 | tf_op jit(solution)/shard_map/product_own/pallas_call | solution.py:155
  60.6 0.1 add.45
  60.7 2.6 %collective-permute-start.9 = (f32[2,128,256]{2,1,0:T(8,128)S(1)}, f32[2,128,256]{2,1,0:T(8,128)S(1)}, u32[]{:S(2)}, u32[]{:S(2)}) collective-permute-start(f32[2,128,256]{2,1,0:T(8,128)S(1)} %slice.82), channel_id=1, source_target_pairs={{0,2},{1,7},{2,0},{3,5},{4,6},{5,3},{6,4},{7,1},{8,10},{9,15},{10,... | collective-permute-start | bytes 786440 | tf_op jit(solution)/shard_map/ppermute | solution.py:189
  63.3 4.5 %product_other.3 = (f32[4,128,256]{2,1,0:T(8,128)S(1)}, bf16[3072,256]{1,0:T(8,128)(2,1)S(1)}, bf16[3072,256]{1,0:T(8,128)(2,1)S(1)}) custom-call(s32[3]{0:T(128)S(1)} %pad_add_fusion.2.place_ref, bf16[4,2,128,3072]{3,2,1,0:T(8,128)(2,1)S(1)} %bitcast.29, bf16[4,2,128,3072]{3,2,1,0:T(8,128)(2,1)S(1)} %bitcast.33, ...), custom_call_target="tpu_custom_call" | custom-call | flops 2415919104 | bytes 6039797 | tf_op jit(solution)/shard_map/product_other/pallas_call | solution.py:155
  67.8 0.3 collective-permute-start.12
  68.1 0.1 collective-permute-start.13
  68.2 3.2 %product_own.3 = f32[4,128,256]{2,1,0:T(8,128)S(1)} custom-call(s32[3]{0:T(128)S(1)} %pad_add_fusion.2.place_ref, bf16[4,2,128,3072]{3,2,1,0:T(8,128)(2,1)S(1)} %bitcast.30, bf16[4,2,128,3072]{3,2,1,0:T(8,128)(2,1)S(1)} %bitcast.34, bf16[3072,256]{1,0:T(8,128)(2,1)S(1)} %get-tuple-element.76.high, bf16[3072,256]{1,0:T(8,128)(2,1)S(1)} %get-tuple-element.77.low), custom_call_target="tpu_custom_call" | custom-call | flops 2415919104 | bytes 6039797 | tf_op jit(solution)/shard_map/product_own/pallas_call | solution.py:155
  71.4 0.1 add.48
  71.5 0.5 collective-permute-done.13.refs_2_
  72.0 1.8 %collective-permute-start.15 = (f32[2,128,256]{2,1,0:T(8,128)S(1)}, f32[2,128,256]{2,1,0:T(8,128)S(1)}, u32[]{:S(2)}, u32[]{:S(2)}) collective-permute-start(f32[2,128,256]{2,1,0:T(8,128)S(1)} %slice.91), channel_id=1, source_target_pairs={{0,2},{1,7},{2,0},{3,5},{4,6},{5,3},{6,4},{7,1},{8,10},{9,15},{10,... | collective-permute-start | bytes 786440 | tf_op jit(solution)/shard_map/ppermute | solution.py:189
  73.8 4.8 %collective-permute-done.15 = f32[2,128,256]{2,1,0:T(8,128)S(1)} collective-permute-done((f32[2,128,256]{2,1,0:T(8,128)S(1)}, f32[2,128,256]{2,1,0:T(8,128)S(1)}, u32[]{:S(2)}, u32[]{:S(2)}) %collective-permute-start.15) | collective-permute-done | bytes 262176 | tf_op jit(solution)/shard_map/ppermute | solution.py:189
  78.6 0.1 collective-permute-start.16
  78.7 0.8 leaf_rows.2
  79.5 4.3 %collective-permute-start.14 = (f32[96,256]{1,0:T(8,128)S(1)}, f32[96,256]{1,0:T(8,128)S(1)}, u32[]{:S(2)}, u32[]{:S(2)}) collective-permute-start(f32[96,256]{1,0:T(8,128)S(1)} %get-tuple-element.83.own_ref.refs_1_), channel_id=1, source_target_pairs={{0,1},{1,0},{2,3},{3,2},{4,5},{5,4},{6,7},{7,6},{8,9},{9,8},{10,11... | collective-permute-start | bytes 294920 | tf_op jit(solution)/shard_map/ppermute | solution.py:21
  83.7 0.8 leaf_rows.3
  84.6 3.9 %collective-permute-start.17 = (f32[96,256]{1,0:T(8,128)S(1)}, f32[96,256]{1,0:T(8,128)S(1)}, u32[]{:S(2)}, u32[]{:S(2)}) collective-permute-start(f32[96,256]{1,0:T(8,128)S(1)} %get-tuple-element.88.own_ref.refs_5_), channel_id=1, source_target_pairs={{0,1},{1,0},{2,3},{3,2},{4,5},{5,4},{6,7},{7,6},{8,9},{9,8},{10,11... | collective-permute-start | bytes 294920 | tf_op jit(solution)/shard_map/ppermute | solution.py:21
  88.5 0.8 mid_rows.2
  89.3 0.1 collective-permute-start.18
  89.4 0.0 collective-permute-done.17.other_ref
  89.4 0.8 mid_rows.3
  90.3 1.7 %collective-permute-start.19 = (f32[96,256]{1,0:T(8,128)S(1)}, f32[96,256]{1,0:T(8,128)S(1)}, u32[]{:S(2)}, u32[]{:S(2)}) collective-permute-start(f32[96,256]{1,0:T(8,128)S(1)} %get-tuple-element.90.refs_7_.own_ref), channel_id=1, source_target_pairs={{0,2},{1,3},{2,0},{3,1},{4,6},{5,7},{6,4},{7,5},{8,10},{9,11},{10,... | collective-permute-start | bytes 294920 | tf_op jit(solution)/shard_map/ppermute | solution.py:21
  92.0 1.8 %collective-permute-done.18.cousin_ref = f32[96,256]{1,0:T(8,128)S(1)} collective-permute-done((f32[96,256]{1,0:T(8,128)S(1)}, f32[96,256]{1,0:T(8,128)S(1)}, u32[]{:S(2)}, u32[]{:S(2)}) %collective-permute-start.18) | collective-permute-done | bytes 98336 | tf_op jit(solution)/shard_map/ppermute | solution.py:21
  93.8 1.2 %upper_sums.1 = (f32[96,256]{1,0:T(8,128)S(1)}, f32[96,96]{1,0:T(8,128)S(1)}, f32[192,96]{1,0:T(8,128)S(1)}) custom-call(s32[1]{0:T(128)} %bitcast.info_ref, s32[224]{0:T(256)S(1)} %pad_add_fusion.1.ranks_ref, s32[3,96]{1,0:T(4,128)S(1)} %pad_add_fusion.pivots_ref, f32[96,256]{1,0:T(8,128)S(1)} %get-tuple-element.85.refs_3_.own_ref, ...), custom_call_target="tpu_custom_call" | custom-call | tf_op jit(solution)/shard_map/upper_sums/pallas_call | solution.py:394
  95.0 1.0 lower_sums.1
  96.0 8.9 %interpolation.1 = (f32[96,128]{1,0:T(8,128)}, f32[96,192]{1,0:T(8,128)}, f32[96,192]{1,0:T(8,128)}, f32[96,512]{1,0:T(8,128)}) custom-call(s32[1]{0:T(128)} %bitcast.info_ref, s32[224]{0:T(256)S(1)} %pad_add_fusion.1.ranks_ref, s32[3,96]{1,0:T(4,128)S(1)} %pad_add_fusion.pivots_ref, f32[96,96]{1,0:T(8,128)S(1)} %get-tuple-element.91.leaf_gram, ...), custom_call_target="tpu_custom_call" | custom-call | tf_op jit(solution)/shard_map/interpolation/pallas_call | solution.py:394
  (20 shorter events, 0.2 us)
Async XLA Ops:
  0.6 20.9 %copy-start = (s32[128,128]{1,0:T(8,128)S(1)}, s32[128,128]{1,0:T(8,128)}, u32[]{:S(2)}) copy-start(s32[128,128]{1,0:T(8,128)} %param.11) | copy-start | bytes 196612
  1.7 5.9 %collective-permute-start = (f32[1,96,512]{2,1,0:T(8,128)S(1)}, f32[1,96,512]{2,1,0:T(8,128)S(1)}, u32[]{:S(2)}, u32[]{:S(2)}) collective-permute-start(f32[1,96,512]{2,1,0:T(8,128)S(1)} %get-tuple-element.115), channel_id=1, source_target_pairs={{0,32},{1,9},{2,34},{3,11},{4,36},{5,13},{6,38},{7,15},{8,40},{9,1... | collective-permute-start | bytes 589832 | tf_op jit(solution)/shard_map/ppermute | solution.py:44
  4.3 7.0 %collective-permute-start.2 = (f32[1,96,512]{2,1,0:T(8,128)S(1)}, f32[1,96,512]{2,1,0:T(8,128)S(1)}, u32[]{:S(2)}, u32[]{:S(2)}) collective-permute-start(f32[1,96,512]{2,1,0:T(8,128)S(1)} %get-tuple-element.114), channel_id=1, source_target_pairs={{0,96},{1,25},{2,98},{3,27},{4,100},{5,29},{6,102},{7,31},{8,104},... | collective-permute-start | bytes 589832 | tf_op jit(solution)/shard_map/ppermute | solution.py:44
  7.7 9.1 %collective-permute-start.1 = (f32[2,96,512]{2,1,0:T(8,128)S(1)}, f32[2,96,512]{2,1,0:T(8,128)S(1)}, u32[]{:S(2)}, u32[]{:S(2)}) collective-permute-start(f32[2,96,512]{2,1,0:T(8,128)S(1)} %pad_maximum_fusion.6), channel_id=1, source_target_pairs={{0,96},{1,25},{2,98},{3,27},{4,100},{5,29},{6,102},{7,31},{8,104},... | collective-permute-start | bytes 1179656 | tf_op jit(solution)/shard_map/ppermute | solution.py:44
  11.4 10.2 %copy-start.1 = (s32[32]{0:T(128)S(1)}, s32[32]{0:T(128)}, u32[]{:S(2)}) copy-start(s32[32]{0:T(128)} %param.14) | copy-start | bytes 388
  11.4 10.2 %copy-start.2 = (s32[64]{0:T(128)S(1)}, s32[64]{0:T(128)}, u32[]{:S(2)}) copy-start(s32[64]{0:T(128)} %param.12) | copy-start | bytes 772
  11.4 10.2 %copy-start.3 = (s32[128]{0:T(128)S(1)}, s32[128]{0:T(128)}, u32[]{:S(2)}) copy-start(s32[128]{0:T(128)} %param.10) | copy-start | bytes 1540
  11.4 7.0 %collective-permute-start.3 = (f32[2,96,512]{2,1,0:T(8,128)S(1)}, f32[2,96,512]{2,1,0:T(8,128)S(1)}, u32[]{:S(2)}, u32[]{:S(2)}) collective-permute-start(f32[2,96,512]{2,1,0:T(8,128)S(1)} %pad_maximum_fusion.7), channel_id=1, source_target_pairs={{0,32},{1,9},{2,34},{3,11},{4,36},{5,13},{6,38},{7,15},{8,40},{9,1... | collective-permute-start | bytes 1179656 | tf_op jit(solution)/shard_map/ppermute | solution.py:44
  18.4 11.3 %collective-permute-start.4 = (f32[4,96,512]{2,1,0:T(8,128)S(1)}, f32[4,96,512]{2,1,0:T(8,128)S(1)}, u32[]{:S(2)}, u32[]{:S(2)}) collective-permute-start(f32[4,96,512]{2,1,0:T(8,128)S(1)} %pad_maximum_fusion), channel_id=1, source_target_pairs={{0,8},{1,33},{2,10},{3,35},{4,12},{5,37},{6,14},{7,39},{8,0},{9,41... | collective-permute-start | bytes 2359304 | tf_op jit(solution)/shard_map/ppermute | solution.py:44
  19.7 12.5 %collective-permute-start.5 = (f32[4,96,512]{2,1,0:T(8,128)S(1)}, f32[4,96,512]{2,1,0:T(8,128)}, u32[]{:S(2)}, u32[]{:S(2)}) collective-permute-start(f32[4,96,512]{2,1,0:T(8,128)S(1)} %pad_maximum_fusion.1), channel_id=1, source_target_pairs={{0,24},{1,97},{2,26},{3,99},{4,28},{5,101},{6,30},{7,103},{8,16},{... | collective-permute-start | bytes 2359304 | tf_op jit(solution)/shard_map/ppermute | solution.py:44
  33.7 12.5 %collective-permute-start.6 = (f32[8,96,256]{2,1,0:T(8,128)S(1)}, f32[8,96,256]{2,1,0:T(8,128)}, u32[]{:S(2)}, u32[]{:S(2)}) collective-permute-start(f32[8,96,256]{2,1,0:T(8,128)S(1)} %pad_maximum_fusion.2.refs_0_), channel_id=1, source_target_pairs={{0,24},{1,97},{2,26},{3,99},{4,28},{5,101},{6,30},{7,103},{8,16},{... | collective-permute-start | bytes 2359304 | tf_op jit(solution)/shard_map/ppermute | solution.py:44
  35.6 11.3 %collective-permute-start.7 = (f32[8,96,256]{2,1,0:T(8,128)S(1)}, f32[8,96,256]{2,1,0:T(8,128)}, u32[]{:S(2)}, u32[]{:S(2)}) collective-permute-start(f32[8,96,256]{2,1,0:T(8,128)S(1)} %pad_maximum_fusion.3.refs_1_), channel_id=1, source_target_pairs={{0,8},{1,33},{2,10},{3,35},{4,12},{5,37},{6,14},{7,39},{8,0},{9,41... | collective-permute-start | bytes 2359304 | tf_op jit(solution)/shard_map/ppermute | solution.py:44
  35.8 27.5 %collective-permute-start.10 = (f32[8,96,256]{2,1,0:T(8,128)S(1)}, f32[8,96,256]{2,1,0:T(8,128)}, u32[]{:S(2)}, u32[]{:S(2)}) collective-permute-start(f32[8,96,256]{2,1,0:T(8,128)S(1)} %pad_maximum_fusion.4.refs_0_), channel_id=1, source_target_pairs={{0,24},{1,97},{2,26},{3,99},{4,28},{5,101},{6,30},{7,103},{8,16},{... | collective-permute-start | bytes 2359304 | tf_op jit(solution)/shard_map/ppermute | solution.py:44
  36.9 26.4 %collective-permute-start.11 = (f32[8,96,256]{2,1,0:T(8,128)S(1)}, f32[8,96,256]{2,1,0:T(8,128)}, u32[]{:S(2)}, u32[]{:S(2)}) collective-permute-start(f32[8,96,256]{2,1,0:T(8,128)S(1)} %pad_maximum_fusion.5.refs_1_), channel_id=1, source_target_pairs={{0,8},{1,33},{2,10},{3,35},{4,12},{5,37},{6,14},{7,39},{8,0},{9,41... | collective-permute-start | bytes 2359304 | tf_op jit(solution)/shard_map/ppermute | solution.py:44
  51.4 9.2 %collective-permute-start.8 = (f32[4,128,256]{2,1,0:T(8,128)S(1)}, f32[4,128,256]{2,1,0:T(8,128)S(1)}, u32[]{:S(2)}, u32[]{:S(2)}) collective-permute-start(f32[4,128,256]{2,1,0:T(8,128)S(1)} %get-tuple-element.72), channel_id=1, source_target_pairs={{0,1},{1,0},{2,3},{3,2},{4,5},{5,4},{6,7},{7,6},{8,9},{9,8},{10,11... | collective-permute-start | bytes 1572872 | tf_op jit(solution)/shard_map/ppermute | solution.py:21
  60.7 7.3 %collective-permute-start.9 = (f32[2,128,256]{2,1,0:T(8,128)S(1)}, f32[2,128,256]{2,1,0:T(8,128)S(1)}, u32[]{:S(2)}, u32[]{:S(2)}) collective-permute-start(f32[2,128,256]{2,1,0:T(8,128)S(1)} %slice.82), channel_id=1, source_target_pairs={{0,2},{1,7},{2,0},{3,5},{4,6},{5,3},{6,4},{7,1},{8,10},{9,15},{10,... | collective-permute-start | bytes 786440 | tf_op jit(solution)/shard_map/ppermute | solution.py:189
  67.8 3.6 %collective-permute-start.12 = (f32[4,128,256]{2,1,0:T(8,128)S(1)}, f32[4,128,256]{2,1,0:T(8,128)S(1)}, u32[]{:S(2)}, u32[]{:S(2)}) collective-permute-start(f32[4,128,256]{2,1,0:T(8,128)S(1)} %get-tuple-element.78), channel_id=1, source_target_pairs={{0,1},{1,0},{2,3},{3,2},{4,5},{5,4},{6,7},{7,6},{8,9},{9,8},{10,11... | collective-permute-start | bytes 1572872 | tf_op jit(solution)/shard_map/ppermute | solution.py:21
  68.1 3.9 %collective-permute-start.13 = (f32[128,256]{1,0:T(8,128)S(1)}, f32[128,256]{1,0:T(8,128)S(1)}, u32[]{:S(2)}, u32[]{:S(2)}) collective-permute-start(f32[128,256]{1,0:T(8,128)S(1)} %get-tuple-element.113), channel_id=1, source_target_pairs={{0,6},{1,3},{2,4},{3,1},{4,2},{5,7},{6,0},{7,5},{8,14},{9,11},{10,... | collective-permute-start | bytes 393224 | tf_op jit(solution)/shard_map/ppermute | solution.py:189
  72.0 6.5 %collective-permute-start.15 = (f32[2,128,256]{2,1,0:T(8,128)S(1)}, f32[2,128,256]{2,1,0:T(8,128)S(1)}, u32[]{:S(2)}, u32[]{:S(2)}) collective-permute-start(f32[2,128,256]{2,1,0:T(8,128)S(1)} %slice.91), channel_id=1, source_target_pairs={{0,2},{1,7},{2,0},{3,5},{4,6},{5,3},{6,4},{7,1},{8,10},{9,15},{10,... | collective-permute-start | bytes 786440 | tf_op jit(solution)/shard_map/ppermute | solution.py:189
  78.6 5.2 %collective-permute-start.16 = (f32[128,256]{1,0:T(8,128)S(1)}, f32[128,256]{1,0:T(8,128)S(1)}, u32[]{:S(2)}, u32[]{:S(2)}) collective-permute-start(f32[128,256]{1,0:T(8,128)S(1)} %get-tuple-element.110), channel_id=1, source_target_pairs={{0,6},{1,3},{2,4},{3,1},{4,2},{5,7},{6,0},{7,5},{8,14},{9,11},{10,... | collective-permute-start | bytes 393224 | tf_op jit(solution)/shard_map/ppermute | solution.py:189
  79.5 9.0 %collective-permute-start.14 = (f32[96,256]{1,0:T(8,128)S(1)}, f32[96,256]{1,0:T(8,128)S(1)}, u32[]{:S(2)}, u32[]{:S(2)}) collective-permute-start(f32[96,256]{1,0:T(8,128)S(1)} %get-tuple-element.83.own_ref.refs_1_), channel_id=1, source_target_pairs={{0,1},{1,0},{2,3},{3,2},{4,5},{5,4},{6,7},{7,6},{8,9},{9,8},{10,11... | collective-permute-start | bytes 294920 | tf_op jit(solution)/shard_map/ppermute | solution.py:21
  84.6 4.9 %collective-permute-start.17 = (f32[96,256]{1,0:T(8,128)S(1)}, f32[96,256]{1,0:T(8,128)S(1)}, u32[]{:S(2)}, u32[]{:S(2)}) collective-permute-start(f32[96,256]{1,0:T(8,128)S(1)} %get-tuple-element.88.own_ref.refs_5_), channel_id=1, source_target_pairs={{0,1},{1,0},{2,3},{3,2},{4,5},{5,4},{6,7},{7,6},{8,9},{9,8},{10,11... | collective-permute-start | bytes 294920 | tf_op jit(solution)/shard_map/ppermute | solution.py:21
  89.3 4.5 %collective-permute-start.18 = (f32[96,256]{1,0:T(8,128)S(1)}, f32[96,256]{1,0:T(8,128)S(1)}, u32[]{:S(2)}, u32[]{:S(2)}) collective-permute-start(f32[96,256]{1,0:T(8,128)S(1)} %get-tuple-element.85.refs_3_.own_ref), channel_id=1, source_target_pairs={{0,2},{1,3},{2,0},{3,1},{4,6},{5,7},{6,4},{7,5},{8,10},{9,11},{10,... | collective-permute-start | bytes 294920 | tf_op jit(solution)/shard_map/ppermute | solution.py:21
  90.3 5.8 %collective-permute-start.19 = (f32[96,256]{1,0:T(8,128)S(1)}, f32[96,256]{1,0:T(8,128)S(1)}, u32[]{:S(2)}, u32[]{:S(2)}) collective-permute-start(f32[96,256]{1,0:T(8,128)S(1)} %get-tuple-element.90.refs_7_.own_ref), channel_id=1, source_target_pairs={{0,2},{1,3},{2,0},{3,1},{4,6},{5,7},{6,4},{7,5},{8,10},{9,11},{10,... | collective-permute-start | bytes 294920 | tf_op jit(solution)/shard_map/ppermute | solution.py:21

commit v9 on v7

--- a/solution.py
+++ b/solution.py
@@ -108,19 +108,40 @@
     )(*[value] * streams)
 
 
-def convert(place_ref, pieces, high, low):
-    parts = len(ORDERS)
+def convert(place_ref, pieces, high, low, received):
     depth = pieces[0].shape[1]
+    count = pieces[0].shape[0]
     for part, masks in enumerate(ORDERS):
-        for at, (mask_0, mask_1) in enumerate(zip(origins(0, masks), origins(1, masks))):
-            source = pieces[part + parts * (at // 8)]
+        found = list(zip(origins(0, masks), origins(1, masks)))
+        for at, (mask_0, mask_1) in enumerate(found[count:] if received else found[:count]):
             mask = jnp.where(place_ref[2] == 0, mask_0, mask_1)
             block = jnp.bitwise_xor(place_ref[0], mask)
-            start = pl.multiple_of((block * parts + part) * depth, depth)
-            value = source[at % 8]
+            start = pl.multiple_of((block * len(ORDERS) + part) * depth, depth)
+            value = pieces[part][at]
             top = value.astype(jnp.bfloat16)
             high[pl.ds(start, depth), :] = top
             low[pl.ds(start, depth), :] = (value - top.astype(jnp.float32)).astype(jnp.bfloat16)
+
+
+def early_kernel(place_ref, *refs):
+    parts = len(ORDERS)
+    for chunk in range(len(WIDTHS)):
+        high, low = refs[parts * len(WIDTHS) + 2 * chunk :][:2]
+        convert(place_ref, refs[parts * chunk :][:parts], high, low, False)
+
+
+def convert_early(own, order, place):
+    in_vmem = pl.BlockSpec(memory_space=pltpu.VMEM)
+    outs = [pltpu.VMEM((order, width), jnp.bfloat16) for width in WIDTHS for _ in range(2)]
+    return pl.pallas_call(
+        early_kernel,
+        out_shape=outs,
+        in_specs=[pl.BlockSpec(memory_space=pltpu.SMEM)] + [in_vmem] * len(own),
+        out_specs=[in_vmem] * len(outs),
+        compiler_params=pltpu.CompilerParams(vmem_limit_bytes=8 * 2**20),
+        cost_estimate=pl.CostEstimate(flops=1, bytes_accessed=1, transcendentals=0),
+        name="convert_early",
+    )(place, *own)
 
 
 def multiply(place_ref, core, a_high, a_low, high, low, total, out_ref):
@@ -139,9 +160,10 @@
 
 
 def other_kernel(place_ref, a_high, a_low, *refs):
-    pieces = refs[: 2 * len(ORDERS)]
-    out_ref, high, low, total = refs[2 * len(ORDERS) :]
-    convert(place_ref, pieces, high, low)
+    parts = len(ORDERS)
+    pieces = refs[:parts]
+    out_ref, high, low, total = refs[parts + 2 :]
+    convert(place_ref, pieces, high, low, True)
     multiply(place_ref, 1 - place_ref[2], a_high, a_low, high, low, total, out_ref)
 
 
@@ -149,7 +171,7 @@
     multiply(place_ref, place_ref[2], a_high, a_low, high, low, total, out_ref)
 
 
-def product(kernel, place, halves, arrays, outs, cost, name):
+def product(kernel, place, halves, arrays, outs, cost, name, aliases):
     in_vmem = pl.BlockSpec(memory_space=pltpu.VMEM)
     halves = [pltpu.with_memory_space_constraint(half, pltpu.VMEM) for half in halves]
     return pl.pallas_call(
@@ -158,6 +180,7 @@
         in_specs=[pl.BlockSpec(memory_space=pltpu.SMEM)] + [in_vmem] * (2 + len(arrays)),
         out_specs=[in_vmem] * len(outs),
         scratch_shapes=[pltpu.VMEM(outs[0].shape, jnp.float32)],
+        input_output_aliases=aliases,
         compiler_params=pltpu.CompilerParams(vmem_limit_bytes=8 * 2**20),
         cost_estimate=pl.CostEstimate(flops=cost, bytes_accessed=cost // 400, transcendentals=0),
         name=name,
@@ -168,9 +191,12 @@
     leaves, _, leaf, order = halves[0].shape
     width = pieces[0].shape[-1]
     outs = [jax.ShapeDtypeStruct((leaves, leaf, width), jnp.float32)]
-    outs += [jax.ShapeDtypeStruct((order, width), jnp.bfloat16)] * 2
+    outs += [pltpu.VMEM((order, width), jnp.bfloat16)] * 2
+    at = 3 + len(ORDERS)
     cost = 6 * leaves * leaf * order * width if last else 1
-    return product(other_kernel, place, halves, pieces, outs, cost, "product_other")
+    return product(
+        other_kernel, place, halves, pieces, outs, cost, "product_other", {at: 1, at + 1: 2}
+    )
 
 
 def product_own(halves, sketch, place, last):
@@ -178,7 +204,7 @@
     width = sketch[0].shape[-1]
     outs = [jax.ShapeDtypeStruct((leaves, leaf, width), jnp.float32)]
     cost = 6 * leaves * leaf * order * width if last else 1
-    return product(own_kernel, place, halves, sketch, outs, cost, "product_own")[0]
+    return product(own_kernel, place, halves, sketch, outs, cost, "product_own", {})[0]
 
 
 def from_x(value, step):
@@ -407,6 +433,13 @@
     chunks, (ranks, pivots), frontal = gather_parts(sketch, frontal, tables, prepare)
     info = jnp.stack([leaf_index]).astype(jnp.int32)
     halves = [part.reshape(SIDE, 2, LEAF, -1) for part in split(frontal)]
+    parts = len(ORDERS)
+    own = [piece for pieces in chunks for piece in pieces[:parts]]
+    own, halves = lax.optimization_barrier((own, halves))
+    early = convert_early(own, halves[0].shape[-1], place)
+    chunks = [
+        [*pieces[parts:], *early[2 * chunk : 2 * chunk + 2]] for chunk, pieces in enumerate(chunks)
+    ]
     groups, core_sum, ready = [], None, ()
     for chunk, pieces in enumerate(chunks):
         last = chunk == len(chunks) - 1
@@ -414,10 +447,10 @@
             place, core_sum = lax.optimization_barrier((place, core_sum))
             group, ready = sum_over_x(core_sum)
             groups.append(group)
-        other, *parts = product_other(halves, pieces, place, last)
+        other, *converted = product_other(halves, pieces, place, last)
         received = from_partner(other, "col", 0)
         place, ready = lax.optimization_barrier((place, ready))
-        core_sum = product_own(halves, parts, place, last) + received
+        core_sum = product_own(halves, converted, place, last) + received
     groups.append(sum_over_x(core_sum)[0])
     arrays = []
     for group, width in zip(groups, WIDTHS):

time: 104 us -> 102 us (0.981)
  starting transfers between devices: 32.5 us -> 28.6 us
  waiting for transfers between devices: 32.5 us -> 35 us
  local copies, waits for them, and re-layouts: 3.27 us -> 2.16 us
    ppermute x10, starting transfers between devices: 15.4 us -> 12.5 us  [from_row(): return lax.ppermute(value, ('row', 'col'), pairs)]
    ppermute x10, waiting for transfers between devices: 21.2 us -> 23.6 us  [from_row(): return lax.ppermute(value, ('row', 'col'), pairs)]
    ppermute x6, starting transfers between devices: 12.7 us -> 11.5 us  [from_partner(): return lax.ppermute(value, axis, pairs)]
    slice x2, local copies, waits for them, and re-layouts: 1.25 us -> 0.14 us  [gather_parts(): other[:, :, columns]]
  transfers between devices with their start and end apart: 20 -> 20, of which waited for: 11 -> 12; matrix products, arithmetic and copies ran while one was open for 1% -> 1% of each run, Pallas kernels for 23% -> 24%
where the time goes in v9:
time: 102 us
  waiting for transfers between devices  35 us (34%)
  Pallas kernels  34.6 us (34%)
  starting transfers between devices  28.6 us (28%)
  local copies, waits for them, and re-layouts  2.16 us (2%)
  between operations  1.03 us (1%)
    ppermute x10, waiting for transfers between devices, from_row(): return lax.ppermute(value, ('row', 'col'), pairs)  23.6 us
    pallas_call x4, Pallas kernels, product(): pl.pallas_call(kernel, out_shape=outs, in_specs=[pl.BlockSpec(memory_spac...  14.9 us
    pallas_call x5, Pallas kernels, call(): pl.pallas_call(kernel, out_shape=[jax.ShapeDtypeStruct(shape, jnp.float32...  13 us
    ppermute x10, starting transfers between devices, from_row(): return lax.ppermute(value, ('row', 'col'), pairs)  12.5 us
    ppermute x6, starting transfers between devices, from_partner(): return lax.ppermute(value, axis, pairs)  11.5 us
    ppermute x4, waiting for transfers between devices, from_x(): return lax.ppermute(value, 'col', pairs)  7.31 us
    pallas_call x1, Pallas kernels, split(): pl.pallas_call(split_kernel, out_shape=[pltpu.VMEM((rows, order), jnp.bfl...  5.76 us
    ppermute x4, starting transfers between devices, from_x(): return lax.ppermute(value, 'col', pairs)  4.61 us
  transfers between devices with their start and end apart: 20, of which 12 were waited for; matrix products, arithmetic and copies ran while one was open for 1% of the time, Pallas kernels for 24%

profile of v9, /device:TPU:1, one launch (start us, length us, event | category | flops | bytes accessed | tf_op | source)
XLA Modules:
  0.0 102.2 jit_solution(15208896908728705756)
XLA Ops:
  0.6 0.0 copy-start
  0.6 1.1 %slice_bitcast_fusion = (f32[1,96,512]{2,1,0:T(8,128)S(1)}, f32[1,96,512]{2,1,0:T(8,128)S(1)}) fusion(f32[192,512]{1,0:T(8,128)} %param.9), kind=kLoop, calls=%fused_computation.8 | loop fusion | bytes 786432 | tf_op jit(solution)/shard_map/broadcast_in_dim | solution.py:56
  1.7 4.7 %collective-permute-start.2 = (f32[1,96,512]{2,1,0:T(8,128)S(1)}, f32[1,96,512]{2,1,0:T(8,128)S(1)}, u32[]{:S(2)}, u32[]{:S(2)}) collective-permute-start(f32[1,96,512]{2,1,0:T(8,128)S(1)} %get-tuple-element.112), channel_id=1, source_target_pairs={{0,96},{1,25},{2,98},{3,27},{4,100},{5,29},{6,102},{7,31},{8,104},... | collective-permute-start | bytes 589832 | tf_op jit(solution)/shard_map/ppermute | solution.py:44
  6.4 0.0 collective-permute-start
  6.4 3.3 %collective-permute-done.2 = f32[1,96,512]{2,1,0:T(8,128)S(1)} collective-permute-done((f32[1,96,512]{2,1,0:T(8,128)S(1)}, f32[1,96,512]{2,1,0:T(8,128)S(1)}, u32[]{:S(2)}, u32[]{:S(2)}) %collective-permute-start.2) | collective-permute-done | bytes 196640 | tf_op jit(solution)/shard_map/ppermute | solution.py:44
  9.7 0.1 collective-permute-start.3
  9.8 1.4 %collective-permute-done = f32[1,96,512]{2,1,0:T(8,128)S(1)} collective-permute-done((f32[1,96,512]{2,1,0:T(8,128)S(1)}, f32[1,96,512]{2,1,0:T(8,128)S(1)}, u32[]{:S(2)}, u32[]{:S(2)}) %collective-permute-start) | collective-permute-done | bytes 196640 | tf_op jit(solution)/shard_map/ppermute | solution.py:44
  11.2 0.0 copy-start.1
  11.3 0.0 copy-start.2
  11.3 0.0 copy-start.3
  11.3 1.4 %collective-permute-start.1 = (f32[2,96,512]{2,1,0:T(8,128)S(1)}, f32[2,96,512]{2,1,0:T(8,128)S(1)}, u32[]{:S(2)}, u32[]{:S(2)}) collective-permute-start(f32[2,96,512]{2,1,0:T(8,128)S(1)} %pad_maximum_fusion.6), channel_id=1, source_target_pairs={{0,96},{1,25},{2,98},{3,27},{4,100},{5,29},{6,102},{7,31},{8,104},... | collective-permute-start | bytes 1179656 | tf_op jit(solution)/shard_map/ppermute | solution.py:44
  12.7 4.0 %collective-permute-done.3 = f32[2,96,512]{2,1,0:T(8,128)S(1)} collective-permute-done((f32[2,96,512]{2,1,0:T(8,128)S(1)}, f32[2,96,512]{2,1,0:T(8,128)S(1)}, u32[]{:S(2)}, u32[]{:S(2)}) %collective-permute-start.3) | collective-permute-done | bytes 393248 | tf_op jit(solution)/shard_map/ppermute | solution.py:44
  16.7 2.7 %collective-permute-done.1 = f32[2,96,512]{2,1,0:T(8,128)S(1)} collective-permute-done((f32[2,96,512]{2,1,0:T(8,128)S(1)}, f32[2,96,512]{2,1,0:T(8,128)S(1)}, u32[]{:S(2)}, u32[]{:S(2)}) %collective-permute-start.1) | collective-permute-done | bytes 393248 | tf_op jit(solution)/shard_map/ppermute | solution.py:44
  19.5 0.1 pad_maximum_fusion.1
  19.5 2.4 %collective-permute-start.5 = (f32[4,96,512]{2,1,0:T(8,128)S(1)}, f32[4,96,512]{2,1,0:T(8,128)S(1)}, u32[]{:S(2)}, u32[]{:S(2)}) collective-permute-start(f32[4,96,512]{2,1,0:T(8,128)S(1)} %pad_maximum_fusion.1), channel_id=1, source_target_pairs={{0,24},{1,97},{2,26},{3,99},{4,28},{5,101},{6,30},{7,103},{8,16},{... | collective-permute-start | bytes 2359304 | tf_op jit(solution)/shard_map/ppermute | solution.py:44
  21.9 0.1 pad_maximum_fusion
  22.0 0.1 collective-permute-start.4
  22.2 0.1 pad_add_fusion.1.ranks_ref
  22.3 0.7 constant_dynamic-slice_fusion
  23.0 9.0 %collective-permute-done.5 = f32[4,96,512]{2,1,0:T(8,128)S(1)} collective-permute-done((f32[4,96,512]{2,1,0:T(8,128)S(1)}, f32[4,96,512]{2,1,0:T(8,128)S(1)}, u32[]{:S(2)}, u32[]{:S(2)}) %collective-permute-start.5) | collective-permute-done | bytes 786464 | tf_op jit(solution)/shard_map/ppermute | solution.py:44
  32.0 1.2 %collective-permute-done.4 = f32[4,96,512]{2,1,0:T(8,128)S(1)} collective-permute-done((f32[4,96,512]{2,1,0:T(8,128)S(1)}, f32[4,96,512]{2,1,0:T(8,128)S(1)}, u32[]{:S(2)}, u32[]{:S(2)}) %collective-permute-start.4) | collective-permute-done | bytes 786464 | tf_op jit(solution)/shard_map/ppermute | solution.py:44
  33.2 0.1 fusion.4
  33.3 0.1 fusion.5
  33.4 0.1 fusion.2
  33.4 0.1 fusion.3
  33.5 0.1 pad_maximum_fusion.3.refs_1_
  33.6 0.1 collective-permute-start.7
  33.7 0.1 pad_maximum_fusion.2.refs_0_
  33.7 1.2 %collective-permute-start.6 = (f32[8,96,256]{2,1,0:T(8,128)S(1)}, f32[8,96,256]{2,1,0:T(8,128)}, u32[]{:S(2)}, u32[]{:S(2)}) collective-permute-start(f32[8,96,256]{2,1,0:T(8,128)S(1)} %pad_maximum_fusion.2.refs_0_), channel_id=1, source_target_pairs={{0,24},{1,97},{2,26},{3,99},{4,28},{5,101},{6,30},{7,103},{8,16},{... | collective-permute-start | bytes 2359304 | tf_op jit(solution)/shard_map/ppermute | solution.py:44
  34.9 0.1 pad_maximum_fusion.5.refs_3_
  35.0 0.9 collective-permute-start.14
  35.9 0.1 pad_maximum_fusion.4.refs_2_
  36.0 1.7 %collective-permute-start.13 = (f32[8,96,256]{2,1,0:T(8,128)S(1)}, f32[8,96,256]{2,1,0:T(8,128)}, u32[]{:S(2)}, u32[]{:S(2)}) collective-permute-start(f32[8,96,256]{2,1,0:T(8,128)S(1)} %pad_maximum_fusion.4.refs_2_), channel_id=1, source_target_pairs={{0,24},{1,97},{2,26},{3,99},{4,28},{5,101},{6,30},{7,103},{8,16},{... | collective-permute-start | bytes 2359304 | tf_op jit(solution)/shard_map/ppermute | solution.py:44
  37.6 0.1 pad_add_fusion.2.place_ref
  37.7 5.8 %split.1 = (bf16[1024,3072]{1,0:T(8,128)(2,1)S(1)}, bf16[1024,3072]{1,0:T(8,128)(2,1)S(1)}) custom-call(f32[1024,3072]{1,0:T(8,128)} %refs_3_, f32[1024,3072]{1,0:T(8,128)} %refs_3_, f32[1024,3072]{1,0:T(8,128)} %refs_3_, f32[1024,3072]{1,0:T(8,128)} %refs_3_), custom_call_target="tpu_custom_call" | custom-call | flops 12582912 | bytes 25165824 | tf_op jit(solution)/shard_map/split/pallas_call | solution.py:97
  43.5 0.9 convert_early.1
  44.4 0.5 collective-permute-done.7.refs_1_
  44.9 1.4 %collective-permute-done.6.refs_0_ = f32[8,96,256]{2,1,0:T(8,128)} collective-permute-done((f32[8,96,256]{2,1,0:T(8,128)S(1)}, f32[8,96,256]{2,1,0:T(8,128)}, u32[]{:S(2)}, u32[]{:S(2)}) %collective-permute-start.6) | collective-permute-done | bytes 786464 | tf_op jit(solution)/shard_map/ppermute | solution.py:44
  46.3 4.2 %product_other.2 = (f32[4,128,256]{2,1,0:T(8,128)S(1)}, bf16[3072,256]{1,0:T(8,128)(2,1)S(1)}, bf16[3072,256]{1,0:T(8,128)(2,1)S(1)}) custom-call(s32[3]{0:T(128)S(1)} %pad_add_fusion.2.place_ref, bf16[4,2,128,3072]{3,2,1,0:T(8,128)(2,1)S(1)} %bitcast.27, bf16[4,2,128,3072]{3,2,1,0:T(8,128)(2,1)S(1)} %bitcast.31, ...), custom_call_target="tpu_custom_call", output_to_operand_aliasing={{1}: (5, {}), {2}: (6, {})} | custom-call | flops 1 | tf_op jit(solution)/shard_map/product_other/pallas_call | solution.py:177
  50.5 5.2 %collective-permute-start.8 = (f32[4,128,256]{2,1,0:T(8,128)S(1)}, f32[4,128,256]{2,1,0:T(8,128)S(1)}, u32[]{:S(2)}, u32[]{:S(2)}) collective-permute-start(f32[4,128,256]{2,1,0:T(8,128)S(1)} %get-tuple-element.79), channel_id=1, source_target_pairs={{0,1},{1,0},{2,3},{3,2},{4,5},{5,4},{6,7},{7,6},{8,9},{9,8},{10,11... | collective-permute-start | bytes 1572872 | tf_op jit(solution)/shard_map/ppermute | solution.py:21
  55.7 3.2 %product_own.2 = f32[4,128,256]{2,1,0:T(8,128)S(1)} custom-call(s32[3]{0:T(128)S(1)} %pad_add_fusion.2.place_ref, bf16[4,2,128,3072]{3,2,1,0:T(8,128)(2,1)S(1)} %bitcast.28, bf16[4,2,128,3072]{3,2,1,0:T(8,128)(2,1)S(1)} %bitcast.32, bf16[3072,256]{1,0:T(8,128)(2,1)S(1)} %get-tuple-element.77.high, bf16[3072,256]{1,0:T(8,128)(2,1)S(1)} %get-tuple-element.78.low), custom_call_target="tpu_custom_call" | custom-call | flops 1 | tf_op jit(solution)/shard_map/product_own/pallas_call | solution.py:177
  58.9 0.0 collective-permute-done.8
  58.9 0.1 add.45
  59.0 2.6 %collective-permute-start.9 = (f32[2,128,256]{2,1,0:T(8,128)S(1)}, f32[2,128,256]{2,1,0:T(8,128)S(1)}, u32[]{:S(2)}, u32[]{:S(2)}) collective-permute-start(f32[2,128,256]{2,1,0:T(8,128)S(1)} %slice.86), channel_id=1, source_target_pairs={{0,2},{1,7},{2,0},{3,5},{4,6},{5,3},{6,4},{7,1},{8,10},{9,15},{10,... | collective-permute-start | bytes 786440 | tf_op jit(solution)/shard_map/ppermute | solution.py:215
  61.5 4.2 %product_other.3 = (f32[4,128,256]{2,1,0:T(8,128)S(1)}, bf16[3072,256]{1,0:T(8,128)(2,1)S(1)}, bf16[3072,256]{1,0:T(8,128)(2,1)S(1)}) custom-call(s32[3]{0:T(128)S(1)} %pad_add_fusion.2.place_ref, bf16[4,2,128,3072]{3,2,1,0:T(8,128)(2,1)S(1)} %bitcast.29, bf16[4,2,128,3072]{3,2,1,0:T(8,128)(2,1)S(1)} %bitcast.33, ...), custom_call_target="tpu_custom_call", output_to_operand_aliasing={{1}: (5, {}), {2}: (6, {})} | custom-call | flops 2415919104 | bytes 6039797 | tf_op jit(solution)/shard_map/product_other/pallas_call | solution.py:177
  65.8 0.3 collective-permute-start.15
  66.1 3.2 %product_own.3 = f32[4,128,256]{2,1,0:T(8,128)S(1)} custom-call(s32[3]{0:T(128)S(1)} %pad_add_fusion.2.place_ref, bf16[4,2,128,3072]{3,2,1,0:T(8,128)(2,1)S(1)} %bitcast.30, bf16[4,2,128,3072]{3,2,1,0:T(8,128)(2,1)S(1)} %bitcast.34, bf16[3072,256]{1,0:T(8,128)(2,1)S(1)} %get-tuple-element.89.high, bf16[3072,256]{1,0:T(8,128)(2,1)S(1)} %get-tuple-element.90.low), custom_call_target="tpu_custom_call" | custom-call | flops 2415919104 | bytes 6039797 | tf_op jit(solution)/shard_map/product_own/pallas_call | solution.py:177
  69.3 0.1 add.48
  69.4 2.0 %collective-permute-start.16 = (f32[2,128,256]{2,1,0:T(8,128)S(1)}, f32[2,128,256]{2,1,0:T(8,128)S(1)}, u32[]{:S(2)}, u32[]{:S(2)}) collective-permute-start(f32[2,128,256]{2,1,0:T(8,128)S(1)} %slice.98), channel_id=1, source_target_pairs={{0,2},{1,7},{2,0},{3,5},{4,6},{5,3},{6,4},{7,1},{8,10},{9,15},{10,... | collective-permute-start | bytes 786440 | tf_op jit(solution)/shard_map/ppermute | solution.py:215
  71.4 6.2 %collective-permute-done.16 = f32[2,128,256]{2,1,0:T(8,128)S(1)} collective-permute-done((f32[2,128,256]{2,1,0:T(8,128)S(1)}, f32[2,128,256]{2,1,0:T(8,128)S(1)}, u32[]{:S(2)}, u32[]{:S(2)}) %collective-permute-start.16) | collective-permute-done | bytes 262176 | tf_op jit(solution)/shard_map/ppermute | solution.py:215
  77.6 0.1 collective-permute-start.17
  77.7 0.8 leaf_rows.2
  78.6 1.9 %collective-permute-start.11 = (f32[96,256]{1,0:T(8,128)S(1)}, f32[96,256]{1,0:T(8,128)S(1)}, u32[]{:S(2)}, u32[]{:S(2)}) collective-permute-start(f32[96,256]{1,0:T(8,128)S(1)} %get-tuple-element.82.own_ref.refs_1_), channel_id=1, source_target_pairs={{0,1},{1,0},{2,3},{3,2},{4,5},{5,4},{6,7},{7,6},{8,9},{9,8},{10,11... | collective-permute-start | bytes 294920 | tf_op jit(solution)/shard_map/ppermute | solution.py:21
  80.4 1.1 %collective-permute-done.17.refs_2_ = f32[128,256]{1,0:T(8,128)S(1)} collective-permute-done((f32[128,256]{1,0:T(8,128)S(1)}, f32[128,256]{1,0:T(8,128)S(1)}, u32[]{:S(2)}, u32[]{:S(2)}) %collective-permute-start.17) | collective-permute-done | bytes 131104 | tf_op jit(solution)/shard_map/ppermute | solution.py:215
  81.5 0.8 leaf_rows.3
  82.4 2.6 %collective-permute-start.18 = (f32[96,256]{1,0:T(8,128)S(1)}, f32[96,256]{1,0:T(8,128)S(1)}, u32[]{:S(2)}, u32[]{:S(2)}) collective-permute-start(f32[96,256]{1,0:T(8,128)S(1)} %get-tuple-element.93.own_ref.refs_6_), channel_id=1, source_target_pairs={{0,1},{1,0},{2,3},{3,2},{4,5},{5,4},{6,7},{7,6},{8,9},{9,8},{10,11... | collective-permute-start | bytes 294920 | tf_op jit(solution)/shard_map/ppermute | solution.py:21
  85.0 0.8 mid_rows.2
  85.8 0.1 collective-permute-start.12
  85.9 0.0 collective-permute-done.18.other_ref
  85.9 0.8 mid_rows.3
  86.7 1.5 %collective-permute-start.19 = (f32[96,256]{1,0:T(8,128)S(1)}, f32[96,256]{1,0:T(8,128)S(1)}, u32[]{:S(2)}, u32[]{:S(2)}) collective-permute-start(f32[96,256]{1,0:T(8,128)S(1)} %get-tuple-element.95.refs_8_), channel_id=1, source_target_pairs={{0,2},{1,3},{2,0},{3,1},{4,6},{5,7},{6,4},{7,5},{8,10},{9,11},{10,... | collective-permute-start | bytes 294920 | tf_op jit(solution)/shard_map/ppermute | solution.py:21
  88.3 2.0 %collective-permute-done.12.refs_4_ = f32[96,256]{1,0:T(8,128)S(1)} collective-permute-done((f32[96,256]{1,0:T(8,128)S(1)}, f32[96,256]{1,0:T(8,128)S(1)}, u32[]{:S(2)}, u32[]{:S(2)}) %collective-permute-start.12) | collective-permute-done | bytes 98336 | tf_op jit(solution)/shard_map/ppermute | solution.py:21
  90.3 2.1 %collective-permute-done.19.refs_9_ = f32[96,256]{1,0:T(8,128)S(1)} collective-permute-done((f32[96,256]{1,0:T(8,128)S(1)}, f32[96,256]{1,0:T(8,128)S(1)}, u32[]{:S(2)}, u32[]{:S(2)}) %collective-permute-start.19) | collective-permute-done | bytes 98336 | tf_op jit(solution)/shard_map/ppermute | solution.py:21
  92.4 9.8 %interpolation.1 = (f32[96,128]{1,0:T(8,128)}, f32[96,192]{1,0:T(8,128)}, f32[96,192]{1,0:T(8,128)}, f32[96,512]{1,0:T(8,128)}) custom-call(s32[1]{0:T(128)} %bitcast.info_ref, s32[224]{0:T(256)S(1)} %pad_add_fusion.1.ranks_ref, s32[3,96]{1,0:T(4,128)S(1)} %pad_add_fusion.pivots_ref, f32[128,256]{1,0:T(8,128)S(1)} %get-tuple-element.81.refs_0_, ...), custom_call_target="tpu_custom_call" | custom-call | tf_op jit(solution)/shard_map/interpolation/pallas_call | solution.py:404
  (19 shorter events, 0.2 us)
Async XLA Ops:
  0.6 21.5 %copy-start = (s32[128,128]{1,0:T(8,128)S(1)}, s32[128,128]{1,0:T(8,128)}, u32[]{:S(2)}) copy-start(s32[128,128]{1,0:T(8,128)} %param.11) | copy-start | bytes 196612
  1.7 8.0 %collective-permute-start.2 = (f32[1,96,512]{2,1,0:T(8,128)S(1)}, f32[1,96,512]{2,1,0:T(8,128)S(1)}, u32[]{:S(2)}, u32[]{:S(2)}) collective-permute-start(f32[1,96,512]{2,1,0:T(8,128)S(1)} %get-tuple-element.112), channel_id=1, source_target_pairs={{0,96},{1,25},{2,98},{3,27},{4,100},{5,29},{6,102},{7,31},{8,104},... | collective-permute-start | bytes 589832 | tf_op jit(solution)/shard_map/ppermute | solution.py:44
  6.4 4.8 %collective-permute-start = (f32[1,96,512]{2,1,0:T(8,128)S(1)}, f32[1,96,512]{2,1,0:T(8,128)S(1)}, u32[]{:S(2)}, u32[]{:S(2)}) collective-permute-start(f32[1,96,512]{2,1,0:T(8,128)S(1)} %get-tuple-element.113), channel_id=1, source_target_pairs={{0,32},{1,9},{2,34},{3,11},{4,36},{5,13},{6,38},{7,15},{8,40},{9,1... | collective-permute-start | bytes 589832 | tf_op jit(solution)/shard_map/ppermute | solution.py:44
  9.7 7.0 %collective-permute-start.3 = (f32[2,96,512]{2,1,0:T(8,128)S(1)}, f32[2,96,512]{2,1,0:T(8,128)S(1)}, u32[]{:S(2)}, u32[]{:S(2)}) collective-permute-start(f32[2,96,512]{2,1,0:T(8,128)S(1)} %pad_maximum_fusion.7), channel_id=1, source_target_pairs={{0,32},{1,9},{2,34},{3,11},{4,36},{5,13},{6,38},{7,15},{8,40},{9,1... | collective-permute-start | bytes 1179656 | tf_op jit(solution)/shard_map/ppermute | solution.py:44
  11.2 10.9 %copy-start.1 = (s32[32]{0:T(128)S(1)}, s32[32]{0:T(128)}, u32[]{:S(2)}) copy-start(s32[32]{0:T(128)} %param.14) | copy-start | bytes 388
  11.3 10.9 %copy-start.2 = (s32[64]{0:T(128)S(1)}, s32[64]{0:T(128)}, u32[]{:S(2)}) copy-start(s32[64]{0:T(128)} %param.12) | copy-start | bytes 772
  11.3 10.9 %copy-start.3 = (s32[128]{0:T(128)S(1)}, s32[128]{0:T(128)}, u32[]{:S(2)}) copy-start(s32[128]{0:T(128)} %param.10) | copy-start | bytes 1540
  11.3 8.2 %collective-permute-start.1 = (f32[2,96,512]{2,1,0:T(8,128)S(1)}, f32[2,96,512]{2,1,0:T(8,128)S(1)}, u32[]{:S(2)}, u32[]{:S(2)}) collective-permute-start(f32[2,96,512]{2,1,0:T(8,128)S(1)} %pad_maximum_fusion.6), channel_id=1, source_target_pairs={{0,96},{1,25},{2,98},{3,27},{4,100},{5,29},{6,102},{7,31},{8,104},... | collective-permute-start | bytes 1179656 | tf_op jit(solution)/shard_map/ppermute | solution.py:44
  19.5 12.4 %collective-permute-start.5 = (f32[4,96,512]{2,1,0:T(8,128)S(1)}, f32[4,96,512]{2,1,0:T(8,128)S(1)}, u32[]{:S(2)}, u32[]{:S(2)}) collective-permute-start(f32[4,96,512]{2,1,0:T(8,128)S(1)} %pad_maximum_fusion.1), channel_id=1, source_target_pairs={{0,24},{1,97},{2,26},{3,99},{4,28},{5,101},{6,30},{7,103},{8,16},{... | collective-permute-start | bytes 2359304 | tf_op jit(solution)/shard_map/ppermute | solution.py:44
  22.0 11.2 %collective-permute-start.4 = (f32[4,96,512]{2,1,0:T(8,128)S(1)}, f32[4,96,512]{2,1,0:T(8,128)S(1)}, u32[]{:S(2)}, u32[]{:S(2)}) collective-permute-start(f32[4,96,512]{2,1,0:T(8,128)S(1)} %pad_maximum_fusion), channel_id=1, source_target_pairs={{0,8},{1,33},{2,10},{3,35},{4,12},{5,37},{6,14},{7,39},{8,0},{9,41... | collective-permute-start | bytes 2359304 | tf_op jit(solution)/shard_map/ppermute | solution.py:44
  33.6 11.3 %collective-permute-start.7 = (f32[8,96,256]{2,1,0:T(8,128)S(1)}, f32[8,96,256]{2,1,0:T(8,128)}, u32[]{:S(2)}, u32[]{:S(2)}) collective-permute-start(f32[8,96,256]{2,1,0:T(8,128)S(1)} %pad_maximum_fusion.3.refs_1_), channel_id=1, source_target_pairs={{0,8},{1,33},{2,10},{3,35},{4,12},{5,37},{6,14},{7,39},{8,0},{9,41... | collective-permute-start | bytes 2359304 | tf_op jit(solution)/shard_map/ppermute | solution.py:44
  33.7 12.5 %collective-permute-start.6 = (f32[8,96,256]{2,1,0:T(8,128)S(1)}, f32[8,96,256]{2,1,0:T(8,128)}, u32[]{:S(2)}, u32[]{:S(2)}) collective-permute-start(f32[8,96,256]{2,1,0:T(8,128)S(1)} %pad_maximum_fusion.2.refs_0_), channel_id=1, source_target_pairs={{0,24},{1,97},{2,26},{3,99},{4,28},{5,101},{6,30},{7,103},{8,16},{... | collective-permute-start | bytes 2359304 | tf_op jit(solution)/shard_map/ppermute | solution.py:44
  35.0 26.6 %collective-permute-start.14 = (f32[8,96,256]{2,1,0:T(8,128)S(1)}, f32[8,96,256]{2,1,0:T(8,128)}, u32[]{:S(2)}, u32[]{:S(2)}) collective-permute-start(f32[8,96,256]{2,1,0:T(8,128)S(1)} %pad_maximum_fusion.5.refs_3_), channel_id=1, source_target_pairs={{0,8},{1,33},{2,10},{3,35},{4,12},{5,37},{6,14},{7,39},{8,0},{9,41... | collective-permute-start | bytes 2359304 | tf_op jit(solution)/shard_map/ppermute | solution.py:44
  36.0 25.6 %collective-permute-start.13 = (f32[8,96,256]{2,1,0:T(8,128)S(1)}, f32[8,96,256]{2,1,0:T(8,128)}, u32[]{:S(2)}, u32[]{:S(2)}) collective-permute-start(f32[8,96,256]{2,1,0:T(8,128)S(1)} %pad_maximum_fusion.4.refs_2_), channel_id=1, source_target_pairs={{0,24},{1,97},{2,26},{3,99},{4,28},{5,101},{6,30},{7,103},{8,16},{... | collective-permute-start | bytes 2359304 | tf_op jit(solution)/shard_map/ppermute | solution.py:44
  50.5 8.4 %collective-permute-start.8 = (f32[4,128,256]{2,1,0:T(8,128)S(1)}, f32[4,128,256]{2,1,0:T(8,128)S(1)}, u32[]{:S(2)}, u32[]{:S(2)}) collective-permute-start(f32[4,128,256]{2,1,0:T(8,128)S(1)} %get-tuple-element.79), channel_id=1, source_target_pairs={{0,1},{1,0},{2,3},{3,2},{4,5},{5,4},{6,7},{7,6},{8,9},{9,8},{10,11... | collective-permute-start | bytes 1572872 | tf_op jit(solution)/shard_map/ppermute | solution.py:21
  59.0 7.1 %collective-permute-start.9 = (f32[2,128,256]{2,1,0:T(8,128)S(1)}, f32[2,128,256]{2,1,0:T(8,128)S(1)}, u32[]{:S(2)}, u32[]{:S(2)}) collective-permute-start(f32[2,128,256]{2,1,0:T(8,128)S(1)} %slice.86), channel_id=1, source_target_pairs={{0,2},{1,7},{2,0},{3,5},{4,6},{5,3},{6,4},{7,1},{8,10},{9,15},{10,... | collective-permute-start | bytes 786440 | tf_op jit(solution)/shard_map/ppermute | solution.py:215
  65.8 3.5 %collective-permute-start.15 = (f32[4,128,256]{2,1,0:T(8,128)S(1)}, f32[4,128,256]{2,1,0:T(8,128)S(1)}, u32[]{:S(2)}, u32[]{:S(2)}) collective-permute-start(f32[4,128,256]{2,1,0:T(8,128)S(1)} %get-tuple-element.91), channel_id=1, source_target_pairs={{0,1},{1,0},{2,3},{3,2},{4,5},{5,4},{6,7},{7,6},{8,9},{9,8},{10,11... | collective-permute-start | bytes 1572872 | tf_op jit(solution)/shard_map/ppermute | solution.py:21
  69.4 8.2 %collective-permute-start.16 = (f32[2,128,256]{2,1,0:T(8,128)S(1)}, f32[2,128,256]{2,1,0:T(8,128)S(1)}, u32[]{:S(2)}, u32[]{:S(2)}) collective-permute-start(f32[2,128,256]{2,1,0:T(8,128)S(1)} %slice.98), channel_id=1, source_target_pairs={{0,2},{1,7},{2,0},{3,5},{4,6},{5,3},{6,4},{7,1},{8,10},{9,15},{10,... | collective-permute-start | bytes 786440 | tf_op jit(solution)/shard_map/ppermute | solution.py:215
  71.4 6.3 %collective-permute-start.10 = (f32[128,256]{1,0:T(8,128)S(1)}, f32[128,256]{1,0:T(8,128)S(1)}, u32[]{:S(2)}, u32[]{:S(2)}) collective-permute-start(f32[128,256]{1,0:T(8,128)S(1)} %get-tuple-element.110), channel_id=1, source_target_pairs={{0,6},{1,3},{2,4},{3,1},{4,2},{5,7},{6,0},{7,5},{8,14},{9,11},{10,... | collective-permute-start | bytes 393224 | tf_op jit(solution)/shard_map/ppermute | solution.py:215
  77.6 3.9 %collective-permute-start.17 = (f32[128,256]{1,0:T(8,128)S(1)}, f32[128,256]{1,0:T(8,128)S(1)}, u32[]{:S(2)}, u32[]{:S(2)}) collective-permute-start(f32[128,256]{1,0:T(8,128)S(1)} %get-tuple-element.108), channel_id=1, source_target_pairs={{0,6},{1,3},{2,4},{3,1},{4,2},{5,7},{6,0},{7,5},{8,14},{9,11},{10,... | collective-permute-start | bytes 393224 | tf_op jit(solution)/shard_map/ppermute | solution.py:215
  78.6 6.4 %collective-permute-start.11 = (f32[96,256]{1,0:T(8,128)S(1)}, f32[96,256]{1,0:T(8,128)S(1)}, u32[]{:S(2)}, u32[]{:S(2)}) collective-permute-start(f32[96,256]{1,0:T(8,128)S(1)} %get-tuple-element.82.own_ref.refs_1_), channel_id=1, source_target_pairs={{0,1},{1,0},{2,3},{3,2},{4,5},{5,4},{6,7},{7,6},{8,9},{9,8},{10,11... | collective-permute-start | bytes 294920 | tf_op jit(solution)/shard_map/ppermute | solution.py:21
  82.4 3.6 %collective-permute-start.18 = (f32[96,256]{1,0:T(8,128)S(1)}, f32[96,256]{1,0:T(8,128)S(1)}, u32[]{:S(2)}, u32[]{:S(2)}) collective-permute-start(f32[96,256]{1,0:T(8,128)S(1)} %get-tuple-element.93.own_ref.refs_6_), channel_id=1, source_target_pairs={{0,1},{1,0},{2,3},{3,2},{4,5},{5,4},{6,7},{7,6},{8,9},{9,8},{10,11... | collective-permute-start | bytes 294920 | tf_op jit(solution)/shard_map/ppermute | solution.py:21
  85.8 4.5 %collective-permute-start.12 = (f32[96,256]{1,0:T(8,128)S(1)}, f32[96,256]{1,0:T(8,128)S(1)}, u32[]{:S(2)}, u32[]{:S(2)}) collective-permute-start(f32[96,256]{1,0:T(8,128)S(1)} %get-tuple-element.84.refs_3_), channel_id=1, source_target_pairs={{0,2},{1,3},{2,0},{3,1},{4,6},{5,7},{6,4},{7,5},{8,10},{9,11},{10,... | collective-permute-start | bytes 294920 | tf_op jit(solution)/shard_map/ppermute | solution.py:21
  86.7 5.7 %collective-permute-start.19 = (f32[96,256]{1,0:T(8,128)S(1)}, f32[96,256]{1,0:T(8,128)S(1)}, u32[]{:S(2)}, u32[]{:S(2)}) collective-permute-start(f32[96,256]{1,0:T(8,128)S(1)} %get-tuple-element.95.refs_8_), channel_id=1, source_target_pairs={{0,2},{1,3},{2,0},{3,1},{4,6},{5,7},{6,4},{7,5},{8,10},{9,11},{10,... | collective-permute-start | bytes 294920 | tf_op jit(solution)/shard_map/ppermute | solution.py:21

commit v10 on v8

--- a/solution.py
+++ b/solution.py
@@ -108,19 +108,40 @@
     )(*[value] * streams)
 
 
-def convert(place_ref, pieces, high, low):
-    parts = len(ORDERS)
+def convert(place_ref, pieces, high, low, received):
     depth = pieces[0].shape[1]
+    count = pieces[0].shape[0]
     for part, masks in enumerate(ORDERS):
-        for at, (mask_0, mask_1) in enumerate(zip(origins(0, masks), origins(1, masks))):
-            source = pieces[part + parts * (at // 8)]
+        found = list(zip(origins(0, masks), origins(1, masks)))
+        for at, (mask_0, mask_1) in enumerate(found[count:] if received else found[:count]):
             mask = jnp.where(place_ref[2] == 0, mask_0, mask_1)
             block = jnp.bitwise_xor(place_ref[0], mask)
-            start = pl.multiple_of((block * parts + part) * depth, depth)
-            value = source[at % 8]
+            start = pl.multiple_of((block * len(ORDERS) + part) * depth, depth)
+            value = pieces[part][at]
             top = value.astype(jnp.bfloat16)
             high[pl.ds(start, depth), :] = top
             low[pl.ds(start, depth), :] = (value - top.astype(jnp.float32)).astype(jnp.bfloat16)
+
+
+def early_kernel(place_ref, *refs):
+    parts = len(ORDERS)
+    for chunk in range(len(WIDTHS)):
+        high, low = refs[parts * len(WIDTHS) + 2 * chunk :][:2]
+        convert(place_ref, refs[parts * chunk :][:parts], high, low, False)
+
+
+def convert_early(own, order, place):
+    in_vmem = pl.BlockSpec(memory_space=pltpu.VMEM)
+    outs = [pltpu.VMEM((order, width), jnp.bfloat16) for width in WIDTHS for _ in range(2)]
+    return pl.pallas_call(
+        early_kernel,
+        out_shape=outs,
+        in_specs=[pl.BlockSpec(memory_space=pltpu.SMEM)] + [in_vmem] * len(own),
+        out_specs=[in_vmem] * len(outs),
+        compiler_params=pltpu.CompilerParams(vmem_limit_bytes=8 * 2**20),
+        cost_estimate=pl.CostEstimate(flops=1, bytes_accessed=1, transcendentals=0),
+        name="convert_early",
+    )(place, *own)
 
 
 def multiply(place_ref, core, a_high, a_low, high, low, total, out_ref):
@@ -139,9 +160,10 @@
 
 
 def other_kernel(place_ref, a_high, a_low, *refs):
-    pieces = refs[: 2 * len(ORDERS)]
-    out_ref, high, low, total = refs[2 * len(ORDERS) :]
-    convert(place_ref, pieces, high, low)
+    parts = len(ORDERS)
+    pieces = refs[:parts]
+    out_ref, high, low, total = refs[parts + 2 :]
+    convert(place_ref, pieces, high, low, True)
     multiply(place_ref, 1 - place_ref[2], a_high, a_low, high, low, total, out_ref)
 
 
@@ -149,7 +171,7 @@
     multiply(place_ref, place_ref[2], a_high, a_low, high, low, total, out_ref)
 
 
-def product(kernel, place, halves, arrays, outs, cost, name):
+def product(kernel, place, halves, arrays, outs, cost, name, aliases):
     in_vmem = pl.BlockSpec(memory_space=pltpu.VMEM)
     halves = [pltpu.with_memory_space_constraint(half, pltpu.VMEM) for half in halves]
     return pl.pallas_call(
@@ -158,6 +180,7 @@
         in_specs=[pl.BlockSpec(memory_space=pltpu.SMEM)] + [in_vmem] * (2 + len(arrays)),
         out_specs=[in_vmem] * len(outs),
         scratch_shapes=[pltpu.VMEM(outs[0].shape, jnp.float32)],
+        input_output_aliases=aliases,
         compiler_params=pltpu.CompilerParams(vmem_limit_bytes=8 * 2**20),
         cost_estimate=pl.CostEstimate(flops=cost, bytes_accessed=cost // 400, transcendentals=0),
         name=name,
@@ -168,9 +191,12 @@
     leaves, _, leaf, order = halves[0].shape
     width = pieces[0].shape[-1]
     outs = [jax.ShapeDtypeStruct((leaves, leaf, width), jnp.float32)]
-    outs += [jax.ShapeDtypeStruct((order, width), jnp.bfloat16)] * 2
+    outs += [pltpu.VMEM((order, width), jnp.bfloat16)] * 2
+    at = 3 + len(ORDERS)
     cost = 6 * leaves * leaf * order * width if last else 1
-    return product(other_kernel, place, halves, pieces, outs, cost, "product_other")
+    return product(
+        other_kernel, place, halves, pieces, outs, cost, "product_other", {at: 1, at + 1: 2}
+    )
 
 
 def product_own(halves, sketch, place, last):
@@ -178,7 +204,7 @@
     width = sketch[0].shape[-1]
     outs = [jax.ShapeDtypeStruct((leaves, leaf, width), jnp.float32)]
     cost = 6 * leaves * leaf * order * width if last else 1
-    return product(own_kernel, place, halves, sketch, outs, cost, "product_own")[0]
+    return product(own_kernel, place, halves, sketch, outs, cost, "product_own", {})[0]
 
 
 def from_x(value, step):
@@ -423,6 +449,13 @@
     chunks, (ranks, pivots), frontal = gather_parts(sketch, frontal, tables, prepare)
     info = jnp.stack([leaf_index]).astype(jnp.int32)
     halves = [part.reshape(SIDE, 2, LEAF, -1) for part in split(frontal)]
+    parts = len(ORDERS)
+    own = [piece for pieces in chunks for piece in pieces[:parts]]
+    own, halves = lax.optimization_barrier((own, halves))
+    early = convert_early(own, halves[0].shape[-1], place)
+    chunks = [
+        [*pieces[parts:], *early[2 * chunk : 2 * chunk + 2]] for chunk, pieces in enumerate(chunks)
+    ]
     groups, core_sum, ready = [], None, ()
     for chunk, pieces in enumerate(chunks):
         last = chunk == len(chunks) - 1
@@ -430,11 +463,10 @@
             place, core_sum = lax.optimization_barrier((place, core_sum))
             group, ready = sum_over_x(core_sum)
             groups.append(group)
-        other, *parts = product_other(halves, pieces, place, last)
+        other, *converted = product_other(halves, pieces, place, last)
         received = from_partner(other, "col", 0)
         place, ready = lax.optimization_barrier((place, ready))
-        core_sum = product_own(halves, parts, place, last) + received
-    core_sum, groups = lax.optimization_barrier((core_sum, groups))
+        core_sum = product_own(halves, converted, place, last) + received
     groups.append(sum_over_x(core_sum)[0])
     tables = (info, ranks, pivots)
     arrays, tops = [], []
@@ -452,6 +484,7 @@
     lower = vmem_call(
         lower_kernel, [square, leaf_cross, square, pair_cross], [], "lower_sums"
     )((), *arrays)
+    tops[0], lower = lax.optimization_barrier((tops[0], lower))
     first = vmem_call(
         upper_kernel,
         [(KMAX, WIDTHS[0]), square, pair_cross],

time: 105 us -> 102 us (0.971)
  starting transfers between devices: 36.2 us -> 28.6 us
  waiting for transfers between devices: 28.3 us -> 32.8 us
  local copies, waits for them, and re-layouts: 3.27 us -> 2.16 us
    ppermute x6, starting transfers between devices: 16.3 us -> 11.5 us  [from_partner(): return lax.ppermute(value, axis, pairs)]
    ppermute x10, starting transfers between devices: 15.4 us -> 12.5 us  [from_row(): return lax.ppermute(value, ('row', 'col'), pairs)]
    ppermute x10, waiting for transfers between devices: 21.2 us -> 23.6 us  [from_row(): return lax.ppermute(value, ('row', 'col'), pairs)]
    ppermute x4, waiting for transfers between devices: 5.28 us -> 7.31 us  [from_x(): return lax.ppermute(value, 'col', pairs)]
    slice x2, local copies, waits for them, and re-layouts: 1.25 us -> 0.14 us  [gather_parts(): other[:, :, columns]]
  transfers between devices with their start and end apart: 20 -> 20, of which waited for: 10 -> 12; matrix products, arithmetic and copies ran while one was open for 1% -> 1% of each run, Pallas kernels for 25% -> 27%
where the time goes in v10:
time: 102 us; the launch traced here: 101 us
  Pallas kernels  35.9 us (35%)
  waiting for transfers between devices  32.8 us (32%)
  starting transfers between devices  28.6 us (28%)
  local copies, waits for them, and re-layouts  2.16 us (2%)
  between operations  1.05 us (1%)
    ppermute x10, waiting for transfers between devices, from_row(): return lax.ppermute(value, ('row', 'col'), pairs)  23.6 us
    pallas_call x4, Pallas kernels, product(): pl.pallas_call(kernel, out_shape=outs, in_specs=[pl.BlockSpec(memory_spac...  14.9 us
    pallas_call x7, Pallas kernels, call(): pl.pallas_call(kernel, out_shape=[jax.ShapeDtypeStruct(shape, jnp.float32...  14.3 us
    ppermute x10, starting transfers between devices, from_row(): return lax.ppermute(value, ('row', 'col'), pairs)  12.5 us
    ppermute x6, starting transfers between devices, from_partner(): return lax.ppermute(value, axis, pairs)  11.5 us
    ppermute x4, waiting for transfers between devices, from_x(): return lax.ppermute(value, 'col', pairs)  7.31 us
    pallas_call x1, Pallas kernels, split(): pl.pallas_call(split_kernel, out_shape=[pltpu.VMEM((rows, order), jnp.bfl...  5.76 us
    ppermute x4, starting transfers between devices, from_x(): return lax.ppermute(value, 'col', pairs)  4.61 us
  transfers between devices with their start and end apart: 20, of which 12 were waited for; matrix products, arithmetic and copies ran while one was open for 1% of the time, Pallas kernels for 27%

profile of v10, /device:TPU:1, one launch (start us, length us, event | category | flops | bytes accessed | tf_op | source)
XLA Modules:
  0.0 101.3 jit_solution(12321397977804476993)
XLA Ops:
  0.6 0.0 copy-start
  0.6 1.1 %slice_bitcast_fusion = (f32[1,96,512]{2,1,0:T(8,128)S(1)}, f32[1,96,512]{2,1,0:T(8,128)S(1)}) fusion(f32[192,512]{1,0:T(8,128)} %param.9), kind=kLoop, calls=%fused_computation.8 | loop fusion | bytes 786432 | tf_op jit(solution)/shard_map/broadcast_in_dim | solution.py:56
  1.7 4.7 %collective-permute-start.2 = (f32[1,96,512]{2,1,0:T(8,128)S(1)}, f32[1,96,512]{2,1,0:T(8,128)S(1)}, u32[]{:S(2)}, u32[]{:S(2)}) collective-permute-start(f32[1,96,512]{2,1,0:T(8,128)S(1)} %get-tuple-element.138), channel_id=1, source_target_pairs={{0,96},{1,25},{2,98},{3,27},{4,100},{5,29},{6,102},{7,31},{8,104},... | collective-permute-start | bytes 589832 | tf_op jit(solution)/shard_map/ppermute | solution.py:44
  6.4 3.3 %collective-permute-done.2 = f32[1,96,512]{2,1,0:T(8,128)S(1)} collective-permute-done((f32[1,96,512]{2,1,0:T(8,128)S(1)}, f32[1,96,512]{2,1,0:T(8,128)S(1)}, u32[]{:S(2)}, u32[]{:S(2)}) %collective-permute-start.2) | collective-permute-done | bytes 196640 | tf_op jit(solution)/shard_map/ppermute | solution.py:44
  9.7 0.1 collective-permute-start.3
  9.8 1.4 %collective-permute-done = f32[1,96,512]{2,1,0:T(8,128)S(1)} collective-permute-done((f32[1,96,512]{2,1,0:T(8,128)S(1)}, f32[1,96,512]{2,1,0:T(8,128)S(1)}, u32[]{:S(2)}, u32[]{:S(2)}) %collective-permute-start) | collective-permute-done | bytes 196640 | tf_op jit(solution)/shard_map/ppermute | solution.py:44
  11.2 0.0 copy-start.1
  11.3 0.0 copy-start.2
  11.3 0.0 copy-start.3
  11.3 1.4 %collective-permute-start.1 = (f32[2,96,512]{2,1,0:T(8,128)S(1)}, f32[2,96,512]{2,1,0:T(8,128)S(1)}, u32[]{:S(2)}, u32[]{:S(2)}) collective-permute-start(f32[2,96,512]{2,1,0:T(8,128)S(1)} %pad_maximum_fusion.6), channel_id=1, source_target_pairs={{0,96},{1,25},{2,98},{3,27},{4,100},{5,29},{6,102},{7,31},{8,104},... | collective-permute-start | bytes 1179656 | tf_op jit(solution)/shard_map/ppermute | solution.py:44
  12.7 4.0 %collective-permute-done.3 = f32[2,96,512]{2,1,0:T(8,128)S(1)} collective-permute-done((f32[2,96,512]{2,1,0:T(8,128)S(1)}, f32[2,96,512]{2,1,0:T(8,128)S(1)}, u32[]{:S(2)}, u32[]{:S(2)}) %collective-permute-start.3) | collective-permute-done | bytes 393248 | tf_op jit(solution)/shard_map/ppermute | solution.py:44
  16.7 2.7 %collective-permute-done.1 = f32[2,96,512]{2,1,0:T(8,128)S(1)} collective-permute-done((f32[2,96,512]{2,1,0:T(8,128)S(1)}, f32[2,96,512]{2,1,0:T(8,128)S(1)}, u32[]{:S(2)}, u32[]{:S(2)}) %collective-permute-start.1) | collective-permute-done | bytes 393248 | tf_op jit(solution)/shard_map/ppermute | solution.py:44
  19.5 0.1 pad_maximum_fusion.1
  19.5 2.4 %collective-permute-start.5 = (f32[4,96,512]{2,1,0:T(8,128)S(1)}, f32[4,96,512]{2,1,0:T(8,128)S(1)}, u32[]{:S(2)}, u32[]{:S(2)}) collective-permute-start(f32[4,96,512]{2,1,0:T(8,128)S(1)} %pad_maximum_fusion.1), channel_id=1, source_target_pairs={{0,24},{1,97},{2,26},{3,99},{4,28},{5,101},{6,30},{7,103},{8,16},{... | collective-permute-start | bytes 2359304 | tf_op jit(solution)/shard_map/ppermute | solution.py:44
  21.9 0.1 pad_maximum_fusion
  22.0 0.1 collective-permute-start.4
  22.2 0.1 pad_add_fusion.1.ranks_ref
  22.3 0.7 constant_dynamic-slice_fusion
  23.0 9.0 %collective-permute-done.5 = f32[4,96,512]{2,1,0:T(8,128)S(1)} collective-permute-done((f32[4,96,512]{2,1,0:T(8,128)S(1)}, f32[4,96,512]{2,1,0:T(8,128)S(1)}, u32[]{:S(2)}, u32[]{:S(2)}) %collective-permute-start.5) | collective-permute-done | bytes 786464 | tf_op jit(solution)/shard_map/ppermute | solution.py:44
  32.0 1.2 %collective-permute-done.4 = f32[4,96,512]{2,1,0:T(8,128)S(1)} collective-permute-done((f32[4,96,512]{2,1,0:T(8,128)S(1)}, f32[4,96,512]{2,1,0:T(8,128)S(1)}, u32[]{:S(2)}, u32[]{:S(2)}) %collective-permute-start.4) | collective-permute-done | bytes 786464 | tf_op jit(solution)/shard_map/ppermute | solution.py:44
  33.2 0.1 fusion.4
  33.3 0.1 fusion.5
  33.4 0.1 fusion.2
  33.4 0.1 fusion.3
  33.5 0.1 pad_maximum_fusion.3.refs_1_
  33.6 0.1 collective-permute-start.7
  33.7 0.1 pad_maximum_fusion.2.refs_0_
  33.7 1.2 %collective-permute-start.6 = (f32[8,96,256]{2,1,0:T(8,128)S(1)}, f32[8,96,256]{2,1,0:T(8,128)}, u32[]{:S(2)}, u32[]{:S(2)}) collective-permute-start(f32[8,96,256]{2,1,0:T(8,128)S(1)} %pad_maximum_fusion.2.refs_0_), channel_id=1, source_target_pairs={{0,24},{1,97},{2,26},{3,99},{4,28},{5,101},{6,30},{7,103},{8,16},{... | collective-permute-start | bytes 2359304 | tf_op jit(solution)/shard_map/ppermute | solution.py:44
  34.9 0.1 pad_maximum_fusion.5.refs_3_
  35.0 0.9 collective-permute-start.14
  35.9 0.1 pad_maximum_fusion.4.refs_2_
  36.0 1.7 %collective-permute-start.13 = (f32[8,96,256]{2,1,0:T(8,128)S(1)}, f32[8,96,256]{2,1,0:T(8,128)}, u32[]{:S(2)}, u32[]{:S(2)}) collective-permute-start(f32[8,96,256]{2,1,0:T(8,128)S(1)} %pad_maximum_fusion.4.refs_2_), channel_id=1, source_target_pairs={{0,24},{1,97},{2,26},{3,99},{4,28},{5,101},{6,30},{7,103},{8,16},{... | collective-permute-start | bytes 2359304 | tf_op jit(solution)/shard_map/ppermute | solution.py:44
  37.6 0.1 pad_add_fusion.2.place_ref
  37.7 5.8 %split.1 = (bf16[1024,3072]{1,0:T(8,128)(2,1)S(1)}, bf16[1024,3072]{1,0:T(8,128)(2,1)S(1)}) custom-call(f32[1024,3072]{1,0:T(8,128)} %refs_3_, f32[1024,3072]{1,0:T(8,128)} %refs_3_, f32[1024,3072]{1,0:T(8,128)} %refs_3_, f32[1024,3072]{1,0:T(8,128)} %refs_3_), custom_call_target="tpu_custom_call" | custom-call | flops 12582912 | bytes 25165824 | tf_op jit(solution)/shard_map/split/pallas_call | solution.py:97
  43.5 0.9 convert_early.1
  44.4 0.5 collective-permute-done.7.refs_1_
  44.9 1.4 %collective-permute-done.6.refs_0_ = f32[8,96,256]{2,1,0:T(8,128)} collective-permute-done((f32[8,96,256]{2,1,0:T(8,128)S(1)}, f32[8,96,256]{2,1,0:T(8,128)}, u32[]{:S(2)}, u32[]{:S(2)}) %collective-permute-start.6) | collective-permute-done | bytes 786464 | tf_op jit(solution)/shard_map/ppermute | solution.py:44
  46.3 4.2 %product_other.2 = (f32[4,128,256]{2,1,0:T(8,128)S(1)}, bf16[3072,256]{1,0:T(8,128)(2,1)S(1)}, bf16[3072,256]{1,0:T(8,128)(2,1)S(1)}) custom-call(s32[3]{0:T(128)S(1)} %pad_add_fusion.2.place_ref, bf16[4,2,128,3072]{3,2,1,0:T(8,128)(2,1)S(1)} %bitcast.27, bf16[4,2,128,3072]{3,2,1,0:T(8,128)(2,1)S(1)} %bitcast.31, ...), custom_call_target="tpu_custom_call", output_to_operand_aliasing={{1}: (5, {}), {2}: (6, {})} | custom-call | flops 1 | tf_op jit(solution)/shard_map/product_other/pallas_call | solution.py:177
  50.5 5.2 %collective-permute-start.8 = (f32[4,128,256]{2,1,0:T(8,128)S(1)}, f32[4,128,256]{2,1,0:T(8,128)S(1)}, u32[]{:S(2)}, u32[]{:S(2)}) collective-permute-start(f32[4,128,256]{2,1,0:T(8,128)S(1)} %get-tuple-element.92), channel_id=1, source_target_pairs={{0,1},{1,0},{2,3},{3,2},{4,5},{5,4},{6,7},{7,6},{8,9},{9,8},{10,11... | collective-permute-start | bytes 1572872 | tf_op jit(solution)/shard_map/ppermute | solution.py:21
  55.7 3.2 %product_own.2 = f32[4,128,256]{2,1,0:T(8,128)S(1)} custom-call(s32[3]{0:T(128)S(1)} %pad_add_fusion.2.place_ref, bf16[4,2,128,3072]{3,2,1,0:T(8,128)(2,1)S(1)} %bitcast.28, bf16[4,2,128,3072]{3,2,1,0:T(8,128)(2,1)S(1)} %bitcast.32, bf16[3072,256]{1,0:T(8,128)(2,1)S(1)} %get-tuple-element.90.high, bf16[3072,256]{1,0:T(8,128)(2,1)S(1)} %get-tuple-element.91.low), custom_call_target="tpu_custom_call" | custom-call | flops 1 | tf_op jit(solution)/shard_map/product_own/pallas_call | solution.py:177
  58.9 0.1 add.45
  59.0 2.6 %collective-permute-start.9 = (f32[2,128,256]{2,1,0:T(8,128)S(1)}, f32[2,128,256]{2,1,0:T(8,128)S(1)}, u32[]{:S(2)}, u32[]{:S(2)}) collective-permute-start(f32[2,128,256]{2,1,0:T(8,128)S(1)} %slice.86), channel_id=1, source_target_pairs={{0,2},{1,7},{2,0},{3,5},{4,6},{5,3},{6,4},{7,1},{8,10},{9,15},{10,... | collective-permute-start | bytes 786440 | tf_op jit(solution)/shard_map/ppermute | solution.py:215
  61.5 4.2 %product_other.3 = (f32[4,128,256]{2,1,0:T(8,128)S(1)}, bf16[3072,256]{1,0:T(8,128)(2,1)S(1)}, bf16[3072,256]{1,0:T(8,128)(2,1)S(1)}) custom-call(s32[3]{0:T(128)S(1)} %pad_add_fusion.2.place_ref, bf16[4,2,128,3072]{3,2,1,0:T(8,128)(2,1)S(1)} %bitcast.29, bf16[4,2,128,3072]{3,2,1,0:T(8,128)(2,1)S(1)} %bitcast.33, ...), custom_call_target="tpu_custom_call", output_to_operand_aliasing={{1}: (5, {}), {2}: (6, {})} | custom-call | flops 2415919104 | bytes 6039797 | tf_op jit(solution)/shard_map/product_other/pallas_call | solution.py:177
  65.8 0.3 collective-permute-start.15
  66.1 3.2 %product_own.3 = f32[4,128,256]{2,1,0:T(8,128)S(1)} custom-call(s32[3]{0:T(128)S(1)} %pad_add_fusion.2.place_ref, bf16[4,2,128,3072]{3,2,1,0:T(8,128)(2,1)S(1)} %bitcast.30, bf16[4,2,128,3072]{3,2,1,0:T(8,128)(2,1)S(1)} %bitcast.34, bf16[3072,256]{1,0:T(8,128)(2,1)S(1)} %get-tuple-element.102.high, bf16[3072,256]{1,0:T(8,128)(2,1)S(1)} %get-tuple-element.103.low), custom_call_target="tpu_custom_call" | custom-call | flops 2415919104 | bytes 6039797 | tf_op jit(solution)/shard_map/product_own/pallas_call | solution.py:177
  69.3 0.1 add.48
  69.4 2.0 %collective-permute-start.16 = (f32[2,128,256]{2,1,0:T(8,128)S(1)}, f32[2,128,256]{2,1,0:T(8,128)S(1)}, u32[]{:S(2)}, u32[]{:S(2)}) collective-permute-start(f32[2,128,256]{2,1,0:T(8,128)S(1)} %slice.98), channel_id=1, source_target_pairs={{0,2},{1,7},{2,0},{3,5},{4,6},{5,3},{6,4},{7,1},{8,10},{9,15},{10,... | collective-permute-start | bytes 786440 | tf_op jit(solution)/shard_map/ppermute | solution.py:215
  71.4 6.2 %collective-permute-done.16 = f32[2,128,256]{2,1,0:T(8,128)S(1)} collective-permute-done((f32[2,128,256]{2,1,0:T(8,128)S(1)}, f32[2,128,256]{2,1,0:T(8,128)S(1)}, u32[]{:S(2)}, u32[]{:S(2)}) %collective-permute-start.16) | collective-permute-done | bytes 262176 | tf_op jit(solution)/shard_map/ppermute | solution.py:215
  77.6 0.1 collective-permute-start.17
  77.7 0.8 leaf_rows.2
  78.6 1.9 %collective-permute-start.11 = (f32[96,256]{1,0:T(8,128)S(1)}, f32[96,256]{1,0:T(8,128)S(1)}, u32[]{:S(2)}, u32[]{:S(2)}) collective-permute-start(f32[96,256]{1,0:T(8,128)S(1)} %get-tuple-element.94.own_ref.refs_1_), channel_id=1, source_target_pairs={{0,1},{1,0},{2,3},{3,2},{4,5},{5,4},{6,7},{7,6},{8,9},{9,8},{10,11... | collective-permute-start | bytes 294920 | tf_op jit(solution)/shard_map/ppermute | solution.py:21
  80.4 1.1 %collective-permute-done.17.refs_2_ = f32[128,256]{1,0:T(8,128)S(1)} collective-permute-done((f32[128,256]{1,0:T(8,128)S(1)}, f32[128,256]{1,0:T(8,128)S(1)}, u32[]{:S(2)}, u32[]{:S(2)}) %collective-permute-start.17) | collective-permute-done | bytes 131104 | tf_op jit(solution)/shard_map/ppermute | solution.py:215
  81.5 0.8 leaf_rows.3
  82.4 2.6 %collective-permute-start.18 = (f32[96,256]{1,0:T(8,128)S(1)}, f32[96,256]{1,0:T(8,128)S(1)}, u32[]{:S(2)}, u32[]{:S(2)}) collective-permute-start(f32[96,256]{1,0:T(8,128)S(1)} %get-tuple-element.106.own_ref.refs_5_), channel_id=1, source_target_pairs={{0,1},{1,0},{2,3},{3,2},{4,5},{5,4},{6,7},{7,6},{8,9},{9,8},{10,11... | collective-permute-start | bytes 294920 | tf_op jit(solution)/shard_map/ppermute | solution.py:21
  85.0 0.8 mid_rows.2
  85.8 0.1 collective-permute-start.12
  85.9 0.0 collective-permute-done.18.other_ref
  85.9 0.8 mid_rows.3
  86.7 1.5 %collective-permute-start.19 = (f32[96,256]{1,0:T(8,128)S(1)}, f32[96,256]{1,0:T(8,128)S(1)}, u32[]{:S(2)}, u32[]{:S(2)}) collective-permute-start(f32[96,256]{1,0:T(8,128)S(1)} %get-tuple-element.108.refs_7_.own_ref), channel_id=1, source_target_pairs={{0,2},{1,3},{2,0},{3,1},{4,6},{5,7},{6,4},{7,5},{8,10},{9,11},{10,... | collective-permute-start | bytes 294920 | tf_op jit(solution)/shard_map/ppermute | solution.py:21
  88.3 1.0 lower_sums.1
  89.2 1.0 %collective-permute-done.12.cousin_ref = f32[96,256]{1,0:T(8,128)S(1)} collective-permute-done((f32[96,256]{1,0:T(8,128)S(1)}, f32[96,256]{1,0:T(8,128)S(1)}, u32[]{:S(2)}, u32[]{:S(2)}) %collective-permute-start.12) | collective-permute-done | bytes 98336 | tf_op jit(solution)/shard_map/ppermute | solution.py:21
  90.3 1.2 %upper_sums.1 = (f32[96,256]{1,0:T(8,128)S(1)}, f32[96,96]{1,0:T(8,128)S(1)}, f32[192,96]{1,0:T(8,128)S(1)}) custom-call(s32[1]{0:T(128)} %bitcast.info_ref, s32[224]{0:T(256)S(1)} %pad_add_fusion.1.ranks_ref, s32[3,96]{1,0:T(4,128)S(1)} %pad_add_fusion.pivots_ref, f32[96,256]{1,0:T(8,128)S(1)} %get-tuple-element.117.refs_3_.own_ref, ...), custom_call_target="tpu_custom_call" | custom-call | tf_op jit(solution)/shard_map/upper_sums/pallas_call | solution.py:420
  91.5 0.9 collective-permute-done.19.cousin_ref
  92.4 8.9 %interpolation.1 = (f32[96,128]{1,0:T(8,128)}, f32[96,192]{1,0:T(8,128)}, f32[96,192]{1,0:T(8,128)}, f32[96,512]{1,0:T(8,128)}) custom-call(s32[1]{0:T(128)} %bitcast.info_ref, s32[224]{0:T(256)S(1)} %pad_add_fusion.1.ranks_ref, s32[3,96]{1,0:T(4,128)S(1)} %pad_add_fusion.pivots_ref, f32[96,96]{1,0:T(8,128)S(1)} %get-tuple-element.113.leaf_gram, ...), custom_call_target="tpu_custom_call" | custom-call | tf_op jit(solution)/shard_map/interpolation/pallas_call | solution.py:420
  (21 shorter events, 0.2 us)
Async XLA Ops:
  0.6 21.5 %copy-start = (s32[128,128]{1,0:T(8,128)S(1)}, s32[128,128]{1,0:T(8,128)}, u32[]{:S(2)}) copy-start(s32[128,128]{1,0:T(8,128)} %param.11) | copy-start | bytes 196612
  1.7 8.0 %collective-permute-start.2 = (f32[1,96,512]{2,1,0:T(8,128)S(1)}, f32[1,96,512]{2,1,0:T(8,128)S(1)}, u32[]{:S(2)}, u32[]{:S(2)}) collective-permute-start(f32[1,96,512]{2,1,0:T(8,128)S(1)} %get-tuple-element.138), channel_id=1, source_target_pairs={{0,96},{1,25},{2,98},{3,27},{4,100},{5,29},{6,102},{7,31},{8,104},... | collective-permute-start | bytes 589832 | tf_op jit(solution)/shard_map/ppermute | solution.py:44
  6.4 4.8 %collective-permute-start = (f32[1,96,512]{2,1,0:T(8,128)S(1)}, f32[1,96,512]{2,1,0:T(8,128)S(1)}, u32[]{:S(2)}, u32[]{:S(2)}) collective-permute-start(f32[1,96,512]{2,1,0:T(8,128)S(1)} %get-tuple-element.139), channel_id=1, source_target_pairs={{0,32},{1,9},{2,34},{3,11},{4,36},{5,13},{6,38},{7,15},{8,40},{9,1... | collective-permute-start | bytes 589832 | tf_op jit(solution)/shard_map/ppermute | solution.py:44
  9.7 7.0 %collective-permute-start.3 = (f32[2,96,512]{2,1,0:T(8,128)S(1)}, f32[2,96,512]{2,1,0:T(8,128)S(1)}, u32[]{:S(2)}, u32[]{:S(2)}) collective-permute-start(f32[2,96,512]{2,1,0:T(8,128)S(1)} %pad_maximum_fusion.7), channel_id=1, source_target_pairs={{0,32},{1,9},{2,34},{3,11},{4,36},{5,13},{6,38},{7,15},{8,40},{9,1... | collective-permute-start | bytes 1179656 | tf_op jit(solution)/shard_map/ppermute | solution.py:44
  11.2 10.9 %copy-start.1 = (s32[32]{0:T(128)S(1)}, s32[32]{0:T(128)}, u32[]{:S(2)}) copy-start(s32[32]{0:T(128)} %param.14) | copy-start | bytes 388
  11.3 10.9 %copy-start.2 = (s32[64]{0:T(128)S(1)}, s32[64]{0:T(128)}, u32[]{:S(2)}) copy-start(s32[64]{0:T(128)} %param.12) | copy-start | bytes 772
  11.3 10.9 %copy-start.3 = (s32[128]{0:T(128)S(1)}, s32[128]{0:T(128)}, u32[]{:S(2)}) copy-start(s32[128]{0:T(128)} %param.10) | copy-start | bytes 1540
  11.3 8.2 %collective-permute-start.1 = (f32[2,96,512]{2,1,0:T(8,128)S(1)}, f32[2,96,512]{2,1,0:T(8,128)S(1)}, u32[]{:S(2)}, u32[]{:S(2)}) collective-permute-start(f32[2,96,512]{2,1,0:T(8,128)S(1)} %pad_maximum_fusion.6), channel_id=1, source_target_pairs={{0,96},{1,25},{2,98},{3,27},{4,100},{5,29},{6,102},{7,31},{8,104},... | collective-permute-start | bytes 1179656 | tf_op jit(solution)/shard_map/ppermute | solution.py:44
  19.5 12.4 %collective-permute-start.5 = (f32[4,96,512]{2,1,0:T(8,128)S(1)}, f32[4,96,512]{2,1,0:T(8,128)S(1)}, u32[]{:S(2)}, u32[]{:S(2)}) collective-permute-start(f32[4,96,512]{2,1,0:T(8,128)S(1)} %pad_maximum_fusion.1), channel_id=1, source_target_pairs={{0,24},{1,97},{2,26},{3,99},{4,28},{5,101},{6,30},{7,103},{8,16},{... | collective-permute-start | bytes 2359304 | tf_op jit(solution)/shard_map/ppermute | solution.py:44
  22.0 11.2 %collective-permute-start.4 = (f32[4,96,512]{2,1,0:T(8,128)S(1)}, f32[4,96,512]{2,1,0:T(8,128)S(1)}, u32[]{:S(2)}, u32[]{:S(2)}) collective-permute-start(f32[4,96,512]{2,1,0:T(8,128)S(1)} %pad_maximum_fusion), channel_id=1, source_target_pairs={{0,8},{1,33},{2,10},{3,35},{4,12},{5,37},{6,14},{7,39},{8,0},{9,41... | collective-permute-start | bytes 2359304 | tf_op jit(solution)/shard_map/ppermute | solution.py:44
  33.6 11.3 %collective-permute-start.7 = (f32[8,96,256]{2,1,0:T(8,128)S(1)}, f32[8,96,256]{2,1,0:T(8,128)}, u32[]{:S(2)}, u32[]{:S(2)}) collective-permute-start(f32[8,96,256]{2,1,0:T(8,128)S(1)} %pad_maximum_fusion.3.refs_1_), channel_id=1, source_target_pairs={{0,8},{1,33},{2,10},{3,35},{4,12},{5,37},{6,14},{7,39},{8,0},{9,41... | collective-permute-start | bytes 2359304 | tf_op jit(solution)/shard_map/ppermute | solution.py:44
  33.7 12.5 %collective-permute-start.6 = (f32[8,96,256]{2,1,0:T(8,128)S(1)}, f32[8,96,256]{2,1,0:T(8,128)}, u32[]{:S(2)}, u32[]{:S(2)}) collective-permute-start(f32[8,96,256]{2,1,0:T(8,128)S(1)} %pad_maximum_fusion.2.refs_0_), channel_id=1, source_target_pairs={{0,24},{1,97},{2,26},{3,99},{4,28},{5,101},{6,30},{7,103},{8,16},{... | collective-permute-start | bytes 2359304 | tf_op jit(solution)/shard_map/ppermute | solution.py:44
  35.0 26.6 %collective-permute-start.14 = (f32[8,96,256]{2,1,0:T(8,128)S(1)}, f32[8,96,256]{2,1,0:T(8,128)}, u32[]{:S(2)}, u32[]{:S(2)}) collective-permute-start(f32[8,96,256]{2,1,0:T(8,128)S(1)} %pad_maximum_fusion.5.refs_3_), channel_id=1, source_target_pairs={{0,8},{1,33},{2,10},{3,35},{4,12},{5,37},{6,14},{7,39},{8,0},{9,41... | collective-permute-start | bytes 2359304 | tf_op jit(solution)/shard_map/ppermute | solution.py:44
  36.0 25.6 %collective-permute-start.13 = (f32[8,96,256]{2,1,0:T(8,128)S(1)}, f32[8,96,256]{2,1,0:T(8,128)}, u32[]{:S(2)}, u32[]{:S(2)}) collective-permute-start(f32[8,96,256]{2,1,0:T(8,128)S(1)} %pad_maximum_fusion.4.refs_2_), channel_id=1, source_target_pairs={{0,24},{1,97},{2,26},{3,99},{4,28},{5,101},{6,30},{7,103},{8,16},{... | collective-permute-start | bytes 2359304 | tf_op jit(solution)/shard_map/ppermute | solution.py:44
  50.5 8.4 %collective-permute-start.8 = (f32[4,128,256]{2,1,0:T(8,128)S(1)}, f32[4,128,256]{2,1,0:T(8,128)S(1)}, u32[]{:S(2)}, u32[]{:S(2)}) collective-permute-start(f32[4,128,256]{2,1,0:T(8,128)S(1)} %get-tuple-element.92), channel_id=1, source_target_pairs={{0,1},{1,0},{2,3},{3,2},{4,5},{5,4},{6,7},{7,6},{8,9},{9,8},{10,11... | collective-permute-start | bytes 1572872 | tf_op jit(solution)/shard_map/ppermute | solution.py:21
  59.0 7.1 %collective-permute-start.9 = (f32[2,128,256]{2,1,0:T(8,128)S(1)}, f32[2,128,256]{2,1,0:T(8,128)S(1)}, u32[]{:S(2)}, u32[]{:S(2)}) collective-permute-start(f32[2,128,256]{2,1,0:T(8,128)S(1)} %slice.86), channel_id=1, source_target_pairs={{0,2},{1,7},{2,0},{3,5},{4,6},{5,3},{6,4},{7,1},{8,10},{9,15},{10,... | collective-permute-start | bytes 786440 | tf_op jit(solution)/shard_map/ppermute | solution.py:215
  65.8 3.5 %collective-permute-start.15 = (f32[4,128,256]{2,1,0:T(8,128)S(1)}, f32[4,128,256]{2,1,0:T(8,128)S(1)}, u32[]{:S(2)}, u32[]{:S(2)}) collective-permute-start(f32[4,128,256]{2,1,0:T(8,128)S(1)} %get-tuple-element.104), channel_id=1, source_target_pairs={{0,1},{1,0},{2,3},{3,2},{4,5},{5,4},{6,7},{7,6},{8,9},{9,8},{10,11... | collective-permute-start | bytes 1572872 | tf_op jit(solution)/shard_map/ppermute | solution.py:21
  69.4 8.2 %collective-permute-start.16 = (f32[2,128,256]{2,1,0:T(8,128)S(1)}, f32[2,128,256]{2,1,0:T(8,128)S(1)}, u32[]{:S(2)}, u32[]{:S(2)}) collective-permute-start(f32[2,128,256]{2,1,0:T(8,128)S(1)} %slice.98), channel_id=1, source_target_pairs={{0,2},{1,7},{2,0},{3,5},{4,6},{5,3},{6,4},{7,1},{8,10},{9,15},{10,... | collective-permute-start | bytes 786440 | tf_op jit(solution)/shard_map/ppermute | solution.py:215
  71.4 6.3 %collective-permute-start.10 = (f32[128,256]{1,0:T(8,128)S(1)}, f32[128,256]{1,0:T(8,128)S(1)}, u32[]{:S(2)}, u32[]{:S(2)}) collective-permute-start(f32[128,256]{1,0:T(8,128)S(1)} %get-tuple-element.136), channel_id=1, source_target_pairs={{0,6},{1,3},{2,4},{3,1},{4,2},{5,7},{6,0},{7,5},{8,14},{9,11},{10,... | collective-permute-start | bytes 393224 | tf_op jit(solution)/shard_map/ppermute | solution.py:215
  77.6 3.9 %collective-permute-start.17 = (f32[128,256]{1,0:T(8,128)S(1)}, f32[128,256]{1,0:T(8,128)S(1)}, u32[]{:S(2)}, u32[]{:S(2)}) collective-permute-start(f32[128,256]{1,0:T(8,128)S(1)} %get-tuple-element.134), channel_id=1, source_target_pairs={{0,6},{1,3},{2,4},{3,1},{4,2},{5,7},{6,0},{7,5},{8,14},{9,11},{10,... | collective-permute-start | bytes 393224 | tf_op jit(solution)/shard_map/ppermute | solution.py:215
  78.6 6.4 %collective-permute-start.11 = (f32[96,256]{1,0:T(8,128)S(1)}, f32[96,256]{1,0:T(8,128)S(1)}, u32[]{:S(2)}, u32[]{:S(2)}) collective-permute-start(f32[96,256]{1,0:T(8,128)S(1)} %get-tuple-element.94.own_ref.refs_1_), channel_id=1, source_target_pairs={{0,1},{1,0},{2,3},{3,2},{4,5},{5,4},{6,7},{7,6},{8,9},{9,8},{10,11... | collective-permute-start | bytes 294920 | tf_op jit(solution)/shard_map/ppermute | solution.py:21
  82.4 3.6 %collective-permute-start.18 = (f32[96,256]{1,0:T(8,128)S(1)}, f32[96,256]{1,0:T(8,128)S(1)}, u32[]{:S(2)}, u32[]{:S(2)}) collective-permute-start(f32[96,256]{1,0:T(8,128)S(1)} %get-tuple-element.106.own_ref.refs_5_), channel_id=1, source_target_pairs={{0,1},{1,0},{2,3},{3,2},{4,5},{5,4},{6,7},{7,6},{8,9},{9,8},{10,11... | collective-permute-start | bytes 294920 | tf_op jit(solution)/shard_map/ppermute | solution.py:21
  85.8 4.5 %collective-permute-start.12 = (f32[96,256]{1,0:T(8,128)S(1)}, f32[96,256]{1,0:T(8,128)S(1)}, u32[]{:S(2)}, u32[]{:S(2)}) collective-permute-start(f32[96,256]{1,0:T(8,128)S(1)} %get-tuple-element.117.refs_3_.own_ref), channel_id=1, source_target_pairs={{0,2},{1,3},{2,0},{3,1},{4,6},{5,7},{6,4},{7,5},{8,10},{9,11},{10,... | collective-permute-start | bytes 294920 | tf_op jit(solution)/shard_map/ppermute | solution.py:21
  86.7 5.7 %collective-permute-start.19 = (f32[96,256]{1,0:T(8,128)S(1)}, f32[96,256]{1,0:T(8,128)S(1)}, u32[]{:S(2)}, u32[]{:S(2)}) collective-permute-start(f32[96,256]{1,0:T(8,128)S(1)} %get-tuple-element.108.refs_7_.own_ref), channel_id=1, source_target_pairs={{0,2},{1,3},{2,0},{3,1},{4,6},{5,7},{6,4},{7,5},{8,10},{9,11},{10,... | collective-permute-start | bytes 294920 | tf_op jit(solution)/shard_map/ppermute | solution.py:21
